TPU v7x, 32 devices: a whole 2x2x4 slice. The times are simulated.
32 devices in a mesh: gx: 4 (over z), gy: 2 (over y), gz: 4 (over x, core).
Axes of the slice: x: 2, y: 2, z: 4, core: 2. Of those that a mesh axis runs over, the one named last changes fastest.
Arguments:
- field: float32 [32, 512, 256], P('gz', 'gx', 'gy'), may hold values from -6 to 6
Outputs:
- coeffs_fine: float32 [32, 512, 256], P('gz', 'gx', 'gy')
- coeffs_middle: float32 [16, 256, 128], P('gz', 'gx', 'gy')
- coeffs_coarse: float32 [8, 128, 64], P('gz', 'gx', 'gy')
- coarsest: float32 [4, 64, 32], P('gz', 'gx', 'gy')
All inputs are finite; a program needn't handle non-finite values.
Results may differ from a plain program's by a relative error of at most 0.0003.
Values sent between devices are 32-bit elements; how exact they have to be, the bound alone decides.
No kernel may reach another device: no remote copies, remote signals or barrier semaphores. Data moves between devices by JAX's collectives and lax.ppermute only.
A program may use at most 64 MiB of HBM per device.

v0:
```python
import math

import jax
import jax.numpy as jnp
import numpy as np
from jax import lax
from jax.sharding import PartitionSpec as P

band_ratio = 2.0 - math.sqrt(3.0)


def passed_along(value, axis, steps):
    count = lax.axis_size(axis)
    leading, last = (max(0, -steps), min(count, count - steps))
    return lax.ppermute(value, axis, [(source, source + steps) for source in range(leading, last)])


def with_halo(cells, sides, width):
    for axis, dim in sides:
        count = lax.axis_size(axis)
        ends = count - 1
        head = lax.slice_in_dim(cells, 0, width, axis=dim)
        tail = lax.slice_in_dim(cells, cells.shape[dim] - width, cells.shape[dim], axis=dim)
        cells = jnp.concatenate(
            [
                lax.ppermute(tail, axis, [(i, (i + 1) % count) for i in range(ends)]),
                cells,
                lax.ppermute(head, axis, [((i + 1) % count, i) for i in range(ends)]),
            ],
            axis=dim,
        )
    return cells


def prefix(part, axis, combine, identity, reverse):
    count = lax.axis_size(axis)
    place = lax.axis_index(axis)
    ahead = count - 1 - place if reverse else place
    gathered = jax.tree.map(lambda a: lax.all_gather(a, axis), part)
    state = jax.tree.map(lambda a, e: jnp.zeros_like(a) + jnp.asarray(e, a.dtype), part, identity)

    def one(turn, state):
        source = count - 1 - turn if reverse else turn
        return combine(
            state, jax.tree.map(lambda a: lax.dynamic_index_in_dim(a, source, 0, False), gathered)
        )

    return lax.fori_loop(0, ahead, one, state)


def along_shape(length, dimension):
    new_shape = [1, 1, 1]
    new_shape[dimension] = length
    return new_shape


def position_of(dimension):
    if dimension == 0:
        return (lax.axis_index("gz"), lax.axis_size("gz"))
    if dimension == 1:
        return (lax.axis_index("gx"), lax.axis_size("gx"))
    return (lax.axis_index("gy"), lax.axis_size("gy"))


def from_next(boundary, dimension):
    if dimension == 0:
        return passed_along(boundary, "gz", -1)
    if dimension == 1:
        return passed_along(boundary, "gx", -1)
    return passed_along(boundary, "gy", -1)


def from_previous(boundary, dimension):
    if dimension == 0:
        return passed_along(boundary, "gz", 1)
    if dimension == 1:
        return passed_along(boundary, "gx", 1)
    return passed_along(boundary, "gy", 1)


def rim_single(values, dimension):
    if dimension == 0:
        return with_halo(values, (("gz", 0),), 1)
    if dimension == 1:
        return with_halo(values, (("gx", 1),), 1)
    return with_halo(values, (("gy", 2),), 1)


def link_maps(earlier, latter):
    return (earlier[0] * latter[0], latter[0] * earlier[1] + latter[1])


def scan_along(affine, dimension, backward):
    identity = (jnp.ones((), jnp.float32), jnp.zeros_like(affine[1]))
    if dimension == 0:
        if backward:
            return prefix(affine, "gz", link_maps, identity, True)
        return prefix(affine, "gz", link_maps, identity, False)
    if dimension == 1:
        if backward:
            return prefix(affine, "gx", link_maps, identity, True)
        return prefix(affine, "gx", link_maps, identity, False)
    if backward:
        return prefix(affine, "gy", link_maps, identity, True)
    return prefix(affine, "gy", link_maps, identity, False)


def carried_in(boundary, dimension, half_len, backward):
    factor = jnp.full((), (-band_ratio) ** half_len, jnp.float32)
    return scan_along((factor, boundary), dimension, backward)[1]


def lower_table(length):
    rows_index = np.arange(length)[:, None]
    cols_index = np.arange(length)[None, :]
    powers = np.maximum(rows_index - cols_index, 0)
    return np.where(rows_index >= cols_index, np.power(-band_ratio, powers), 0.0).astype(np.float32)


def apply_along(source, table, dimension):
    letters = ["a", "b", "c"]
    source_spec = "".join(letters)
    letters[dimension] = "k"
    target_spec = "".join(letters)
    formula = "k" + source_spec[dimension] + "," + source_spec + "->" + target_spec
    return jnp.einsum(formula, jnp.asarray(table), source, precision=lax.Precision.HIGHEST)


def prolong(coarse, dimension):
    length = coarse.shape[dimension]
    first_row = lax.slice_in_dim(coarse, 0, 1, axis=dimension)
    last_row = lax.slice_in_dim(coarse, length - 1, length, axis=dimension)
    arrived = from_next(first_row, dimension)
    own_index, axis_count = position_of(dimension)
    arrived = jnp.where(own_index == axis_count - 1, last_row, arrived)
    following = jnp.concatenate(
        [lax.slice_in_dim(coarse, 1, length, axis=dimension), arrived], axis=dimension
    )
    middle = 0.5 * (coarse + following)
    stacked = jnp.stack([coarse, middle], axis=dimension + 1)
    new_shape = list(coarse.shape)
    new_shape[dimension] = 2 * length
    return stacked.reshape(new_shape)


def restrict_mass(coeffs, dimension):
    length = coeffs.shape[dimension]
    own_index, axis_count = position_of(dimension)
    padded = rim_single(coeffs, dimension)
    mass = (
        lax.slice_in_dim(padded, 0, length, axis=dimension)
        + 4.0 * lax.slice_in_dim(padded, 1, length + 1, axis=dimension)
        + lax.slice_in_dim(padded, 2, length + 2, axis=dimension)
    )
    earlier_mass = from_previous(
        lax.slice_in_dim(mass, length - 1, length, axis=dimension), dimension
    )
    even_part = lax.slice_in_dim(mass, 0, length, 2, dimension)
    odd_part = lax.slice_in_dim(mass, 1, length, 2, dimension)
    half_len = length // 2
    last_weight = jnp.where(own_index == axis_count - 1, 1.0, 0.5)
    weights = (
        jnp.where(jnp.arange(half_len) == half_len - 1, last_weight, 0.5)
        .astype(jnp.float32)
        .reshape(along_shape(half_len, dimension))
    )
    earlier = jnp.concatenate(
        [earlier_mass, lax.slice_in_dim(odd_part, 0, half_len - 1, axis=dimension)], axis=dimension
    )
    return 0.5 * band_ratio * (even_part + weights * odd_part + 0.5 * earlier)


def solve_band(source, dimension):
    half_len = source.shape[dimension]
    table = lower_table(half_len)
    local_lower = apply_along(source, table, dimension)
    entering = carried_in(
        lax.slice_in_dim(local_lower, half_len - 1, half_len, axis=dimension),
        dimension,
        half_len,
        False,
    )
    growth = (
        np.power(-band_ratio, np.arange(1, half_len + 1))
        .astype(np.float32)
        .reshape(along_shape(half_len, dimension))
    )
    lower = local_lower + jnp.asarray(growth) * entering
    local_upper = apply_along(lower, table.T, dimension)
    entering_back = carried_in(
        lax.slice_in_dim(local_upper, 0, 1, axis=dimension), dimension, half_len, True
    )
    decline = (
        np.power(-band_ratio, np.arange(half_len, 0, -1))
        .astype(np.float32)
        .reshape(along_shape(half_len, dimension))
    )
    return local_upper + jnp.asarray(decline) * entering_back


def whole_prolong(coarse, dimension):
    length = coarse.shape[dimension]
    following = jnp.concatenate(
        [
            lax.slice_in_dim(coarse, 1, length, axis=dimension),
            lax.slice_in_dim(coarse, length - 1, length, axis=dimension),
        ],
        axis=dimension,
    )
    middle = 0.5 * (coarse + following)
    stacked = jnp.stack([coarse, middle], axis=dimension + 1)
    new_shape = list(coarse.shape)
    new_shape[dimension] = 2 * length
    return stacked.reshape(new_shape)


def whole_restrict(coeffs, dimension):
    length = coeffs.shape[dimension]
    widths = [(0, 0), (0, 0), (0, 0)]
    widths[dimension] = (1, 1)
    padded = jnp.pad(coeffs, widths)
    mass = (
        lax.slice_in_dim(padded, 0, length, axis=dimension)
        + 4.0 * lax.slice_in_dim(padded, 1, length + 1, axis=dimension)
        + lax.slice_in_dim(padded, 2, length + 2, axis=dimension)
    )
    even_part = lax.slice_in_dim(mass, 0, length, 2, dimension)
    odd_part = lax.slice_in_dim(mass, 1, length, 2, dimension)
    half_len = length // 2
    weights = (
        jnp.where(jnp.arange(half_len) == half_len - 1, 1.0, 0.5)
        .astype(jnp.float32)
        .reshape(along_shape(half_len, dimension))
    )
    earlier = jnp.concatenate(
        [
            jnp.zeros_like(lax.slice_in_dim(odd_part, 0, 1, axis=dimension)),
            lax.slice_in_dim(odd_part, 0, half_len - 1, axis=dimension),
        ],
        axis=dimension,
    )
    return 0.5 * band_ratio * (even_part + weights * odd_part + 0.5 * earlier)


def whole_solve(source, dimension):
    table = lower_table(source.shape[dimension])
    return apply_along(apply_along(source, table, dimension), table.T, dimension)


def spread_level(current):
    coarse = current[::2, ::2, ::2]
    interp = prolong(prolong(prolong(coarse, 2), 1), 0)
    coeffs = current - interp
    correction = coeffs
    for dimension in (1, 2, 0):
        correction = solve_band(restrict_mass(correction, dimension), dimension)
    return (coeffs, coarse + correction)


def gathered_level(current):
    block_shape = current.shape
    whole = lax.all_gather(current, "gz", axis=0, tiled=True)
    whole = lax.all_gather(whole, "gx", axis=1, tiled=True)
    whole = lax.all_gather(whole, "gy", axis=2, tiled=True)
    coarse = whole[::2, ::2, ::2]
    interp = whole_prolong(whole_prolong(whole_prolong(coarse, 2), 1), 0)
    coeffs = whole - interp
    correction = coeffs
    for dimension in (1, 2, 0):
        correction = whole_solve(whole_restrict(correction, dimension), dimension)
    updated = coarse + correction
    plane_start = lax.axis_index("gz") * block_shape[0]
    xline_start = lax.axis_index("gx") * block_shape[1]
    yline_start = lax.axis_index("gy") * block_shape[2]
    own_coeffs = lax.dynamic_slice(coeffs, (plane_start, xline_start, yline_start), block_shape)
    half_shape = (block_shape[0] // 2, block_shape[1] // 2, block_shape[2] // 2)
    own_updated = lax.dynamic_slice(
        updated, (plane_start // 2, xline_start // 2, yline_start // 2), half_shape
    )
    return (own_coeffs, own_updated)


def shards(field):
    current = field
    results = []
    for level_index in range(3):
        if level_index == 2:
            coeffs, current = gathered_level(current)
        else:
            coeffs, current = spread_level(current)
        results.append(coeffs)
    return (results[0], results[1], results[2], current)


def solution(mesh):
    in_specs = (P("gz", "gx", "gy"),)
    out_specs = (P("gz", "gx", "gy"), P("gz", "gx", "gy"), P("gz", "gx", "gy"), P("gz", "gx", "gy"))
    return jax.shard_map(shards, mesh=mesh, in_specs=in_specs, out_specs=out_specs, check_vma=False)
```

profile of v0, /device:TPU:1, one launch (start us, length us, event | category | flops | bytes accessed | tf_op | source)
XLA Modules:
  0.0 309.3 jit_solution(3527420228288102)
XLA Ops:
  0.6 3.7 %slice.334 = f32[4,64,64]{2,1,0:T(8,128)S(1)} slice(f32[8,128,128]{2,1,0:T(8,128)} %param.55), slice={[0:8:2], [0:128:2], [0:128:2]} | slice | bytes 131072 | tf_op jit(solution)/shard_map/slice | solution.py:251
  10.5 7.4 %collective-permute-done.1 = f32[4,1,128]{1,2,0:T(8,128)S(1)} collective-permute-done((f32[4,1,128]{1,2,0:T(8,128)S(1)}, f32[4,1,128]{1,2,0:T(8,128)S(1)}, u32[]{:S(2)}, u32[]{:S(2)}) %collective-permute-start.1) | collective-permute-done | bytes 2080 | tf_op jit(solution)/shard_map/ppermute | solution.py:15
  18.4 4.4 %collective-permute-start.2 = (f32[1,128,128]{2,1,0:T(8,128)S(1)}, f32[1,128,128]{2,1,0:T(8,128)S(1)}, u32[]{:S(2)}, u32[]{:S(2)}) collective-permute-start(f32[1,128,128]{2,1,0:T(8,128)S(1)} %bitcast.348), channel_id=1, source_target_pairs={{1,0},{2,1},{3,2},{5,4},{6,5},{7,6},{9,8},{10,9},{11,10},{13,12},{... | collective-permute-start | bytes 196616 | tf_op jit(solution)/shard_map/ppermute | solution.py:15
  34.9 3.7 %collective-permute-start.5 = (f32[8,1,128]{2,1,0:T(1,128)S(1)}, f32[8,1,128]{2,1,0:T(1,128)S(1)}, u32[]{:S(2)}, u32[]{:S(2)}) collective-permute-start(f32[8,1,128]{2,1,0:T(1,128)S(1)} %slice.453), channel_id=1, source_target_pairs={{0,8},{8,16},{16,24},{1,9},{9,17},{17,25},{2,10},{10,18},{18,26},{... | collective-permute-start | bytes 12296 | tf_op jit(solution)/shard_map/ppermute | solution.py:15
  38.6 7.9 %all-reduce.13 = (f32[4]{0:T(128)S(1)}, f32[4]{0:T(128)S(1)}) all-reduce(f32[4]{0:T(128)S(1)} %dynamic-update-slice, f32[4]{0:T(128)S(1)} %dynamic-update-slice.3), channel_id=1, replica_groups=mesh['gx'=4,'gy'=2,'gz'=4] {'gx'}, use_global_device_ids=true, to_apply=%add.6 | all-reduce | flops 8 | bytes 64
  48.0 10.2 %all-gather = f32[32,1,128]{2,1,0:T(1,128)S(1)} all-gather(f32[8,1,128]{2,1,0:T(1,128)S(1)} %slice.455), channel_id=2, replica_groups=mesh['gx'=4,'gy'=2,'gz'=4] {'gx'}, dimensions={0}, use_global_device_ids=true | all-gather | bytes 20480 | tf_op jit(solution)/shard_map/all_gather | solution.py:39
  59.4 11.3 %all-gather.1 = f32[32,1,128]{2,1,0:T(1,128)S(1)} all-gather(f32[8,1,128]{2,1,0:T(1,128)S(1)} %slice.456), channel_id=3, replica_groups=mesh['gx'=4,'gy'=2,'gz'=4] {'gx'}, dimensions={0}, use_global_device_ids=true | all-gather | bytes 20480 | tf_op jit(solution)/shard_map/all_gather | solution.py:39
  70.8 3.8 %while.157 = (s32[]{:T(128)}, f32[8,1,128]{2,1,0:T(1,128)S(1)}, s32[]{:T(128)}, f32[4]{0:T(128)S(1)}, f32[4,8,1,128]{3,1,2,0:T(8,128)S(1)}, /*index=5*/s32[]{:T(128)}, s32[]{:T(128)}, s32[]{:T(128)}, s32[]{:T(128)}) while((s32[]{:T(128)}, f32[8,1,128]{2,1,0:T(1,128)S(1)}, s32[]{:T(128)}, f32[4]{0:T(128)S(1)}, f32[4,8,1,128]{3,1,2,0:T(8,128)S(1)}, ...), condition=%wide.region_3.4_spmd, body=%wide.region_2.3_spmd.sunk | while | flops 2054 | bytes 20647 | solution.py:48
  80.6 3.7 %collective-permute-done.7 = f32[8,64,1]{2,1,0:T(8,128)S(1)} collective-permute-done((f32[8,64,1]{2,1,0:T(8,128)S(1)}, f32[8,64,1]{2,1,0:T(8,128)S(1)}, u32[]{:S(2)}, u32[]{:S(2)}) %collective-permute-start.7) | collective-permute-done | bytes 2080 | tf_op jit(solution)/shard_map/ppermute | solution.py:28
  86.2 4.3 %all-reduce.14 = (f32[2]{0:T(128)S(1)}, f32[2]{0:T(128)S(1)}) all-reduce(f32[2]{0:T(128)S(1)} %dynamic-update-slice.1, f32[2]{0:T(128)S(1)} %dynamic-update-slice.4), channel_id=1, replica_groups=mesh['gx'=4,'gy'=2,'gz'=4] {'gy'}, use_global_device_ids=true, to_apply=%add.7 | all-reduce | flops 4 | bytes 32
  90.5 4.5 %slice.361 = f32[8,64,64]{2,1,0:T(8,128)S(1)} slice(f32[8,64,128]{2,1,0:T(8,128)S(1)} %fusion.9), slice={[0:8:1], [0:64:1], [1:128:2]} | slice | bytes 262144 | tf_op jit(solution)/shard_map/slice | solution.py:159
  95.1 4.5 %slice.360 = f32[8,64,64]{2,1,0:T(8,128)S(1)} slice(f32[8,64,128]{2,1,0:T(8,128)S(1)} %fusion.9), slice={[0:8:1], [0:64:1], [0:128:2]} | slice | bytes 262144 | tf_op jit(solution)/shard_map/slice | solution.py:158
  104.6 4.4 %all-gather.3 = f32[16,64,1]{1,2,0:T(1,128)S(1)} all-gather(f32[8,64,1]{1,2,0:T(1,128)S(1)} %slice.462), channel_id=5, replica_groups=mesh['gx'=4,'gy'=2,'gz'=4] {'gy'}, dimensions={0}, use_global_device_ids=true | all-gather | bytes 6144 | tf_op jit(solution)/shard_map/all_gather | solution.py:39
  110.4 13.9 %collective-permute-start.9 = (f32[1,64,64]{1,2,0:T(8,128)S(1)}, f32[1,64,64]{1,2,0:T(8,128)S(1)}, u32[]{:S(2)}, u32[]{:S(2)}) collective-permute-start(f32[1,64,64]{1,2,0:T(8,128)S(1)} %get-tuple-element.1218), channel_id=1, source_target_pairs={{0,1},{1,2},{2,3},{4,5},{5,6},{6,7},{8,9},{9,10},{10,11},{12,13},{... | collective-permute-start | bytes 49160 | tf_op jit(solution)/shard_map/ppermute | solution.py:26
  132.1 5.1 %all-reduce.12 = (f32[4]{0:T(128)S(1)}, f32[4]{0:T(128)S(1)}) all-reduce(f32[4]{0:T(128)S(1)} %dynamic-update-slice.2, f32[4]{0:T(128)S(1)} %dynamic-update-slice.5), channel_id=1, replica_groups=mesh['gx'=4,'gy'=2,'gz'=4] {'gz'}, use_global_device_ids=true, to_apply=%add.8 | all-reduce | flops 8 | bytes 64
  138.4 6.3 %all-gather.4 = f32[4,64,64]{2,1,0:T(8,128)S(1)} all-gather(f32[1,64,64]{2,1,0:T(8,128)S(1)} %bitcast.339), channel_id=6, replica_groups=mesh['gx'=4,'gy'=2,'gz'=4] {'gz'}, dimensions={0}, use_global_device_ids=true | all-gather | bytes 81920 | tf_op jit(solution)/shard_map/all_gather | solution.py:39
  147.3 8.1 %all-gather.5 = f32[4,64,64]{2,1,0:T(8,128)S(1)} all-gather(f32[1,64,64]{2,1,0:T(8,128)S(1)} %bitcast.338), channel_id=7, replica_groups=mesh['gx'=4,'gy'=2,'gz'=4] {'gz'}, dimensions={0}, use_global_device_ids=true | all-gather | bytes 81920 | tf_op jit(solution)/shard_map/all_gather | solution.py:39
  164.9 3.6 %collective-permute-done.13 = f32[2,1,64]{1,2,0:T(8,128)S(1)} collective-permute-done((f32[2,1,64]{1,2,0:T(8,128)S(1)}, f32[2,1,64]{1,2,0:T(8,128)S(1)}, u32[]{:S(2)}, u32[]{:S(2)}) %collective-permute-start.13) | collective-permute-done | bytes 544 | tf_op jit(solution)/shard_map/ppermute | solution.py:15
  168.8 5.6 %collective-permute-start.14 = (f32[1,64,64]{2,1,0:T(8,128)S(1)}, f32[1,64,64]{2,1,0:T(8,128)S(1)}, u32[]{:S(2)}, u32[]{:S(2)}) collective-permute-start(f32[1,64,64]{2,1,0:T(8,128)S(1)} %bitcast.355), channel_id=1, source_target_pairs={{1,0},{2,1},{3,2},{5,4},{6,5},{7,6},{9,8},{10,9},{11,10},{13,12},{... | collective-permute-start | bytes 49160 | tf_op jit(solution)/shard_map/ppermute | solution.py:15
  180.3 3.8 %collective-permute-done.16 = f32[4,1,64]{1,2,0:T(8,128)S(1)} collective-permute-done((f32[4,1,64]{1,2,0:T(8,128)S(1)}, f32[4,1,64]{1,2,0:T(8,128)S(1)}, u32[]{:S(2)}, u32[]{:S(2)}) %collective-permute-start.16) | collective-permute-done | bytes 1056 | tf_op jit(solution)/shard_map/ppermute | solution.py:28
  189.5 9.3 %all-gather.6 = f32[16,1,64]{2,1,0:T(1,128)S(1)} all-gather(f32[4,1,64]{2,1,0:T(1,128)S(1)} %slice.483), channel_id=8, replica_groups=mesh['gx'=4,'gy'=2,'gz'=4] {'gx'}, dimensions={0}, use_global_device_ids=true | all-gather | bytes 5120 | tf_op jit(solution)/shard_map/all_gather | solution.py:39
  199.8 10.4 %all-gather.7 = f32[16,1,64]{2,1,0:T(1,128)S(1)} all-gather(f32[4,1,64]{2,1,0:T(1,128)S(1)} %slice.484), channel_id=9, replica_groups=mesh['gx'=4,'gy'=2,'gz'=4] {'gx'}, dimensions={0}, use_global_device_ids=true | all-gather | bytes 5120 | tf_op jit(solution)/shard_map/all_gather | solution.py:39
  210.1 3.8 %while.163 = (s32[]{:T(128)}, f32[4,1,64]{2,1,0:T(1,128)S(1)}, s32[]{:T(128)}, f32[4]{0:T(128)S(1)}, f32[4,4,1,64]{3,1,2,0:T(4,128)S(1)}, /*index=5*/s32[]{:T(128)}, s32[]{:T(128)}, s32[]{:T(128)}, s32[]{:T(128)}) while((s32[]{:T(128)}, f32[4,1,64]{2,1,0:T(1,128)S(1)}, s32[]{:T(128)}, f32[4]{0:T(128)S(1)}, f32[4,4,1,64]{3,1,2,0:T(4,128)S(1)}, ...), condition=%wide.region_15.16_spmd, body=%wide.region_14.15_spmd.sunk | while | flops 518 | bytes 5287 | solution.py:48
  217.4 3.7 %collective-permute-done.19 = f32[4,32,1]{2,1,0:T(8,128)S(1)} collective-permute-done((f32[4,32,1]{2,1,0:T(8,128)S(1)}, f32[4,32,1]{2,1,0:T(8,128)S(1)}, u32[]{:S(2)}, u32[]{:S(2)}) %collective-permute-start.19) | collective-permute-done | bytes 544 | tf_op jit(solution)/shard_map/ppermute | solution.py:28
  228.5 4.4 %all-gather.9 = f32[8,32,1]{1,2,0:T(1,128)S(1)} all-gather(f32[4,32,1]{1,2,0:T(1,128)S(1)} %slice.490), channel_id=11, replica_groups=mesh['gx'=4,'gy'=2,'gz'=4] {'gy'}, dimensions={0}, use_global_device_ids=true | all-gather | bytes 1536 | tf_op jit(solution)/shard_map/all_gather | solution.py:39
  234.2 11.5 %collective-permute-start.21 = (f32[1,32,32]{1,2,0:T(8,128)S(1)}, f32[1,32,32]{1,2,0:T(8,128)S(1)}, u32[]{:S(2)}, u32[]{:S(2)}) collective-permute-start(f32[1,32,32]{1,2,0:T(8,128)S(1)} %get-tuple-element.1228), channel_id=1, source_target_pairs={{0,1},{1,2},{2,3},{4,5},{5,6},{6,7},{8,9},{9,10},{10,11},{12,13},{... | collective-permute-start | bytes 12296 | tf_op jit(solution)/shard_map/ppermute | solution.py:26
  255.0 5.4 %all-gather.10 = f32[4,32,32]{2,1,0:T(8,128)S(1)} all-gather(f32[1,32,32]{2,1,0:T(8,128)S(1)} %bitcast.350), channel_id=12, replica_groups=mesh['gx'=4,'gy'=2,'gz'=4] {'gz'}, dimensions={0}, use_global_device_ids=true | all-gather | bytes 20480 | tf_op jit(solution)/shard_map/all_gather | solution.py:39
  262.8 8.1 %all-gather.11 = f32[4,32,32]{2,1,0:T(8,128)S(1)} all-gather(f32[1,32,32]{2,1,0:T(8,128)S(1)} %bitcast.349), channel_id=13, replica_groups=mesh['gx'=4,'gy'=2,'gz'=4] {'gz'}, dimensions={0}, use_global_device_ids=true | all-gather | bytes 20480 | tf_op jit(solution)/shard_map/all_gather | solution.py:39
  274.2 6.7 %all_gather.135 = f32[8,32,32]{2,1,0:T(8,128)S(1)} all-gather(f32[2,32,32]{2,1,0:T(8,128)S(1)} %copy.248), channel_id=1, replica_groups=mesh['gx'=4,'gy'=2,'gz'=4] {'gz'}, dimensions={0}, use_global_device_ids=true | all-gather | bytes 40960 | tf_op jit(solution)/shard_map/all_gather | solution.py:262
  280.9 12.9 %all_gather.136 = f32[8,128,32]{2,1,0:T(8,128)S(1)} all-gather(f32[8,32,32]{2,1,0:T(8,128)S(1)} %all_gather.135), channel_id=1, replica_groups=mesh['gx'=4,'gy'=2,'gz'=4] {'gx'}, dimensions={1}, use_global_device_ids=true | all-gather | bytes 163840 | tf_op jit(solution)/shard_map/all_gather | solution.py:263
  294.0 4.5 %all_gather.137 = f32[8,128,64]{1,0,2:T(8,128)S(1)} all-gather(f32[8,128,32]{1,0,2:T(8,128)S(1)} %copy.249), channel_id=1, replica_groups=mesh['gx'=4,'gy'=2,'gz'=4] {'gy'}, dimensions={2}, use_global_device_ids=true | all-gather | bytes 393216 | tf_op jit(solution)/shard_map/all_gather | solution.py:264
  298.5 4.8 %slice.417 = f32[4,64,32]{1,0,2:T(4,128)S(1)} slice(f32[8,128,64]{1,0,2:T(8,128)S(1)} %all_gather.137), slice={[0:8:2], [0:128:2], [0:64:2]} | slice | bytes 65536 | tf_op jit(solution)/shard_map/slice | solution.py:265
  (314 shorter events, 118.7 us)
Async XLA Ops:
  4.4 4.3 %collective-permute-start = (f32[4,64,1]{1,2,0:T(1,128)S(1)}, f32[4,64,1]{1,2,0:T(1,128)S(1)}, u32[]{:S(2)}, u32[]{:S(2)}) collective-permute-start(f32[4,64,1]{1,2,0:T(1,128)S(1)} %slice.441), channel_id=1, source_target_pairs={{4,0},{5,1},{6,2},{7,3},{12,8},{13,9},{14,10},{15,11},{20,16},{21,... | collective-permute-start | bytes 3080 | tf_op jit(solution)/shard_map/ppermute | solution.py:15
  9.0 8.8 %collective-permute-start.1 = (f32[4,1,128]{1,2,0:T(8,128)S(1)}, f32[4,1,128]{1,2,0:T(8,128)S(1)}, u32[]{:S(2)}, u32[]{:S(2)}) collective-permute-start(f32[4,1,128]{1,2,0:T(8,128)S(1)} %bitcast.273), channel_id=1, source_target_pairs={{8,0},{16,8},{24,16},{9,1},{17,9},{25,17},{10,2},{18,10},{26,18},{... | collective-permute-start | bytes 6152 | tf_op jit(solution)/shard_map/ppermute | solution.py:15
  18.4 7.6 %collective-permute-start.2 = (f32[1,128,128]{2,1,0:T(8,128)S(1)}, f32[1,128,128]{2,1,0:T(8,128)S(1)}, u32[]{:S(2)}, u32[]{:S(2)}) collective-permute-start(f32[1,128,128]{2,1,0:T(8,128)S(1)} %bitcast.348), channel_id=1, source_target_pairs={{1,0},{2,1},{3,2},{5,4},{6,5},{7,6},{9,8},{10,9},{11,10},{13,12},{... | collective-permute-start | bytes 196616 | tf_op jit(solution)/shard_map/ppermute | solution.py:15
  26.1 1.0 copy-start.1
  27.2 7.7 %copy-start = (f32[8,128,128]{2,1,0:T(8,128)}, f32[8,128,128]{2,1,0:T(8,128)S(1)}, u32[]{:S(2)}) copy-start(f32[8,128,128]{2,1,0:T(8,128)S(1)} %bitcast_subtract_fusion.1) | copy-start | bytes 1572868
  27.2 7.3 %collective-permute-start.3 = (f32[8,1,128]{2,1,0:T(1,128)S(1)}, f32[8,1,128]{2,1,0:T(1,128)S(1)}, u32[]{:S(2)}, u32[]{:S(2)}) collective-permute-start(f32[8,1,128]{2,1,0:T(1,128)S(1)} %get-tuple-element.1214), channel_id=1, source_target_pairs={{0,8},{8,16},{16,24},{1,9},{9,17},{17,25},{2,10},{10,18},{18,26},{... | collective-permute-start | bytes 12296 | tf_op jit(solution)/shard_map/ppermute | solution.py:26
  30.4 4.4 %collective-permute-start.4 = (f32[8,1,128]{2,1,0:T(1,128)S(1)}, f32[8,1,128]{2,1,0:T(1,128)S(1)}, u32[]{:S(2)}, u32[]{:S(2)}) collective-permute-start(f32[8,1,128]{2,1,0:T(1,128)S(1)} %get-tuple-element.1215), channel_id=1, source_target_pairs={{8,0},{16,8},{24,16},{9,1},{17,9},{25,17},{10,2},{18,10},{26,18},{... | collective-permute-start | bytes 12296 | tf_op jit(solution)/shard_map/ppermute | solution.py:28
  34.9 11.9 %collective-permute-start.5 = (f32[8,1,128]{2,1,0:T(1,128)S(1)}, f32[8,1,128]{2,1,0:T(1,128)S(1)}, u32[]{:S(2)}, u32[]{:S(2)}) collective-permute-start(f32[8,1,128]{2,1,0:T(1,128)S(1)} %slice.453), channel_id=1, source_target_pairs={{0,8},{8,16},{16,24},{1,9},{9,17},{17,25},{2,10},{10,18},{18,26},{... | collective-permute-start | bytes 12296 | tf_op jit(solution)/shard_map/ppermute | solution.py:15
  46.7 0.8 copy-start.3
  58.2 0.8 copy-start.2
  58.2 0.8 copy-start.11
  75.5 5.1 %collective-permute-start.6 = (f32[8,64,1]{2,1,0:T(8,128)S(1)}, f32[8,64,1]{2,1,0:T(8,128)S(1)}, u32[]{:S(2)}, u32[]{:S(2)}) collective-permute-start(f32[8,64,1]{2,1,0:T(8,128)S(1)} %get-tuple-element.1220), channel_id=1, source_target_pairs={{0,4},{1,5},{2,6},{3,7},{8,12},{9,13},{10,14},{11,15},{16,20},{17,... | collective-permute-start | bytes 6152 | tf_op jit(solution)/shard_map/ppermute | solution.py:26
  77.2 1.3 copy-start.17
  77.2 7.1 %collective-permute-start.7 = (f32[8,64,1]{2,1,0:T(8,128)S(1)}, f32[8,64,1]{2,1,0:T(8,128)S(1)}, u32[]{:S(2)}, u32[]{:S(2)}) collective-permute-start(f32[8,64,1]{2,1,0:T(8,128)S(1)} %get-tuple-element.1221), channel_id=1, source_target_pairs={{4,0},{5,1},{6,2},{7,3},{12,8},{13,9},{14,10},{15,11},{20,16},{21,... | collective-permute-start | bytes 6152 | tf_op jit(solution)/shard_map/ppermute | solution.py:28
  84.7 14.9 %collective-permute-start.8 = (f32[8,64,1]{2,1,0:T(8,128)S(1)}, f32[8,64,1]{2,1,0:T(8,128)S(1)}, u32[]{:S(2)}, u32[]{:S(2)}) collective-permute-start(f32[8,64,1]{2,1,0:T(8,128)S(1)} %slice.459), channel_id=1, source_target_pairs={{0,4},{1,5},{2,6},{3,7},{8,12},{9,13},{10,14},{11,15},{16,20},{17,... | collective-permute-start | bytes 6152 | tf_op jit(solution)/shard_map/ppermute | solution.py:15
  110.4 18.0 %collective-permute-start.9 = (f32[1,64,64]{1,2,0:T(8,128)S(1)}, f32[1,64,64]{1,2,0:T(8,128)S(1)}, u32[]{:S(2)}, u32[]{:S(2)}) collective-permute-start(f32[1,64,64]{1,2,0:T(8,128)S(1)} %get-tuple-element.1218), channel_id=1, source_target_pairs={{0,1},{1,2},{2,3},{4,5},{5,6},{6,7},{8,9},{9,10},{10,11},{12,13},{... | collective-permute-start | bytes 49160 | tf_op jit(solution)/shard_map/ppermute | solution.py:26
  124.3 1.9 copy-start.16
  124.3 5.2 %collective-permute-start.10 = (f32[1,64,64]{1,2,0:T(8,128)S(1)}, f32[1,64,64]{1,2,0:T(8,128)S(1)}, u32[]{:S(2)}, u32[]{:S(2)}) collective-permute-start(f32[1,64,64]{1,2,0:T(8,128)S(1)} %get-tuple-element.1219), channel_id=1, source_target_pairs={{1,0},{2,1},{3,2},{5,4},{6,5},{7,6},{9,8},{10,9},{11,10},{13,12},{... | collective-permute-start | bytes 49160 | tf_op jit(solution)/shard_map/ppermute | solution.py:28
  129.6 7.6 %collective-permute-start.11 = (f32[1,64,64]{1,2,0:T(8,128)S(1)}, f32[1,64,64]{1,2,0:T(8,128)S(1)}, u32[]{:S(2)}, u32[]{:S(2)}) collective-permute-start(f32[1,64,64]{1,2,0:T(8,128)S(1)} %slice.465), channel_id=1, source_target_pairs={{0,1},{1,2},{2,3},{4,5},{5,6},{6,7},{8,9},{9,10},{10,11},{12,13},{... | collective-permute-start | bytes 49160 | tf_op jit(solution)/shard_map/ppermute | solution.py:15
  159.1 4.3 %collective-permute-start.12 = (f32[2,32,1]{1,2,0:T(1,128)S(1)}, f32[2,32,1]{1,2,0:T(1,128)S(1)}, u32[]{:S(2)}, u32[]{:S(2)}) collective-permute-start(f32[2,32,1]{1,2,0:T(1,128)S(1)} %slice.471), channel_id=1, source_target_pairs={{4,0},{5,1},{6,2},{7,3},{12,8},{13,9},{14,10},{15,11},{20,16},{21,... | collective-permute-start | bytes 776 | tf_op jit(solution)/shard_map/ppermute | solution.py:15
  163.5 5.0 %collective-permute-start.13 = (f32[2,1,64]{1,2,0:T(8,128)S(1)}, f32[2,1,64]{1,2,0:T(8,128)S(1)}, u32[]{:S(2)}, u32[]{:S(2)}) collective-permute-start(f32[2,1,64]{1,2,0:T(8,128)S(1)} %bitcast.292), channel_id=1, source_target_pairs={{8,0},{16,8},{24,16},{9,1},{17,9},{25,17},{10,2},{18,10},{26,18},{... | collective-permute-start | bytes 1544 | tf_op jit(solution)/shard_map/ppermute | solution.py:15
  168.8 6.5 %collective-permute-start.14 = (f32[1,64,64]{2,1,0:T(8,128)S(1)}, f32[1,64,64]{2,1,0:T(8,128)S(1)}, u32[]{:S(2)}, u32[]{:S(2)}) collective-permute-start(f32[1,64,64]{2,1,0:T(8,128)S(1)} %bitcast.355), channel_id=1, source_target_pairs={{1,0},{2,1},{3,2},{5,4},{6,5},{7,6},{9,8},{10,9},{11,10},{13,12},{... | collective-permute-start | bytes 49160 | tf_op jit(solution)/shard_map/ppermute | solution.py:15
  175.6 4.7 %collective-permute-start.15 = (f32[4,1,64]{1,2,0:T(8,128)S(1)}, f32[4,1,64]{1,2,0:T(8,128)S(1)}, u32[]{:S(2)}, u32[]{:S(2)}) collective-permute-start(f32[4,1,64]{1,2,0:T(8,128)S(1)} %get-tuple-element.1222), channel_id=1, source_target_pairs={{0,8},{8,16},{16,24},{1,9},{9,17},{17,25},{2,10},{10,18},{18,26},{... | collective-permute-start | bytes 3080 | tf_op jit(solution)/shard_map/ppermute | solution.py:26
  177.8 6.3 %collective-permute-start.16 = (f32[4,1,64]{1,2,0:T(8,128)S(1)}, f32[4,1,64]{1,2,0:T(8,128)S(1)}, u32[]{:S(2)}, u32[]{:S(2)}) collective-permute-start(f32[4,1,64]{1,2,0:T(8,128)S(1)} %get-tuple-element.1223), channel_id=1, source_target_pairs={{8,0},{16,8},{24,16},{9,1},{17,9},{25,17},{10,2},{18,10},{26,18},{... | collective-permute-start | bytes 3080 | tf_op jit(solution)/shard_map/ppermute | solution.py:28
  184.3 4.6 %collective-permute-start.17 = (f32[4,1,64]{1,2,0:T(8,128)S(1)}, f32[4,1,64]{1,2,0:T(8,128)S(1)}, u32[]{:S(2)}, u32[]{:S(2)}) collective-permute-start(f32[4,1,64]{1,2,0:T(8,128)S(1)} %slice.481), channel_id=1, source_target_pairs={{0,8},{8,16},{16,24},{1,9},{9,17},{17,25},{2,10},{10,18},{18,26},{... | collective-permute-start | bytes 3080 | tf_op jit(solution)/shard_map/ppermute | solution.py:15
  187.8 1.2 copy-start.5
  214.7 2.7 collective-permute-start.18
  216.1 5.0 %collective-permute-start.19 = (f32[4,32,1]{2,1,0:T(8,128)S(1)}, f32[4,32,1]{2,1,0:T(8,128)S(1)}, u32[]{:S(2)}, u32[]{:S(2)}) collective-permute-start(f32[4,32,1]{2,1,0:T(8,128)S(1)} %get-tuple-element.1231), channel_id=1, source_target_pairs={{4,0},{5,1},{6,2},{7,3},{12,8},{13,9},{14,10},{15,11},{20,16},{21,... | collective-permute-start | bytes 1544 | tf_op jit(solution)/shard_map/ppermute | solution.py:28
  221.3 2.9 collective-permute-start.20
  234.2 14.8 %collective-permute-start.21 = (f32[1,32,32]{1,2,0:T(8,128)S(1)}, f32[1,32,32]{1,2,0:T(8,128)S(1)}, u32[]{:S(2)}, u32[]{:S(2)}) collective-permute-start(f32[1,32,32]{1,2,0:T(8,128)S(1)} %get-tuple-element.1228), channel_id=1, source_target_pairs={{0,1},{1,2},{2,3},{4,5},{5,6},{6,7},{8,9},{9,10},{10,11},{12,13},{... | collective-permute-start | bytes 12296 | tf_op jit(solution)/shard_map/ppermute | solution.py:26
  245.8 5.1 %collective-permute-start.22 = (f32[1,32,32]{1,2,0:T(8,128)S(1)}, f32[1,32,32]{1,2,0:T(8,128)S(1)}, u32[]{:S(2)}, u32[]{:S(2)}) collective-permute-start(f32[1,32,32]{1,2,0:T(8,128)S(1)} %get-tuple-element.1229), channel_id=1, source_target_pairs={{1,0},{2,1},{3,2},{5,4},{6,5},{7,6},{9,8},{10,9},{11,10},{13,12},{... | collective-permute-start | bytes 12296 | tf_op jit(solution)/shard_map/ppermute | solution.py:28
  250.9 3.1 collective-permute-start.23
  (13 other events, 8.8 us)
where the time goes:
time: 315 us; the launch traced here: 309 us
  blocking collectives  126 us (40%)
  starting transfers between devices  72.8 us (23%)
  local copies, waits for them, and re-layouts  51.6 us (16%)
  waiting for transfers between devices  36.5 us (12%)
  other arithmetic  12.1 us (4%)
  matrix products  7.39 us (2%)
    all_gather x12, blocking collectives, prefix(): gathered = jax.tree.map(lambda a: lax.all_gather(a, axis), part)  84.9 us
    ppermute x6, starting transfers between devices, with_halo(): lax.ppermute(tail, axis, [(i, (i + 1) % count) for i in range(ends)])  33.9 us
    ppermute x12, starting transfers between devices, passed_along(): lax.ppermute(value, axis, [(source, source + steps) for source in range(l...  28.6 us
    ppermute x12, waiting for transfers between devices, passed_along(): lax.ppermute(value, axis, [(source, source + steps) for source in range(l...  20.8 us
    unnamed x3, blocking collectives  17.4 us
    unnamed x61, local copies, waits for them, and re-layouts  16.5 us
    ppermute x6, waiting for transfers between devices, with_halo(): lax.ppermute(head, axis, [((i + 1) % count, i) for i in range(ends)])  14.5 us
    all_gather x1, blocking collectives, gathered_level(): whole = lax.all_gather(whole, 'gx', axis=1, tiled=True)  12.9 us
  transfers between devices with their start and end apart: 24, of which 15 were waited for; matrix products, arithmetic and copies ran while one was open for 7% of the time, Pallas kernels for 0%

commit v1 on v0

v1 whole, which is shorter than its diff:
```python
import functools
import math

import jax
import jax.numpy as jnp
import numpy as np
from jax import lax
from jax.experimental import pallas as pl
from jax.experimental.pallas import tpu as pltpu
from jax.sharding import PartitionSpec as P

band_ratio = 2.0 - math.sqrt(3.0)
f32 = np.float32


def round_up(value, unit):
    return -(-value // unit) * unit


def dense(fine):
    n = fine // 2
    steps = np.arange(n)[:, None] - np.arange(n)[None, :]
    lower = np.where(steps >= 0, (-band_ratio) ** np.maximum(steps, 0), 0.0)
    inverse = lower.T @ lower
    mass = 4.0 * np.eye(fine) + np.eye(fine, k=1) + np.eye(fine, k=-1)
    weights = np.where(np.arange(n) == n - 1, 1.0, 0.5)[:, None]
    earlier = np.concatenate([np.zeros((1, fine)), mass[1::2][:-1]])
    product = inverse @ (0.5 * band_ratio * (mass[0::2] + weights * mass[1::2] + 0.5 * earlier))
    return product, inverse[:, 0] * (3 * band_ratio - 1), inverse[:, -1] * (2 * band_ratio)


class Level:
    def __init__(self, whole, count, following):
        self.count, self.fine = count, whole // count
        self.n = self.fine // 2
        self.product, self.first, self.last = dense(whole)
        self.following = following
        self.kept = following.functional_count if following else 0
        self.functional_count = 4 + 2 * self.kept
        self.even = np.zeros((self.n, self.fine))
        self.even[np.arange(self.n), 2 * np.arange(self.n)] = 1.0
        self.v = [self.towards(i, i * self.n - 1) for i in range(count)]
        self.w = [self.towards(i, (i + 1) * self.n) for i in range(count)]
        self.functionals = []
        for i in range(count):
            own = np.zeros((4, self.fine))
            own[0, 0] = own[1, self.fine - 2] = 1.0
            own[2], own[3] = self.v[i], self.w[i]
            if following:
                inner = following.functionals[i]
                own = np.concatenate([own, inner @ self.even, inner @ self.block(i, i)])
            self.functionals.append(own)

    def rows(self, i):
        return slice(i * self.n, (i + 1) * self.n)

    def block(self, i, j):
        return self.product[self.rows(i), j * self.fine : (j + 1) * self.fine]

    def towards(self, i, row):
        if not 0 <= row < self.count * self.n:
            return np.zeros(self.fine)
        values = self.product[row, i * self.fine : (i + 1) * self.fine]
        return values / np.abs(values).max()

    def reach(self, i, j):
        side = self.v[j] if j > i else self.w[j]
        best = np.argmax(np.abs(side))
        return self.block(i, j)[:, best] / side[best]

    def side(self, i, j):
        return 2 if j > i else 3

    def tables(self, j):
        own, kept, many, n, fine = self.n, self.kept, self.functional_count, self.n, self.fine
        others = [j ^ k for k in range(1, self.count)]
        shape = (own + kept * len(others), fine + many * len(others))
        product, even = np.zeros(shape), np.zeros(shape)
        at = {i: fine + many * place for place, i in enumerate(others)}
        product[:n, :fine] = self.block(j, j)
        even[:n, :fine] = self.even
        first, last = [self.first[self.rows(j)]], [self.last[self.rows(j)]]
        for i in others:
            product[:n, at[i] + self.side(j, i)] = self.reach(j, i)
        for place, i in enumerate(others):
            if not kept:
                break
            inner = self.following.functionals[i]
            target = n + kept * place + np.arange(kept)
            product[target, :fine] = inner @ self.block(i, j)
            product[target, at[i] + 4 + kept + np.arange(kept)] = 1.0
            even[target, at[i] + 4 + np.arange(kept)] = 1.0
            for other in others:
                if other != i:
                    product[target, at[other] + self.side(i, other)] = inner @ self.reach(i, other)
            first.append(inner @ self.first[self.rows(i)])
            last.append(inner @ self.last[self.rows(i)])
        around = even.copy()
        around[:, 0 if j == 0 else at[0]] += np.concatenate(first)
        end = self.count - 1
        around[:, fine - 2 if j == end else at[end] + 1] += np.concatenate(last)
        return product, even, around

    def next_first(self, j, stride):
        if j == self.count - 1:
            return self.fine - 2
        return self.fine + stride * ((j ^ (j + 1)) - 1)


def interpolation(level, j, inputs, stride, coarse):
    table = np.zeros((level.fine, inputs))
    if coarse:
        places = list(range(level.n))
        last = level.n - 1 if j == level.count - 1 else level.n + stride * ((j ^ (j + 1)) - 1)
    else:
        places = [2 * c for c in range(level.n)]
        last = level.next_first(j, stride)
    places.append(last)
    for c in range(level.n):
        table[2 * c, places[c]] = 1.0
        table[2 * c + 1, places[c]] += 0.5
        table[2 * c + 1, places[c + 1]] += 0.5
    return table


def chain(whole, count, levels):
    made = None
    for depth in reversed(range(levels)):
        made = Level(whole >> depth, count, made)
    return made


def padded(table, rows, cols):
    out = np.zeros((rows, cols))
    out[: table.shape[0], : table.shape[1]] = table
    return out


highest = lax.Precision.HIGHEST


def dot(a, b, dims=((1,), (0,))):
    return lax.dot_general(a, b, (dims, ((), ())), precision=highest, preferred_element_type=jnp.float32)


def kernel_call(body, outs, arrays, scalars=0, scratch=()):
    specs = [pl.BlockSpec(memory_space=pltpu.VMEM)] * (len(arrays) - scalars)
    specs += [pl.BlockSpec(memory_space=pltpu.SMEM)] * scalars
    return pl.pallas_call(
        body,
        out_shape=[jax.ShapeDtypeStruct(shape, jnp.float32) for shape in outs],
        in_specs=specs,
        out_specs=[pl.BlockSpec(memory_space=pltpu.VMEM)] * len(outs),
        scratch_shapes=list(scratch),
        compiler_params=pltpu.CompilerParams(vmem_limit_bytes=40 << 20),
    )(*arrays)


def swapped(value, axis):
    count = lax.axis_size(axis)
    return [lax.ppermute(value, axis, [(i, i ^ k) for i in range(count)]) for k in range(1, count)]


def iota(shape, dim):
    return lax.broadcasted_iota(jnp.int32, shape, dim)


def shards(counts, field):
    dz, dx, dy = counts
    lz, lx, ly = field.shape
    nz, nx, ny = lz * dz, lx * dx, ly * dy

    yone = chain(ny, dy, 3)
    ytwo, ythree = yone.following, yone.following.following
    xone = chain(nx, dx, 1)
    xtwo = chain(nx // 2, dx, 2)
    xthree = xtwo.following
    zone = Level(nz, dz, None)

    ky, ky2, ky3 = yone.kept, ytwo.kept, ythree.kept
    kya = round_up(ky + 3, 16)
    kys = round_up(ky + 2, 16)
    wide = round_up(yone.n + ky * (dy - 1) + 1, 128)
    wide2 = ytwo.n + ky2 * (dy - 1)
    packed = round_up(3 * wide2, 128)
    kx = round_up(xtwo.functional_count, 8)
    rowsx = xtwo.fine + kx * (dx - 1)
    tall = round_up(xtwo.n + xtwo.kept * (dx - 1), 8)

    fya = np.zeros((dy, kya, ly))
    fys = np.zeros((dy, kys, ly))
    ta = np.zeros((dy, ly, wide))
    wa = np.zeros((dy, max(dy - 1, 1) * kya, wide))
    tsm = np.zeros((dy, ly, 2 * wide))
    wsm = np.zeros((dy, max(dy - 1, 1) * kys, 2 * wide))
    for j in range(dy):
        pick_a = [2, 3] + list(range(4 + ky, 4 + 2 * ky)) + [0]
        pick_s = [0, 1] + list(range(4, 4 + ky))
        fya[j, : len(pick_a)] = yone.functionals[j][pick_a]
        fys[j, : len(pick_s)] = yone.functionals[j][pick_s]
        product, even, around = yone.tables(j)
        used = product.shape[0]
        for source, to, across, pick, k in (
            (product, ta[j], wa[j], pick_a[:-1], kya),
            (even, tsm[j][:, :wide], wsm[j][:, :wide], pick_s, kys),
            (around, tsm[j][:, wide:], wsm[j][:, wide:], pick_s, kys),
        ):
            to[:, :used] = source[:, :ly].T
            for place in range(dy - 1):
                begin = ly + yone.functional_count * place
                part = source[:, begin : begin + yone.functional_count].T[pick]
                across[k * place : k * place + len(pick), :used] = part
        if j == dy - 1:
            ta[j, ly - 2, wide - 1] = 0.5
        else:
            wa[j, kya * ((j ^ (j + 1)) - 1) + len(pick_a) - 1, wide - 1] = 0.5

    fx = np.zeros((dx, 8, lx))
    txa = np.zeros((dx, xone.n, lx + 8 * (dx - 1)))
    txm = np.zeros((dx, xone.n, xone.n + 8 * (dx - 1)))
    hx = np.zeros((dx, dx))
    for j in range(dx):
        fx[j, :2] = xone.functionals[j][2:4]
        product, even, around = xone.tables(j)
        txa[j, :, :lx] = product[:, :lx]
        txm[j, :, : xone.n] = around[:, :lx:2]
        for place in range(dx - 1):
            txa[j, :, lx + 8 * place : lx + 8 * place + 2] = product[:, lx + 4 * place + 2 : lx + 4 * place + 4]
            begin = xone.n + 8 * place
            txm[j, :, begin + 2 : begin + 4] = around[:, lx + 4 * place : lx + 4 * place + 2]
        hx[j, 0 if j == dx - 1 else j ^ (j + 1)] = 1.0

    zn = zone.n
    zs = np.zeros((dz, 2 * lz + 2 + zn * (lz + dz + 1)))
    for j in range(dz):
        cv, cw = zone.v[j], zone.w[j]
        k_last = (zone.last[zone.rows(0)] / zone.reach(0, j))[0] if 0 < j == dz - 1 else 0.0
        k_first = (zone.first[zone.rows(dz - 1)] / zone.reach(dz - 1, j))[-1] if j == 0 and dz > 1 else 0.0
        parts = [cv, cw, [k_last, k_first], zone.block(j, j).reshape(-1)]
        parts += [zone.reach(j, j ^ k) for k in range(1, dz)]
        parts += [zone.first[zone.rows(j)] * (j == 0), zone.last[zone.rows(j)] * (j == dz - 1)]
        zs[j] = np.concatenate([np.asarray(p, np.float64) for p in parts])
    at_local = 2 * lz + 2
    at_reach = at_local + zn * lz
    at_first = at_reach + zn * (dz - 1)
    at_last = at_first + zn

    f2x = np.stack([padded(xtwo.functionals[j], kx, xtwo.fine) for j in range(dx)])
    tx2 = np.zeros((dx, 3 * tall, rowsx))
    qx2 = np.zeros((dx, xtwo.fine, rowsx))
    tx3 = np.zeros((dx, 3 * xthree.n, tall))
    qx3 = np.zeros((dx, xthree.fine, tall))
    px3 = np.zeros((dx, xtwo.fine, tall))
    for j in range(dx):
        for c, table in enumerate(xtwo.tables(j)):
            tx2[j, c * tall : c * tall + table.shape[0], : xtwo.fine] = table[:, : xtwo.fine]
            for place in range(dx - 1):
                begin = xtwo.fine + xtwo.functional_count * place
                target = xtwo.fine + kx * place
                tx2[j, c * tall : c * tall + table.shape[0], target : target + xtwo.functional_count] = table[
                    :, begin : begin + xtwo.functional_count
                ]
        qx2[j] = interpolation(xtwo, j, rowsx, kx, False)
        for c, table in enumerate(xthree.tables(j)):
            tx3[j, c * xthree.n : (c + 1) * xthree.n, : table.shape[1]] = table
        qx3[j] = interpolation(xthree, j, tall, xthree.functional_count, False)
        px3[j] = interpolation(xtwo, j, tall, xtwo.kept, True)

    ty2 = np.zeros((dy, 3 * wide, packed))
    qy2 = np.zeros((dy, wide, round_up(ytwo.fine, 128)))
    ty3 = np.zeros((dy, 3 * packed, 128))
    qy3 = np.zeros((dy, packed, 128))
    py3 = np.zeros((dy, packed, round_up(ytwo.fine, 128)))
    for j in range(dy):
        for c, table in enumerate(ytwo.tables(j)):
            ty2[j, c * wide : c * wide + table.shape[1], c * wide2 : c * wide2 + wide2] = table.T
        qy2[j, :, : ytwo.fine] = interpolation(ytwo, j, wide, ky, False).T
        for c, table in enumerate(ythree.tables(j)):
            ty3[j, c * packed : c * packed + table.shape[1], : ythree.n] = (-1.0 if c == 2 else 1.0) * table.T
        qy3[j, :, : ythree.fine] = interpolation(ythree, j, packed, ky2, False).T
        py3[j, wide2:, : ytwo.fine] = interpolation(ytwo, j, packed - wide2, ky2, True).T
    az2, first2, last2 = (t.tolist() for t in dense(nz // 2))
    az3, first3, last3 = dense(nz // 4)
    z2, z3 = nz // 2, nz // 4
    lz2, lz3 = lz // 2, lz // 4
    zt = np.concatenate([az3, first3[:, None], last3[:, None]], axis=1)
    zt = zt.reshape(dz, (lz // 8) * (z3 + 2))
    lz4 = lz // 8

    to32 = lambda *tables: [jnp.asarray(t, jnp.float32) for t in tables]
    hz, hx1 = lz // 2, lx // 2

    def y_messages(u_ref, fya_ref, fys_ref, out_ref):
        j = lax.axis_index("gy")
        nt = ((1,), (1,))
        out_ref[:kya, : lz * lx] = dot(fya_ref[j], u_ref[...].reshape(lz * lx, ly), nt)
        even = jnp.concatenate([u_ref[2 * z, pl.ds(0, hx1, stride=2), :] for z in range(hz)], axis=0)
        out_ref[:kys, lz * lx :] = dot(fys_ref[j], even, nt)

    def y_apply(*refs):
        u_ref, came = refs[0], refs[1:dy]
        ta_ref, wa_ref, tsm_ref, wsm_ref, fx_ref, ta_out, tsm_out, iy_out, xm_out = refs[dy:]
        j, jx = lax.axis_index("gy"), lax.axis_index("gx")
        tn = ((0,), (0,))
        ta_all = dot(u_ref[...].reshape(lz * lx, ly), ta_ref[j])
        even = jnp.concatenate([u_ref[2 * z, pl.ds(0, hx1, stride=2), :] for z in range(hz)], axis=0)
        tsm_all = dot(even, tsm_ref[j])
        for k, ref in enumerate(came):
            ta_all += dot(ref[:kya, : lz * lx], wa_ref[j, kya * k : kya * (k + 1), :], tn)
            tsm_all += dot(ref[:kys, lz * lx :], wsm_ref[j, kys * k : kys * (k + 1), :], tn)
        ta_out[...] = ta_all
        tsm_out[...] = tsm_all
        xm_out[...] = jnp.zeros_like(xm_out)
        lane = iota((lx, ly), 1)
        for z in range(lz):
            part = ta_all[z * lx : (z + 1) * lx]
            xm_out[z, 0:2, :wide] = dot(fx_ref[jx], part)[0:2]
            if z % 2 == 0:
                half = z // 2
                tm = tsm_all[half * hx1 : (half + 1) * hx1, wide:]
                xm_out[z, 2:3, :wide] = tm[0:1]
                xm_out[z, 3:4, :wide] = tm[hx1 - 1 : hx1]
                u = u_ref[z]
                before, after = pltpu.roll(u, 1, 1), pltpu.roll(u, ly - 1, 1)
                middle = 0.5 * (before + after)
                edge = 0.5 * before + jnp.broadcast_to(part[:, wide - 1 : wide], (lx, ly))
                iy = jnp.where(lane == ly - 1, edge, jnp.where(lane % 2 == 1, middle, u))
                iy_out[half] = iy
                xm_out[z, 4:5, :ly] = iy[0:1]

    def x_apply(*refs):
        ta_ref, tsm_ref, iy_ref, own_ref = refs[:4]
        came = refs[4 : 3 + dx]
        txa_ref, txm_ref, hx_ref, zs_ref = refs[3 + dx : 7 + dx]
        ixy_out, first_out, u1_out = refs[7 + dx : 10 + dx]
        planes_out = refs[10 + dx :]
        jx, jz = lax.axis_index("gx"), lax.axis_index("gz")
        xa, xm, diff = [], [], []
        for z in range(lz):
            stacked = jnp.concatenate([ta_ref[z * lx : (z + 1) * lx, :]] + [r[z, :, :wide] for r in came], axis=0)
            xa.append(dot(txa_ref[jx], stacked))
        row = iota((lx, ly), 0)
        for half in range(hz):
            part = tsm_ref[half * hx1 : (half + 1) * hx1, :]
            stacked = jnp.concatenate([part[:, wide:]] + [r[2 * half, :, :wide] for r in came], axis=0)
            xm.append(dot(txm_ref[jx], stacked))
            diff.append(part[:, :wide] - xm[-1])
            iy = iy_ref[half]
            halo = hx_ref[jx, 0] * iy[lx - 2 : lx - 1]
            for k, r in enumerate(came):
                halo += hx_ref[jx, k + 1] * r[2 * half, 4:5, :ly]
            before, after = pltpu.roll(iy, 1, 0), pltpu.roll(iy, lx - 1, 0)
            after = jnp.where(row == lx - 1, jnp.broadcast_to(halo, (lx, ly)), after)
            ixy = jnp.where(row % 2 == 1, 0.5 * (before + after), iy)
            ixy_out[half] = ixy
            if half == 0:
                first_out[...] = ixy
        scalar = lambda place: zs_ref[jz, place]
        for zc in range(zn):
            total = diff[zc] - scalar(at_first + zc) * xm[0] - scalar(at_last + zc) * xm[hz - 1]
            for z in range(lz):
                total += scalar(at_local + zc * lz + z) * xa[z]
            u1_out[zc] = total
        v = -scalar(2 * lz) * xm[hz - 1]
        w = -scalar(2 * lz + 1) * xm[0]
        for z in range(lz):
            v += scalar(z) * xa[z]
            w += scalar(lz + z) * xa[z]
        for k, out in enumerate(planes_out):
            out[...] = jnp.where((jz ^ (k + 1)) > jz, w, v)

    def z_apply(*refs):
        part_ref, came = refs[0], refs[1:dz]
        f2x_ref, zs_ref, u1_out, xt_out = refs[dz:]
        jx, jz = lax.axis_index("gx"), lax.axis_index("gz")
        for zc in range(zn):
            total = part_ref[zc]
            for k, r in enumerate(came):
                total += zs_ref[jz, at_reach + k * zn + zc] * r[...]
            u1_out[zc] = total
            xt_out[:, zc * wide : (zc + 1) * wide] = dot(f2x_ref[jx], total)

    def fine_coefficients(u_ref, ixy_ref, halo_ref, out_ref):
        jz = lax.axis_index("gz")
        for half in range(hz):
            here = ixy_ref[half]
            out_ref[2 * half] = u_ref[2 * half] - here
            after = ixy_ref[half + 1] if half + 1 < hz else jnp.where(jz == dz - 1, here, halo_ref[...])
            out_ref[2 * half + 1] = u_ref[2 * half + 1] - 0.5 * (here + after)

    def second_apply(*refs):
        u1_ref, came = refs[0], refs[1:dx]
        tx2_ref, qx2_ref, ty2_ref, qy2_ref, zt_out, i2_out = refs[dx:]
        jx, jy = lax.axis_index("gx"), lax.axis_index("gy")
        own = jnp.concatenate([u1_ref[z] for z in range(lz2)], axis=1)
        state = jnp.concatenate([own] + [r[...] for r in came], axis=0)
        across = dot(tx2_ref[jx], state)
        spread = dot(qx2_ref[jx], state)
        for z in range(lz2):
            cut = across[:, z * wide : (z + 1) * wide]
            joined = jnp.concatenate([cut[c * tall : (c + 1) * tall] for c in range(3)], axis=1)
            zt_out[z] = dot(joined, ty2_ref[jy])
            if z % 2 == 0:
                i2_out[z // 2] = dot(spread[:, z * wide : (z + 1) * wide], qy2_ref[jy])

    def third_apply(*refs):
        u1_ref, i2_ref, own_ref = refs[:3]
        came = refs[3 : 2 + dz]
        px3_ref, py3_ref, tx3_ref, ty3_ref, qx3_ref, qy3_ref, zt_ref = refs[2 + dz : 9 + dz]
        middle_out, coarse_out, coarsest_out, zbuf, ubuf = refs[9 + dz :]
        jx, jy, jz = lax.axis_index("gx"), lax.axis_index("gy"), lax.axis_index("gz")
        zbuf[pl.ds(jz * lz2, lz2)] = own_ref[...]
        for k, r in enumerate(came):
            zbuf[pl.ds((jz ^ (k + 1)) * lz2, lz2)] = r[...]
        at = jnp.minimum((jz + 1) * lz2, z2 - 2)
        halo = dot(dot(px3_ref[jx], zbuf[at]), py3_ref[jy])
        fy = ytwo.fine
        for half in range(lz2 // 2):
            here = i2_ref[half]
            after = i2_ref[half + 1] if half + 1 < lz2 // 2 else halo
            middle_out[2 * half] = (u1_ref[2 * half][:, :fy] - here[:, :fy])
            middle_out[2 * half + 1] = u1_ref[2 * half + 1][:, :fy] - (0.5 * (here + after))[:, :fy]
        everything = [zbuf[z] for z in range(z2)]
        evens = [pltpu.roll(everything[z], packed - wide2, 1) for z in range(0, z2, 2)]
        arounds = [pltpu.roll(everything[z], packed - 2 * wide2, 1) for z in range(0, z2, 2)]
        for zc in range(z3):
            total = evens[zc] - arounds[zc] - first2[zc] * arounds[0] - last2[zc] * arounds[-1]
            for z in range(z2):
                total += az2[zc][z] * everything[z]
            ubuf[zc] = total
        fy3 = ythree.fine
        spread = []
        for half in range(lz3 // 2 + 1):
            at = jnp.minimum(jz * lz3 + 2 * half, z3 - 2)
            spread.append(dot(dot(qx3_ref[jx], ubuf[at]), qy3_ref[jy])[:, :fy3])
        for half in range(lz3 // 2):
            at = jz * lz3 + 2 * half
            coarse_out[2 * half] = ubuf[at][: xthree.fine, :fy3] - spread[half]
            coarse_out[2 * half + 1] = ubuf[at + 1][: xthree.fine, :fy3] - 0.5 * (spread[half] + spread[half + 1])
        n3 = xthree.n
        for zc in range(lz4):
            base = zc * (z3 + 2)
            along = zt_ref[jz, base] * ubuf[0]
            for z in range(1, z3):
                along += zt_ref[jz, base + z] * ubuf[z]
            even = ubuf[2 * (jz * lz4 + zc)]
            around = even + zt_ref[jz, base + z3] * ubuf[0] + zt_ref[jz, base + z3 + 1] * ubuf[z3 - 2]
            joined = jnp.concatenate(
                [
                    dot(tx3_ref[jx, c * n3 : (c + 1) * n3, :], plane)
                    for c, plane in enumerate((along, even, around))
                ],
                axis=1,
            )
            coarsest_out[zc] = dot(joined, ty3_ref[jy])[:, : ythree.n]

    (ym,) = kernel_call(y_messages, [(max(kya, kys), lz * lx + hz * hx1)], [field, *to32(fya, fys)])
    ycame = swapped(ym, "gy")
    xw = max(wide, ly)
    ta_v, tsm_v, iy, xm = kernel_call(
        y_apply,
        [(lz * lx, wide), (hz * hx1, 2 * wide), (hz, lx, ly), (lz, 8, xw)],
        [field, *ycame, *to32(ta, wa, tsm, wsm, fx)],
    )
    xcame = swapped(xm, "gx")
    ixy, zfirst, u1_part, *planes = kernel_call(
        x_apply,
        [(hz, lx, ly), (lx, ly), (zn, xone.n, wide)] + [(xone.n, wide)] * (dz - 1),
        [ta_v, tsm_v, iy, xm, *xcame, *to32(txa, txm, hx, zs)],
        scalars=2,
    )
    zcame = [
        lax.ppermute(plane, "gz", [(i, i ^ (k + 1)) for i in range(dz)]) for k, plane in enumerate(planes)
    ]
    zhalo = lax.ppermute(zfirst, "gz", [(i + 1, i) for i in range(dz - 1)])
    u1, xt = kernel_call(
        z_apply,
        [(zn, xone.n, wide), (kx, zn * wide)],
        [u1_part, *zcame, *to32(f2x, zs)],
        scalars=1,
    )
    xtcame = swapped(xt, "gx")
    (fine,) = kernel_call(fine_coefficients, [(lz, lx, ly)], [field, ixy, zhalo])
    zmsg, i2 = kernel_call(
        second_apply,
        [(lz2, tall, packed), (lz2 // 2, xtwo.fine, round_up(ytwo.fine, 128))],
        [u1, *xtcame, *to32(tx2, qx2, ty2, qy2)],
    )
    ztcame = swapped(zmsg, "gz")
    middle, coarse, coarsest = kernel_call(
        third_apply,
        [(lz2, xtwo.fine, ytwo.fine), (lz3, xthree.fine, ythree.fine), (lz4, xthree.n, ythree.n)],
        [u1, i2, zmsg, *ztcame, *to32(px3, py3, tx3, ty3, qx3, qy3, zt)],
        scalars=1,
        scratch=[pltpu.VMEM((z2, tall, packed), jnp.float32), pltpu.VMEM((z3, tall, packed), jnp.float32)],
    )
    return fine, middle, coarse, coarsest


def solution(mesh):
    spec = P("gz", "gx", "gy")
    counts = tuple(mesh.shape[a] for a in ("gz", "gx", "gy"))
    return jax.shard_map(
        functools.partial(shards, counts), mesh=mesh, in_specs=(spec,), out_specs=(spec,) * 4, check_vma=False
    )
```

time: 315 us -> 47.1 us (0.15); the launches traced: 309 us -> 46.7 us
  blocking collectives: 126 us -> 0 us
  starting transfers between devices: 72.8 us -> 19.2 us
  local copies, waits for them, and re-layouts: 51.6 us -> 2.95 us
  waiting for transfers between devices: 36.5 us -> 13.9 us
  other arithmetic: 12.1 us -> 0 us
  Pallas kernels: 0 us -> 9.84 us
  matrix products: 7.39 us -> 0 us
    all_gather x15 -> x0, blocking collectives: 109 us -> none  [the longest x12 84.9 us: prefix(): gathered = jax.tree.map(lambda a: lax.all_gather(a, axis), part)]
    ppermute x24 -> x14, starting transfers between devices: 72.8 us -> 19.2 us  [the longest x10 11.8 us: swapped(): lax.ppermute(value, axis, [(i, i ^ k) for i in range(count)])]
    slice x58 -> x0, local copies, waits for them, and re-layouts: 23.7 us -> none  [the longest x6 6.41 us: restrict_mass(): odd_part = lax.slice_in_dim(mass, 1, length, 2, dimension)]
    ppermute x24 -> x14, waiting for transfers between devices: 36.5 us -> 13.9 us  [the longest x10 7.83 us: swapped(): lax.ppermute(value, axis, [(i, i ^ k) for i in range(count)])]
    unnamed x3 -> x0, blocking collectives: 17.4 us -> none
    unnamed x61 -> x50, local copies, waits for them, and re-layouts: 16.5 us -> 2.95 us
    add x30 -> x0, other arithmetic: 10.7 us -> none  [the longest x14 9.12 us: link_maps(): return (earlier[0] * latter[0], latter[0] * earlier[1] + latter[1])]
    pallas_call x0 -> x7, Pallas kernels: none -> 9.84 us  [kernel_call(): pl.pallas_call(body, out_shape=[jax.ShapeDtypeStruct(shape, jnp.float32)...]
  transfers between devices with their start and end apart: 24 -> 14, of which waited for: 15 -> 9; matrix products, arithmetic and copies ran while one was open for 7% -> 0% of each run, Pallas kernels for 0% -> 2%
where the time goes in v1:
time: 47.1 us; the launch traced here: 46.7 us
  starting transfers between devices  19.2 us (41%)
  waiting for transfers between devices  13.9 us (30%)
  Pallas kernels  9.84 us (21%)
  local copies, waits for them, and re-layouts  2.95 us (6%)
  between operations  0.81 us (2%)
    ppermute x10, starting transfers between devices, swapped(): lax.ppermute(value, axis, [(i, i ^ k) for i in range(count)])  11.8 us
    pallas_call x7, Pallas kernels, kernel_call(): pl.pallas_call(body, out_shape=[jax.ShapeDtypeStruct(shape, jnp.float32)...  9.84 us
    ppermute x10, waiting for transfers between devices, swapped(): lax.ppermute(value, axis, [(i, i ^ k) for i in range(count)])  7.83 us
    ppermute x3, starting transfers between devices, shards(): lax.ppermute(plane, 'gz', [(i, i ^ k + 1) for i in range(dz)])  4.99 us
    ppermute x1, waiting for transfers between devices, shards(): zhalo = lax.ppermute(zfirst, 'gz', [(i + 1, i) for i in range(dz - 1)])  3.16 us
    unnamed x50, local copies, waits for them, and re-layouts  2.95 us
    ppermute x3, waiting for transfers between devices, shards(): lax.ppermute(plane, 'gz', [(i, i ^ k + 1) for i in range(dz)])  2.86 us
    ppermute x1, starting transfers between devices, shards(): zhalo = lax.ppermute(zfirst, 'gz', [(i + 1, i) for i in range(dz - 1)])  2.4 us
  transfers between devices with their start and end apart: 14, of which 9 were waited for; matrix products, arithmetic and copies ran while one was open for 0% of the time, Pallas kernels for 2%

profile of v1, /device:TPU:1, one launch (start us, length us, event | category | flops | bytes accessed | tf_op | source)
XLA Modules:
  0.0 46.7 jit_solution(7301176242891605009)
XLA Ops:
  0.7 0.7 %copy-done.20 = f32[2,16,128]{2,1,0:T(8,128)S(1)} copy-done((f32[2,16,128]{2,1,0:T(8,128)S(1)}, f32[2,16,128]{2,1,0:T(8,128)}, u32[]{:S(2)}) %copy-start.20) | copy-done | bytes 16408
  1.4 1.0 %copy-done = f32[8,128,128]{2,1,0:T(8,128)S(1)} copy-done((f32[8,128,128]{2,1,0:T(8,128)S(1)}, f32[8,128,128]{2,1,0:T(8,128)}, u32[]{:S(2)}) %copy-start) | copy-done | bytes 524312
  2.4 0.6 %shard_map.264 = f32[16,1280]{1,0:T(8,128)S(1)} custom-call(f32[8,128,128]{2,1,0:T(8,128)S(1)} %copy-done, f32[2,16,128]{2,1,0:T(8,128)S(1)} %copy-done.21, f32[2,16,128]{2,1,0:T(8,128)S(1)} %copy-done.20), custom_call_target="tpu_custom_call" | custom-call | tf_op jit(solution)/shard_map/pallas_call | solution.py:149
  3.1 2.1 %collective-permute-start = (f32[16,1280]{1,0:T(8,128)S(1)}, f32[16,1280]{1,0:T(8,128)S(1)}, u32[]{:S(2)}, u32[]{:S(2)}) collective-permute-start(f32[16,1280]{1,0:T(8,128)S(1)} %shard_map.264), channel_id=1, source_target_pairs={{0,4},{4,0},{1,5},{5,1},{2,6},{6,2},{3,7},{7,3},{8,12},{12,8},{9,1... | collective-permute-start | bytes 245768 | tf_op jit(solution)/shard_map/ppermute | solution.py:161
  5.2 2.2 %collective-permute-done.refs_1_ = f32[16,1280]{1,0:T(8,128)S(1)} collective-permute-done((f32[16,1280]{1,0:T(8,128)S(1)}, f32[16,1280]{1,0:T(8,128)S(1)}, u32[]{:S(2)}, u32[]{:S(2)}) %collective-permute-start) | collective-permute-done | bytes 81952 | tf_op jit(solution)/shard_map/ppermute | solution.py:161
  7.4 2.6 %shard_map.265 = (f32[1024,128]{1,0:T(8,128)S(1)}, f32[256,256]{1,0:T(8,128)S(1)}, f32[4,128,128]{2,1,0:T(8,128)S(1)}, f32[8,8,128]{2,1,0:T(8,128)S(1)}) custom-call(f32[8,128,128]{2,1,0:T(8,128)S(1)} %copy-done, f32[16,1280]{1,0:T(8,128)S(1)} %collective-permute-done.refs_1_, f32[2,128,128]{2,1,0:T(8,128)S(1)} %copy-done.13, f32[2,16,128]{2,1,0:T(8,128)S(1)} %copy-done.19, ...), custom_call_target="tpu_custom_call" | custom-call | tf_op jit(solution)/shard_map/pallas_call | solution.py:149
  10.0 3.2 %collective-permute-start.3 = (f32[8,8,128]{2,1,0:T(8,128)S(1)}, f32[8,8,128]{2,1,0:T(8,128)S(1)}, u32[]{:S(2)}, u32[]{:S(2)}) collective-permute-start(f32[8,8,128]{2,1,0:T(8,128)S(1)} %get-tuple-element.24.refs_3_), channel_id=1, source_target_pairs={{0,24},{8,16},{16,8},{24,0},{1,25},{9,17},{17,9},{25,1},{2,26},{10... | collective-permute-start | bytes 98312 | tf_op jit(solution)/shard_map/ppermute | solution.py:161
  13.3 0.3 collective-permute-start.1
  13.6 1.0 %collective-permute-done.3.refs_6_ = f32[8,8,128]{2,1,0:T(8,128)S(1)} collective-permute-done((f32[8,8,128]{2,1,0:T(8,128)S(1)}, f32[8,8,128]{2,1,0:T(8,128)S(1)}, u32[]{:S(2)}, u32[]{:S(2)}) %collective-permute-start.3) | collective-permute-done | bytes 32800 | tf_op jit(solution)/shard_map/ppermute | solution.py:161
  14.6 2.3 %collective-permute-done.2.refs_5_ = f32[8,8,128]{2,1,0:T(8,128)S(1)} collective-permute-done((f32[8,8,128]{2,1,0:T(8,128)S(1)}, f32[8,8,128]{2,1,0:T(8,128)S(1)}, u32[]{:S(2)}, u32[]{:S(2)}) %collective-permute-start.2) | collective-permute-done | bytes 32800 | tf_op jit(solution)/shard_map/ppermute | solution.py:161
  17.0 0.7 %copy-done.24 = f32[4,4]{1,0:T(4,128)S(1)} copy-done((f32[4,4]{1,0:T(4,128)S(1)}, f32[4,4]{1,0:T(4,128)}, u32[]{:S(2)}) %copy-start.24) | copy-done | bytes 88
  17.7 1.6 %shard_map.266 = (f32[4,128,128]{2,1,0:T(8,128)S(1)}, f32[128,128]{1,0:T(8,128)S(1)}, f32[4,64,128]{2,1,0:T(8,128)S(1)}, f32[64,128]{1,0:T(8,128)S(1)}, f32[64,128]{1,0:T(8,128)S(1)}, /*index=5*/f32[64,128]{1,0:T(8,128)S(1)}) custom-call(f32[1024,128]{1,0:T(8,128)S(1)} %get-tuple-element.21.refs_0_, f32[256,256]{1,0:T(8,128)S(1)} %get-tuple-element.22.refs_1_, ...), custom_call_target="tpu_custom_call" | custom-call | tf_op jit(solution)/shard_map/pallas_call | solution.py:149
  19.3 3.3 %collective-permute-start.5 = (f32[64,128]{1,0:T(8,128)S(1)}, f32[64,128]{1,0:T(8,128)S(1)}, u32[]{:S(2)}, u32[]{:S(2)}) collective-permute-start(f32[64,128]{1,0:T(8,128)S(1)} %get-tuple-element.28), channel_id=1, source_target_pairs={{0,1},{1,0},{2,3},{3,2},{4,5},{5,4},{6,7},{7,6},{8,9},{9,8},{10,11... | collective-permute-start | bytes 98312 | tf_op jit(solution)/shard_map/ppermute | solution.py:473
  22.5 1.2 %collective-permute-start.6 = (f32[64,128]{1,0:T(8,128)S(1)}, f32[64,128]{1,0:T(8,128)S(1)}, u32[]{:S(2)}, u32[]{:S(2)}) collective-permute-start(f32[64,128]{1,0:T(8,128)S(1)} %get-tuple-element.29), channel_id=1, source_target_pairs={{0,2},{1,3},{2,0},{3,1},{4,6},{5,7},{6,4},{7,5},{8,10},{9,11},{10,... | collective-permute-start | bytes 98312 | tf_op jit(solution)/shard_map/ppermute | solution.py:473
  23.8 0.5 %collective-permute-start.7 = (f32[64,128]{1,0:T(8,128)S(1)}, f32[64,128]{1,0:T(8,128)S(1)}, u32[]{:S(2)}, u32[]{:S(2)}) collective-permute-start(f32[64,128]{1,0:T(8,128)S(1)} %get-tuple-element.30), channel_id=1, source_target_pairs={{0,3},{1,2},{2,1},{3,0},{4,7},{5,6},{6,5},{7,4},{8,11},{9,10},{10,... | collective-permute-start | bytes 98312 | tf_op jit(solution)/shard_map/ppermute | solution.py:473
  24.3 1.1 %collective-permute-done.6.refs_2_ = f32[64,128]{1,0:T(8,128)S(1)} collective-permute-done((f32[64,128]{1,0:T(8,128)S(1)}, f32[64,128]{1,0:T(8,128)S(1)}, u32[]{:S(2)}, u32[]{:S(2)}) %collective-permute-start.6) | collective-permute-done | bytes 32800 | tf_op jit(solution)/shard_map/ppermute | solution.py:473
  25.3 1.8 %collective-permute-done.7.refs_3_ = f32[64,128]{1,0:T(8,128)S(1)} collective-permute-done((f32[64,128]{1,0:T(8,128)S(1)}, f32[64,128]{1,0:T(8,128)S(1)}, u32[]{:S(2)}, u32[]{:S(2)}) %collective-permute-start.7) | collective-permute-done | bytes 32800 | tf_op jit(solution)/shard_map/ppermute | solution.py:473
  27.1 0.8 %shard_map.268 = (f32[4,64,128]{2,1,0:T(8,128)S(1)}, f32[16,512]{1,0:T(8,128)S(1)}) custom-call(f32[4,64,128]{2,1,0:T(8,128)S(1)} %get-tuple-element.27.refs_0_, f32[64,128]{1,0:T(8,128)S(1)} %collective-permute-done.5.refs_1_, f32[64,128]{1,0:T(8,128)S(1)} %collective-permute-done.6.refs_2_, f32[64,128]{1,0:T(8,128)S(1)} %collective-permute-done.7.refs_3_, ...), custom_call_target="tpu_custom_call" | custom-call | tf_op jit(solution)/shard_map/pallas_call | solution.py:149
  27.9 1.2 %collective-permute-start.10 = (f32[16,512]{1,0:T(8,128)S(1)}, f32[16,512]{1,0:T(8,128)S(1)}, u32[]{:S(2)}, u32[]{:S(2)}) collective-permute-start(f32[16,512]{1,0:T(8,128)S(1)} %get-tuple-element.32), channel_id=1, source_target_pairs={{0,24},{8,16},{16,8},{24,0},{1,25},{9,17},{17,9},{25,1},{2,26},{10... | collective-permute-start | bytes 98312 | tf_op jit(solution)/shard_map/ppermute | solution.py:161
  29.1 0.6 %collective-permute-start.9 = (f32[16,512]{1,0:T(8,128)S(1)}, f32[16,512]{1,0:T(8,128)S(1)}, u32[]{:S(2)}, u32[]{:S(2)}) collective-permute-start(f32[16,512]{1,0:T(8,128)S(1)} %get-tuple-element.32), channel_id=1, source_target_pairs={{0,16},{8,24},{16,0},{24,8},{1,17},{9,25},{17,1},{25,9},{2,18},{10... | collective-permute-start | bytes 98312 | tf_op jit(solution)/shard_map/ppermute | solution.py:161
  29.7 1.8 %collective-permute-start.8 = (f32[16,512]{1,0:T(8,128)S(1)}, f32[16,512]{1,0:T(8,128)S(1)}, u32[]{:S(2)}, u32[]{:S(2)}) collective-permute-start(f32[16,512]{1,0:T(8,128)S(1)} %get-tuple-element.32), channel_id=1, source_target_pairs={{0,8},{8,0},{16,24},{24,16},{1,9},{9,1},{17,25},{25,17},{2,10},{10... | collective-permute-start | bytes 98312 | tf_op jit(solution)/shard_map/ppermute | solution.py:161
  31.5 1.0 %collective-permute-done.10.refs_3_ = f32[16,512]{1,0:T(8,128)S(1)} collective-permute-done((f32[16,512]{1,0:T(8,128)S(1)}, f32[16,512]{1,0:T(8,128)S(1)}, u32[]{:S(2)}, u32[]{:S(2)}) %collective-permute-start.10) | collective-permute-done | bytes 32800 | tf_op jit(solution)/shard_map/ppermute | solution.py:161
  32.5 0.4 collective-permute-done.9.refs_2_
  32.9 0.9 %collective-permute-done.8.refs_1_ = f32[16,512]{1,0:T(8,128)S(1)} collective-permute-done((f32[16,512]{1,0:T(8,128)S(1)}, f32[16,512]{1,0:T(8,128)S(1)}, u32[]{:S(2)}, u32[]{:S(2)}) %collective-permute-start.8) | collective-permute-done | bytes 32800 | tf_op jit(solution)/shard_map/ppermute | solution.py:161
  33.8 1.0 %shard_map.269 = (f32[4,48,128]{2,1,0:T(8,128)S(1)}, f32[2,64,128]{2,1,0:T(8,128)S(1)}) custom-call(f32[4,64,128]{2,1,0:T(8,128)S(1)} %get-tuple-element.31.refs_0_, f32[16,512]{1,0:T(8,128)S(1)} %collective-permute-done.8.refs_1_, f32[16,512]{1,0:T(8,128)S(1)} %collective-permute-done.9.refs_2_, f32[16,512]{1,0:T(8,128)S(1)} %collective-permute-done.10.refs_3_, ...), custom_call_target="tpu_custom_call" | custom-call | tf_op jit(solution)/shard_map/pallas_call | solution.py:149
  34.8 1.8 %collective-permute-start.13 = (f32[4,48,128]{2,1,0:T(8,128)S(1)}, f32[4,48,128]{2,1,0:T(8,128)S(1)}, u32[]{:S(2)}, u32[]{:S(2)}) collective-permute-start(f32[4,48,128]{2,1,0:T(8,128)S(1)} %get-tuple-element.34.refs_2_), channel_id=1, source_target_pairs={{0,3},{1,2},{2,1},{3,0},{4,7},{5,6},{6,5},{7,4},{8,11},{9,10},{10,... | collective-permute-start | bytes 294920 | tf_op jit(solution)/shard_map/ppermute | solution.py:161
  36.6 0.8 %collective-permute-start.12 = (f32[4,48,128]{2,1,0:T(8,128)S(1)}, f32[4,48,128]{2,1,0:T(8,128)S(1)}, u32[]{:S(2)}, u32[]{:S(2)}) collective-permute-start(f32[4,48,128]{2,1,0:T(8,128)S(1)} %get-tuple-element.34.refs_2_), channel_id=1, source_target_pairs={{0,2},{1,3},{2,0},{3,1},{4,6},{5,7},{6,4},{7,5},{8,10},{9,11},{10,... | collective-permute-start | bytes 294920 | tf_op jit(solution)/shard_map/ppermute | solution.py:161
  37.4 2.4 %collective-permute-start.4 = (f32[128,128]{1,0:T(8,128)S(1)}, f32[128,128]{1,0:T(8,128)S(1)}, u32[]{:S(2)}, u32[]{:S(2)}) collective-permute-start(f32[128,128]{1,0:T(8,128)S(1)} %get-tuple-element.26), channel_id=1, source_target_pairs={{1,0},{2,1},{3,2},{5,4},{6,5},{7,6},{9,8},{10,9},{11,10},{13,12},{... | collective-permute-start | bytes 196616 | tf_op jit(solution)/shard_map/ppermute | solution.py:475
  39.8 3.2 %collective-permute-done.4.halo_ref = f32[128,128]{1,0:T(8,128)S(1)} collective-permute-done((f32[128,128]{1,0:T(8,128)S(1)}, f32[128,128]{1,0:T(8,128)S(1)}, u32[]{:S(2)}, u32[]{:S(2)}) %collective-permute-start.4) | collective-permute-done | bytes 65568 | tf_op jit(solution)/shard_map/ppermute | solution.py:475
  43.1 0.8 %shard_map.267 = f32[8,128,128]{2,1,0:T(8,128)} custom-call(f32[8,128,128]{2,1,0:T(8,128)S(1)} %copy-done.1, f32[4,128,128]{2,1,0:T(8,128)S(1)} %get-tuple-element.25.ixy_ref, f32[128,128]{1,0:T(8,128)S(1)} %collective-permute-done.4.halo_ref), custom_call_target="tpu_custom_call" | custom-call | tf_op jit(solution)/shard_map/pallas_call | solution.py:149
  44.0 0.1 copy-done.7
  44.4 2.3 %shard_map.270 = (f32[4,64,64]{2,1,0:T(8,128)}, f32[2,32,32]{2,1,0:T(8,128)}, f32[1,16,16]{2,1,0:T(8,128)}) custom-call(f32[4,64,128]{2,1,0:T(8,128)S(1)} %get-tuple-element.31.refs_0_, f32[2,64,128]{2,1,0:T(8,128)S(1)} %get-tuple-element.33.refs_1_, f32[4,48,128]{2,1,0:T(8,128)S(1)} %get-tuple-element.34.refs_2_, ...), custom_call_target="tpu_custom_call" | custom-call | tf_op jit(solution)/shard_map/pallas_call | solution.py:149
  (53 shorter events, 0.4 us)
Async XLA Ops:
  2.4 5.0 %copy-start.6 = (f32[2,128,256]{2,1,0:T(8,128)S(1)}, f32[2,128,256]{2,1,0:T(8,128)}, u32[]{:S(2)}) copy-start(f32[2,128,256]{2,1,0:T(8,128)} %constant.50.clone.refs_4_) | copy-start | bytes 786436
  2.4 5.0 %copy-start.13 = (f32[2,128,128]{2,1,0:T(8,128)S(1)}, f32[2,128,128]{2,1,0:T(8,128)}, u32[]{:S(2)}) copy-start(f32[2,128,128]{2,1,0:T(8,128)} %constant.48.clone.refs_2_) | copy-start | bytes 393220
  2.4 5.0 %copy-start.16 = (f32[2,16,256]{2,1,0:T(8,128)S(1)}, f32[2,16,256]{2,1,0:T(8,128)}, u32[]{:S(2)}) copy-start(f32[2,16,256]{2,1,0:T(8,128)} %constant.51.clone.refs_5_) | copy-start | bytes 98308
  2.4 5.0 %copy-start.18 = (f32[4,8,128]{2,1,0:T(8,128)S(1)}, f32[4,8,128]{2,1,0:T(8,128)}, u32[]{:S(2)}) copy-start(f32[4,8,128]{2,1,0:T(8,128)} %constant.52.clone.refs_6_) | copy-start | bytes 49156
  2.4 5.0 %copy-start.19 = (f32[2,16,128]{2,1,0:T(8,128)S(1)}, f32[2,16,128]{2,1,0:T(8,128)}, u32[]{:S(2)}) copy-start(f32[2,16,128]{2,1,0:T(8,128)} %constant.49.clone.refs_3_) | copy-start | bytes 49156
  3.1 13.9 %copy-start.5 = (f32[4,64,152]{2,1,0:T(8,128)S(1)}, f32[4,64,152]{2,1,0:T(8,128)}, u32[]{:S(2)}) copy-start(f32[4,64,152]{2,1,0:T(8,128)} %constant.53.clone.refs_7_) | copy-start | bytes 466948
  3.1 13.9 %copy-start.12 = (f32[4,64,88]{2,1,0:T(8,128)S(1)}, f32[4,64,88]{2,1,0:T(8,128)}, u32[]{:S(2)}) copy-start(f32[4,64,88]{2,1,0:T(8,128)} %constant.54.clone.refs_8_) | copy-start | bytes 270340
  3.1 4.3 %collective-permute-start = (f32[16,1280]{1,0:T(8,128)S(1)}, f32[16,1280]{1,0:T(8,128)S(1)}, u32[]{:S(2)}, u32[]{:S(2)}) collective-permute-start(f32[16,1280]{1,0:T(8,128)S(1)} %shard_map.264), channel_id=1, source_target_pairs={{0,4},{4,0},{1,5},{5,1},{2,6},{6,2},{3,7},{7,3},{8,12},{12,8},{9,1... | collective-permute-start | bytes 245768 | tf_op jit(solution)/shard_map/ppermute | solution.py:161
  10.0 4.6 %collective-permute-start.3 = (f32[8,8,128]{2,1,0:T(8,128)S(1)}, f32[8,8,128]{2,1,0:T(8,128)S(1)}, u32[]{:S(2)}, u32[]{:S(2)}) collective-permute-start(f32[8,8,128]{2,1,0:T(8,128)S(1)} %get-tuple-element.24.refs_3_), channel_id=1, source_target_pairs={{0,24},{8,16},{16,8},{24,0},{1,25},{9,17},{17,9},{25,1},{2,26},{10... | collective-permute-start | bytes 98312 | tf_op jit(solution)/shard_map/ppermute | solution.py:161
  13.3 3.7 %collective-permute-start.2 = (f32[8,8,128]{2,1,0:T(8,128)S(1)}, f32[8,8,128]{2,1,0:T(8,128)S(1)}, u32[]{:S(2)}, u32[]{:S(2)}) collective-permute-start(f32[8,8,128]{2,1,0:T(8,128)S(1)} %get-tuple-element.24.refs_3_), channel_id=1, source_target_pairs={{0,16},{8,24},{16,0},{24,8},{1,17},{9,25},{17,1},{25,9},{2,18},{10... | collective-permute-start | bytes 98312 | tf_op jit(solution)/shard_map/ppermute | solution.py:161
  13.3 3.7 %collective-permute-start.1 = (f32[8,8,128]{2,1,0:T(8,128)S(1)}, f32[8,8,128]{2,1,0:T(8,128)S(1)}, u32[]{:S(2)}, u32[]{:S(2)}) collective-permute-start(f32[8,8,128]{2,1,0:T(8,128)S(1)} %get-tuple-element.24.refs_3_), channel_id=1, source_target_pairs={{0,8},{8,0},{16,24},{24,16},{1,9},{9,1},{17,25},{25,17},{2,10},{10... | collective-permute-start | bytes 98312 | tf_op jit(solution)/shard_map/ppermute | solution.py:161
  17.7 9.4 %copy-start.17 = (f32[4,16,64]{2,1,0:T(8,128)S(1)}, f32[4,16,64]{2,1,0:T(8,128)}, u32[]{:S(2)}) copy-start(f32[4,16,64]{2,1,0:T(8,128)} %constant.57.clone.refs_4_) | copy-start | bytes 49156
  17.7 16.1 %copy-start.3 = (f32[2,384,128]{2,1,0:T(8,128)S(1)}, f32[2,384,128]{2,1,0:T(8,128)}, u32[]{:S(2)}) copy-start(f32[2,384,128]{2,1,0:T(8,128)} %constant.60.clone.refs_6_) | copy-start | bytes 1179652
  17.7 16.1 %copy-start.4 = (f32[4,144,112]{2,1,0:T(8,128)S(1)}, f32[4,144,112]{2,1,0:T(8,128)}, u32[]{:S(2)}) copy-start(f32[4,144,112]{2,1,0:T(8,128)} %constant.58.clone.refs_4_) | copy-start | bytes 774148
  19.3 5.0 %collective-permute-start.5 = (f32[64,128]{1,0:T(8,128)S(1)}, f32[64,128]{1,0:T(8,128)S(1)}, u32[]{:S(2)}, u32[]{:S(2)}) collective-permute-start(f32[64,128]{1,0:T(8,128)S(1)} %get-tuple-element.28), channel_id=1, source_target_pairs={{0,1},{1,0},{2,3},{3,2},{4,5},{5,4},{6,7},{7,6},{8,9},{9,8},{10,11... | collective-permute-start | bytes 98312 | tf_op jit(solution)/shard_map/ppermute | solution.py:473
  22.5 2.8 %collective-permute-start.6 = (f32[64,128]{1,0:T(8,128)S(1)}, f32[64,128]{1,0:T(8,128)S(1)}, u32[]{:S(2)}, u32[]{:S(2)}) collective-permute-start(f32[64,128]{1,0:T(8,128)S(1)} %get-tuple-element.29), channel_id=1, source_target_pairs={{0,2},{1,3},{2,0},{3,1},{4,6},{5,7},{6,4},{7,5},{8,10},{9,11},{10,... | collective-permute-start | bytes 98312 | tf_op jit(solution)/shard_map/ppermute | solution.py:473
  23.8 3.3 %collective-permute-start.7 = (f32[64,128]{1,0:T(8,128)S(1)}, f32[64,128]{1,0:T(8,128)S(1)}, u32[]{:S(2)}, u32[]{:S(2)}) collective-permute-start(f32[64,128]{1,0:T(8,128)S(1)} %get-tuple-element.30), channel_id=1, source_target_pairs={{0,3},{1,2},{2,1},{3,0},{4,7},{5,6},{6,5},{7,4},{8,11},{9,10},{10,... | collective-permute-start | bytes 98312 | tf_op jit(solution)/shard_map/ppermute | solution.py:473
  27.1 6.7 %copy-start.10 = (f32[2,128,128]{2,1,0:T(8,128)S(1)}, f32[2,128,128]{2,1,0:T(8,128)}, u32[]{:S(2)}) copy-start(f32[2,128,128]{2,1,0:T(8,128)} %constant.61.clone.refs_7_) | copy-start | bytes 393220
  27.1 6.7 %copy-start.11 = (f32[4,64,112]{2,1,0:T(8,128)S(1)}, f32[4,64,112]{2,1,0:T(8,128)}, u32[]{:S(2)}) copy-start(f32[4,64,112]{2,1,0:T(8,128)} %constant.59.clone.refs_5_) | copy-start | bytes 344068
  27.9 4.6 %collective-permute-start.10 = (f32[16,512]{1,0:T(8,128)S(1)}, f32[16,512]{1,0:T(8,128)S(1)}, u32[]{:S(2)}, u32[]{:S(2)}) collective-permute-start(f32[16,512]{1,0:T(8,128)S(1)} %get-tuple-element.32), channel_id=1, source_target_pairs={{0,24},{8,16},{16,8},{24,0},{1,25},{9,17},{17,9},{25,1},{2,26},{10... | collective-permute-start | bytes 98312 | tf_op jit(solution)/shard_map/ppermute | solution.py:161
  29.1 3.8 %collective-permute-start.9 = (f32[16,512]{1,0:T(8,128)S(1)}, f32[16,512]{1,0:T(8,128)S(1)}, u32[]{:S(2)}, u32[]{:S(2)}) collective-permute-start(f32[16,512]{1,0:T(8,128)S(1)} %get-tuple-element.32), channel_id=1, source_target_pairs={{0,16},{8,24},{16,0},{24,8},{1,17},{9,25},{17,1},{25,9},{2,18},{10... | collective-permute-start | bytes 98312 | tf_op jit(solution)/shard_map/ppermute | solution.py:161
  29.7 4.1 %collective-permute-start.8 = (f32[16,512]{1,0:T(8,128)S(1)}, f32[16,512]{1,0:T(8,128)S(1)}, u32[]{:S(2)}, u32[]{:S(2)}) collective-permute-start(f32[16,512]{1,0:T(8,128)S(1)} %get-tuple-element.32), channel_id=1, source_target_pairs={{0,8},{8,0},{16,24},{24,16},{1,9},{9,1},{17,25},{25,17},{2,10},{10... | collective-permute-start | bytes 98312 | tf_op jit(solution)/shard_map/ppermute | solution.py:161
  33.8 9.2 %copy-start.1 = (f32[8,128,128]{2,1,0:T(8,128)S(1)}, f32[8,128,128]{2,1,0:T(8,128)}, u32[]{:S(2)}) copy-start(f32[8,128,128]{2,1,0:T(8,128)} %u_ref.3) | copy-start | bytes 1572868
  34.8 9.1 %collective-permute-start.13 = (f32[4,48,128]{2,1,0:T(8,128)S(1)}, f32[4,48,128]{2,1,0:T(8,128)S(1)}, u32[]{:S(2)}, u32[]{:S(2)}) collective-permute-start(f32[4,48,128]{2,1,0:T(8,128)S(1)} %get-tuple-element.34.refs_2_), channel_id=1, source_target_pairs={{0,3},{1,2},{2,1},{3,0},{4,7},{5,6},{6,5},{7,4},{8,11},{9,10},{10,... | collective-permute-start | bytes 294920 | tf_op jit(solution)/shard_map/ppermute | solution.py:161
  36.6 7.3 %collective-permute-start.12 = (f32[4,48,128]{2,1,0:T(8,128)S(1)}, f32[4,48,128]{2,1,0:T(8,128)S(1)}, u32[]{:S(2)}, u32[]{:S(2)}) collective-permute-start(f32[4,48,128]{2,1,0:T(8,128)S(1)} %get-tuple-element.34.refs_2_), channel_id=1, source_target_pairs={{0,2},{1,3},{2,0},{3,1},{4,6},{5,7},{6,4},{7,5},{8,10},{9,11},{10,... | collective-permute-start | bytes 294920 | tf_op jit(solution)/shard_map/ppermute | solution.py:161
  37.4 6.5 %collective-permute-start.11 = (f32[4,48,128]{2,1,0:T(8,128)S(1)}, f32[4,48,128]{2,1,0:T(8,128)S(1)}, u32[]{:S(2)}, u32[]{:S(2)}) collective-permute-start(f32[4,48,128]{2,1,0:T(8,128)S(1)} %get-tuple-element.34.refs_2_), channel_id=1, source_target_pairs={{0,1},{1,0},{2,3},{3,2},{4,5},{5,4},{6,7},{7,6},{8,9},{9,8},{10,11... | collective-permute-start | bytes 294920 | tf_op jit(solution)/shard_map/ppermute | solution.py:161
  37.4 5.6 %collective-permute-start.4 = (f32[128,128]{1,0:T(8,128)S(1)}, f32[128,128]{1,0:T(8,128)S(1)}, u32[]{:S(2)}, u32[]{:S(2)}) collective-permute-start(f32[128,128]{1,0:T(8,128)S(1)} %get-tuple-element.26), channel_id=1, source_target_pairs={{1,0},{2,1},{3,2},{5,4},{6,5},{7,6},{9,8},{10,9},{11,10},{13,12},{... | collective-permute-start | bytes 196616 | tf_op jit(solution)/shard_map/ppermute | solution.py:475
  43.0 1.3 %copy-start.8 = (f32[2,128,128]{2,1,0:T(8,128)S(1)}, f32[2,128,128]{2,1,0:T(8,128)}, u32[]{:S(2)}) copy-start(f32[2,128,128]{2,1,0:T(8,128)} %constant.63.clone.refs_7_) | copy-start | bytes 393220
  43.0 1.3 %copy-start.9 = (f32[4,64,48]{2,1,0:T(8,128)S(1)}, f32[4,64,48]{2,1,0:T(8,128)}, u32[]{:S(2)}) copy-start(f32[4,64,48]{2,1,0:T(8,128)} %constant.62.clone.refs_6_) | copy-start | bytes 147460
  43.0 1.3 %copy-start.14 = (f32[4,48,48]{2,1,0:T(8,128)S(1)}, f32[4,48,48]{2,1,0:T(8,128)}, u32[]{:S(2)}) copy-start(f32[4,48,48]{2,1,0:T(8,128)} %constant.64.clone.refs_8_) | copy-start | bytes 110596
  43.1 1.3 %copy-start.15 = (f32[4,32,48]{2,1,0:T(8,128)S(1)}, f32[4,32,48]{2,1,0:T(8,128)}, u32[]{:S(2)}) copy-start(f32[4,32,48]{2,1,0:T(8,128)} %constant.66.clone.refs_10_) | copy-start | bytes 73732
  43.1 1.3 %copy-start.23 = (f32[4,10]{1,0:T(4,128)S(1)}, f32[4,10]{1,0:T(4,128)}, u32[]{:S(2)}) copy-start(f32[4,10]{1,0:T(4,128)} %constant.68.clone.refs_12_) | copy-start | bytes 484
  (7 other events, 6.0 us)

commit v2 on v1

--- a/solution.py
+++ b/solution.py
@@ -143,15 +143,15 @@
     return lax.dot_general(a, b, (dims, ((), ())), precision=highest, preferred_element_type=jnp.float32)
 
 
-def kernel_call(body, outs, arrays, scalars=0, scratch=()):
-    specs = [pl.BlockSpec(memory_space=pltpu.VMEM)] * (len(arrays) - scalars)
-    specs += [pl.BlockSpec(memory_space=pltpu.SMEM)] * scalars
+def kernel_call(body, outs, arrays, scratch=(), left=(), left_out=(), aliases={}):
+    space = lambda place, where: pl.BlockSpec(memory_space=pl.ANY if place in where else pltpu.VMEM)
     return pl.pallas_call(
         body,
         out_shape=[jax.ShapeDtypeStruct(shape, jnp.float32) for shape in outs],
-        in_specs=specs,
-        out_specs=[pl.BlockSpec(memory_space=pltpu.VMEM)] * len(outs),
+        in_specs=[space(i, left) for i in range(len(arrays))],
+        out_specs=[space(i, left_out) for i in range(len(outs))],
         scratch_shapes=list(scratch),
+        input_output_aliases=aliases,
         compiler_params=pltpu.CompilerParams(vmem_limit_bytes=40 << 20),
     )(*arrays)
 
@@ -159,6 +159,14 @@
 def swapped(value, axis):
     count = lax.axis_size(axis)
     return [lax.ppermute(value, axis, [(i, i ^ k) for i in range(count)]) for k in range(1, count)]
+
+
+def chosen_by(values, j):
+    chosen = float(values[0])
+    for place in range(1, len(values)):
+        if any(values[place] != values[0] for place in range(len(values))):
+            chosen = jnp.where(j == place, f32(values[place]), chosen)
+    return chosen
 
 
 def iota(shape, dim):
@@ -180,9 +188,9 @@
     ky, ky2, ky3 = yone.kept, ytwo.kept, ythree.kept
     kya = round_up(ky + 3, 16)
     kys = round_up(ky + 2, 16)
-    wide = round_up(yone.n + ky * (dy - 1) + 1, 128)
+    wide1 = yone.n + ky * (dy - 1)
     wide2 = ytwo.n + ky2 * (dy - 1)
-    packed = round_up(3 * wide2, 128)
+    wide = packed = round_up(max(wide1 + 1, 3 * wide2, wide2 + wide1), 128)
     kx = round_up(xtwo.functional_count, 8)
     rowsx = xtwo.fine + kx * (dx - 1)
     tall = round_up(xtwo.n + xtwo.kept * (dx - 1), 8)
@@ -215,12 +223,11 @@
         else:
             wa[j, kya * ((j ^ (j + 1)) - 1) + len(pick_a) - 1, wide - 1] = 0.5
 
-    fx = np.zeros((dx, 8, lx))
+    fx = np.zeros((dx, lx, 8))
     txa = np.zeros((dx, xone.n, lx + 8 * (dx - 1)))
     txm = np.zeros((dx, xone.n, xone.n + 8 * (dx - 1)))
-    hx = np.zeros((dx, dx))
     for j in range(dx):
-        fx[j, :2] = xone.functionals[j][2:4]
+        fx[j, :, :2] = xone.functionals[j][2:4].T
         product, even, around = xone.tables(j)
         txa[j, :, :lx] = product[:, :lx]
         txm[j, :, : xone.n] = around[:, :lx:2]
@@ -228,7 +235,6 @@
             txa[j, :, lx + 8 * place : lx + 8 * place + 2] = product[:, lx + 4 * place + 2 : lx + 4 * place + 4]
             begin = xone.n + 8 * place
             txm[j, :, begin + 2 : begin + 4] = around[:, lx + 4 * place : lx + 4 * place + 2]
-        hx[j, 0 if j == dx - 1 else j ^ (j + 1)] = 1.0
 
     zn = zone.n
     zs = np.zeros((dz, 2 * lz + 2 + zn * (lz + dz + 1)))
@@ -271,6 +277,8 @@
     ty3 = np.zeros((dy, 3 * packed, 128))
     qy3 = np.zeros((dy, packed, 128))
     py3 = np.zeros((dy, packed, round_up(ytwo.fine, 128)))
+    px1 = np.zeros((lx, 2 * tall))
+    py1 = np.zeros((dy, packed, ly))
     for j in range(dy):
         for c, table in enumerate(ytwo.tables(j)):
             ty2[j, c * wide : c * wide + table.shape[1], c * wide2 : c * wide2 + wide2] = table.T
@@ -278,7 +286,12 @@
         for c, table in enumerate(ythree.tables(j)):
             ty3[j, c * packed : c * packed + table.shape[1], : ythree.n] = (-1.0 if c == 2 else 1.0) * table.T
         qy3[j, :, : ythree.fine] = interpolation(ythree, j, packed, ky2, False).T
+        py1[j, wide2:] = interpolation(yone, j, packed - wide2, ky, True).T
         py3[j, wide2:, : ytwo.fine] = interpolation(ytwo, j, packed - wide2, ky2, True).T
+    for c in range(xone.n):
+        begin = c if c < xtwo.n else tall + c - xtwo.n
+        px1[2 * c, begin] = 1.0
+        px1[2 * c + 1, begin : begin + 2] = 0.5
     az2, first2, last2 = (t.tolist() for t in dense(nz // 2))
     az3, first3, last3 = dense(nz // 4)
     z2, z3 = nz // 2, nz // 4
@@ -312,9 +325,12 @@
         tsm_out[...] = tsm_all
         xm_out[...] = jnp.zeros_like(xm_out)
         lane = iota((lx, ly), 1)
+        weights = [jnp.broadcast_to(fx_ref[jx, :, c : c + 1], (lx, wide)) for c in range(2)]
+        xm_out[0, 5:6, :wide] = tsm_all[0:1, :wide]
         for z in range(lz):
             part = ta_all[z * lx : (z + 1) * lx]
-            xm_out[z, 0:2, :wide] = dot(fx_ref[jx], part)[0:2]
+            for c in range(2):
+                xm_out[z, c : c + 1, :wide] = jnp.sum(part * weights[c], axis=0, keepdims=True)
             if z % 2 == 0:
                 half = z // 2
                 tm = tsm_all[half * hx1 : (half + 1) * hx1, wide:]
@@ -331,14 +347,23 @@
     def x_apply(*refs):
         ta_ref, tsm_ref, iy_ref, own_ref = refs[:4]
         came = refs[4 : 3 + dx]
-        txa_ref, txm_ref, hx_ref, zs_ref = refs[3 + dx : 7 + dx]
-        ixy_out, first_out, u1_out = refs[7 + dx : 10 + dx]
-        planes_out = refs[10 + dx :]
+        txa_ref, txm_ref, ixy_out, zc_out, u1_out = refs[3 + dx : 8 + dx]
+        planes_out = refs[8 + dx :]
         jx, jz = lax.axis_index("gx"), lax.axis_index("gz")
         xa, xm, diff = [], [], []
-        for z in range(lz):
-            stacked = jnp.concatenate([ta_ref[z * lx : (z + 1) * lx, :]] + [r[z, :, :wide] for r in came], axis=0)
-            xa.append(dot(txa_ref[jx], stacked))
+        def from_next(own, rows):
+            for k, rest in enumerate(rows):
+                own = jnp.where((jx ^ (k + 1)) == jx + 1, rest, own)
+            return own
+
+        for z in range(0, lz, 2):
+            pair = jnp.concatenate([ta_ref[z * lx : (z + 1) * lx, :], ta_ref[(z + 1) * lx : (z + 2) * lx, :]], axis=1)
+            rest = [jnp.concatenate([r[z, :, :wide], r[z + 1, :, :wide]], axis=1) for r in came]
+            both = dot(txa_ref[jx], jnp.concatenate([pair] + rest, axis=0))
+            xa += [both[:, :wide], both[:, wide:]]
+        zc_out[...] = jnp.zeros_like(zc_out)
+        zc_out[:hx1] = tsm_ref[:hx1, :wide]
+        zc_out[hx1 : hx1 + 1] = from_next(tsm_ref[hx1 - 1 : hx1, :wide], [r[0, 5:6, :wide] for r in came])
         row = iota((lx, ly), 0)
         for half in range(hz):
             part = tsm_ref[half * hx1 : (half + 1) * hx1, :]
@@ -346,16 +371,12 @@
             xm.append(dot(txm_ref[jx], stacked))
             diff.append(part[:, :wide] - xm[-1])
             iy = iy_ref[half]
-            halo = hx_ref[jx, 0] * iy[lx - 2 : lx - 1]
-            for k, r in enumerate(came):
-                halo += hx_ref[jx, k + 1] * r[2 * half, 4:5, :ly]
+            halo = from_next(iy[lx - 2 : lx - 1], [r[2 * half, 4:5, :ly] for r in came])
             before, after = pltpu.roll(iy, 1, 0), pltpu.roll(iy, lx - 1, 0)
             after = jnp.where(row == lx - 1, jnp.broadcast_to(halo, (lx, ly)), after)
             ixy = jnp.where(row % 2 == 1, 0.5 * (before + after), iy)
             ixy_out[half] = ixy
-            if half == 0:
-                first_out[...] = ixy
-        scalar = lambda place: zs_ref[jz, place]
+        scalar = lambda place: chosen_by(zs[:, place], jz)
         for zc in range(zn):
             total = diff[zc] - scalar(at_first + zc) * xm[0] - scalar(at_last + zc) * xm[hz - 1]
             for z in range(lz):
@@ -371,26 +392,25 @@
 
     def z_apply(*refs):
         part_ref, came = refs[0], refs[1:dz]
-        f2x_ref, zs_ref, u1_out, xt_out = refs[dz:]
+        f2x_ref, u1_out, xt_out = refs[dz:]
         jx, jz = lax.axis_index("gx"), lax.axis_index("gz")
         for zc in range(zn):
             total = part_ref[zc]
             for k, r in enumerate(came):
-                total += zs_ref[jz, at_reach + k * zn + zc] * r[...]
+                total += chosen_by(zs[:, at_reach + k * zn + zc], jz) * r[...]
             u1_out[zc] = total
             xt_out[:, zc * wide : (zc + 1) * wide] = dot(f2x_ref[jx], total)
 
-    def fine_coefficients(u_ref, ixy_ref, halo_ref, out_ref):
-        jz = lax.axis_index("gz")
+    def fine_coefficients(u_ref, ixy_ref, out_ref):
         for half in range(hz):
             here = ixy_ref[half]
             out_ref[2 * half] = u_ref[2 * half] - here
-            after = ixy_ref[half + 1] if half + 1 < hz else jnp.where(jz == dz - 1, here, halo_ref[...])
-            out_ref[2 * half + 1] = u_ref[2 * half + 1] - 0.5 * (here + after)
+            if half + 1 < hz:
+                out_ref[2 * half + 1] = u_ref[2 * half + 1] - 0.5 * (here + ixy_ref[half + 1])
 
     def second_apply(*refs):
-        u1_ref, came = refs[0], refs[1:dx]
-        tx2_ref, qx2_ref, ty2_ref, qy2_ref, zt_out, i2_out = refs[dx:]
+        u1_ref, zc_ref, came = refs[0], refs[1], refs[2 : dx + 1]
+        tx2_ref, qx2_ref, ty2_ref, qy2_ref, zt_out, i2_out = refs[dx + 1 :]
         jx, jy = lax.axis_index("gx"), lax.axis_index("gy")
         own = jnp.concatenate([u1_ref[z] for z in range(lz2)], axis=1)
         state = jnp.concatenate([own] + [r[...] for r in came], axis=0)
@@ -398,20 +418,33 @@
         spread = dot(qx2_ref[jx], state)
         for z in range(lz2):
             cut = across[:, z * wide : (z + 1) * wide]
-            joined = jnp.concatenate([cut[c * tall : (c + 1) * tall] for c in range(3)], axis=1)
-            zt_out[z] = dot(joined, ty2_ref[jy])
-            if z % 2 == 0:
+            if z % 2 == 1:
+                moved = dot(cut[:tall], ty2_ref[jy, :wide])
+                if z < 4:
+                    begin = xtwo.n * (z // 2)
+                    moved += pltpu.roll(zc_ref[begin : begin + tall], wide2, 1)
+                zt_out[z] = moved
+            else:
+                joined = jnp.concatenate([cut[c * tall : (c + 1) * tall] for c in range(3)], axis=1)
+                zt_out[z] = dot(joined, ty2_ref[jy])
                 i2_out[z // 2] = dot(spread[:, z * wide : (z + 1) * wide], qy2_ref[jy])
 
     def third_apply(*refs):
-        u1_ref, i2_ref, own_ref = refs[:3]
-        came = refs[3 : 2 + dz]
-        px3_ref, py3_ref, tx3_ref, ty3_ref, qx3_ref, qy3_ref, zt_ref = refs[2 + dz : 9 + dz]
-        middle_out, coarse_out, coarsest_out, zbuf, ubuf = refs[9 + dz :]
+        u1_ref, i2_ref, u_ref, ixy_ref, _, own_ref = refs[:6]
+        came = refs[6 : 5 + dz]
+        px1_ref, py1_ref, px3_ref, py3_ref, tx3_ref, ty3_ref, qx3_ref, qy3_ref = refs[5 + dz : 13 + dz]
+        fine_out, middle_out, coarse_out, coarsest_out, zbuf, ubuf, last, sem = refs[13 + dz :]
         jx, jy, jz = lax.axis_index("gx"), lax.axis_index("gy"), lax.axis_index("gz")
         zbuf[pl.ds(jz * lz2, lz2)] = own_ref[...]
         for k, r in enumerate(came):
             zbuf[pl.ds((jz ^ (k + 1)) * lz2, lz2)] = r[...]
+        at = jnp.minimum(jz + 1, dz - 1) * lz2
+        first = jnp.concatenate([zbuf[at + 1], zbuf[at + 3]], axis=0)
+        halo = dot(dot(px1_ref[...], first), py1_ref[jy])
+        here = ixy_ref[hz - 1]
+        last[...] = u_ref[lz - 1] - 0.5 * (here + jnp.where(jz == dz - 1, here, halo))
+        copy = pltpu.make_async_copy(last, fine_out.at[lz - 1], sem)
+        copy.start()
         at = jnp.minimum((jz + 1) * lz2, z2 - 2)
         halo = dot(dot(px3_ref[jx], zbuf[at]), py3_ref[jy])
         fy = ytwo.fine
@@ -440,11 +473,11 @@
         n3 = xthree.n
         for zc in range(lz4):
             base = zc * (z3 + 2)
-            along = zt_ref[jz, base] * ubuf[0]
+            along = chosen_by(zt[:, base], jz) * ubuf[0]
             for z in range(1, z3):
-                along += zt_ref[jz, base + z] * ubuf[z]
+                along += chosen_by(zt[:, base + z], jz) * ubuf[z]
             even = ubuf[2 * (jz * lz4 + zc)]
-            around = even + zt_ref[jz, base + z3] * ubuf[0] + zt_ref[jz, base + z3 + 1] * ubuf[z3 - 2]
+            around = even + chosen_by(zt[:, base + z3], jz) * ubuf[0] + chosen_by(zt[:, base + z3 + 1], jz) * ubuf[z3 - 2]
             joined = jnp.concatenate(
                 [
                     dot(tx3_ref[jx, c * n3 : (c + 1) * n3, :], plane)
@@ -453,6 +486,7 @@
                 axis=1,
             )
             coarsest_out[zc] = dot(joined, ty3_ref[jy])[:, : ythree.n]
+        copy.wait()
 
     (ym,) = kernel_call(y_messages, [(max(kya, kys), lz * lx + hz * hx1)], [field, *to32(fya, fys)])
     ycame = swapped(ym, "gy")
@@ -463,38 +497,37 @@
         [field, *ycame, *to32(ta, wa, tsm, wsm, fx)],
     )
     xcame = swapped(xm, "gx")
-    ixy, zfirst, u1_part, *planes = kernel_call(
+    ixy, zc, u1_part, *planes = kernel_call(
         x_apply,
-        [(hz, lx, ly), (lx, ly), (zn, xone.n, wide)] + [(xone.n, wide)] * (dz - 1),
-        [ta_v, tsm_v, iy, xm, *xcame, *to32(txa, txm, hx, zs)],
-        scalars=2,
+        [(hz, lx, ly), (xtwo.n + tall, wide), (zn, xone.n, wide)] + [(xone.n, wide)] * (dz - 1),
+        [ta_v, tsm_v, iy, xm, *xcame, *to32(txa, txm)],
     )
     zcame = [
         lax.ppermute(plane, "gz", [(i, i ^ (k + 1)) for i in range(dz)]) for k, plane in enumerate(planes)
     ]
-    zhalo = lax.ppermute(zfirst, "gz", [(i + 1, i) for i in range(dz - 1)])
-    u1, xt = kernel_call(
-        z_apply,
-        [(zn, xone.n, wide), (kx, zn * wide)],
-        [u1_part, *zcame, *to32(f2x, zs)],
-        scalars=1,
-    )
+    u1, xt = kernel_call(z_apply, [(zn, xone.n, wide), (kx, zn * wide)], [u1_part, *zcame, *to32(f2x)])
     xtcame = swapped(xt, "gx")
-    (fine,) = kernel_call(fine_coefficients, [(lz, lx, ly)], [field, ixy, zhalo])
     zmsg, i2 = kernel_call(
         second_apply,
         [(lz2, tall, packed), (lz2 // 2, xtwo.fine, round_up(ytwo.fine, 128))],
-        [u1, *xtcame, *to32(tx2, qx2, ty2, qy2)],
+        [u1, zc, *xtcame, *to32(tx2, qx2, ty2, qy2)],
     )
     ztcame = swapped(zmsg, "gz")
-    middle, coarse, coarsest = kernel_call(
+    (fine,) = kernel_call(fine_coefficients, [(lz, lx, ly)], [field, ixy])
+    return kernel_call(
         third_apply,
-        [(lz2, xtwo.fine, ytwo.fine), (lz3, xthree.fine, ythree.fine), (lz4, xthree.n, ythree.n)],
-        [u1, i2, zmsg, *ztcame, *to32(px3, py3, tx3, ty3, qx3, qy3, zt)],
-        scalars=1,
-        scratch=[pltpu.VMEM((z2, tall, packed), jnp.float32), pltpu.VMEM((z3, tall, packed), jnp.float32)],
+        [(lz, lx, ly), (lz2, xtwo.fine, ytwo.fine), (lz3, xthree.fine, ythree.fine), (lz4, xthree.n, ythree.n)],
+        [u1, i2, field, ixy, fine, zmsg, *ztcame, *to32(px1, py1, px3, py3, tx3, ty3, qx3, qy3)],
+        scratch=[
+            pltpu.VMEM((z2, tall, packed), jnp.float32),
+            pltpu.VMEM((z3, tall, packed), jnp.float32),
+            pltpu.VMEM((lx, ly), jnp.float32),
+            pltpu.SemaphoreType.DMA,
+        ],
+        left=(4,),
+        left_out=(0,),
+        aliases={4: 0},
     )
-    return fine, middle, coarse, coarsest
 
 
 def solution(mesh):

time: 47.1 us -> 42.7 us (0.907)
  Pallas kernels: 9.84 us -> 7.21 us
  starting transfers between devices: 19.2 us -> 16.9 us
  waiting for transfers between devices: 13.9 us -> 14.4 us
    ppermute x10, waiting for transfers between devices: 7.83 us -> 11.5 us  [swapped(): lax.ppermute(value, axis, [(i, i ^ k) for i in range(count)])]
    ppermute x1 -> x0, waiting for transfers between devices: 3.16 us -> none  [shards(): zhalo = lax.ppermute(zfirst, 'gz', [(i + 1, i) for i in range(dz - 1)])]
    pallas_call x7, Pallas kernels: 9.84 us -> 7.21 us  [kernel_call(): pl.pallas_call(body, out_shape=[jax.ShapeDtypeStruct(shape, jnp.float32)...]
    ppermute x1 -> x0, starting transfers between devices: 2.4 us -> none  [shards(): zhalo = lax.ppermute(zfirst, 'gz', [(i + 1, i) for i in range(dz - 1)])]
    unnamed x50 -> x48, local copies, waits for them, and re-layouts: 2.95 us -> 2.77 us
  transfers between devices with their start and end apart: 14 -> 13, of which waited for: 9 -> 10; matrix products, arithmetic and copies ran while one was open for 0% -> 0% of each run, Pallas kernels for 2% -> 2%
where the time goes in v2:
time: 42.7 us; the launch traced here: 42.2 us
  starting transfers between devices  16.9 us (40%)
  waiting for transfers between devices  14.4 us (34%)
  Pallas kernels  7.21 us (17%)
  local copies, waits for them, and re-layouts  2.77 us (6%)
  between operations  0.88 us (2%)
    ppermute x10, starting transfers between devices, swapped(): lax.ppermute(value, axis, [(i, i ^ k) for i in range(count)])  11.9 us
    ppermute x10, waiting for transfers between devices, swapped(): lax.ppermute(value, axis, [(i, i ^ k) for i in range(count)])  11.5 us
    pallas_call x7, Pallas kernels, kernel_call(): pl.pallas_call(body, out_shape=[jax.ShapeDtypeStruct(shape, jnp.float32)...  7.21 us
    ppermute x3, starting transfers between devices, shards(): lax.ppermute(plane, 'gz', [(i, i ^ k + 1) for i in range(dz)])  4.99 us
    ppermute x3, waiting for transfers between devices, shards(): lax.ppermute(plane, 'gz', [(i, i ^ k + 1) for i in range(dz)])  2.86 us
    unnamed x48, local copies, waits for them, and re-layouts  2.77 us
  transfers between devices with their start and end apart: 13, of which 10 were waited for; matrix products, arithmetic and copies ran while one was open for 0% of the time, Pallas kernels for 2%

profile of v2, /device:TPU:1, one launch (start us, length us, event | category | flops | bytes accessed | tf_op | source)
XLA Modules:
  0.0 42.2 jit_solution(4687785737666481095)
XLA Ops:
  0.7 0.7 %copy-done.22 = f32[2,16,128]{2,1,0:T(8,128)S(1)} copy-done((f32[2,16,128]{2,1,0:T(8,128)S(1)}, f32[2,16,128]{2,1,0:T(8,128)}, u32[]{:S(2)}) %copy-start.22) | copy-done | bytes 16408
  1.4 0.0 copy-done.23
  1.4 1.0 %copy-done = f32[8,128,128]{2,1,0:T(8,128)S(1)} copy-done((f32[8,128,128]{2,1,0:T(8,128)S(1)}, f32[8,128,128]{2,1,0:T(8,128)}, u32[]{:S(2)}) %copy-start) | copy-done | bytes 524312
  2.4 0.6 %shard_map.246 = f32[16,1280]{1,0:T(8,128)S(1)} custom-call(f32[8,128,128]{2,1,0:T(8,128)S(1)} %copy-done, f32[2,16,128]{2,1,0:T(8,128)S(1)} %copy-done.23, f32[2,16,128]{2,1,0:T(8,128)S(1)} %copy-done.22), custom_call_target="tpu_custom_call" | custom-call | tf_op jit(solution)/shard_map/pallas_call | solution.py:148
  3.1 2.1 %collective-permute-start = (f32[16,1280]{1,0:T(8,128)S(1)}, f32[16,1280]{1,0:T(8,128)S(1)}, u32[]{:S(2)}, u32[]{:S(2)}) collective-permute-start(f32[16,1280]{1,0:T(8,128)S(1)} %shard_map.246), channel_id=1, source_target_pairs={{0,4},{4,0},{1,5},{5,1},{2,6},{6,2},{3,7},{7,3},{8,12},{12,8},{9,1... | collective-permute-start | bytes 245768 | tf_op jit(solution)/shard_map/ppermute | solution.py:161
  5.2 2.2 %collective-permute-done.refs_1_ = f32[16,1280]{1,0:T(8,128)S(1)} collective-permute-done((f32[16,1280]{1,0:T(8,128)S(1)}, f32[16,1280]{1,0:T(8,128)S(1)}, u32[]{:S(2)}, u32[]{:S(2)}) %collective-permute-start) | collective-permute-done | bytes 81952 | tf_op jit(solution)/shard_map/ppermute | solution.py:161
  7.4 0.9 %copy-done.15 = f32[2,128,128]{2,1,0:T(8,128)S(1)} copy-done((f32[2,128,128]{2,1,0:T(8,128)S(1)}, f32[2,128,128]{2,1,0:T(8,128)}, u32[]{:S(2)}) %copy-start.15) | copy-done | bytes 131096
  8.3 1.5 %shard_map.247 = (f32[1024,128]{1,0:T(8,128)S(1)}, f32[256,256]{1,0:T(8,128)S(1)}, f32[4,128,128]{2,1,0:T(8,128)S(1)}, f32[8,8,128]{2,1,0:T(8,128)S(1)}) custom-call(f32[8,128,128]{2,1,0:T(8,128)S(1)} %copy-done, f32[16,1280]{1,0:T(8,128)S(1)} %collective-permute-done.refs_1_, f32[2,128,128]{2,1,0:T(8,128)S(1)} %copy-done.15, f32[2,16,128]{2,1,0:T(8,128)S(1)} %copy-done.21, ...), custom_call_target="tpu_custom_call" | custom-call | tf_op jit(solution)/shard_map/pallas_call | solution.py:148
  9.8 3.3 %collective-permute-start.3 = (f32[8,8,128]{2,1,0:T(8,128)S(1)}, f32[8,8,128]{2,1,0:T(8,128)S(1)}, u32[]{:S(2)}, u32[]{:S(2)}) collective-permute-start(f32[8,8,128]{2,1,0:T(8,128)S(1)} %get-tuple-element.21.refs_3_), channel_id=1, source_target_pairs={{0,24},{8,16},{16,8},{24,0},{1,25},{9,17},{17,9},{25,1},{2,26},{10... | collective-permute-start | bytes 98312 | tf_op jit(solution)/shard_map/ppermute | solution.py:161
  13.1 0.4 collective-permute-start.1
  13.4 1.0 %collective-permute-done.3.refs_6_ = f32[8,8,128]{2,1,0:T(8,128)S(1)} collective-permute-done((f32[8,8,128]{2,1,0:T(8,128)S(1)}, f32[8,8,128]{2,1,0:T(8,128)S(1)}, u32[]{:S(2)}, u32[]{:S(2)}) %collective-permute-start.3) | collective-permute-done | bytes 32800 | tf_op jit(solution)/shard_map/ppermute | solution.py:161
  14.4 2.3 %collective-permute-done.2.refs_5_ = f32[8,8,128]{2,1,0:T(8,128)S(1)} collective-permute-done((f32[8,8,128]{2,1,0:T(8,128)S(1)}, f32[8,8,128]{2,1,0:T(8,128)S(1)}, u32[]{:S(2)}, u32[]{:S(2)}) %collective-permute-start.2) | collective-permute-done | bytes 32800 | tf_op jit(solution)/shard_map/ppermute | solution.py:161
  16.8 0.8 %shard_map.248 = (f32[4,128,128]{2,1,0:T(8,128)S(1)}, f32[80,128]{1,0:T(8,128)S(1)}, f32[4,64,128]{2,1,0:T(8,128)S(1)}, f32[64,128]{1,0:T(8,128)S(1)}, f32[64,128]{1,0:T(8,128)S(1)}, /*index=5*/f32[64,128]{1,0:T(8,128)S(1)}) custom-call(f32[1024,128]{1,0:T(8,128)S(1)} %get-tuple-element.18.refs_0_, f32[256,256]{1,0:T(8,128)S(1)} %get-tuple-element.19.refs_1_, ...), custom_call_target="tpu_custom_call" | custom-call | tf_op jit(solution)/shard_map/pallas_call | solution.py:148
  17.6 3.3 %collective-permute-start.4 = (f32[64,128]{1,0:T(8,128)S(1)}, f32[64,128]{1,0:T(8,128)S(1)}, u32[]{:S(2)}, u32[]{:S(2)}) collective-permute-start(f32[64,128]{1,0:T(8,128)S(1)} %get-tuple-element.23), channel_id=1, source_target_pairs={{0,1},{1,0},{2,3},{3,2},{4,5},{5,4},{6,7},{7,6},{8,9},{9,8},{10,11... | collective-permute-start | bytes 98312 | tf_op jit(solution)/shard_map/ppermute | solution.py:506
  20.9 1.2 %collective-permute-start.5 = (f32[64,128]{1,0:T(8,128)S(1)}, f32[64,128]{1,0:T(8,128)S(1)}, u32[]{:S(2)}, u32[]{:S(2)}) collective-permute-start(f32[64,128]{1,0:T(8,128)S(1)} %get-tuple-element.24), channel_id=1, source_target_pairs={{0,2},{1,3},{2,0},{3,1},{4,6},{5,7},{6,4},{7,5},{8,10},{9,11},{10,... | collective-permute-start | bytes 98312 | tf_op jit(solution)/shard_map/ppermute | solution.py:506
  22.1 0.5 %collective-permute-start.6 = (f32[64,128]{1,0:T(8,128)S(1)}, f32[64,128]{1,0:T(8,128)S(1)}, u32[]{:S(2)}, u32[]{:S(2)}) collective-permute-start(f32[64,128]{1,0:T(8,128)S(1)} %get-tuple-element.25), channel_id=1, source_target_pairs={{0,3},{1,2},{2,1},{3,0},{4,7},{5,6},{6,5},{7,4},{8,11},{9,10},{10,... | collective-permute-start | bytes 98312 | tf_op jit(solution)/shard_map/ppermute | solution.py:506
  22.6 1.1 %collective-permute-done.5.refs_2_ = f32[64,128]{1,0:T(8,128)S(1)} collective-permute-done((f32[64,128]{1,0:T(8,128)S(1)}, f32[64,128]{1,0:T(8,128)S(1)}, u32[]{:S(2)}, u32[]{:S(2)}) %collective-permute-start.5) | collective-permute-done | bytes 32800 | tf_op jit(solution)/shard_map/ppermute | solution.py:506
  23.7 1.8 %collective-permute-done.6.refs_3_ = f32[64,128]{1,0:T(8,128)S(1)} collective-permute-done((f32[64,128]{1,0:T(8,128)S(1)}, f32[64,128]{1,0:T(8,128)S(1)}, u32[]{:S(2)}, u32[]{:S(2)}) %collective-permute-start.6) | collective-permute-done | bytes 32800 | tf_op jit(solution)/shard_map/ppermute | solution.py:506
  25.5 0.2 shard_map.249
  25.7 1.2 %collective-permute-start.9 = (f32[16,512]{1,0:T(8,128)S(1)}, f32[16,512]{1,0:T(8,128)S(1)}, u32[]{:S(2)}, u32[]{:S(2)}) collective-permute-start(f32[16,512]{1,0:T(8,128)S(1)} %get-tuple-element.28), channel_id=1, source_target_pairs={{0,24},{8,16},{16,8},{24,0},{1,25},{9,17},{17,9},{25,1},{2,26},{10... | collective-permute-start | bytes 98312 | tf_op jit(solution)/shard_map/ppermute | solution.py:161
  26.9 0.6 %collective-permute-start.8 = (f32[16,512]{1,0:T(8,128)S(1)}, f32[16,512]{1,0:T(8,128)S(1)}, u32[]{:S(2)}, u32[]{:S(2)}) collective-permute-start(f32[16,512]{1,0:T(8,128)S(1)} %get-tuple-element.28), channel_id=1, source_target_pairs={{0,16},{8,24},{16,0},{24,8},{1,17},{9,25},{17,1},{25,9},{2,18},{10... | collective-permute-start | bytes 98312 | tf_op jit(solution)/shard_map/ppermute | solution.py:161
  27.5 1.8 %collective-permute-start.7 = (f32[16,512]{1,0:T(8,128)S(1)}, f32[16,512]{1,0:T(8,128)S(1)}, u32[]{:S(2)}, u32[]{:S(2)}) collective-permute-start(f32[16,512]{1,0:T(8,128)S(1)} %get-tuple-element.28), channel_id=1, source_target_pairs={{0,8},{8,0},{16,24},{24,16},{1,9},{9,1},{17,25},{25,17},{2,10},{10... | collective-permute-start | bytes 98312 | tf_op jit(solution)/shard_map/ppermute | solution.py:161
  29.3 1.0 %collective-permute-done.9.refs_4_ = f32[16,512]{1,0:T(8,128)S(1)} collective-permute-done((f32[16,512]{1,0:T(8,128)S(1)}, f32[16,512]{1,0:T(8,128)S(1)}, u32[]{:S(2)}, u32[]{:S(2)}) %collective-permute-start.9) | collective-permute-done | bytes 32800 | tf_op jit(solution)/shard_map/ppermute | solution.py:161
  30.3 0.4 collective-permute-done.8.refs_3_
  30.7 0.9 %collective-permute-done.7.refs_2_ = f32[16,512]{1,0:T(8,128)S(1)} collective-permute-done((f32[16,512]{1,0:T(8,128)S(1)}, f32[16,512]{1,0:T(8,128)S(1)}, u32[]{:S(2)}, u32[]{:S(2)}) %collective-permute-start.7) | collective-permute-done | bytes 32800 | tf_op jit(solution)/shard_map/ppermute | solution.py:161
  31.6 0.9 %shard_map.250 = (f32[4,48,128]{2,1,0:T(8,128)S(1)}, f32[2,64,128]{2,1,0:T(8,128)S(1)}) custom-call(f32[4,64,128]{2,1,0:T(8,128)S(1)} %get-tuple-element.26.refs_0_, f32[80,128]{1,0:T(8,128)S(1)} %get-tuple-element.27.refs_1_, f32[16,512]{1,0:T(8,128)S(1)} %collective-permute-done.7.refs_2_, f32[16,512]{1,0:T(8,128)S(1)} %collective-permute-done.8.refs_3_, ...), custom_call_target="tpu_custom_call" | custom-call | tf_op jit(solution)/shard_map/pallas_call | solution.py:148
  32.5 1.8 %collective-permute-start.12 = (f32[4,48,128]{2,1,0:T(8,128)S(1)}, f32[4,48,128]{2,1,0:T(8,128)S(1)}, u32[]{:S(2)}, u32[]{:S(2)}) collective-permute-start(f32[4,48,128]{2,1,0:T(8,128)S(1)} %get-tuple-element.31.refs_5_), channel_id=1, source_target_pairs={{0,3},{1,2},{2,1},{3,0},{4,7},{5,6},{6,5},{7,4},{8,11},{9,10},{10,... | collective-permute-start | bytes 294920 | tf_op jit(solution)/shard_map/ppermute | solution.py:161
  34.3 0.8 %collective-permute-start.11 = (f32[4,48,128]{2,1,0:T(8,128)S(1)}, f32[4,48,128]{2,1,0:T(8,128)S(1)}, u32[]{:S(2)}, u32[]{:S(2)}) collective-permute-start(f32[4,48,128]{2,1,0:T(8,128)S(1)} %get-tuple-element.31.refs_5_), channel_id=1, source_target_pairs={{0,2},{1,3},{2,0},{3,1},{4,6},{5,7},{6,4},{7,5},{8,10},{9,11},{10,... | collective-permute-start | bytes 294920 | tf_op jit(solution)/shard_map/ppermute | solution.py:161
  35.2 0.8 %shard_map.251.refs_4_ = f32[8,128,128]{2,1,0:T(8,128)} custom-call(f32[8,128,128]{2,1,0:T(8,128)S(1)} %copy-done.1, f32[4,128,128]{2,1,0:T(8,128)S(1)} %get-tuple-element.30.ixy_ref.refs_3_), custom_call_target="tpu_custom_call" | custom-call | tf_op jit(solution)/shard_map/pallas_call | solution.py:148
  36.0 1.5 %collective-permute-done.12.refs_8_ = f32[4,48,128]{2,1,0:T(8,128)S(1)} collective-permute-done((f32[4,48,128]{2,1,0:T(8,128)S(1)}, f32[4,48,128]{2,1,0:T(8,128)S(1)}, u32[]{:S(2)}, u32[]{:S(2)}) %collective-permute-start.12) | collective-permute-done | bytes 98336 | tf_op jit(solution)/shard_map/ppermute | solution.py:161
  37.5 2.3 %collective-permute-done.11.refs_7_ = f32[4,48,128]{2,1,0:T(8,128)S(1)} collective-permute-done((f32[4,48,128]{2,1,0:T(8,128)S(1)}, f32[4,48,128]{2,1,0:T(8,128)S(1)}, u32[]{:S(2)}, u32[]{:S(2)}) %collective-permute-start.11) | collective-permute-done | bytes 98336 | tf_op jit(solution)/shard_map/ppermute | solution.py:161
  39.8 2.3 %shard_map.252 = (f32[8,128,128]{2,1,0:T(8,128)}, f32[4,64,64]{2,1,0:T(8,128)}, f32[2,32,32]{2,1,0:T(8,128)}, f32[1,16,16]{2,1,0:T(8,128)}) custom-call(f32[4,64,128]{2,1,0:T(8,128)S(1)} %get-tuple-element.26.refs_0_, f32[2,64,128]{2,1,0:T(8,128)S(1)} %get-tuple-element.29.refs_1_, f32[8,128,128]{2,1,0:T(8,128)S(1)} %copy-done.1, ...), custom_call_target="tpu_custom_call", output_to_operand_aliasing={{0}: (4, {})} | custom-call | tf_op jit(solution)/shard_map/pallas_call | solution.py:148
  (49 shorter events, 0.1 us)
Async XLA Ops:
  2.4 5.0 %copy-start.5 = (f32[4,128,8]{2,1,0:T(8,128)S(1)}, f32[4,128,8]{2,1,0:T(8,128)}, u32[]{:S(2)}) copy-start(f32[4,128,8]{2,1,0:T(8,128)} %constant.50.clone.refs_6_) | copy-start | bytes 49156
  2.4 5.0 %copy-start.6 = (f32[2,128,256]{2,1,0:T(8,128)S(1)}, f32[2,128,256]{2,1,0:T(8,128)}, u32[]{:S(2)}) copy-start(f32[2,128,256]{2,1,0:T(8,128)} %constant.48.clone.refs_4_) | copy-start | bytes 786436
  2.4 5.0 %copy-start.19 = (f32[2,16,256]{2,1,0:T(8,128)S(1)}, f32[2,16,256]{2,1,0:T(8,128)}, u32[]{:S(2)}) copy-start(f32[2,16,256]{2,1,0:T(8,128)} %constant.49.clone.refs_5_) | copy-start | bytes 98308
  2.4 5.0 %copy-start.21 = (f32[2,16,128]{2,1,0:T(8,128)S(1)}, f32[2,16,128]{2,1,0:T(8,128)}, u32[]{:S(2)}) copy-start(f32[2,16,128]{2,1,0:T(8,128)} %constant.47.clone.refs_3_) | copy-start | bytes 49156
  3.0 13.7 %copy-start.7 = (f32[4,64,152]{2,1,0:T(8,128)S(1)}, f32[4,64,152]{2,1,0:T(8,128)}, u32[]{:S(2)}) copy-start(f32[4,64,152]{2,1,0:T(8,128)} %constant.51.clone.refs_7_) | copy-start | bytes 466948
  3.0 13.7 %copy-start.14 = (f32[4,64,88]{2,1,0:T(8,128)S(1)}, f32[4,64,88]{2,1,0:T(8,128)}, u32[]{:S(2)}) copy-start(f32[4,64,88]{2,1,0:T(8,128)} %constant.52.clone.refs_8_) | copy-start | bytes 270340
  3.1 4.3 %collective-permute-start = (f32[16,1280]{1,0:T(8,128)S(1)}, f32[16,1280]{1,0:T(8,128)S(1)}, u32[]{:S(2)}, u32[]{:S(2)}) collective-permute-start(f32[16,1280]{1,0:T(8,128)S(1)} %shard_map.246), channel_id=1, source_target_pairs={{0,4},{4,0},{1,5},{5,1},{2,6},{6,2},{3,7},{7,3},{8,12},{12,8},{9,1... | collective-permute-start | bytes 245768 | tf_op jit(solution)/shard_map/ppermute | solution.py:161
  9.8 4.6 %collective-permute-start.3 = (f32[8,8,128]{2,1,0:T(8,128)S(1)}, f32[8,8,128]{2,1,0:T(8,128)S(1)}, u32[]{:S(2)}, u32[]{:S(2)}) collective-permute-start(f32[8,8,128]{2,1,0:T(8,128)S(1)} %get-tuple-element.21.refs_3_), channel_id=1, source_target_pairs={{0,24},{8,16},{16,8},{24,0},{1,25},{9,17},{17,9},{25,1},{2,26},{10... | collective-permute-start | bytes 98312 | tf_op jit(solution)/shard_map/ppermute | solution.py:161
  13.1 3.7 %collective-permute-start.2 = (f32[8,8,128]{2,1,0:T(8,128)S(1)}, f32[8,8,128]{2,1,0:T(8,128)S(1)}, u32[]{:S(2)}, u32[]{:S(2)}) collective-permute-start(f32[8,8,128]{2,1,0:T(8,128)S(1)} %get-tuple-element.21.refs_3_), channel_id=1, source_target_pairs={{0,16},{8,24},{16,0},{24,8},{1,17},{9,25},{17,1},{25,9},{2,18},{10... | collective-permute-start | bytes 98312 | tf_op jit(solution)/shard_map/ppermute | solution.py:161
  13.1 3.7 %collective-permute-start.1 = (f32[8,8,128]{2,1,0:T(8,128)S(1)}, f32[8,8,128]{2,1,0:T(8,128)S(1)}, u32[]{:S(2)}, u32[]{:S(2)}) collective-permute-start(f32[8,8,128]{2,1,0:T(8,128)S(1)} %get-tuple-element.21.refs_3_), channel_id=1, source_target_pairs={{0,8},{8,0},{16,24},{24,16},{1,9},{9,1},{17,25},{25,17},{2,10},{10... | collective-permute-start | bytes 98312 | tf_op jit(solution)/shard_map/ppermute | solution.py:161
  16.8 8.7 %copy-start.20 = (f32[4,16,64]{2,1,0:T(8,128)S(1)}, f32[4,16,64]{2,1,0:T(8,128)}, u32[]{:S(2)}) copy-start(f32[4,16,64]{2,1,0:T(8,128)} %constant.53.clone.refs_4_) | copy-start | bytes 49156
  16.8 14.8 %copy-start.3 = (f32[2,384,128]{2,1,0:T(8,128)S(1)}, f32[2,384,128]{2,1,0:T(8,128)}, u32[]{:S(2)}) copy-start(f32[2,384,128]{2,1,0:T(8,128)} %constant.56.clone.refs_7_) | copy-start | bytes 1179652
  16.8 14.8 %copy-start.4 = (f32[4,144,112]{2,1,0:T(8,128)S(1)}, f32[4,144,112]{2,1,0:T(8,128)}, u32[]{:S(2)}) copy-start(f32[4,144,112]{2,1,0:T(8,128)} %constant.54.clone.refs_5_) | copy-start | bytes 774148
  17.6 5.0 %collective-permute-start.4 = (f32[64,128]{1,0:T(8,128)S(1)}, f32[64,128]{1,0:T(8,128)S(1)}, u32[]{:S(2)}, u32[]{:S(2)}) collective-permute-start(f32[64,128]{1,0:T(8,128)S(1)} %get-tuple-element.23), channel_id=1, source_target_pairs={{0,1},{1,0},{2,3},{3,2},{4,5},{5,4},{6,7},{7,6},{8,9},{9,8},{10,11... | collective-permute-start | bytes 98312 | tf_op jit(solution)/shard_map/ppermute | solution.py:506
  20.9 2.8 %collective-permute-start.5 = (f32[64,128]{1,0:T(8,128)S(1)}, f32[64,128]{1,0:T(8,128)S(1)}, u32[]{:S(2)}, u32[]{:S(2)}) collective-permute-start(f32[64,128]{1,0:T(8,128)S(1)} %get-tuple-element.24), channel_id=1, source_target_pairs={{0,2},{1,3},{2,0},{3,1},{4,6},{5,7},{6,4},{7,5},{8,10},{9,11},{10,... | collective-permute-start | bytes 98312 | tf_op jit(solution)/shard_map/ppermute | solution.py:506
  22.1 3.3 %collective-permute-start.6 = (f32[64,128]{1,0:T(8,128)S(1)}, f32[64,128]{1,0:T(8,128)S(1)}, u32[]{:S(2)}, u32[]{:S(2)}) collective-permute-start(f32[64,128]{1,0:T(8,128)S(1)} %get-tuple-element.25), channel_id=1, source_target_pairs={{0,3},{1,2},{2,1},{3,0},{4,7},{5,6},{6,5},{7,4},{8,11},{9,10},{10,... | collective-permute-start | bytes 98312 | tf_op jit(solution)/shard_map/ppermute | solution.py:506
  25.5 6.1 %copy-start.12 = (f32[2,128,128]{2,1,0:T(8,128)S(1)}, f32[2,128,128]{2,1,0:T(8,128)}, u32[]{:S(2)}) copy-start(f32[2,128,128]{2,1,0:T(8,128)} %constant.57.clone.refs_8_) | copy-start | bytes 393220
  25.5 6.1 %copy-start.13 = (f32[4,64,112]{2,1,0:T(8,128)S(1)}, f32[4,64,112]{2,1,0:T(8,128)}, u32[]{:S(2)}) copy-start(f32[4,64,112]{2,1,0:T(8,128)} %constant.55.clone.refs_6_) | copy-start | bytes 344068
  25.7 4.6 %collective-permute-start.9 = (f32[16,512]{1,0:T(8,128)S(1)}, f32[16,512]{1,0:T(8,128)S(1)}, u32[]{:S(2)}, u32[]{:S(2)}) collective-permute-start(f32[16,512]{1,0:T(8,128)S(1)} %get-tuple-element.28), channel_id=1, source_target_pairs={{0,24},{8,16},{16,8},{24,0},{1,25},{9,17},{17,9},{25,1},{2,26},{10... | collective-permute-start | bytes 98312 | tf_op jit(solution)/shard_map/ppermute | solution.py:161
  26.9 3.8 %collective-permute-start.8 = (f32[16,512]{1,0:T(8,128)S(1)}, f32[16,512]{1,0:T(8,128)S(1)}, u32[]{:S(2)}, u32[]{:S(2)}) collective-permute-start(f32[16,512]{1,0:T(8,128)S(1)} %get-tuple-element.28), channel_id=1, source_target_pairs={{0,16},{8,24},{16,0},{24,8},{1,17},{9,25},{17,1},{25,9},{2,18},{10... | collective-permute-start | bytes 98312 | tf_op jit(solution)/shard_map/ppermute | solution.py:161
  27.5 4.1 %collective-permute-start.7 = (f32[16,512]{1,0:T(8,128)S(1)}, f32[16,512]{1,0:T(8,128)S(1)}, u32[]{:S(2)}, u32[]{:S(2)}) collective-permute-start(f32[16,512]{1,0:T(8,128)S(1)} %get-tuple-element.28), channel_id=1, source_target_pairs={{0,8},{8,0},{16,24},{24,16},{1,9},{9,1},{17,25},{25,17},{2,10},{10... | collective-permute-start | bytes 98312 | tf_op jit(solution)/shard_map/ppermute | solution.py:161
  32.5 5.0 %collective-permute-start.12 = (f32[4,48,128]{2,1,0:T(8,128)S(1)}, f32[4,48,128]{2,1,0:T(8,128)S(1)}, u32[]{:S(2)}, u32[]{:S(2)}) collective-permute-start(f32[4,48,128]{2,1,0:T(8,128)S(1)} %get-tuple-element.31.refs_5_), channel_id=1, source_target_pairs={{0,3},{1,2},{2,1},{3,0},{4,7},{5,6},{6,5},{7,4},{8,11},{9,10},{10,... | collective-permute-start | bytes 294920 | tf_op jit(solution)/shard_map/ppermute | solution.py:161
  34.3 5.5 %collective-permute-start.11 = (f32[4,48,128]{2,1,0:T(8,128)S(1)}, f32[4,48,128]{2,1,0:T(8,128)S(1)}, u32[]{:S(2)}, u32[]{:S(2)}) collective-permute-start(f32[4,48,128]{2,1,0:T(8,128)S(1)} %get-tuple-element.31.refs_5_), channel_id=1, source_target_pairs={{0,2},{1,3},{2,0},{3,1},{4,6},{5,7},{6,4},{7,5},{8,10},{9,11},{10,... | collective-permute-start | bytes 294920 | tf_op jit(solution)/shard_map/ppermute | solution.py:161
  35.1 4.6 %collective-permute-start.10 = (f32[4,48,128]{2,1,0:T(8,128)S(1)}, f32[4,48,128]{2,1,0:T(8,128)S(1)}, u32[]{:S(2)}, u32[]{:S(2)}) collective-permute-start(f32[4,48,128]{2,1,0:T(8,128)S(1)} %get-tuple-element.31.refs_5_), channel_id=1, source_target_pairs={{0,1},{1,0},{2,3},{3,2},{4,5},{5,4},{6,7},{7,6},{8,9},{9,8},{10,11... | collective-permute-start | bytes 294920 | tf_op jit(solution)/shard_map/ppermute | solution.py:161
  35.1 4.6 %copy-start.2 = (f32[2,384,128]{2,1,0:T(8,128)S(1)}, f32[2,384,128]{2,1,0:T(8,128)}, u32[]{:S(2)}) copy-start(f32[2,384,128]{2,1,0:T(8,128)} %constant.63.clone.refs_14_) | copy-start | bytes 1179652
  35.1 4.6 %copy-start.8 = (f32[2,128,128]{2,1,0:T(8,128)S(1)}, f32[2,128,128]{2,1,0:T(8,128)}, u32[]{:S(2)}) copy-start(f32[2,128,128]{2,1,0:T(8,128)} %constant.65.clone.refs_16_) | copy-start | bytes 393220
  35.1 4.6 %copy-start.9 = (f32[2,128,128]{2,1,0:T(8,128)S(1)}, f32[2,128,128]{2,1,0:T(8,128)}, u32[]{:S(2)}) copy-start(f32[2,128,128]{2,1,0:T(8,128)} %constant.61.clone.refs_12_) | copy-start | bytes 393220
  35.1 4.6 %copy-start.10 = (f32[4,64,48]{2,1,0:T(8,128)S(1)}, f32[4,64,48]{2,1,0:T(8,128)}, u32[]{:S(2)}) copy-start(f32[4,64,48]{2,1,0:T(8,128)} %constant.60.clone.refs_11_) | copy-start | bytes 147460
  35.2 4.6 %copy-start.11 = (f32[2,128,128]{2,1,0:T(8,128)S(1)}, f32[2,128,128]{2,1,0:T(8,128)}, u32[]{:S(2)}) copy-start(f32[2,128,128]{2,1,0:T(8,128)} %constant.59.clone.refs_10_) | copy-start | bytes 393220
  35.2 4.6 %copy-start.16 = (f32[4,48,48]{2,1,0:T(8,128)S(1)}, f32[4,48,48]{2,1,0:T(8,128)}, u32[]{:S(2)}) copy-start(f32[4,48,48]{2,1,0:T(8,128)} %constant.62.clone.refs_13_) | copy-start | bytes 110596
  35.2 4.6 %copy-start.17 = (f32[4,32,48]{2,1,0:T(8,128)S(1)}, f32[4,32,48]{2,1,0:T(8,128)}, u32[]{:S(2)}) copy-start(f32[4,32,48]{2,1,0:T(8,128)} %constant.64.clone.refs_15_) | copy-start | bytes 73732
  35.2 4.6 %copy-start.18 = (f32[128,96]{1,0:T(8,128)S(1)}, f32[128,96]{1,0:T(8,128)}, u32[]{:S(2)}) copy-start(f32[128,96]{1,0:T(8,128)} %constant.58.clone.refs_9_) | copy-start | bytes 147460
  (5 other events, 6.9 us)

commit v3 on v2

--- a/solution.py
+++ b/solution.py
@@ -161,6 +161,15 @@
     return [lax.ppermute(value, axis, [(i, i ^ k) for i in range(count)]) for k in range(1, count)]
 
 
+def gathered(value, axis):
+    count = lax.axis_size(axis)
+    if count != 4:
+        return swapped(value, axis)
+    by = lambda k, what: lax.ppermute(what, axis, [(i, i ^ k) for i in range(count)])
+    far = by(2, value)
+    return [by(1, value), far, by(1, far)]
+
+
 def chosen_by(values, j):
     chosen = float(values[0])
     for place in range(1, len(values)):
@@ -300,27 +309,53 @@
     zt = zt.reshape(dz, (lz // 8) * (z3 + 2))
     lz4 = lz // 8
 
-    to32 = lambda *tables: [jnp.asarray(t, jnp.float32) for t in tables]
+    to32 = lambda table: jnp.asarray(table, jnp.float32)
+
+    def stacked(*tables):
+        cols = max(t.shape[2] for t in tables)
+        starts = np.cumsum([0] + [round_up(t.shape[1], 8) for t in tables])
+        out = np.zeros((tables[0].shape[0], starts[-1], cols))
+        for t, begin in zip(tables, starts):
+            out[:, begin : begin + t.shape[1], : t.shape[2]] = t
+        return to32(out), [int(v) for v in starts]
+
+    messages_y, _ = stacked(fya, fys)
+    tables_y, _ = stacked(np.concatenate([ta, tsm], axis=2), np.concatenate([wa, np.zeros((dy, wa.shape[1], 2 * wide))], axis=2),
+                          np.concatenate([np.zeros((dy, wsm.shape[1], wide)), wsm], axis=2))
+    tables_x, _ = stacked(txa, txm)
+    tables_x2, _ = stacked(tx2, qx2)
+    tables_y2, _ = stacked(ty2, qy2)
+    tables_x3, at_x3 = stacked(tx3, qx3, px3)
+    tables_y3, at_y3 = stacked(ty3, qy3, py3, py1)
     hz, hx1 = lz // 2, lx // 2
 
-    def y_messages(u_ref, fya_ref, fys_ref, out_ref):
+    def y_messages(u_hbm, table_hbm, out_ref, u_ref, table, sems):
         j = lax.axis_index("gy")
         nt = ((1,), (1,))
-        out_ref[:kya, : lz * lx] = dot(fya_ref[j], u_ref[...].reshape(lz * lx, ly), nt)
+        copies = [pltpu.make_async_copy(table_hbm.at[j], table, sems.at[lz])]
+        copies += [pltpu.make_async_copy(u_hbm.at[z], u_ref.at[z], sems.at[z]) for z in range(lz)]
+        for copy in copies:
+            copy.start()
+        copies[0].wait()
+        for z in range(lz):
+            copies[z + 1].wait()
+            out_ref[:kya, z * lx : (z + 1) * lx] = dot(table[:kya], u_ref[z], nt)
         even = jnp.concatenate([u_ref[2 * z, pl.ds(0, hx1, stride=2), :] for z in range(hz)], axis=0)
-        out_ref[:kys, lz * lx :] = dot(fys_ref[j], even, nt)
+        out_ref[:kys, lz * lx :] = dot(table[kya : kya + kys], even, nt)
 
     def y_apply(*refs):
         u_ref, came = refs[0], refs[1:dy]
-        ta_ref, wa_ref, tsm_ref, wsm_ref, fx_ref, ta_out, tsm_out, iy_out, xm_out = refs[dy:]
+        ty_ref, fx_ref, ta_out, tsm_out, iy_out, xm_out = refs[dy:]
         j, jx = lax.axis_index("gy"), lax.axis_index("gx")
         tn = ((0,), (0,))
-        ta_all = dot(u_ref[...].reshape(lz * lx, ly), ta_ref[j])
+        ta_all = dot(u_ref[...].reshape(lz * lx, ly), ty_ref[j, :ly, :wide])
         even = jnp.concatenate([u_ref[2 * z, pl.ds(0, hx1, stride=2), :] for z in range(hz)], axis=0)
-        tsm_all = dot(even, tsm_ref[j])
+        tsm_all = dot(even, ty_ref[j, :ly, wide:])
         for k, ref in enumerate(came):
-            ta_all += dot(ref[:kya, : lz * lx], wa_ref[j, kya * k : kya * (k + 1), :], tn)
-            tsm_all += dot(ref[:kys, lz * lx :], wsm_ref[j, kys * k : kys * (k + 1), :], tn)
+            begin = ly + kya * k
+            ta_all += dot(ref[:kya, : lz * lx], ty_ref[j, begin : begin + kya, :wide], tn)
+            begin = ly + kya * (dy - 1) + kys * k
+            tsm_all += dot(ref[:kys, lz * lx :], ty_ref[j, begin : begin + kys, wide:], tn)
         ta_out[...] = ta_all
         tsm_out[...] = tsm_all
         xm_out[...] = jnp.zeros_like(xm_out)
@@ -347,8 +382,8 @@
     def x_apply(*refs):
         ta_ref, tsm_ref, iy_ref, own_ref = refs[:4]
         came = refs[4 : 3 + dx]
-        txa_ref, txm_ref, ixy_out, zc_out, u1_out = refs[3 + dx : 8 + dx]
-        planes_out = refs[8 + dx :]
+        tx_ref, ixy_out, zc_out, u1_out = refs[3 + dx : 7 + dx]
+        planes_out = refs[7 + dx :]
         jx, jz = lax.axis_index("gx"), lax.axis_index("gz")
         xa, xm, diff = [], [], []
         def from_next(own, rows):
@@ -359,7 +394,7 @@
         for z in range(0, lz, 2):
             pair = jnp.concatenate([ta_ref[z * lx : (z + 1) * lx, :], ta_ref[(z + 1) * lx : (z + 2) * lx, :]], axis=1)
             rest = [jnp.concatenate([r[z, :, :wide], r[z + 1, :, :wide]], axis=1) for r in came]
-            both = dot(txa_ref[jx], jnp.concatenate([pair] + rest, axis=0))
+            both = dot(tx_ref[jx, : xone.n], jnp.concatenate([pair] + rest, axis=0))
             xa += [both[:, :wide], both[:, wide:]]
         zc_out[...] = jnp.zeros_like(zc_out)
         zc_out[:hx1] = tsm_ref[:hx1, :wide]
@@ -368,7 +403,7 @@
         for half in range(hz):
             part = tsm_ref[half * hx1 : (half + 1) * hx1, :]
             stacked = jnp.concatenate([part[:, wide:]] + [r[2 * half, :, :wide] for r in came], axis=0)
-            xm.append(dot(txm_ref[jx], stacked))
+            xm.append(dot(tx_ref[jx, xone.n :, : xone.n + 8 * (dx - 1)], stacked))
             diff.append(part[:, :wide] - xm[-1])
             iy = iy_ref[half]
             halo = from_next(iy[lx - 2 : lx - 1], [r[2 * half, 4:5, :ly] for r in came])
@@ -410,12 +445,12 @@
 
     def second_apply(*refs):
         u1_ref, zc_ref, came = refs[0], refs[1], refs[2 : dx + 1]
-        tx2_ref, qx2_ref, ty2_ref, qy2_ref, zt_out, i2_out = refs[dx + 1 :]
+        tx2_ref, ty2_ref, zt_out, i2_out = refs[dx + 1 :]
         jx, jy = lax.axis_index("gx"), lax.axis_index("gy")
         own = jnp.concatenate([u1_ref[z] for z in range(lz2)], axis=1)
         state = jnp.concatenate([own] + [r[...] for r in came], axis=0)
         across = dot(tx2_ref[jx], state)
-        spread = dot(qx2_ref[jx], state)
+        spread = across[3 * tall :]
         for z in range(lz2):
             cut = across[:, z * wide : (z + 1) * wide]
             if z % 2 == 1:
@@ -426,33 +461,36 @@
                 zt_out[z] = moved
             else:
                 joined = jnp.concatenate([cut[c * tall : (c + 1) * tall] for c in range(3)], axis=1)
-                zt_out[z] = dot(joined, ty2_ref[jy])
-                i2_out[z // 2] = dot(spread[:, z * wide : (z + 1) * wide], qy2_ref[jy])
+                zt_out[z] = dot(joined, ty2_ref[jy, : 3 * wide])
+                i2_out[z // 2] = dot(spread[:, z * wide : (z + 1) * wide], ty2_ref[jy, 3 * wide :, : round_up(ytwo.fine, 128)])
 
     def third_apply(*refs):
         u1_ref, i2_ref, u_ref, ixy_ref, _, own_ref = refs[:6]
         came = refs[6 : 5 + dz]
-        px1_ref, py1_ref, px3_ref, py3_ref, tx3_ref, ty3_ref, qx3_ref, qy3_ref = refs[5 + dz : 13 + dz]
-        fine_out, middle_out, coarse_out, coarsest_out, zbuf, ubuf, last, sem = refs[13 + dz :]
+        px1_ref, tx_ref, ty_ref, fine_out, middle_out, coarse_out, coarsest_out = refs[5 + dz : 12 + dz]
+        zbuf, ubuf, last, middle, sems = refs[12 + dz :]
+        part = lambda ref, j, starts, which: ref[j, starts[which] : starts[which + 1]]
         jx, jy, jz = lax.axis_index("gx"), lax.axis_index("gy"), lax.axis_index("gz")
         zbuf[pl.ds(jz * lz2, lz2)] = own_ref[...]
         for k, r in enumerate(came):
             zbuf[pl.ds((jz ^ (k + 1)) * lz2, lz2)] = r[...]
         at = jnp.minimum(jz + 1, dz - 1) * lz2
         first = jnp.concatenate([zbuf[at + 1], zbuf[at + 3]], axis=0)
-        halo = dot(dot(px1_ref[...], first), py1_ref[jy])
+        halo = dot(dot(px1_ref[...], first), part(ty_ref, jy, at_y3, 3))
         here = ixy_ref[hz - 1]
         last[...] = u_ref[lz - 1] - 0.5 * (here + jnp.where(jz == dz - 1, here, halo))
-        copy = pltpu.make_async_copy(last, fine_out.at[lz - 1], sem)
-        copy.start()
+        copies = [pltpu.make_async_copy(last, fine_out.at[lz - 1], sems.at[0])]
+        copies[0].start()
+        fy = ytwo.fine
         at = jnp.minimum((jz + 1) * lz2, z2 - 2)
-        halo = dot(dot(px3_ref[jx], zbuf[at]), py3_ref[jy])
-        fy = ytwo.fine
+        halo = dot(dot(part(tx_ref, jx, at_x3, 2), zbuf[at]), part(ty_ref, jy, at_y3, 2))[:, :fy]
         for half in range(lz2 // 2):
-            here = i2_ref[half]
-            after = i2_ref[half + 1] if half + 1 < lz2 // 2 else halo
-            middle_out[2 * half] = (u1_ref[2 * half][:, :fy] - here[:, :fy])
-            middle_out[2 * half + 1] = u1_ref[2 * half + 1][:, :fy] - (0.5 * (here + after))[:, :fy]
+            here = i2_ref[half][:, :fy]
+            after = i2_ref[half + 1][:, :fy] if half + 1 < lz2 // 2 else halo
+            middle[2 * half] = u1_ref[2 * half][:, :fy] - here
+            middle[2 * half + 1] = u1_ref[2 * half + 1][:, :fy] - 0.5 * (here + after)
+        copies.append(pltpu.make_async_copy(middle, middle_out, sems.at[1]))
+        copies[1].start()
         everything = [zbuf[z] for z in range(z2)]
         evens = [pltpu.roll(everything[z], packed - wide2, 1) for z in range(0, z2, 2)]
         arounds = [pltpu.roll(everything[z], packed - 2 * wide2, 1) for z in range(0, z2, 2)]
@@ -465,7 +503,7 @@
         spread = []
         for half in range(lz3 // 2 + 1):
             at = jnp.minimum(jz * lz3 + 2 * half, z3 - 2)
-            spread.append(dot(dot(qx3_ref[jx], ubuf[at]), qy3_ref[jy])[:, :fy3])
+            spread.append(dot(dot(part(tx_ref, jx, at_x3, 1), ubuf[at]), part(ty_ref, jy, at_y3, 1))[:, :fy3])
         for half in range(lz3 // 2):
             at = jz * lz3 + 2 * half
             coarse_out[2 * half] = ubuf[at][: xthree.fine, :fy3] - spread[half]
@@ -480,52 +518,60 @@
             around = even + chosen_by(zt[:, base + z3], jz) * ubuf[0] + chosen_by(zt[:, base + z3 + 1], jz) * ubuf[z3 - 2]
             joined = jnp.concatenate(
                 [
-                    dot(tx3_ref[jx, c * n3 : (c + 1) * n3, :], plane)
+                    dot(tx_ref[jx, c * n3 : (c + 1) * n3, :], plane)
                     for c, plane in enumerate((along, even, around))
                 ],
                 axis=1,
             )
-            coarsest_out[zc] = dot(joined, ty3_ref[jy])[:, : ythree.n]
-        copy.wait()
-
-    (ym,) = kernel_call(y_messages, [(max(kya, kys), lz * lx + hz * hx1)], [field, *to32(fya, fys)])
+            coarsest_out[zc] = dot(joined, part(ty_ref, jy, at_y3, 0))[:, : ythree.n]
+        for copy in copies:
+            copy.wait()
+
+    ym, u = kernel_call(
+        y_messages,
+        [(max(kya, kys), lz * lx + hz * hx1), (lz, lx, ly)],
+        [field, messages_y],
+        scratch=[pltpu.VMEM((kya + kys, ly), jnp.float32), pltpu.SemaphoreType.DMA((lz + 1,))],
+        left=(0, 1),
+    )
     ycame = swapped(ym, "gy")
     xw = max(wide, ly)
     ta_v, tsm_v, iy, xm = kernel_call(
         y_apply,
         [(lz * lx, wide), (hz * hx1, 2 * wide), (hz, lx, ly), (lz, 8, xw)],
-        [field, *ycame, *to32(ta, wa, tsm, wsm, fx)],
+        [u, *ycame, tables_y, to32(fx)],
     )
     xcame = swapped(xm, "gx")
     ixy, zc, u1_part, *planes = kernel_call(
         x_apply,
         [(hz, lx, ly), (xtwo.n + tall, wide), (zn, xone.n, wide)] + [(xone.n, wide)] * (dz - 1),
-        [ta_v, tsm_v, iy, xm, *xcame, *to32(txa, txm)],
+        [ta_v, tsm_v, iy, xm, *xcame, tables_x],
     )
     zcame = [
         lax.ppermute(plane, "gz", [(i, i ^ (k + 1)) for i in range(dz)]) for k, plane in enumerate(planes)
     ]
-    u1, xt = kernel_call(z_apply, [(zn, xone.n, wide), (kx, zn * wide)], [u1_part, *zcame, *to32(f2x)])
+    u1, xt = kernel_call(z_apply, [(zn, xone.n, wide), (kx, zn * wide)], [u1_part, *zcame, to32(f2x)])
     xtcame = swapped(xt, "gx")
     zmsg, i2 = kernel_call(
         second_apply,
         [(lz2, tall, packed), (lz2 // 2, xtwo.fine, round_up(ytwo.fine, 128))],
-        [u1, zc, *xtcame, *to32(tx2, qx2, ty2, qy2)],
+        [u1, zc, *xtcame, tables_x2, tables_y2],
     )
-    ztcame = swapped(zmsg, "gz")
-    (fine,) = kernel_call(fine_coefficients, [(lz, lx, ly)], [field, ixy])
+    ztcame = gathered(zmsg, "gz")
+    (fine,) = kernel_call(fine_coefficients, [(lz, lx, ly)], [u, ixy])
     return kernel_call(
         third_apply,
         [(lz, lx, ly), (lz2, xtwo.fine, ytwo.fine), (lz3, xthree.fine, ythree.fine), (lz4, xthree.n, ythree.n)],
-        [u1, i2, field, ixy, fine, zmsg, *ztcame, *to32(px1, py1, px3, py3, tx3, ty3, qx3, qy3)],
+        [u1, i2, u, ixy, fine, zmsg, *ztcame, to32(px1), tables_x3, tables_y3],
         scratch=[
             pltpu.VMEM((z2, tall, packed), jnp.float32),
             pltpu.VMEM((z3, tall, packed), jnp.float32),
             pltpu.VMEM((lx, ly), jnp.float32),
-            pltpu.SemaphoreType.DMA,
+            pltpu.VMEM((lz2, xtwo.fine, ytwo.fine), jnp.float32),
+            pltpu.SemaphoreType.DMA((2,)),
         ],
         left=(4,),
-        left_out=(0,),
+        left_out=(0, 1),
         aliases={4: 0},
     )
 

time: 42.7 us -> 45 us (1.054)
  Pallas kernels: 7.21 us -> 9.98 us
  waiting for transfers between devices: 14.4 us -> 12.1 us
  starting transfers between devices: 16.9 us -> 18.8 us
    ppermute x0 -> x3, starting transfers between devices: none -> 4.49 us  [gathered(): lax.ppermute(what, axis, [(i, i ^ k) for i in range(count)])]
    ppermute x10 -> x7, waiting for transfers between devices: 11.5 us -> 7.79 us  [swapped(): lax.ppermute(value, axis, [(i, i ^ k) for i in range(count)])]
    pallas_call x7, Pallas kernels: 7.21 us -> 9.98 us  [kernel_call(): pl.pallas_call(body, out_shape=[jax.ShapeDtypeStruct(shape, jnp.float32)...]
    ppermute x10 -> x7, starting transfers between devices: 11.9 us -> 9.32 us  [swapped(): lax.ppermute(value, axis, [(i, i ^ k) for i in range(count)])]
    ppermute x0 -> x3, waiting for transfers between devices: none -> 1.49 us  [gathered(): lax.ppermute(what, axis, [(i, i ^ k) for i in range(count)])]
    unnamed x48 -> x22, local copies, waits for them, and re-layouts: 2.77 us -> 2.9 us
where the time goes in v3:
time: 45 us; the launch traced here: 44.5 us
  starting transfers between devices  18.8 us (42%)
  waiting for transfers between devices  12.1 us (27%)
  Pallas kernels  9.98 us (22%)
  local copies, waits for them, and re-layouts  2.9 us (6%)
  between operations  0.7 us (2%)
    pallas_call x7, Pallas kernels, kernel_call(): pl.pallas_call(body, out_shape=[jax.ShapeDtypeStruct(shape, jnp.float32)...  9.98 us
    ppermute x7, starting transfers between devices, swapped(): lax.ppermute(value, axis, [(i, i ^ k) for i in range(count)])  9.32 us
    ppermute x7, waiting for transfers between devices, swapped(): lax.ppermute(value, axis, [(i, i ^ k) for i in range(count)])  7.79 us
    ppermute x3, starting transfers between devices, shards(): lax.ppermute(plane, 'gz', [(i, i ^ k + 1) for i in range(dz)])  4.99 us
    ppermute x3, starting transfers between devices, gathered(): lax.ppermute(what, axis, [(i, i ^ k) for i in range(count)])  4.49 us
    unnamed x22, local copies, waits for them, and re-layouts  2.9 us
    ppermute x3, waiting for transfers between devices, shards(): lax.ppermute(plane, 'gz', [(i, i ^ k + 1) for i in range(dz)])  2.86 us
    ppermute x3, waiting for transfers between devices, gathered(): lax.ppermute(what, axis, [(i, i ^ k) for i in range(count)])  1.49 us
  transfers between devices with their start and end apart: 13, of which 10 were waited for; matrix products, arithmetic and copies ran while one was open for 0% of the time, Pallas kernels for 2%

profile of v3, /device:TPU:1, one launch (start us, length us, event | category | flops | bytes accessed | tf_op | source)
XLA Modules:
  0.0 44.5 jit_solution(7056500774211874)
XLA Ops:
  0.6 1.0 %copy-done.2 = f32[8,128,128]{2,1,0:T(8,128)S(1)} copy-done((f32[8,128,128]{2,1,0:T(8,128)S(1)}, f32[8,128,128]{2,1,0:T(8,128)}, u32[]{:S(2)}) %copy-start.2) | copy-done | bytes 524312
  1.7 0.8 %copy-done.9 = f32[2,32,128]{2,1,0:T(8,128)S(1)} copy-done((f32[2,32,128]{2,1,0:T(8,128)S(1)}, f32[2,32,128]{2,1,0:T(8,128)}, u32[]{:S(2)}) %copy-start.9) | copy-done | bytes 32792
  2.4 3.2 %shard_map.138 = (f32[16,1280]{1,0:T(8,128)S(1)}, f32[8,128,128]{2,1,0:T(8,128)S(1)}) custom-call(f32[8,128,128]{2,1,0:T(8,128)S(1)} %copy-done.2, f32[2,32,128]{2,1,0:T(8,128)S(1)} %copy-done.9), custom_call_target="tpu_custom_call" | custom-call | tf_op jit(solution)/shard_map/pallas_call | solution.py:148
  5.7 2.1 %collective-permute-start = (f32[16,1280]{1,0:T(8,128)S(1)}, f32[16,1280]{1,0:T(8,128)S(1)}, u32[]{:S(2)}, u32[]{:S(2)}) collective-permute-start(f32[16,1280]{1,0:T(8,128)S(1)} %get-tuple-element.21), channel_id=1, source_target_pairs={{0,4},{4,0},{1,5},{5,1},{2,6},{6,2},{3,7},{7,3},{8,12},{12,8},{9,1... | collective-permute-start | bytes 245768 | tf_op jit(solution)/shard_map/ppermute | solution.py:161
  7.8 2.2 %collective-permute-done.refs_1_ = f32[16,1280]{1,0:T(8,128)S(1)} collective-permute-done((f32[16,1280]{1,0:T(8,128)S(1)}, f32[16,1280]{1,0:T(8,128)S(1)}, u32[]{:S(2)}, u32[]{:S(2)}) %collective-permute-start) | collective-permute-done | bytes 81952 | tf_op jit(solution)/shard_map/ppermute | solution.py:161
  10.0 0.9 %copy-done.7 = f32[4,128,8]{2,1,0:T(8,128)S(1)} copy-done((f32[4,128,8]{2,1,0:T(8,128)S(1)}, f32[4,128,8]{2,1,0:T(8,128)}, u32[]{:S(2)}) %copy-start.7) | copy-done | bytes 16408
  10.9 1.5 %shard_map.139 = (f32[1024,128]{1,0:T(8,128)S(1)}, f32[256,256]{1,0:T(8,128)S(1)}, f32[4,128,128]{2,1,0:T(8,128)S(1)}, f32[8,8,128]{2,1,0:T(8,128)S(1)}) custom-call(f32[8,128,128]{2,1,0:T(8,128)S(1)} %get-tuple-element.20.refs_0_.u_ref.refs_2_, f32[16,1280]{1,0:T(8,128)S(1)} %collective-permute-done.refs_1_, f32[2,160,384]{2,1,0:T(8,128)S(1)} %copy-done.4, ...), custom_call_target="tpu_custom_call" | custom-call | tf_op jit(solution)/shard_map/pallas_call | solution.py:148
  12.4 3.3 %collective-permute-start.3 = (f32[8,8,128]{2,1,0:T(8,128)S(1)}, f32[8,8,128]{2,1,0:T(8,128)S(1)}, u32[]{:S(2)}, u32[]{:S(2)}) collective-permute-start(f32[8,8,128]{2,1,0:T(8,128)S(1)} %get-tuple-element.25.refs_3_), channel_id=1, source_target_pairs={{0,24},{8,16},{16,8},{24,0},{1,25},{9,17},{17,9},{25,1},{2,26},{10... | collective-permute-start | bytes 98312 | tf_op jit(solution)/shard_map/ppermute | solution.py:161
  15.7 0.4 collective-permute-start.1
  16.0 1.0 %collective-permute-done.3.refs_6_ = f32[8,8,128]{2,1,0:T(8,128)S(1)} collective-permute-done((f32[8,8,128]{2,1,0:T(8,128)S(1)}, f32[8,8,128]{2,1,0:T(8,128)S(1)}, u32[]{:S(2)}, u32[]{:S(2)}) %collective-permute-start.3) | collective-permute-done | bytes 32800 | tf_op jit(solution)/shard_map/ppermute | solution.py:161
  17.0 2.3 %collective-permute-done.2.refs_5_ = f32[8,8,128]{2,1,0:T(8,128)S(1)} collective-permute-done((f32[8,8,128]{2,1,0:T(8,128)S(1)}, f32[8,8,128]{2,1,0:T(8,128)S(1)}, u32[]{:S(2)}, u32[]{:S(2)}) %collective-permute-start.2) | collective-permute-done | bytes 32800 | tf_op jit(solution)/shard_map/ppermute | solution.py:161
  19.4 0.8 %shard_map.140 = (f32[4,128,128]{2,1,0:T(8,128)S(1)}, f32[80,128]{1,0:T(8,128)S(1)}, f32[4,64,128]{2,1,0:T(8,128)S(1)}, f32[64,128]{1,0:T(8,128)S(1)}, f32[64,128]{1,0:T(8,128)S(1)}, /*index=5*/f32[64,128]{1,0:T(8,128)S(1)}) custom-call(f32[1024,128]{1,0:T(8,128)S(1)} %get-tuple-element.22.refs_0_, f32[256,256]{1,0:T(8,128)S(1)} %get-tuple-element.23.refs_1_, ...), custom_call_target="tpu_custom_call" | custom-call | tf_op jit(solution)/shard_map/pallas_call | solution.py:148
  20.2 3.3 %collective-permute-start.4 = (f32[64,128]{1,0:T(8,128)S(1)}, f32[64,128]{1,0:T(8,128)S(1)}, u32[]{:S(2)}, u32[]{:S(2)}) collective-permute-start(f32[64,128]{1,0:T(8,128)S(1)} %get-tuple-element.27), channel_id=1, source_target_pairs={{0,1},{1,0},{2,3},{3,2},{4,5},{5,4},{6,7},{7,6},{8,9},{9,8},{10,11... | collective-permute-start | bytes 98312 | tf_op jit(solution)/shard_map/ppermute | solution.py:551
  23.5 1.2 %collective-permute-start.5 = (f32[64,128]{1,0:T(8,128)S(1)}, f32[64,128]{1,0:T(8,128)S(1)}, u32[]{:S(2)}, u32[]{:S(2)}) collective-permute-start(f32[64,128]{1,0:T(8,128)S(1)} %get-tuple-element.28), channel_id=1, source_target_pairs={{0,2},{1,3},{2,0},{3,1},{4,6},{5,7},{6,4},{7,5},{8,10},{9,11},{10,... | collective-permute-start | bytes 98312 | tf_op jit(solution)/shard_map/ppermute | solution.py:551
  24.7 0.5 %collective-permute-start.6 = (f32[64,128]{1,0:T(8,128)S(1)}, f32[64,128]{1,0:T(8,128)S(1)}, u32[]{:S(2)}, u32[]{:S(2)}) collective-permute-start(f32[64,128]{1,0:T(8,128)S(1)} %get-tuple-element.29), channel_id=1, source_target_pairs={{0,3},{1,2},{2,1},{3,0},{4,7},{5,6},{6,5},{7,4},{8,11},{9,10},{10,... | collective-permute-start | bytes 98312 | tf_op jit(solution)/shard_map/ppermute | solution.py:551
  25.2 1.1 %collective-permute-done.5.refs_2_ = f32[64,128]{1,0:T(8,128)S(1)} collective-permute-done((f32[64,128]{1,0:T(8,128)S(1)}, f32[64,128]{1,0:T(8,128)S(1)}, u32[]{:S(2)}, u32[]{:S(2)}) %collective-permute-start.5) | collective-permute-done | bytes 32800 | tf_op jit(solution)/shard_map/ppermute | solution.py:551
  26.3 1.8 %collective-permute-done.6.refs_3_ = f32[64,128]{1,0:T(8,128)S(1)} collective-permute-done((f32[64,128]{1,0:T(8,128)S(1)}, f32[64,128]{1,0:T(8,128)S(1)}, u32[]{:S(2)}, u32[]{:S(2)}) %collective-permute-start.6) | collective-permute-done | bytes 32800 | tf_op jit(solution)/shard_map/ppermute | solution.py:551
  28.1 0.2 shard_map.141
  28.3 1.2 %collective-permute-start.9 = (f32[16,512]{1,0:T(8,128)S(1)}, f32[16,512]{1,0:T(8,128)S(1)}, u32[]{:S(2)}, u32[]{:S(2)}) collective-permute-start(f32[16,512]{1,0:T(8,128)S(1)} %get-tuple-element.32), channel_id=1, source_target_pairs={{0,24},{8,16},{16,8},{24,0},{1,25},{9,17},{17,9},{25,1},{2,26},{10... | collective-permute-start | bytes 98312 | tf_op jit(solution)/shard_map/ppermute | solution.py:161
  29.5 0.6 %collective-permute-start.8 = (f32[16,512]{1,0:T(8,128)S(1)}, f32[16,512]{1,0:T(8,128)S(1)}, u32[]{:S(2)}, u32[]{:S(2)}) collective-permute-start(f32[16,512]{1,0:T(8,128)S(1)} %get-tuple-element.32), channel_id=1, source_target_pairs={{0,16},{8,24},{16,0},{24,8},{1,17},{9,25},{17,1},{25,9},{2,18},{10... | collective-permute-start | bytes 98312 | tf_op jit(solution)/shard_map/ppermute | solution.py:161
  30.1 1.8 %collective-permute-start.7 = (f32[16,512]{1,0:T(8,128)S(1)}, f32[16,512]{1,0:T(8,128)S(1)}, u32[]{:S(2)}, u32[]{:S(2)}) collective-permute-start(f32[16,512]{1,0:T(8,128)S(1)} %get-tuple-element.32), channel_id=1, source_target_pairs={{0,8},{8,0},{16,24},{24,16},{1,9},{9,1},{17,25},{25,17},{2,10},{10... | collective-permute-start | bytes 98312 | tf_op jit(solution)/shard_map/ppermute | solution.py:161
  31.9 1.0 %collective-permute-done.9.refs_4_ = f32[16,512]{1,0:T(8,128)S(1)} collective-permute-done((f32[16,512]{1,0:T(8,128)S(1)}, f32[16,512]{1,0:T(8,128)S(1)}, u32[]{:S(2)}, u32[]{:S(2)}) %collective-permute-start.9) | collective-permute-done | bytes 32800 | tf_op jit(solution)/shard_map/ppermute | solution.py:161
  32.9 0.4 collective-permute-done.8.refs_3_
  33.3 0.9 %collective-permute-done.7.refs_2_ = f32[16,512]{1,0:T(8,128)S(1)} collective-permute-done((f32[16,512]{1,0:T(8,128)S(1)}, f32[16,512]{1,0:T(8,128)S(1)}, u32[]{:S(2)}, u32[]{:S(2)}) %collective-permute-start.7) | collective-permute-done | bytes 32800 | tf_op jit(solution)/shard_map/ppermute | solution.py:161
  34.2 1.0 %shard_map.142 = (f32[4,48,128]{2,1,0:T(8,128)S(1)}, f32[2,64,128]{2,1,0:T(8,128)S(1)}) custom-call(f32[4,64,128]{2,1,0:T(8,128)S(1)} %get-tuple-element.30.refs_0_, f32[80,128]{1,0:T(8,128)S(1)} %get-tuple-element.31.refs_1_, f32[16,512]{1,0:T(8,128)S(1)} %collective-permute-done.7.refs_2_, f32[16,512]{1,0:T(8,128)S(1)} %collective-permute-done.8.refs_3_, ...), custom_call_target="tpu_custom_call" | custom-call | tf_op jit(solution)/shard_map/pallas_call | solution.py:148
  35.1 0.7 %collective-permute-start.11 = (f32[4,48,128]{2,1,0:T(8,128)S(1)}, f32[4,48,128]{2,1,0:T(8,128)S(1)}, u32[]{:S(2)}, u32[]{:S(2)}) collective-permute-start(f32[4,48,128]{2,1,0:T(8,128)S(1)} %get-tuple-element.35.refs_5_), channel_id=1, source_target_pairs={{0,2},{1,3},{2,0},{3,1},{4,6},{5,7},{6,4},{7,5},{8,10},{9,11},{10,... | collective-permute-start | bytes 294920 | tf_op jit(solution)/shard_map/ppermute | solution.py:168
  35.8 1.5 %collective-permute-start.10 = (f32[4,48,128]{2,1,0:T(8,128)S(1)}, f32[4,48,128]{2,1,0:T(8,128)S(1)}, u32[]{:S(2)}, u32[]{:S(2)}) collective-permute-start(f32[4,48,128]{2,1,0:T(8,128)S(1)} %get-tuple-element.35.refs_5_), channel_id=1, source_target_pairs={{0,1},{1,0},{2,3},{3,2},{4,5},{5,4},{6,7},{7,6},{8,9},{9,8},{10,11... | collective-permute-start | bytes 294920 | tf_op jit(solution)/shard_map/ppermute | solution.py:168
  37.3 1.4 %collective-permute-done.11.refs_7_ = f32[4,48,128]{2,1,0:T(8,128)S(1)} collective-permute-done((f32[4,48,128]{2,1,0:T(8,128)S(1)}, f32[4,48,128]{2,1,0:T(8,128)S(1)}, u32[]{:S(2)}, u32[]{:S(2)}) %collective-permute-start.11) | collective-permute-done | bytes 98336 | tf_op jit(solution)/shard_map/ppermute | solution.py:168
  38.7 2.3 %collective-permute-start.12 = (f32[4,48,128]{2,1,0:T(8,128)S(1)}, f32[4,48,128]{2,1,0:T(8,128)S(1)}, u32[]{:S(2)}, u32[]{:S(2)}) collective-permute-start(f32[4,48,128]{2,1,0:T(8,128)S(1)} %collective-permute-done.11.refs_7_), channel_id=1, source_target_pairs={{0,1},{1,0},{2,3},{3,2},{4,5},{5,4},{6,7},{7,6},{8,9},{9,8},{10,11... | collective-permute-start | bytes 294920 | tf_op jit(solution)/shard_map/ppermute | solution.py:168
  41.0 0.8 %shard_map.143.refs_4_ = f32[8,128,128]{2,1,0:T(8,128)} custom-call(f32[8,128,128]{2,1,0:T(8,128)S(1)} %get-tuple-element.20.refs_0_.u_ref.refs_2_, f32[4,128,128]{2,1,0:T(8,128)S(1)} %get-tuple-element.34.ixy_ref.refs_3_), custom_call_target="tpu_custom_call" | custom-call | tf_op jit(solution)/shard_map/pallas_call | solution.py:148
  41.8 0.1 collective-permute-done.12.refs_8_
  42.1 2.4 %shard_map.144 = (f32[8,128,128]{2,1,0:T(8,128)}, f32[4,64,64]{2,1,0:T(8,128)}, f32[2,32,32]{2,1,0:T(8,128)}, f32[1,16,16]{2,1,0:T(8,128)}) custom-call(f32[4,64,128]{2,1,0:T(8,128)S(1)} %get-tuple-element.30.refs_0_, f32[2,64,128]{2,1,0:T(8,128)S(1)} %get-tuple-element.33.refs_1_, ...), custom_call_target="tpu_custom_call", output_to_operand_aliasing={{0}: (4, {})} | custom-call | tf_op jit(solution)/shard_map/pallas_call | solution.py:148
  (23 shorter events, 0.2 us)
Async XLA Ops:
  0.6 1.0 %copy-start.2 = (f32[8,128,128]{2,1,0:T(8,128)S(1)}, f32[8,128,128]{2,1,0:T(8,128)}, u32[]{:S(2)}) copy-start(f32[8,128,128]{2,1,0:T(8,128)} %u_hbm.1) | copy-start | bytes 1572868
  1.7 0.8 %copy-start.9 = (f32[2,32,128]{2,1,0:T(8,128)S(1)}, f32[2,32,128]{2,1,0:T(8,128)}, u32[]{:S(2)}) copy-start(f32[2,32,128]{2,1,0:T(8,128)} %constant.20.clone.table_hbm) | copy-start | bytes 98308
  2.4 7.5 %copy-start.4 = (f32[2,160,384]{2,1,0:T(8,128)S(1)}, f32[2,160,384]{2,1,0:T(8,128)}, u32[]{:S(2)}) copy-start(f32[2,160,384]{2,1,0:T(8,128)} %constant.21.clone.refs_2_) | copy-start | bytes 1474564
  5.7 4.3 %collective-permute-start = (f32[16,1280]{1,0:T(8,128)S(1)}, f32[16,1280]{1,0:T(8,128)S(1)}, u32[]{:S(2)}, u32[]{:S(2)}) collective-permute-start(f32[16,1280]{1,0:T(8,128)S(1)} %get-tuple-element.21), channel_id=1, source_target_pairs={{0,4},{4,0},{1,5},{5,1},{2,6},{6,2},{3,7},{7,3},{8,12},{12,8},{9,1... | collective-permute-start | bytes 245768 | tf_op jit(solution)/shard_map/ppermute | solution.py:161
  10.0 1.0 %copy-start.7 = (f32[4,128,8]{2,1,0:T(8,128)S(1)}, f32[4,128,8]{2,1,0:T(8,128)}, u32[]{:S(2)}) copy-start(f32[4,128,8]{2,1,0:T(8,128)} %constant.27.clone.refs_3_) | copy-start | bytes 49156
  10.9 8.5 %copy-start.3 = (f32[4,128,152]{2,1,0:T(8,128)S(1)}, f32[4,128,152]{2,1,0:T(8,128)}, u32[]{:S(2)}) copy-start(f32[4,128,152]{2,1,0:T(8,128)} %constant.22.clone.refs_7_) | copy-start | bytes 933892
  12.4 4.6 %collective-permute-start.3 = (f32[8,8,128]{2,1,0:T(8,128)S(1)}, f32[8,8,128]{2,1,0:T(8,128)S(1)}, u32[]{:S(2)}, u32[]{:S(2)}) collective-permute-start(f32[8,8,128]{2,1,0:T(8,128)S(1)} %get-tuple-element.25.refs_3_), channel_id=1, source_target_pairs={{0,24},{8,16},{16,8},{24,0},{1,25},{9,17},{17,9},{25,1},{2,26},{10... | collective-permute-start | bytes 98312 | tf_op jit(solution)/shard_map/ppermute | solution.py:161
  15.7 3.7 %collective-permute-start.2 = (f32[8,8,128]{2,1,0:T(8,128)S(1)}, f32[8,8,128]{2,1,0:T(8,128)S(1)}, u32[]{:S(2)}, u32[]{:S(2)}) collective-permute-start(f32[8,8,128]{2,1,0:T(8,128)S(1)} %get-tuple-element.25.refs_3_), channel_id=1, source_target_pairs={{0,16},{8,24},{16,0},{24,8},{1,17},{9,25},{17,1},{25,9},{2,18},{10... | collective-permute-start | bytes 98312 | tf_op jit(solution)/shard_map/ppermute | solution.py:161
  15.7 3.7 %collective-permute-start.1 = (f32[8,8,128]{2,1,0:T(8,128)S(1)}, f32[8,8,128]{2,1,0:T(8,128)S(1)}, u32[]{:S(2)}, u32[]{:S(2)}) collective-permute-start(f32[8,8,128]{2,1,0:T(8,128)S(1)} %get-tuple-element.25.refs_3_), channel_id=1, source_target_pairs={{0,8},{8,0},{16,24},{24,16},{1,9},{9,1},{17,25},{25,17},{2,10},{10... | collective-permute-start | bytes 98312 | tf_op jit(solution)/shard_map/ppermute | solution.py:161
  19.4 8.7 %copy-start.10 = (f32[4,16,64]{2,1,0:T(8,128)S(1)}, f32[4,16,64]{2,1,0:T(8,128)}, u32[]{:S(2)}) copy-start(f32[4,16,64]{2,1,0:T(8,128)} %constant.28.clone.refs_4_) | copy-start | bytes 49156
  19.4 14.8 %copy-start.1 = (f32[2,512,128]{2,1,0:T(8,128)S(1)}, f32[2,512,128]{2,1,0:T(8,128)}, u32[]{:S(2)}) copy-start(f32[2,512,128]{2,1,0:T(8,128)} %constant.24.clone.refs_6_) | copy-start | bytes 1572868
  19.4 14.7 %copy-start.5 = (f32[4,208,112]{2,1,0:T(8,128)S(1)}, f32[4,208,112]{2,1,0:T(8,128)}, u32[]{:S(2)}) copy-start(f32[4,208,112]{2,1,0:T(8,128)} %constant.23.clone.refs_5_) | copy-start | bytes 1118212
  20.2 5.0 %collective-permute-start.4 = (f32[64,128]{1,0:T(8,128)S(1)}, f32[64,128]{1,0:T(8,128)S(1)}, u32[]{:S(2)}, u32[]{:S(2)}) collective-permute-start(f32[64,128]{1,0:T(8,128)S(1)} %get-tuple-element.27), channel_id=1, source_target_pairs={{0,1},{1,0},{2,3},{3,2},{4,5},{5,4},{6,7},{7,6},{8,9},{9,8},{10,11... | collective-permute-start | bytes 98312 | tf_op jit(solution)/shard_map/ppermute | solution.py:551
  23.5 2.8 %collective-permute-start.5 = (f32[64,128]{1,0:T(8,128)S(1)}, f32[64,128]{1,0:T(8,128)S(1)}, u32[]{:S(2)}, u32[]{:S(2)}) collective-permute-start(f32[64,128]{1,0:T(8,128)S(1)} %get-tuple-element.28), channel_id=1, source_target_pairs={{0,2},{1,3},{2,0},{3,1},{4,6},{5,7},{6,4},{7,5},{8,10},{9,11},{10,... | collective-permute-start | bytes 98312 | tf_op jit(solution)/shard_map/ppermute | solution.py:551
  24.7 3.3 %collective-permute-start.6 = (f32[64,128]{1,0:T(8,128)S(1)}, f32[64,128]{1,0:T(8,128)S(1)}, u32[]{:S(2)}, u32[]{:S(2)}) collective-permute-start(f32[64,128]{1,0:T(8,128)S(1)} %get-tuple-element.29), channel_id=1, source_target_pairs={{0,3},{1,2},{2,1},{3,0},{4,7},{5,6},{6,5},{7,4},{8,11},{9,10},{10,... | collective-permute-start | bytes 98312 | tf_op jit(solution)/shard_map/ppermute | solution.py:551
  28.3 4.6 %collective-permute-start.9 = (f32[16,512]{1,0:T(8,128)S(1)}, f32[16,512]{1,0:T(8,128)S(1)}, u32[]{:S(2)}, u32[]{:S(2)}) collective-permute-start(f32[16,512]{1,0:T(8,128)S(1)} %get-tuple-element.32), channel_id=1, source_target_pairs={{0,24},{8,16},{16,8},{24,0},{1,25},{9,17},{17,9},{25,1},{2,26},{10... | collective-permute-start | bytes 98312 | tf_op jit(solution)/shard_map/ppermute | solution.py:161
  29.5 3.8 %collective-permute-start.8 = (f32[16,512]{1,0:T(8,128)S(1)}, f32[16,512]{1,0:T(8,128)S(1)}, u32[]{:S(2)}, u32[]{:S(2)}) collective-permute-start(f32[16,512]{1,0:T(8,128)S(1)} %get-tuple-element.32), channel_id=1, source_target_pairs={{0,16},{8,24},{16,0},{24,8},{1,17},{9,25},{17,1},{25,9},{2,18},{10... | collective-permute-start | bytes 98312 | tf_op jit(solution)/shard_map/ppermute | solution.py:161
  30.1 4.1 %collective-permute-start.7 = (f32[16,512]{1,0:T(8,128)S(1)}, f32[16,512]{1,0:T(8,128)S(1)}, u32[]{:S(2)}, u32[]{:S(2)}) collective-permute-start(f32[16,512]{1,0:T(8,128)S(1)} %get-tuple-element.32), channel_id=1, source_target_pairs={{0,8},{8,0},{16,24},{24,16},{1,9},{9,1},{17,25},{25,17},{2,10},{10... | collective-permute-start | bytes 98312 | tf_op jit(solution)/shard_map/ppermute | solution.py:161
  35.1 6.8 %copy-start = (f32[2,768,128]{2,1,0:T(8,128)S(1)}, f32[2,768,128]{2,1,0:T(8,128)}, u32[]{:S(2)}) copy-start(f32[2,768,128]{2,1,0:T(8,128)} %constant.26.clone.refs_11_) | copy-start | bytes 2359300
  35.1 3.5 %collective-permute-start.11 = (f32[4,48,128]{2,1,0:T(8,128)S(1)}, f32[4,48,128]{2,1,0:T(8,128)S(1)}, u32[]{:S(2)}, u32[]{:S(2)}) collective-permute-start(f32[4,48,128]{2,1,0:T(8,128)S(1)} %get-tuple-element.35.refs_5_), channel_id=1, source_target_pairs={{0,2},{1,3},{2,0},{3,1},{4,6},{5,7},{6,4},{7,5},{8,10},{9,11},{10,... | collective-permute-start | bytes 294920 | tf_op jit(solution)/shard_map/ppermute | solution.py:168
  35.8 6.1 %collective-permute-start.10 = (f32[4,48,128]{2,1,0:T(8,128)S(1)}, f32[4,48,128]{2,1,0:T(8,128)S(1)}, u32[]{:S(2)}, u32[]{:S(2)}) collective-permute-start(f32[4,48,128]{2,1,0:T(8,128)S(1)} %get-tuple-element.35.refs_5_), channel_id=1, source_target_pairs={{0,1},{1,0},{2,3},{3,2},{4,5},{5,4},{6,7},{7,6},{8,9},{9,8},{10,11... | collective-permute-start | bytes 294920 | tf_op jit(solution)/shard_map/ppermute | solution.py:168
  38.7 3.3 %collective-permute-start.12 = (f32[4,48,128]{2,1,0:T(8,128)S(1)}, f32[4,48,128]{2,1,0:T(8,128)S(1)}, u32[]{:S(2)}, u32[]{:S(2)}) collective-permute-start(f32[4,48,128]{2,1,0:T(8,128)S(1)} %collective-permute-done.11.refs_7_), channel_id=1, source_target_pairs={{0,1},{1,0},{2,3},{3,2},{4,5},{5,4},{6,7},{7,6},{8,9},{9,8},{10,11... | collective-permute-start | bytes 294920 | tf_op jit(solution)/shard_map/ppermute | solution.py:168
  41.0 1.0 %copy-start.6 = (f32[4,144,48]{2,1,0:T(8,128)S(1)}, f32[4,144,48]{2,1,0:T(8,128)}, u32[]{:S(2)}) copy-start(f32[4,144,48]{2,1,0:T(8,128)} %constant.25.clone.refs_10_) | copy-start | bytes 331780
  41.0 1.1 %copy-start.8 = (f32[128,96]{1,0:T(8,128)S(1)}, f32[128,96]{1,0:T(8,128)}, u32[]{:S(2)}) copy-start(f32[128,96]{1,0:T(8,128)} %constant.29.clone.refs_9_) | copy-start | bytes 147460

commit v4 on v3

--- a/solution.py
+++ b/solution.py
@@ -144,7 +144,7 @@
 
 
 def kernel_call(body, outs, arrays, scratch=(), left=(), left_out=(), aliases={}):
-    space = lambda place, where: pl.BlockSpec(memory_space=pl.ANY if place in where else pltpu.VMEM)
+    space = lambda place, where: pl.BlockSpec(memory_space=pltpu.HBM if place in where else pltpu.VMEM)
     return pl.pallas_call(
         body,
         out_shape=[jax.ShapeDtypeStruct(shape, jnp.float32) for shape in outs],
@@ -153,7 +153,7 @@
         scratch_shapes=list(scratch),
         input_output_aliases=aliases,
         compiler_params=pltpu.CompilerParams(vmem_limit_bytes=40 << 20),
-    )(*arrays)
+    )(*(pltpu.with_memory_space_constraint(a, pltpu.HBM) if i in left else a for i, a in enumerate(arrays)))
 
 
 def swapped(value, axis):
@@ -161,13 +161,13 @@
     return [lax.ppermute(value, axis, [(i, i ^ k) for i in range(count)]) for k in range(1, count)]
 
 
-def gathered(value, axis):
+def gathered(value, axis, beside):
     count = lax.axis_size(axis)
     if count != 4:
-        return swapped(value, axis)
+        return swapped(value, axis), beside
     by = lambda k, what: lax.ppermute(what, axis, [(i, i ^ k) for i in range(count)])
-    far = by(2, value)
-    return [by(1, value), far, by(1, far)]
+    far, beside = lax.optimization_barrier((by(2, value), beside))
+    return [by(1, value), far, by(1, far)], beside
 
 
 def chosen_by(values, j):
@@ -329,38 +329,40 @@
     tables_y3, at_y3 = stacked(ty3, qy3, py3, py1)
     hz, hx1 = lz // 2, lx // 2
 
-    def y_messages(u_hbm, table_hbm, out_ref, u_ref, table, sems):
+    def y_messages(u_hbm, table_hbm, ty_hbm, fx_hbm, out_ref, u_ref, ty_ref, fx_ref, table, sems):
         j = lax.axis_index("gy")
         nt = ((1,), (1,))
-        copies = [pltpu.make_async_copy(table_hbm.at[j], table, sems.at[lz])]
-        copies += [pltpu.make_async_copy(u_hbm.at[z], u_ref.at[z], sems.at[z]) for z in range(lz)]
+        copies = [pltpu.make_async_copy(table_hbm.at[j], table, sems.at[0])]
+        copies.append(pltpu.make_async_copy(u_hbm, u_ref, sems.at[1]))
+        copies.append(pltpu.make_async_copy(ty_hbm.at[j], ty_ref, sems.at[2]))
+        copies.append(pltpu.make_async_copy(fx_hbm.at[lax.axis_index("gx")], fx_ref, sems.at[3]))
         for copy in copies:
             copy.start()
-        copies[0].wait()
-        for z in range(lz):
-            copies[z + 1].wait()
-            out_ref[:kya, z * lx : (z + 1) * lx] = dot(table[:kya], u_ref[z], nt)
+        for copy in copies[:2]:
+            copy.wait()
+        out_ref[:kya, : lz * lx] = dot(table[:kya], u_ref[...].reshape(lz * lx, ly), nt)
         even = jnp.concatenate([u_ref[2 * z, pl.ds(0, hx1, stride=2), :] for z in range(hz)], axis=0)
         out_ref[:kys, lz * lx :] = dot(table[kya : kya + kys], even, nt)
+        for copy in copies[2:]:
+            copy.wait()
 
     def y_apply(*refs):
         u_ref, came = refs[0], refs[1:dy]
         ty_ref, fx_ref, ta_out, tsm_out, iy_out, xm_out = refs[dy:]
-        j, jx = lax.axis_index("gy"), lax.axis_index("gx")
         tn = ((0,), (0,))
-        ta_all = dot(u_ref[...].reshape(lz * lx, ly), ty_ref[j, :ly, :wide])
+        ta_all = dot(u_ref[...].reshape(lz * lx, ly), ty_ref[:ly, :wide])
         even = jnp.concatenate([u_ref[2 * z, pl.ds(0, hx1, stride=2), :] for z in range(hz)], axis=0)
-        tsm_all = dot(even, ty_ref[j, :ly, wide:])
+        tsm_all = dot(even, ty_ref[:ly, wide:])
         for k, ref in enumerate(came):
             begin = ly + kya * k
-            ta_all += dot(ref[:kya, : lz * lx], ty_ref[j, begin : begin + kya, :wide], tn)
+            ta_all += dot(ref[:kya, : lz * lx], ty_ref[begin : begin + kya, :wide], tn)
             begin = ly + kya * (dy - 1) + kys * k
-            tsm_all += dot(ref[:kys, lz * lx :], ty_ref[j, begin : begin + kys, wide:], tn)
+            tsm_all += dot(ref[:kys, lz * lx :], ty_ref[begin : begin + kys, wide:], tn)
         ta_out[...] = ta_all
         tsm_out[...] = tsm_all
         xm_out[...] = jnp.zeros_like(xm_out)
         lane = iota((lx, ly), 1)
-        weights = [jnp.broadcast_to(fx_ref[jx, :, c : c + 1], (lx, wide)) for c in range(2)]
+        weights = [jnp.broadcast_to(fx_ref[:, c : c + 1], (lx, wide)) for c in range(2)]
         xm_out[0, 5:6, :wide] = tsm_all[0:1, :wide]
         for z in range(lz):
             part = ta_all[z * lx : (z + 1) * lx]
@@ -527,19 +529,19 @@
         for copy in copies:
             copy.wait()
 
-    ym, u = kernel_call(
+    ym, u, own_ty, own_fx = kernel_call(
         y_messages,
-        [(max(kya, kys), lz * lx + hz * hx1), (lz, lx, ly)],
-        [field, messages_y],
-        scratch=[pltpu.VMEM((kya + kys, ly), jnp.float32), pltpu.SemaphoreType.DMA((lz + 1,))],
-        left=(0, 1),
+        [(max(kya, kys), lz * lx + hz * hx1), (lz, lx, ly), tables_y.shape[1:], fx.shape[1:]],
+        [field, messages_y, tables_y, to32(fx)],
+        scratch=[pltpu.VMEM((kya + kys, ly), jnp.float32), pltpu.SemaphoreType.DMA((4,))],
+        left=(0, 1, 2, 3),
     )
     ycame = swapped(ym, "gy")
     xw = max(wide, ly)
     ta_v, tsm_v, iy, xm = kernel_call(
         y_apply,
         [(lz * lx, wide), (hz * hx1, 2 * wide), (hz, lx, ly), (lz, 8, xw)],
-        [u, *ycame, tables_y, to32(fx)],
+        [u, *ycame, own_ty, own_fx],
     )
     xcame = swapped(xm, "gx")
     ixy, zc, u1_part, *planes = kernel_call(
@@ -557,8 +559,8 @@
         [(lz2, tall, packed), (lz2 // 2, xtwo.fine, round_up(ytwo.fine, 128))],
         [u1, zc, *xtcame, tables_x2, tables_y2],
     )
-    ztcame = gathered(zmsg, "gz")
     (fine,) = kernel_call(fine_coefficients, [(lz, lx, ly)], [u, ixy])
+    ztcame, fine = gathered(zmsg, "gz", fine)
     return kernel_call(
         third_apply,
         [(lz, lx, ly), (lz2, xtwo.fine, ytwo.fine), (lz3, xthree.fine, ythree.fine), (lz4, xthree.n, ythree.n)],

time: 45 us -> 40.7 us (0.904)
  local copies, waits for them, and re-layouts: 2.9 us -> 0.04 us
  Pallas kernels: 9.98 us -> 8.52 us
    unnamed x22 -> x14, local copies, waits for them, and re-layouts: 2.9 us -> 0.04 us
    pallas_call x7, Pallas kernels: 9.98 us -> 8.52 us  [kernel_call(): pl.pallas_call(body, out_shape=[jax.ShapeDtypeStruct(shape, jnp.float32)...]
where the time goes in v4:
time: 40.7 us; the launch traced here: 40.2 us
  starting transfers between devices  18.8 us (46%)
  waiting for transfers between devices  12.1 us (30%)
  Pallas kernels  8.52 us (21%)
  between operations  0.7 us (2%)
    ppermute x7, starting transfers between devices, swapped(): lax.ppermute(value, axis, [(i, i ^ k) for i in range(count)])  9.31 us
    pallas_call x7, Pallas kernels, kernel_call(): pl.pallas_call(body, out_shape=[jax.ShapeDtypeStruct(shape, jnp.float32)...  8.52 us
    ppermute x7, waiting for transfers between devices, swapped(): lax.ppermute(value, axis, [(i, i ^ k) for i in range(count)])  7.79 us
    ppermute x3, starting transfers between devices, shards(): lax.ppermute(plane, 'gz', [(i, i ^ k + 1) for i in range(dz)])  4.99 us
    ppermute x3, starting transfers between devices, gathered(): lax.ppermute(what, axis, [(i, i ^ k) for i in range(count)])  4.51 us
    ppermute x3, waiting for transfers between devices, shards(): lax.ppermute(plane, 'gz', [(i, i ^ k + 1) for i in range(dz)])  2.86 us
    ppermute x3, waiting for transfers between devices, gathered(): lax.ppermute(what, axis, [(i, i ^ k) for i in range(count)])  1.48 us
  transfers between devices with their start and end apart: 13, of which 10 were waited for; matrix products, arithmetic and copies ran while one was open for 0% of the time, Pallas kernels for 2%

profile of v4, /device:TPU:1, one launch (start us, length us, event | category | flops | bytes accessed | tf_op | source)
XLA Modules:
  0.0 40.2 jit_solution(5652277733560490366)
XLA Ops:
  0.6 1.7 %shard_map.138 = (f32[16,1280]{1,0:T(8,128)S(1)}, f32[8,128,128]{2,1,0:T(8,128)S(1)}, f32[160,384]{1,0:T(8,128)S(1)}, f32[128,8]{1,0:T(8,128)S(1)}) custom-call(f32[8,128,128]{2,1,0:T(8,128)} %u_hbm.1, f32[2,32,128]{2,1,0:T(8,128)} %constant.20.clone.table_hbm, f32[2,160,384]{2,1,0:T(8,128)} %constant.21.clone.ty_hbm, f32[4,128,8]{2,1,0:T(8,128)} %constant.27.clone.fx_hbm), custom_call_target="tpu_custom_call" | custom-call | tf_op jit(solution)/shard_map/pallas_call | solution.py:148
  2.4 0.0 copy-start.2
  2.4 2.1 %collective-permute-start = (f32[16,1280]{1,0:T(8,128)S(1)}, f32[16,1280]{1,0:T(8,128)S(1)}, u32[]{:S(2)}, u32[]{:S(2)}) collective-permute-start(f32[16,1280]{1,0:T(8,128)S(1)} %get-tuple-element.25), channel_id=1, source_target_pairs={{0,4},{4,0},{1,5},{5,1},{2,6},{6,2},{3,7},{7,3},{8,12},{12,8},{9,1... | collective-permute-start | bytes 245768 | tf_op jit(solution)/shard_map/ppermute | solution.py:161
  4.5 2.2 %collective-permute-done.refs_1_ = f32[16,1280]{1,0:T(8,128)S(1)} collective-permute-done((f32[16,1280]{1,0:T(8,128)S(1)}, f32[16,1280]{1,0:T(8,128)S(1)}, u32[]{:S(2)}, u32[]{:S(2)}) %collective-permute-start) | collective-permute-done | bytes 81952 | tf_op jit(solution)/shard_map/ppermute | solution.py:161
  6.7 1.5 %shard_map.139 = (f32[1024,128]{1,0:T(8,128)S(1)}, f32[256,256]{1,0:T(8,128)S(1)}, f32[4,128,128]{2,1,0:T(8,128)S(1)}, f32[8,8,128]{2,1,0:T(8,128)S(1)}) custom-call(f32[8,128,128]{2,1,0:T(8,128)S(1)} %get-tuple-element.24.refs_0_.u_ref.refs_2_, f32[16,1280]{1,0:T(8,128)S(1)} %collective-permute-done.refs_1_, f32[160,384]{1,0:T(8,128)S(1)} %get-tuple-element.26.refs_2_, ...), custom_call_target="tpu_custom_call" | custom-call | tf_op jit(solution)/shard_map/pallas_call | solution.py:148
  8.2 3.3 %collective-permute-start.3 = (f32[8,8,128]{2,1,0:T(8,128)S(1)}, f32[8,8,128]{2,1,0:T(8,128)S(1)}, u32[]{:S(2)}, u32[]{:S(2)}) collective-permute-start(f32[8,8,128]{2,1,0:T(8,128)S(1)} %get-tuple-element.31.refs_3_), channel_id=1, source_target_pairs={{0,24},{8,16},{16,8},{24,0},{1,25},{9,17},{17,9},{25,1},{2,26},{10... | collective-permute-start | bytes 98312 | tf_op jit(solution)/shard_map/ppermute | solution.py:161
  11.5 0.4 collective-permute-start.1
  11.8 1.0 %collective-permute-done.3.refs_6_ = f32[8,8,128]{2,1,0:T(8,128)S(1)} collective-permute-done((f32[8,8,128]{2,1,0:T(8,128)S(1)}, f32[8,8,128]{2,1,0:T(8,128)S(1)}, u32[]{:S(2)}, u32[]{:S(2)}) %collective-permute-start.3) | collective-permute-done | bytes 32800 | tf_op jit(solution)/shard_map/ppermute | solution.py:161
  12.8 2.3 %collective-permute-done.2.refs_5_ = f32[8,8,128]{2,1,0:T(8,128)S(1)} collective-permute-done((f32[8,8,128]{2,1,0:T(8,128)S(1)}, f32[8,8,128]{2,1,0:T(8,128)S(1)}, u32[]{:S(2)}, u32[]{:S(2)}) %collective-permute-start.2) | collective-permute-done | bytes 32800 | tf_op jit(solution)/shard_map/ppermute | solution.py:161
  15.2 0.0 copy-start.1
  15.2 0.0 copy-start.3
  15.2 0.8 %shard_map.140 = (f32[4,128,128]{2,1,0:T(8,128)S(1)}, f32[80,128]{1,0:T(8,128)S(1)}, f32[4,64,128]{2,1,0:T(8,128)S(1)}, f32[64,128]{1,0:T(8,128)S(1)}, f32[64,128]{1,0:T(8,128)S(1)}, /*index=5*/f32[64,128]{1,0:T(8,128)S(1)}) custom-call(f32[1024,128]{1,0:T(8,128)S(1)} %get-tuple-element.28.refs_0_, f32[256,256]{1,0:T(8,128)S(1)} %get-tuple-element.29.refs_1_, ...), custom_call_target="tpu_custom_call" | custom-call | tf_op jit(solution)/shard_map/pallas_call | solution.py:148
  16.0 3.3 %collective-permute-start.4 = (f32[64,128]{1,0:T(8,128)S(1)}, f32[64,128]{1,0:T(8,128)S(1)}, u32[]{:S(2)}, u32[]{:S(2)}) collective-permute-start(f32[64,128]{1,0:T(8,128)S(1)} %get-tuple-element.33), channel_id=1, source_target_pairs={{0,1},{1,0},{2,3},{3,2},{4,5},{5,4},{6,7},{7,6},{8,9},{9,8},{10,11... | collective-permute-start | bytes 98312 | tf_op jit(solution)/shard_map/ppermute | solution.py:553
  19.3 1.2 %collective-permute-start.5 = (f32[64,128]{1,0:T(8,128)S(1)}, f32[64,128]{1,0:T(8,128)S(1)}, u32[]{:S(2)}, u32[]{:S(2)}) collective-permute-start(f32[64,128]{1,0:T(8,128)S(1)} %get-tuple-element.34), channel_id=1, source_target_pairs={{0,2},{1,3},{2,0},{3,1},{4,6},{5,7},{6,4},{7,5},{8,10},{9,11},{10,... | collective-permute-start | bytes 98312 | tf_op jit(solution)/shard_map/ppermute | solution.py:553
  20.5 0.5 %collective-permute-start.6 = (f32[64,128]{1,0:T(8,128)S(1)}, f32[64,128]{1,0:T(8,128)S(1)}, u32[]{:S(2)}, u32[]{:S(2)}) collective-permute-start(f32[64,128]{1,0:T(8,128)S(1)} %get-tuple-element.35), channel_id=1, source_target_pairs={{0,3},{1,2},{2,1},{3,0},{4,7},{5,6},{6,5},{7,4},{8,11},{9,10},{10,... | collective-permute-start | bytes 98312 | tf_op jit(solution)/shard_map/ppermute | solution.py:553
  21.0 1.1 %collective-permute-done.5.refs_2_ = f32[64,128]{1,0:T(8,128)S(1)} collective-permute-done((f32[64,128]{1,0:T(8,128)S(1)}, f32[64,128]{1,0:T(8,128)S(1)}, u32[]{:S(2)}, u32[]{:S(2)}) %collective-permute-start.5) | collective-permute-done | bytes 32800 | tf_op jit(solution)/shard_map/ppermute | solution.py:553
  22.1 1.8 %collective-permute-done.6.refs_3_ = f32[64,128]{1,0:T(8,128)S(1)} collective-permute-done((f32[64,128]{1,0:T(8,128)S(1)}, f32[64,128]{1,0:T(8,128)S(1)}, u32[]{:S(2)}, u32[]{:S(2)}) %collective-permute-start.6) | collective-permute-done | bytes 32800 | tf_op jit(solution)/shard_map/ppermute | solution.py:553
  23.9 0.2 shard_map.141
  24.1 1.2 %collective-permute-start.9 = (f32[16,512]{1,0:T(8,128)S(1)}, f32[16,512]{1,0:T(8,128)S(1)}, u32[]{:S(2)}, u32[]{:S(2)}) collective-permute-start(f32[16,512]{1,0:T(8,128)S(1)} %get-tuple-element.38), channel_id=1, source_target_pairs={{0,24},{8,16},{16,8},{24,0},{1,25},{9,17},{17,9},{25,1},{2,26},{10... | collective-permute-start | bytes 98312 | tf_op jit(solution)/shard_map/ppermute | solution.py:161
  25.3 0.6 %collective-permute-start.8 = (f32[16,512]{1,0:T(8,128)S(1)}, f32[16,512]{1,0:T(8,128)S(1)}, u32[]{:S(2)}, u32[]{:S(2)}) collective-permute-start(f32[16,512]{1,0:T(8,128)S(1)} %get-tuple-element.38), channel_id=1, source_target_pairs={{0,16},{8,24},{16,0},{24,8},{1,17},{9,25},{17,1},{25,9},{2,18},{10... | collective-permute-start | bytes 98312 | tf_op jit(solution)/shard_map/ppermute | solution.py:161
  25.9 1.8 %collective-permute-start.7 = (f32[16,512]{1,0:T(8,128)S(1)}, f32[16,512]{1,0:T(8,128)S(1)}, u32[]{:S(2)}, u32[]{:S(2)}) collective-permute-start(f32[16,512]{1,0:T(8,128)S(1)} %get-tuple-element.38), channel_id=1, source_target_pairs={{0,8},{8,0},{16,24},{24,16},{1,9},{9,1},{17,25},{25,17},{2,10},{10... | collective-permute-start | bytes 98312 | tf_op jit(solution)/shard_map/ppermute | solution.py:161
  27.7 1.0 %collective-permute-done.9.refs_4_ = f32[16,512]{1,0:T(8,128)S(1)} collective-permute-done((f32[16,512]{1,0:T(8,128)S(1)}, f32[16,512]{1,0:T(8,128)S(1)}, u32[]{:S(2)}, u32[]{:S(2)}) %collective-permute-start.9) | collective-permute-done | bytes 32800 | tf_op jit(solution)/shard_map/ppermute | solution.py:161
  28.7 0.4 collective-permute-done.8.refs_3_
  29.1 0.9 %collective-permute-done.7.refs_2_ = f32[16,512]{1,0:T(8,128)S(1)} collective-permute-done((f32[16,512]{1,0:T(8,128)S(1)}, f32[16,512]{1,0:T(8,128)S(1)}, u32[]{:S(2)}, u32[]{:S(2)}) %collective-permute-start.7) | collective-permute-done | bytes 32800 | tf_op jit(solution)/shard_map/ppermute | solution.py:161
  30.0 1.0 %shard_map.142 = (f32[4,48,128]{2,1,0:T(8,128)S(1)}, f32[2,64,128]{2,1,0:T(8,128)S(1)}) custom-call(f32[4,64,128]{2,1,0:T(8,128)S(1)} %get-tuple-element.36.refs_0_, f32[80,128]{1,0:T(8,128)S(1)} %get-tuple-element.37.refs_1_, f32[16,512]{1,0:T(8,128)S(1)} %collective-permute-done.7.refs_2_, f32[16,512]{1,0:T(8,128)S(1)} %collective-permute-done.8.refs_3_, ...), custom_call_target="tpu_custom_call" | custom-call | tf_op jit(solution)/shard_map/pallas_call | solution.py:148
  30.9 0.7 %collective-permute-start.10 = (f32[4,48,128]{2,1,0:T(8,128)S(1)}, f32[4,48,128]{2,1,0:T(8,128)S(1)}, u32[]{:S(2)}, u32[]{:S(2)}) collective-permute-start(f32[4,48,128]{2,1,0:T(8,128)S(1)} %get-tuple-element.41.refs_5_), channel_id=1, source_target_pairs={{0,2},{1,3},{2,0},{3,1},{4,6},{5,7},{6,4},{7,5},{8,10},{9,11},{10,... | collective-permute-start | bytes 294920 | tf_op jit(solution)/shard_map/ppermute | solution.py:168
  31.6 0.8 %shard_map.143.refs_4_ = f32[8,128,128]{2,1,0:T(8,128)} custom-call(f32[8,128,128]{2,1,0:T(8,128)S(1)} %get-tuple-element.24.refs_0_.u_ref.refs_2_, f32[4,128,128]{2,1,0:T(8,128)S(1)} %get-tuple-element.40.ixy_ref.refs_3_), custom_call_target="tpu_custom_call" | custom-call | tf_op jit(solution)/shard_map/pallas_call | solution.py:148
  32.4 1.5 %collective-permute-start.11 = (f32[4,48,128]{2,1,0:T(8,128)S(1)}, f32[4,48,128]{2,1,0:T(8,128)S(1)}, u32[]{:S(2)}, u32[]{:S(2)}) collective-permute-start(f32[4,48,128]{2,1,0:T(8,128)S(1)} %get-tuple-element.41.refs_5_), channel_id=1, source_target_pairs={{0,1},{1,0},{2,3},{3,2},{4,5},{5,4},{6,7},{7,6},{8,9},{9,8},{10,11... | collective-permute-start | bytes 294920 | tf_op jit(solution)/shard_map/ppermute | solution.py:168
  33.9 0.5 %collective-permute-done.10.refs_7_ = f32[4,48,128]{2,1,0:T(8,128)S(1)} collective-permute-done((f32[4,48,128]{2,1,0:T(8,128)S(1)}, f32[4,48,128]{2,1,0:T(8,128)S(1)}, u32[]{:S(2)}, u32[]{:S(2)}) %collective-permute-start.10) | collective-permute-done | bytes 98336 | tf_op jit(solution)/shard_map/ppermute | solution.py:168
  34.4 2.4 %collective-permute-start.12 = (f32[4,48,128]{2,1,0:T(8,128)S(1)}, f32[4,48,128]{2,1,0:T(8,128)S(1)}, u32[]{:S(2)}, u32[]{:S(2)}) collective-permute-start(f32[4,48,128]{2,1,0:T(8,128)S(1)} %collective-permute-done.10.refs_7_), channel_id=1, source_target_pairs={{0,1},{1,0},{2,3},{3,2},{4,5},{5,4},{6,7},{7,6},{8,9},{9,8},{10,11... | collective-permute-start | bytes 294920 | tf_op jit(solution)/shard_map/ppermute | solution.py:168
  36.8 0.9 %collective-permute-done.12.refs_8_ = f32[4,48,128]{2,1,0:T(8,128)S(1)} collective-permute-done((f32[4,48,128]{2,1,0:T(8,128)S(1)}, f32[4,48,128]{2,1,0:T(8,128)S(1)}, u32[]{:S(2)}, u32[]{:S(2)}) %collective-permute-start.12) | collective-permute-done | bytes 98336 | tf_op jit(solution)/shard_map/ppermute | solution.py:168
  37.8 2.4 %shard_map.144 = (f32[8,128,128]{2,1,0:T(8,128)}, f32[4,64,64]{2,1,0:T(8,128)}, f32[2,32,32]{2,1,0:T(8,128)}, f32[1,16,16]{2,1,0:T(8,128)}) custom-call(f32[4,64,128]{2,1,0:T(8,128)S(1)} %get-tuple-element.36.refs_0_, f32[2,64,128]{2,1,0:T(8,128)S(1)} %get-tuple-element.39.refs_1_, ...), custom_call_target="tpu_custom_call", output_to_operand_aliasing={{0}: (4, {})} | custom-call | tf_op jit(solution)/shard_map/pallas_call | solution.py:148
  (15 shorter events, 0.0 us)
Async XLA Ops:
  2.4 12.8 %copy-start.2 = (f32[4,128,152]{2,1,0:T(8,128)S(1)}, f32[4,128,152]{2,1,0:T(8,128)}, u32[]{:S(2)}) copy-start(f32[4,128,152]{2,1,0:T(8,128)} %constant.22.clone.refs_7_) | copy-start | bytes 933892
  2.4 4.3 %collective-permute-start = (f32[16,1280]{1,0:T(8,128)S(1)}, f32[16,1280]{1,0:T(8,128)S(1)}, u32[]{:S(2)}, u32[]{:S(2)}) collective-permute-start(f32[16,1280]{1,0:T(8,128)S(1)} %get-tuple-element.25), channel_id=1, source_target_pairs={{0,4},{4,0},{1,5},{5,1},{2,6},{6,2},{3,7},{7,3},{8,12},{12,8},{9,1... | collective-permute-start | bytes 245768 | tf_op jit(solution)/shard_map/ppermute | solution.py:161
  8.2 4.6 %collective-permute-start.3 = (f32[8,8,128]{2,1,0:T(8,128)S(1)}, f32[8,8,128]{2,1,0:T(8,128)S(1)}, u32[]{:S(2)}, u32[]{:S(2)}) collective-permute-start(f32[8,8,128]{2,1,0:T(8,128)S(1)} %get-tuple-element.31.refs_3_), channel_id=1, source_target_pairs={{0,24},{8,16},{16,8},{24,0},{1,25},{9,17},{17,9},{25,1},{2,26},{10... | collective-permute-start | bytes 98312 | tf_op jit(solution)/shard_map/ppermute | solution.py:161
  11.5 3.7 %collective-permute-start.2 = (f32[8,8,128]{2,1,0:T(8,128)S(1)}, f32[8,8,128]{2,1,0:T(8,128)S(1)}, u32[]{:S(2)}, u32[]{:S(2)}) collective-permute-start(f32[8,8,128]{2,1,0:T(8,128)S(1)} %get-tuple-element.31.refs_3_), channel_id=1, source_target_pairs={{0,16},{8,24},{16,0},{24,8},{1,17},{9,25},{17,1},{25,9},{2,18},{10... | collective-permute-start | bytes 98312 | tf_op jit(solution)/shard_map/ppermute | solution.py:161
  11.5 3.7 %collective-permute-start.1 = (f32[8,8,128]{2,1,0:T(8,128)S(1)}, f32[8,8,128]{2,1,0:T(8,128)S(1)}, u32[]{:S(2)}, u32[]{:S(2)}) collective-permute-start(f32[8,8,128]{2,1,0:T(8,128)S(1)} %get-tuple-element.31.refs_3_), channel_id=1, source_target_pairs={{0,8},{8,0},{16,24},{24,16},{1,9},{9,1},{17,25},{25,17},{2,10},{10... | collective-permute-start | bytes 98312 | tf_op jit(solution)/shard_map/ppermute | solution.py:161
  15.2 8.7 %copy-start.6 = (f32[4,16,64]{2,1,0:T(8,128)S(1)}, f32[4,16,64]{2,1,0:T(8,128)}, u32[]{:S(2)}) copy-start(f32[4,16,64]{2,1,0:T(8,128)} %constant.28.clone.refs_4_) | copy-start | bytes 49156
  15.2 14.8 %copy-start.1 = (f32[2,512,128]{2,1,0:T(8,128)S(1)}, f32[2,512,128]{2,1,0:T(8,128)}, u32[]{:S(2)}) copy-start(f32[2,512,128]{2,1,0:T(8,128)} %constant.24.clone.refs_6_) | copy-start | bytes 1572868
  15.2 14.8 %copy-start.3 = (f32[4,208,112]{2,1,0:T(8,128)S(1)}, f32[4,208,112]{2,1,0:T(8,128)}, u32[]{:S(2)}) copy-start(f32[4,208,112]{2,1,0:T(8,128)} %constant.23.clone.refs_5_) | copy-start | bytes 1118212
  16.0 5.0 %collective-permute-start.4 = (f32[64,128]{1,0:T(8,128)S(1)}, f32[64,128]{1,0:T(8,128)S(1)}, u32[]{:S(2)}, u32[]{:S(2)}) collective-permute-start(f32[64,128]{1,0:T(8,128)S(1)} %get-tuple-element.33), channel_id=1, source_target_pairs={{0,1},{1,0},{2,3},{3,2},{4,5},{5,4},{6,7},{7,6},{8,9},{9,8},{10,11... | collective-permute-start | bytes 98312 | tf_op jit(solution)/shard_map/ppermute | solution.py:553
  19.3 2.8 %collective-permute-start.5 = (f32[64,128]{1,0:T(8,128)S(1)}, f32[64,128]{1,0:T(8,128)S(1)}, u32[]{:S(2)}, u32[]{:S(2)}) collective-permute-start(f32[64,128]{1,0:T(8,128)S(1)} %get-tuple-element.34), channel_id=1, source_target_pairs={{0,2},{1,3},{2,0},{3,1},{4,6},{5,7},{6,4},{7,5},{8,10},{9,11},{10,... | collective-permute-start | bytes 98312 | tf_op jit(solution)/shard_map/ppermute | solution.py:553
  20.5 3.3 %collective-permute-start.6 = (f32[64,128]{1,0:T(8,128)S(1)}, f32[64,128]{1,0:T(8,128)S(1)}, u32[]{:S(2)}, u32[]{:S(2)}) collective-permute-start(f32[64,128]{1,0:T(8,128)S(1)} %get-tuple-element.35), channel_id=1, source_target_pairs={{0,3},{1,2},{2,1},{3,0},{4,7},{5,6},{6,5},{7,4},{8,11},{9,10},{10,... | collective-permute-start | bytes 98312 | tf_op jit(solution)/shard_map/ppermute | solution.py:553
  24.1 4.6 %collective-permute-start.9 = (f32[16,512]{1,0:T(8,128)S(1)}, f32[16,512]{1,0:T(8,128)S(1)}, u32[]{:S(2)}, u32[]{:S(2)}) collective-permute-start(f32[16,512]{1,0:T(8,128)S(1)} %get-tuple-element.38), channel_id=1, source_target_pairs={{0,24},{8,16},{16,8},{24,0},{1,25},{9,17},{17,9},{25,1},{2,26},{10... | collective-permute-start | bytes 98312 | tf_op jit(solution)/shard_map/ppermute | solution.py:161
  25.3 3.8 %collective-permute-start.8 = (f32[16,512]{1,0:T(8,128)S(1)}, f32[16,512]{1,0:T(8,128)S(1)}, u32[]{:S(2)}, u32[]{:S(2)}) collective-permute-start(f32[16,512]{1,0:T(8,128)S(1)} %get-tuple-element.38), channel_id=1, source_target_pairs={{0,16},{8,24},{16,0},{24,8},{1,17},{9,25},{17,1},{25,9},{2,18},{10... | collective-permute-start | bytes 98312 | tf_op jit(solution)/shard_map/ppermute | solution.py:161
  25.9 4.1 %collective-permute-start.7 = (f32[16,512]{1,0:T(8,128)S(1)}, f32[16,512]{1,0:T(8,128)S(1)}, u32[]{:S(2)}, u32[]{:S(2)}) collective-permute-start(f32[16,512]{1,0:T(8,128)S(1)} %get-tuple-element.38), channel_id=1, source_target_pairs={{0,8},{8,0},{16,24},{24,16},{1,9},{9,1},{17,25},{25,17},{2,10},{10... | collective-permute-start | bytes 98312 | tf_op jit(solution)/shard_map/ppermute | solution.py:161
  30.9 6.8 %copy-start = (f32[2,768,128]{2,1,0:T(8,128)S(1)}, f32[2,768,128]{2,1,0:T(8,128)}, u32[]{:S(2)}) copy-start(f32[2,768,128]{2,1,0:T(8,128)} %constant.26.clone.refs_11_) | copy-start | bytes 2359300
  30.9 3.5 %collective-permute-start.10 = (f32[4,48,128]{2,1,0:T(8,128)S(1)}, f32[4,48,128]{2,1,0:T(8,128)S(1)}, u32[]{:S(2)}, u32[]{:S(2)}) collective-permute-start(f32[4,48,128]{2,1,0:T(8,128)S(1)} %get-tuple-element.41.refs_5_), channel_id=1, source_target_pairs={{0,2},{1,3},{2,0},{3,1},{4,6},{5,7},{6,4},{7,5},{8,10},{9,11},{10,... | collective-permute-start | bytes 294920 | tf_op jit(solution)/shard_map/ppermute | solution.py:168
  31.6 6.2 %copy-start.4 = (f32[4,144,48]{2,1,0:T(8,128)S(1)}, f32[4,144,48]{2,1,0:T(8,128)}, u32[]{:S(2)}) copy-start(f32[4,144,48]{2,1,0:T(8,128)} %constant.25.clone.refs_10_) | copy-start | bytes 331780
  31.6 6.2 %copy-start.5 = (f32[128,96]{1,0:T(8,128)S(1)}, f32[128,96]{1,0:T(8,128)}, u32[]{:S(2)}) copy-start(f32[128,96]{1,0:T(8,128)} %constant.29.clone.refs_9_) | copy-start | bytes 147460
  32.4 4.4 %collective-permute-start.11 = (f32[4,48,128]{2,1,0:T(8,128)S(1)}, f32[4,48,128]{2,1,0:T(8,128)S(1)}, u32[]{:S(2)}, u32[]{:S(2)}) collective-permute-start(f32[4,48,128]{2,1,0:T(8,128)S(1)} %get-tuple-element.41.refs_5_), channel_id=1, source_target_pairs={{0,1},{1,0},{2,3},{3,2},{4,5},{5,4},{6,7},{7,6},{8,9},{9,8},{10,11... | collective-permute-start | bytes 294920 | tf_op jit(solution)/shard_map/ppermute | solution.py:168
  34.4 3.3 %collective-permute-start.12 = (f32[4,48,128]{2,1,0:T(8,128)S(1)}, f32[4,48,128]{2,1,0:T(8,128)S(1)}, u32[]{:S(2)}, u32[]{:S(2)}) collective-permute-start(f32[4,48,128]{2,1,0:T(8,128)S(1)} %collective-permute-done.10.refs_7_), channel_id=1, source_target_pairs={{0,1},{1,0},{2,3},{3,2},{4,5},{5,4},{6,7},{7,6},{8,9},{9,8},{10,11... | collective-permute-start | bytes 294920 | tf_op jit(solution)/shard_map/ppermute | solution.py:168

commit v5 on v4

--- a/solution.py
+++ b/solution.py
@@ -50,6 +50,9 @@
                 inner = following.functionals[i]
                 own = np.concatenate([own, inner @ self.even, inner @ self.block(i, i)])
             self.functionals.append(own)
+        built = [self.build(j) for j in range(count)]
+        self.needs = [needs for needs, _ in built]
+        self.tables = [tables for _, tables in built]
 
     def rows(self, i):
         return slice(i * self.n, (i + 1) * self.n)
@@ -71,50 +74,66 @@
     def side(self, i, j):
         return 2 if j > i else 3
 
-    def tables(self, j):
-        own, kept, many, n, fine = self.n, self.kept, self.functional_count, self.n, self.fine
+    def through_even(self, f):
+        return 4 + f if f else 0
+
+    def build(self, j):
+        n, fine, many, end = self.n, self.fine, self.functional_count, self.count - 1
+        targets = self.following.needs[j] if self.following else []
         others = [j ^ k for k in range(1, self.count)]
-        shape = (own + kept * len(others), fine + many * len(others))
-        product, even = np.zeros(shape), np.zeros(shape)
-        at = {i: fine + many * place for place, i in enumerate(others)}
+        at = lambda i, f: fine + many * ((i ^ j) - 1) + f
+        product = np.zeros((n + len(targets), fine + many * len(others)))
+        even, used = np.zeros_like(product), np.zeros(product.shape[1], bool)
+        used[:fine] = True
         product[:n, :fine] = self.block(j, j)
         even[:n, :fine] = self.even
         first, last = [self.first[self.rows(j)]], [self.last[self.rows(j)]]
         for i in others:
-            product[:n, at[i] + self.side(j, i)] = self.reach(j, i)
-        for place, i in enumerate(others):
-            if not kept:
-                break
-            inner = self.following.functionals[i]
-            target = n + kept * place + np.arange(kept)
-            product[target, :fine] = inner @ self.block(i, j)
-            product[target, at[i] + 4 + kept + np.arange(kept)] = 1.0
-            even[target, at[i] + 4 + np.arange(kept)] = 1.0
+            product[:n, at(i, self.side(j, i))] = self.reach(j, i)
+            used[at(i, self.side(j, i))] = True
+        for row, (i, f) in enumerate(targets, n):
+            inner = self.following.functionals[i][f]
+            product[row, :fine] = inner @ self.block(i, j)
+            product[row, at(i, 4 + self.kept + f)] = 1.0
+            even[row, at(i, self.through_even(f))] = 1.0
+            used[at(i, 4 + self.kept + f)] = used[at(i, self.through_even(f))] = True
             for other in others:
                 if other != i:
-                    product[target, at[other] + self.side(i, other)] = inner @ self.reach(i, other)
-            first.append(inner @ self.first[self.rows(i)])
-            last.append(inner @ self.last[self.rows(i)])
+                    product[row, at(other, self.side(i, other))] = inner @ self.reach(i, other)
+                    used[at(other, self.side(i, other))] = True
+            first.append([inner @ self.first[self.rows(i)]])
+            last.append([inner @ self.last[self.rows(i)]])
         around = even.copy()
-        around[:, 0 if j == 0 else at[0]] += np.concatenate(first)
-        end = self.count - 1
-        around[:, fine - 2 if j == end else at[end] + 1] += np.concatenate(last)
-        return product, even, around
-
-    def next_first(self, j, stride):
-        if j == self.count - 1:
-            return self.fine - 2
-        return self.fine + stride * ((j ^ (j + 1)) - 1)
-
-
-def interpolation(level, j, inputs, stride, coarse):
+        from_first, from_last = 0 if j == 0 else at(0, 0), fine - 2 if j == end else at(end, 1)
+        around[:, from_first] += np.concatenate(first)
+        around[:, from_last] += np.concatenate(last)
+        used[from_first] = used[from_last] = True
+        if j < end:
+            used[at(j + 1, 0)] = True
+        needs = [(j ^ (1 + place // many), place % many) for place in np.flatnonzero(used[fine:])]
+        return needs, (product[:, used], even[:, used], around[:, used])
+
+    def sent(self, i, k):
+        return [f for block, f in self.needs[i ^ k] if block == i]
+
+    def most_sent(self):
+        return max([len(self.sent(i, k)) for i in range(self.count) for k in range(1, self.count)] + [1])
+
+    def most_needed(self):
+        return max(len(needs) for needs in self.needs)
+
+    def next_first(self, j, own, fallback):
+        return fallback if j == self.count - 1 else own + self.needs[j].index((j + 1, 0))
+
+
+def interpolation(level, j, inputs, coarse=False):
     table = np.zeros((level.fine, inputs))
     if coarse:
         places = list(range(level.n))
-        last = level.n - 1 if j == level.count - 1 else level.n + stride * ((j ^ (j + 1)) - 1)
+        last = level.following.next_first(j, level.n, level.n - 1)
     else:
         places = [2 * c for c in range(level.n)]
-        last = level.next_first(j, stride)
+        last = level.next_first(j, level.fine, level.fine - 2)
     places.append(last)
     for c in range(level.n):
         table[2 * c, places[c]] = 1.0
@@ -156,15 +175,15 @@
     )(*(pltpu.with_memory_space_constraint(a, pltpu.HBM) if i in left else a for i, a in enumerate(arrays)))
 
 
-def swapped(value, axis):
+def swapped(values, axis):
     count = lax.axis_size(axis)
-    return [lax.ppermute(value, axis, [(i, i ^ k) for i in range(count)]) for k in range(1, count)]
+    return [lax.ppermute(v, axis, [(i, i ^ k) for i in range(count)]) for k, v in enumerate(values, 1)]
 
 
 def gathered(value, axis, beside):
     count = lax.axis_size(axis)
     if count != 4:
-        return swapped(value, axis), beside
+        return swapped([value] * (count - 1), axis), beside
     by = lambda k, what: lax.ppermute(what, axis, [(i, i ^ k) for i in range(count)])
     far, beside = lax.optimization_barrier((by(2, value), beside))
     return [by(1, value), far, by(1, far)], beside
@@ -194,56 +213,67 @@
     xthree = xtwo.following
     zone = Level(nz, dz, None)
 
-    ky, ky2, ky3 = yone.kept, ytwo.kept, ythree.kept
-    kya = round_up(ky + 3, 16)
-    kys = round_up(ky + 2, 16)
-    wide1 = yone.n + ky * (dy - 1)
-    wide2 = ytwo.n + ky2 * (dy - 1)
+    points_a = lambda fs: [f for f in fs if f in (2, 3) or f >= 4 + yone.kept]
+    points_s = lambda fs: [f for f in fs if f not in (2, 3) and f < 4 + yone.kept]
+    pairs_y = [(i, k) for i in range(dy) for k in range(1, dy)]
+    sa = max([len(points_a(yone.sent(i, k))) for i, k in pairs_y] + [0]) + 1
+    ss = max([len(points_s(yone.sent(i, k))) for i, k in pairs_y] + [1])
+    per_row = (lz * lx) // ((lz // 2) * (lx // 2))
+    rowsy = round_up(sa + -(-ss // per_row), 8)
+    sa8, ss8 = round_up(sa, 8), round_up(ss, 8)
+    wide1 = yone.n + ytwo.most_needed()
+    wide2 = ytwo.n + ythree.most_needed()
     wide = packed = round_up(max(wide1 + 1, 3 * wide2, wide2 + wide1), 128)
-    kx = round_up(xtwo.functional_count, 8)
+    kx = round_up(xtwo.most_sent(), 8)
     rowsx = xtwo.fine + kx * (dx - 1)
-    tall = round_up(xtwo.n + xtwo.kept * (dx - 1), 8)
-
-    fya = np.zeros((dy, kya, ly))
-    fys = np.zeros((dy, kys, ly))
+    tall = round_up(max(xtwo.n + xthree.most_needed(), xone.n // 2 + 1), 8)
+
+    others_y = max(dy - 1, 1)
+    fya = np.zeros((dy, others_y * sa8, ly))
+    fys = np.zeros((dy, others_y * ss8, ly))
     ta = np.zeros((dy, ly, wide))
-    wa = np.zeros((dy, max(dy - 1, 1) * kya, wide))
+    wa = np.zeros((dy, others_y * rowsy, wide))
     tsm = np.zeros((dy, ly, 2 * wide))
-    wsm = np.zeros((dy, max(dy - 1, 1) * kys, 2 * wide))
+    wsm = np.zeros((dy, others_y * ss8, 2 * wide))
     for j in range(dy):
-        pick_a = [2, 3] + list(range(4 + ky, 4 + 2 * ky)) + [0]
-        pick_s = [0, 1] + list(range(4, 4 + ky))
-        fya[j, : len(pick_a)] = yone.functionals[j][pick_a]
-        fys[j, : len(pick_s)] = yone.functionals[j][pick_s]
-        product, even, around = yone.tables(j)
+        product, even, around = yone.tables[j]
         used = product.shape[0]
-        for source, to, across, pick, k in (
-            (product, ta[j], wa[j], pick_a[:-1], kya),
-            (even, tsm[j][:, :wide], wsm[j][:, :wide], pick_s, kys),
-            (around, tsm[j][:, wide:], wsm[j][:, wide:], pick_s, kys),
-        ):
-            to[:, :used] = source[:, :ly].T
-            for place in range(dy - 1):
-                begin = ly + yone.functional_count * place
-                part = source[:, begin : begin + yone.functional_count].T[pick]
-                across[k * place : k * place + len(pick), :used] = part
+        ta[j, :, :used] = product[:, :ly].T
+        tsm[j, :, :used] = even[:, :ly].T
+        tsm[j, :, wide : wide + used] = around[:, :ly].T
+        for k in range(1, dy):
+            mine = yone.sent(j, k)
+            fya[j, (k - 1) * sa8 :][: len(points_a(mine))] = yone.functionals[j][points_a(mine)]
+            fya[j, (k - 1) * sa8 + sa - 1] = yone.functionals[j][0]
+            fys[j, (k - 1) * ss8 :][: len(points_s(mine))] = yone.functionals[j][points_s(mine)]
+            came = yone.sent(j ^ k, k)
+            for f in came:
+                column = ly + yone.needs[j].index((j ^ k, f))
+                if f in points_a(came):
+                    wa[j, (k - 1) * rowsy + points_a(came).index(f), :used] = product[:, column]
+                else:
+                    row = (k - 1) * ss8 + points_s(came).index(f)
+                    wsm[j, row, :used] = even[:, column]
+                    wsm[j, row, wide : wide + used] = around[:, column]
         if j == dy - 1:
             ta[j, ly - 2, wide - 1] = 0.5
         else:
-            wa[j, kya * ((j ^ (j + 1)) - 1) + len(pick_a) - 1, wide - 1] = 0.5
-
+            wa[j, rowsy * ((j ^ (j + 1)) - 1) + sa - 1, wide - 1] = 0.5
+
+    ext = round_up(max(dx - 1, 1), 8)
     fx = np.zeros((dx, lx, 8))
-    txa = np.zeros((dx, xone.n, lx + 8 * (dx - 1)))
-    txm = np.zeros((dx, xone.n, xone.n + 8 * (dx - 1)))
+    txa = np.zeros((dx, xone.n, lx + ext))
+    txm = np.zeros((dx, xone.n, xone.n + ext))
     for j in range(dx):
         fx[j, :, :2] = xone.functionals[j][2:4].T
-        product, even, around = xone.tables(j)
+        product, even, around = xone.tables[j]
         txa[j, :, :lx] = product[:, :lx]
         txm[j, :, : xone.n] = around[:, :lx:2]
-        for place in range(dx - 1):
-            txa[j, :, lx + 8 * place : lx + 8 * place + 2] = product[:, lx + 4 * place + 2 : lx + 4 * place + 4]
-            begin = xone.n + 8 * place
-            txm[j, :, begin + 2 : begin + 4] = around[:, lx + 4 * place : lx + 4 * place + 2]
+        for column, (i, f) in enumerate(xone.needs[j], lx):
+            if f in (2, 3):
+                txa[j, :, lx + (i ^ j) - 1] = product[:, column]
+            else:
+                txm[j, :, xone.n + (i ^ j) - 1] += around[:, column] * ((f == 0 and i == 0) or (f == 1 and i == dx - 1))
 
     zn = zone.n
     zs = np.zeros((dz, 2 * lz + 2 + zn * (lz + dz + 1)))
@@ -260,26 +290,26 @@
     at_first = at_reach + zn * (dz - 1)
     at_last = at_first + zn
 
-    f2x = np.stack([padded(xtwo.functionals[j], kx, xtwo.fine) for j in range(dx)])
+    f2x = np.zeros((dx, max(dx - 1, 1) * kx, xtwo.fine))
     tx2 = np.zeros((dx, 3 * tall, rowsx))
     qx2 = np.zeros((dx, xtwo.fine, rowsx))
     tx3 = np.zeros((dx, 3 * xthree.n, tall))
     qx3 = np.zeros((dx, xthree.fine, tall))
     px3 = np.zeros((dx, xtwo.fine, tall))
     for j in range(dx):
-        for c, table in enumerate(xtwo.tables(j)):
-            tx2[j, c * tall : c * tall + table.shape[0], : xtwo.fine] = table[:, : xtwo.fine]
-            for place in range(dx - 1):
-                begin = xtwo.fine + xtwo.functional_count * place
-                target = xtwo.fine + kx * place
-                tx2[j, c * tall : c * tall + table.shape[0], target : target + xtwo.functional_count] = table[
-                    :, begin : begin + xtwo.functional_count
-                ]
-        qx2[j] = interpolation(xtwo, j, rowsx, kx, False)
-        for c, table in enumerate(xthree.tables(j)):
+        columns = list(range(xtwo.fine))
+        for i, f in xtwo.needs[j]:
+            columns.append(xtwo.fine + kx * ((i ^ j) - 1) + xtwo.sent(i, i ^ j).index(f))
+        for c, table in enumerate(xtwo.tables[j]):
+            tx2[j, c * tall : c * tall + table.shape[0], columns] = table.T
+        qx2[j][:, columns] = interpolation(xtwo, j, len(columns))
+        for k in range(1, dx):
+            mine = xtwo.sent(j, k)
+            f2x[j, (k - 1) * kx :][: len(mine)] = xtwo.functionals[j][mine]
+        for c, table in enumerate(xthree.tables[j]):
             tx3[j, c * xthree.n : (c + 1) * xthree.n, : table.shape[1]] = table
-        qx3[j] = interpolation(xthree, j, tall, xthree.functional_count, False)
-        px3[j] = interpolation(xtwo, j, tall, xtwo.kept, True)
+        qx3[j] = interpolation(xthree, j, tall)
+        px3[j] = interpolation(xtwo, j, tall, True)
 
     ty2 = np.zeros((dy, 3 * wide, packed))
     qy2 = np.zeros((dy, wide, round_up(ytwo.fine, 128)))
@@ -289,14 +319,14 @@
     px1 = np.zeros((lx, 2 * tall))
     py1 = np.zeros((dy, packed, ly))
     for j in range(dy):
-        for c, table in enumerate(ytwo.tables(j)):
-            ty2[j, c * wide : c * wide + table.shape[1], c * wide2 : c * wide2 + wide2] = table.T
-        qy2[j, :, : ytwo.fine] = interpolation(ytwo, j, wide, ky, False).T
-        for c, table in enumerate(ythree.tables(j)):
+        for c, table in enumerate(ytwo.tables[j]):
+            ty2[j, c * wide : c * wide + table.shape[1], c * wide2 : c * wide2 + table.shape[0]] = table.T
+        qy2[j, :, : ytwo.fine] = interpolation(ytwo, j, wide).T
+        for c, table in enumerate(ythree.tables[j]):
             ty3[j, c * packed : c * packed + table.shape[1], : ythree.n] = (-1.0 if c == 2 else 1.0) * table.T
-        qy3[j, :, : ythree.fine] = interpolation(ythree, j, packed, ky2, False).T
-        py1[j, wide2:] = interpolation(yone, j, packed - wide2, ky, True).T
-        py3[j, wide2:, : ytwo.fine] = interpolation(ytwo, j, packed - wide2, ky2, True).T
+        qy3[j, :, : ythree.fine] = interpolation(ythree, j, packed).T
+        py1[j, wide2:] = interpolation(yone, j, packed - wide2, True).T
+        py3[j, wide2:, : ytwo.fine] = interpolation(ytwo, j, packed - wide2, True).T
     for c in range(xone.n):
         begin = c if c < xtwo.n else tall + c - xtwo.n
         px1[2 * c, begin] = 1.0
@@ -329,90 +359,120 @@
     tables_y3, at_y3 = stacked(ty3, qy3, py3, py1)
     hz, hx1 = lz // 2, lx // 2
 
-    def y_messages(u_hbm, table_hbm, ty_hbm, fx_hbm, out_ref, u_ref, ty_ref, fx_ref, table, sems):
+    def y_messages(u_hbm, table_hbm, ty_hbm, fx_hbm, u_ref, ty_ref, fx_ref, *refs):
+        outs, (table, sems) = refs[:-2], refs[-2:]
         j = lax.axis_index("gy")
         nt = ((1,), (1,))
-        copies = [pltpu.make_async_copy(table_hbm.at[j], table, sems.at[0])]
-        copies.append(pltpu.make_async_copy(u_hbm, u_ref, sems.at[1]))
-        copies.append(pltpu.make_async_copy(ty_hbm.at[j], ty_ref, sems.at[2]))
-        copies.append(pltpu.make_async_copy(fx_hbm.at[lax.axis_index("gx")], fx_ref, sems.at[3]))
+        copies = [
+            pltpu.make_async_copy(table_hbm.at[j], table, sems.at[0]),
+            pltpu.make_async_copy(u_hbm, u_ref, sems.at[1]),
+            pltpu.make_async_copy(ty_hbm.at[j], ty_ref, sems.at[2]),
+            pltpu.make_async_copy(fx_hbm.at[lax.axis_index("gx")], fx_ref, sems.at[3]),
+        ]
         for copy in copies:
             copy.start()
         for copy in copies[:2]:
             copy.wait()
-        out_ref[:kya, : lz * lx] = dot(table[:kya], u_ref[...].reshape(lz * lx, ly), nt)
+        lines = dot(table[: others_y * sa8], u_ref[...].reshape(lz * lx, ly), nt)
         even = jnp.concatenate([u_ref[2 * z, pl.ds(0, hx1, stride=2), :] for z in range(hz)], axis=0)
-        out_ref[:kys, lz * lx :] = dot(table[kya : kya + kys], even, nt)
+        points = dot(table[others_y * sa8 :], even, nt)
+        for k, out in enumerate(outs):
+            out[: min(sa8, rowsy)] = lines[k * sa8 : k * sa8 + min(sa8, rowsy)]
+            if rowsy > sa8:
+                out[sa8:] = jnp.zeros_like(out[sa8:])
+            for f in range(ss):
+                begin = hz * hx1 * (f % per_row)
+                row = sa + f // per_row
+                out[row : row + 1, begin : begin + hz * hx1] = points[k * ss8 + f : k * ss8 + f + 1]
         for copy in copies[2:]:
             copy.wait()
 
     def y_apply(*refs):
         u_ref, came = refs[0], refs[1:dy]
-        ty_ref, fx_ref, ta_out, tsm_out, iy_out, xm_out = refs[dy:]
+        ty_ref, fx_ref, ta_out, tsm_out, iy_out = refs[dy : dy + 5]
+        xm_outs, points = refs[dy + 5 : -1], refs[-1]
+        jx = lax.axis_index("gx")
         tn = ((0,), (0,))
         ta_all = dot(u_ref[...].reshape(lz * lx, ly), ty_ref[:ly, :wide])
         even = jnp.concatenate([u_ref[2 * z, pl.ds(0, hx1, stride=2), :] for z in range(hz)], axis=0)
         tsm_all = dot(even, ty_ref[:ly, wide:])
         for k, ref in enumerate(came):
-            begin = ly + kya * k
-            ta_all += dot(ref[:kya, : lz * lx], ty_ref[begin : begin + kya, :wide], tn)
-            begin = ly + kya * (dy - 1) + kys * k
-            tsm_all += dot(ref[:kys, lz * lx :], ty_ref[begin : begin + kys, wide:], tn)
+            begin = ly + rowsy * k
+            ta_all += dot(ref[...], ty_ref[begin : begin + rowsy, :wide], tn)
+            points[...] = jnp.zeros_like(points)
+            for f in range(ss):
+                begin = hz * hx1 * (f % per_row)
+                row = sa + f // per_row
+                points[f : f + 1] = ref[row : row + 1, begin : begin + hz * hx1]
+            begin = ly + rowsy * (dy - 1) + ss8 * k
+            tsm_all += dot(points[...], ty_ref[begin : begin + ss8, wide:], tn)
         ta_out[...] = ta_all
         tsm_out[...] = tsm_all
-        xm_out[...] = jnp.zeros_like(xm_out)
         lane = iota((lx, ly), 1)
         weights = [jnp.broadcast_to(fx_ref[:, c : c + 1], (lx, wide)) for c in range(2)]
-        xm_out[0, 5:6, :wide] = tsm_all[0:1, :wide]
+        for out in xm_outs:
+            out[lz + 2 * hz :] = jnp.zeros_like(out[lz + 2 * hz :])
+            out[lz + 2 * hz : lz + 2 * hz + 1, :wide] = tsm_all[0:1, :wide]
         for z in range(lz):
             part = ta_all[z * lx : (z + 1) * lx]
-            for c in range(2):
-                xm_out[z, c : c + 1, :wide] = jnp.sum(part * weights[c], axis=0, keepdims=True)
+            v, w = (jnp.sum(part * weight, axis=0, keepdims=True) for weight in weights)
+            for k, out in enumerate(xm_outs):
+                out[z : z + 1, :wide] = jnp.where((jx ^ (k + 1)) < jx, v, w)
             if z % 2 == 0:
                 half = z // 2
                 tm = tsm_all[half * hx1 : (half + 1) * hx1, wide:]
-                xm_out[z, 2:3, :wide] = tm[0:1]
-                xm_out[z, 3:4, :wide] = tm[hx1 - 1 : hx1]
                 u = u_ref[z]
                 before, after = pltpu.roll(u, 1, 1), pltpu.roll(u, ly - 1, 1)
                 middle = 0.5 * (before + after)
                 edge = 0.5 * before + jnp.broadcast_to(part[:, wide - 1 : wide], (lx, ly))
                 iy = jnp.where(lane == ly - 1, edge, jnp.where(lane % 2 == 1, middle, u))
                 iy_out[half] = iy
-                xm_out[z, 4:5, :ly] = iy[0:1]
+                for out in xm_outs:
+                    out[lz + half : lz + half + 1, :wide] = jnp.where(jx == 0, tm[0:1], tm[hx1 - 1 : hx1])
+                    out[lz + hz + half : lz + hz + half + 1, :ly] = iy[0:1]
 
     def x_apply(*refs):
-        ta_ref, tsm_ref, iy_ref, own_ref = refs[:4]
-        came = refs[4 : 3 + dx]
-        tx_ref, ixy_out, zc_out, u1_out = refs[3 + dx : 7 + dx]
-        planes_out = refs[7 + dx :]
+        ta_ref, tsm_ref, iy_ref = refs[:3]
+        came = refs[3 : 2 + dx][::-1]
+        tx_ref, ixy_out, zc_out, u1_out = refs[2 + dx : 6 + dx]
+        planes_out, rest = refs[6 + dx : -1], refs[-1]
         jx, jz = lax.axis_index("gx"), lax.axis_index("gz")
         xa, xm, diff = [], [], []
+
         def from_next(own, rows):
-            for k, rest in enumerate(rows):
-                own = jnp.where((jx ^ (k + 1)) == jx + 1, rest, own)
+            for k, other in enumerate(rows):
+                own = jnp.where((jx ^ (k + 1)) == jx + 1, other, own)
             return own
 
+        rest[...] = jnp.zeros_like(rest)
+        for k, r in enumerate(came):
+            for z in range(lz):
+                rest[z, k : k + 1, :wide] = r[z : z + 1, :wide]
+            for half in range(hz):
+                rest[half, k : k + 1, wide:] = r[lz + half : lz + half + 1, :wide]
         for z in range(0, lz, 2):
             pair = jnp.concatenate([ta_ref[z * lx : (z + 1) * lx, :], ta_ref[(z + 1) * lx : (z + 2) * lx, :]], axis=1)
-            rest = [jnp.concatenate([r[z, :, :wide], r[z + 1, :, :wide]], axis=1) for r in came]
-            both = dot(tx_ref[jx, : xone.n], jnp.concatenate([pair] + rest, axis=0))
+            more = jnp.concatenate([rest[z, :, :wide], rest[z + 1, :, :wide]], axis=1)
+            both = dot(tx_ref[jx, : xone.n], jnp.concatenate([pair, more], axis=0))
             xa += [both[:, :wide], both[:, wide:]]
         zc_out[...] = jnp.zeros_like(zc_out)
         zc_out[:hx1] = tsm_ref[:hx1, :wide]
-        zc_out[hx1 : hx1 + 1] = from_next(tsm_ref[hx1 - 1 : hx1, :wide], [r[0, 5:6, :wide] for r in came])
+        begin = lz + 2 * hz
+        zc_out[hx1 : hx1 + 1] = from_next(tsm_ref[hx1 - 1 : hx1, :wide], [r[begin : begin + 1, :wide] for r in came])
         row = iota((lx, ly), 0)
+        for half in range(0, hz, 2):
+            pair = jnp.concatenate([tsm_ref[h * hx1 : (h + 1) * hx1, wide:] for h in (half, half + 1)], axis=1)
+            more = jnp.concatenate([rest[half, :, wide:], rest[half + 1, :, wide:]], axis=1)
+            both = dot(tx_ref[jx, xone.n :, : xone.n + ext], jnp.concatenate([pair, more], axis=0))
+            xm += [both[:, :wide], both[:, wide:]]
         for half in range(hz):
-            part = tsm_ref[half * hx1 : (half + 1) * hx1, :]
-            stacked = jnp.concatenate([part[:, wide:]] + [r[2 * half, :, :wide] for r in came], axis=0)
-            xm.append(dot(tx_ref[jx, xone.n :, : xone.n + 8 * (dx - 1)], stacked))
-            diff.append(part[:, :wide] - xm[-1])
+            diff.append(tsm_ref[half * hx1 : (half + 1) * hx1, :wide] - xm[half])
             iy = iy_ref[half]
-            halo = from_next(iy[lx - 2 : lx - 1], [r[2 * half, 4:5, :ly] for r in came])
+            begin = lz + hz + half
+            halo = from_next(iy[lx - 2 : lx - 1], [r[begin : begin + 1, :ly] for r in came])
             before, after = pltpu.roll(iy, 1, 0), pltpu.roll(iy, lx - 1, 0)
             after = jnp.where(row == lx - 1, jnp.broadcast_to(halo, (lx, ly)), after)
-            ixy = jnp.where(row % 2 == 1, 0.5 * (before + after), iy)
-            ixy_out[half] = ixy
+            ixy_out[half] = jnp.where(row % 2 == 1, 0.5 * (before + after), iy)
         scalar = lambda place: chosen_by(zs[:, place], jz)
         for zc in range(zn):
             total = diff[zc] - scalar(at_first + zc) * xm[0] - scalar(at_last + zc) * xm[hz - 1]
@@ -428,15 +488,19 @@
             out[...] = jnp.where((jz ^ (k + 1)) > jz, w, v)
 
     def z_apply(*refs):
-        part_ref, came = refs[0], refs[1:dz]
-        f2x_ref, u1_out, xt_out = refs[dz:]
+        part_ref, came = refs[0], refs[1:dz][::-1]
+        f2x_ref, u1_out, xt_outs = refs[dz], refs[dz + 1], refs[dz + 2 :]
         jx, jz = lax.axis_index("gx"), lax.axis_index("gz")
+        totals = []
         for zc in range(zn):
             total = part_ref[zc]
             for k, r in enumerate(came):
                 total += chosen_by(zs[:, at_reach + k * zn + zc], jz) * r[...]
             u1_out[zc] = total
-            xt_out[:, zc * wide : (zc + 1) * wide] = dot(f2x_ref[jx], total)
+            totals.append(total)
+        sent = dot(f2x_ref[jx], jnp.concatenate(totals, axis=1))
+        for k, out in enumerate(xt_outs):
+            out[...] = sent[k * kx : (k + 1) * kx]
 
     def fine_coefficients(u_ref, ixy_ref, out_ref):
         for half in range(hz):
@@ -446,7 +510,7 @@
                 out_ref[2 * half + 1] = u_ref[2 * half + 1] - 0.5 * (here + ixy_ref[half + 1])
 
     def second_apply(*refs):
-        u1_ref, zc_ref, came = refs[0], refs[1], refs[2 : dx + 1]
+        u1_ref, zc_ref, came = refs[0], refs[1], refs[2 : dx + 1][::-1]
         tx2_ref, ty2_ref, zt_out, i2_out = refs[dx + 1 :]
         jx, jy = lax.axis_index("gx"), lax.axis_index("gy")
         own = jnp.concatenate([u1_ref[z] for z in range(lz2)], axis=1)
@@ -529,35 +593,39 @@
         for copy in copies:
             copy.wait()
 
-    ym, u, own_ty, own_fx = kernel_call(
+    u, own_ty, own_fx, *ym = kernel_call(
         y_messages,
-        [(max(kya, kys), lz * lx + hz * hx1), (lz, lx, ly), tables_y.shape[1:], fx.shape[1:]],
+        [(lz, lx, ly), tables_y.shape[1:], fx.shape[1:]] + [(rowsy, lz * lx)] * (dy - 1),
         [field, messages_y, tables_y, to32(fx)],
-        scratch=[pltpu.VMEM((kya + kys, ly), jnp.float32), pltpu.SemaphoreType.DMA((4,))],
+        scratch=[pltpu.VMEM(messages_y.shape[1:], jnp.float32), pltpu.SemaphoreType.DMA((4,))],
         left=(0, 1, 2, 3),
     )
     ycame = swapped(ym, "gy")
-    xw = max(wide, ly)
-    ta_v, tsm_v, iy, xm = kernel_call(
+    ta_v, tsm_v, iy, *xm = kernel_call(
         y_apply,
-        [(lz * lx, wide), (hz * hx1, 2 * wide), (hz, lx, ly), (lz, 8, xw)],
+        [(lz * lx, wide), (hz * hx1, 2 * wide), (hz, lx, ly)]
+        + [(round_up(lz + 2 * hz + 1, 8), max(wide, ly))] * (dx - 1),
         [u, *ycame, own_ty, own_fx],
+        scratch=[pltpu.VMEM((ss8, hz * hx1), jnp.float32)],
     )
     xcame = swapped(xm, "gx")
     ixy, zc, u1_part, *planes = kernel_call(
         x_apply,
         [(hz, lx, ly), (xtwo.n + tall, wide), (zn, xone.n, wide)] + [(xone.n, wide)] * (dz - 1),
-        [ta_v, tsm_v, iy, xm, *xcame, tables_x],
+        [ta_v, tsm_v, iy, *xcame[::-1], tables_x],
+        scratch=[pltpu.VMEM((lz, ext, 2 * wide), jnp.float32)],
     )
-    zcame = [
-        lax.ppermute(plane, "gz", [(i, i ^ (k + 1)) for i in range(dz)]) for k, plane in enumerate(planes)
-    ]
-    u1, xt = kernel_call(z_apply, [(zn, xone.n, wide), (kx, zn * wide)], [u1_part, *zcame, to32(f2x)])
+    zcame = swapped(planes, "gz")
+    u1, *xt = kernel_call(
+        z_apply,
+        [(zn, xone.n, wide)] + [(kx, zn * wide)] * (dx - 1),
+        [u1_part, *zcame[::-1], to32(f2x)],
+    )
     xtcame = swapped(xt, "gx")
     zmsg, i2 = kernel_call(
         second_apply,
         [(lz2, tall, packed), (lz2 // 2, xtwo.fine, round_up(ytwo.fine, 128))],
-        [u1, zc, *xtcame, tables_x2, tables_y2],
+        [u1, zc, *xtcame[::-1], tables_x2, tables_y2],
     )
     (fine,) = kernel_call(fine_coefficients, [(lz, lx, ly)], [u, ixy])
     ztcame, fine = gathered(zmsg, "gz", fine)

time: 40.7 us -> 38.7 us (0.951)
  waiting for transfers between devices: 12.1 us -> 9.53 us
  starting transfers between devices: 18.8 us -> 19.5 us
    ppermute x10, waiting for transfers between devices: 10.7 us -> 8.61 us  [swapped(): lax.ppermute(v, axis, [(i, i ^ k) for i in range(count)])]
    ppermute x3, waiting for transfers between devices: 1.48 us -> 0.93 us  [gathered(): lax.ppermute(what, axis, [(i, i ^ k) for i in range(count)])]
    ppermute x3, starting transfers between devices: 4.51 us -> 4.98 us  [gathered(): lax.ppermute(what, axis, [(i, i ^ k) for i in range(count)])]
  transfers between devices with their start and end apart: 13 -> 13, of which waited for: 10 -> 9; matrix products, arithmetic and copies ran while one was open for 0% -> 0% of each run, Pallas kernels for 2% -> 2%
where the time goes in v5:
time: 38.7 us; the launch traced here: 38.2 us
  starting transfers between devices  19.5 us (50%)
  waiting for transfers between devices  9.53 us (25%)
  Pallas kernels  8.42 us (22%)
  between operations  0.71 us (2%)
    ppermute x10, starting transfers between devices, swapped(): lax.ppermute(v, axis, [(i, i ^ k) for i in range(count)])  14.5 us
    ppermute x10, waiting for transfers between devices, swapped(): lax.ppermute(v, axis, [(i, i ^ k) for i in range(count)])  8.61 us
    pallas_call x7, Pallas kernels, kernel_call(): pl.pallas_call(body, out_shape=[jax.ShapeDtypeStruct(shape, jnp.float32)...  8.42 us
    ppermute x3, starting transfers between devices, gathered(): lax.ppermute(what, axis, [(i, i ^ k) for i in range(count)])  4.98 us
    ppermute x3, waiting for transfers between devices, gathered(): lax.ppermute(what, axis, [(i, i ^ k) for i in range(count)])  0.93 us
  transfers between devices with their start and end apart: 13, of which 9 were waited for; matrix products, arithmetic and copies ran while one was open for 0% of the time, Pallas kernels for 2%

profile of v5, /device:TPU:1, one launch (start us, length us, event | category | flops | bytes accessed | tf_op | source)
XLA Modules:
  0.0 38.2 jit_solution(17283998086960562987)
XLA Ops:
  0.6 1.8 %shard_map.138 = (f32[8,128,128]{2,1,0:T(8,128)S(1)}, f32[160,384]{1,0:T(8,128)S(1)}, f32[128,8]{1,0:T(8,128)S(1)}, f32[16,1024]{1,0:T(8,128)S(1)}) custom-call(f32[8,128,128]{2,1,0:T(8,128)} %u_hbm.1, f32[2,32,128]{2,1,0:T(8,128)} %constant.20.clone.table_hbm, f32[2,160,384]{2,1,0:T(8,128)} %constant.21.clone.ty_hbm, f32[4,128,8]{2,1,0:T(8,128)} %constant.27.clone.fx_hbm), custom_call_target="tpu_custom_call" | custom-call | tf_op jit(solution)/shard_map/pallas_call | solution.py:167
  2.4 0.0 copy-start.1
  2.4 2.1 %collective-permute-start = (f32[16,1024]{1,0:T(8,128)S(1)}, f32[16,1024]{1,0:T(8,128)S(1)}, u32[]{:S(2)}, u32[]{:S(2)}) collective-permute-start(f32[16,1024]{1,0:T(8,128)S(1)} %get-tuple-element.29), channel_id=1, source_target_pairs={{0,4},{4,0},{1,5},{5,1},{2,6},{6,2},{3,7},{7,3},{8,12},{12,8},{9,1... | collective-permute-start | bytes 196616 | tf_op jit(solution)/shard_map/ppermute | solution.py:180
  4.5 1.7 %collective-permute-done.refs_1_ = f32[16,1024]{1,0:T(8,128)S(1)} collective-permute-done((f32[16,1024]{1,0:T(8,128)S(1)}, f32[16,1024]{1,0:T(8,128)S(1)}, u32[]{:S(2)}, u32[]{:S(2)}) %collective-permute-start) | collective-permute-done | bytes 65568 | tf_op jit(solution)/shard_map/ppermute | solution.py:180
  6.2 1.5 %shard_map.139 = (f32[1024,128]{1,0:T(8,128)S(1)}, f32[256,256]{1,0:T(8,128)S(1)}, f32[4,128,128]{2,1,0:T(8,128)S(1)}, f32[24,128]{1,0:T(8,128)S(1)}, f32[24,128]{1,0:T(8,128)S(1)}, /*index=5*/f32[24,128]{1,0:T(8,128)S(1)}) custom-call(f32[8,128,128]{2,1,0:T(8,128)S(1)} %get-tuple-element.28.refs_0_.u_ref.refs_2_, ...), custom_call_target="tpu_custom_call" | custom-call | tf_op jit(solution)/shard_map/pallas_call | solution.py:167
  7.7 3.6 %collective-permute-start.1 = (f32[24,128]{1,0:T(8,128)S(1)}, f32[24,128]{1,0:T(8,128)S(1)}, u32[]{:S(2)}, u32[]{:S(2)}) collective-permute-start(f32[24,128]{1,0:T(8,128)S(1)} %get-tuple-element.35), channel_id=1, source_target_pairs={{0,24},{8,16},{16,8},{24,0},{1,25},{9,17},{17,9},{25,1},{2,26},{10... | collective-permute-start | bytes 36872 | tf_op jit(solution)/shard_map/ppermute | solution.py:180
  11.3 0.4 collective-permute-start.3
  11.7 0.7 %collective-permute-done.1.refs_3_ = f32[24,128]{1,0:T(8,128)S(1)} collective-permute-done((f32[24,128]{1,0:T(8,128)S(1)}, f32[24,128]{1,0:T(8,128)S(1)}, u32[]{:S(2)}, u32[]{:S(2)}) %collective-permute-start.1) | collective-permute-done | bytes 12320 | tf_op jit(solution)/shard_map/ppermute | solution.py:180
  12.4 2.4 %collective-permute-done.2.refs_4_ = f32[24,128]{1,0:T(8,128)S(1)} collective-permute-done((f32[24,128]{1,0:T(8,128)S(1)}, f32[24,128]{1,0:T(8,128)S(1)}, u32[]{:S(2)}, u32[]{:S(2)}) %collective-permute-start.2) | collective-permute-done | bytes 12320 | tf_op jit(solution)/shard_map/ppermute | solution.py:180
  14.8 0.0 copy-start.2
  14.8 0.0 copy-start.3
  14.8 0.8 %shard_map.140 = (f32[4,128,128]{2,1,0:T(8,128)S(1)}, f32[72,128]{1,0:T(8,128)S(1)}, f32[4,64,128]{2,1,0:T(8,128)S(1)}, f32[64,128]{1,0:T(8,128)S(1)}, f32[64,128]{1,0:T(8,128)S(1)}, /*index=5*/f32[64,128]{1,0:T(8,128)S(1)}) custom-call(f32[1024,128]{1,0:T(8,128)S(1)} %get-tuple-element.32.refs_0_, f32[256,256]{1,0:T(8,128)S(1)} %get-tuple-element.33.refs_1_, ...), custom_call_target="tpu_custom_call" | custom-call | tf_op jit(solution)/shard_map/pallas_call | solution.py:167
  15.5 4.4 %collective-permute-start.4 = (f32[64,128]{1,0:T(8,128)S(1)}, f32[64,128]{1,0:T(8,128)S(1)}, u32[]{:S(2)}, u32[]{:S(2)}) collective-permute-start(f32[64,128]{1,0:T(8,128)S(1)} %get-tuple-element.39), channel_id=1, source_target_pairs={{0,3},{1,2},{2,1},{3,0},{4,7},{5,6},{6,5},{7,4},{8,11},{9,10},{10,... | collective-permute-start | bytes 98312 | tf_op jit(solution)/shard_map/ppermute | solution.py:180
  20.0 0.3 collective-permute-start.5
  20.2 0.2 collective-permute-start.6
  20.4 1.7 %collective-permute-done.4.refs_1_ = f32[64,128]{1,0:T(8,128)S(1)} collective-permute-done((f32[64,128]{1,0:T(8,128)S(1)}, f32[64,128]{1,0:T(8,128)S(1)}, u32[]{:S(2)}, u32[]{:S(2)}) %collective-permute-start.4) | collective-permute-done | bytes 32800 | tf_op jit(solution)/shard_map/ppermute | solution.py:180
  22.1 0.6 %collective-permute-done.5.refs_2_ = f32[64,128]{1,0:T(8,128)S(1)} collective-permute-done((f32[64,128]{1,0:T(8,128)S(1)}, f32[64,128]{1,0:T(8,128)S(1)}, u32[]{:S(2)}, u32[]{:S(2)}) %collective-permute-start.5) | collective-permute-done | bytes 32800 | tf_op jit(solution)/shard_map/ppermute | solution.py:180
  22.7 0.2 shard_map.141
  23.0 1.2 %collective-permute-start.7 = (f32[8,512]{1,0:T(8,128)S(1)}, f32[8,512]{1,0:T(8,128)S(1)}, u32[]{:S(2)}, u32[]{:S(2)}) collective-permute-start(f32[8,512]{1,0:T(8,128)S(1)} %get-tuple-element.44), channel_id=1, source_target_pairs={{0,24},{8,16},{16,8},{24,0},{1,25},{9,17},{17,9},{25,1},{2,26},{10... | collective-permute-start | bytes 49160 | tf_op jit(solution)/shard_map/ppermute | solution.py:180
  24.1 0.6 %collective-permute-start.8 = (f32[8,512]{1,0:T(8,128)S(1)}, f32[8,512]{1,0:T(8,128)S(1)}, u32[]{:S(2)}, u32[]{:S(2)}) collective-permute-start(f32[8,512]{1,0:T(8,128)S(1)} %get-tuple-element.45), channel_id=1, source_target_pairs={{0,16},{8,24},{16,0},{24,8},{1,17},{9,25},{17,1},{25,9},{2,18},{10... | collective-permute-start | bytes 49160 | tf_op jit(solution)/shard_map/ppermute | solution.py:180
  24.7 1.8 %collective-permute-start.9 = (f32[8,512]{1,0:T(8,128)S(1)}, f32[8,512]{1,0:T(8,128)S(1)}, u32[]{:S(2)}, u32[]{:S(2)}) collective-permute-start(f32[8,512]{1,0:T(8,128)S(1)} %get-tuple-element.46), channel_id=1, source_target_pairs={{0,8},{8,0},{16,24},{24,16},{1,9},{9,1},{17,25},{25,17},{2,10},{10... | collective-permute-start | bytes 49160 | tf_op jit(solution)/shard_map/ppermute | solution.py:180
  26.5 0.8 %collective-permute-done.7.refs_2_ = f32[8,512]{1,0:T(8,128)S(1)} collective-permute-done((f32[8,512]{1,0:T(8,128)S(1)}, f32[8,512]{1,0:T(8,128)S(1)}, u32[]{:S(2)}, u32[]{:S(2)}) %collective-permute-start.7) | collective-permute-done | bytes 16416 | tf_op jit(solution)/shard_map/ppermute | solution.py:180
  27.3 0.6 %collective-permute-done.8.refs_3_ = f32[8,512]{1,0:T(8,128)S(1)} collective-permute-done((f32[8,512]{1,0:T(8,128)S(1)}, f32[8,512]{1,0:T(8,128)S(1)}, u32[]{:S(2)}, u32[]{:S(2)}) %collective-permute-start.8) | collective-permute-done | bytes 16416 | tf_op jit(solution)/shard_map/ppermute | solution.py:180
  27.9 0.2 collective-permute-done.9.refs_4_
  28.1 0.9 %shard_map.142 = (f32[4,40,128]{2,1,0:T(8,128)S(1)}, f32[2,64,128]{2,1,0:T(8,128)S(1)}) custom-call(f32[4,64,128]{2,1,0:T(8,128)S(1)} %get-tuple-element.42.refs_0_, f32[72,128]{1,0:T(8,128)S(1)} %get-tuple-element.43.refs_1_, f32[8,512]{1,0:T(8,128)S(1)} %collective-permute-done.7.refs_2_, f32[8,512]{1,0:T(8,128)S(1)} %collective-permute-done.8.refs_3_, ...), custom_call_target="tpu_custom_call" | custom-call | tf_op jit(solution)/shard_map/pallas_call | solution.py:167
  29.0 0.0 copy-start
  29.0 0.8 %collective-permute-start.10 = (f32[4,40,128]{2,1,0:T(8,128)S(1)}, f32[4,40,128]{2,1,0:T(8,128)S(1)}, u32[]{:S(2)}, u32[]{:S(2)}) collective-permute-start(f32[4,40,128]{2,1,0:T(8,128)S(1)} %get-tuple-element.49.refs_5_), channel_id=1, source_target_pairs={{0,2},{1,3},{2,0},{3,1},{4,6},{5,7},{6,4},{7,5},{8,10},{9,11},{10,... | collective-permute-start | bytes 245768 | tf_op jit(solution)/shard_map/ppermute | solution.py:187
  29.8 0.8 %shard_map.143.refs_4_ = f32[8,128,128]{2,1,0:T(8,128)} custom-call(f32[8,128,128]{2,1,0:T(8,128)S(1)} %get-tuple-element.28.refs_0_.u_ref.refs_2_, f32[4,128,128]{2,1,0:T(8,128)S(1)} %get-tuple-element.48.ixy_ref.refs_3_), custom_call_target="tpu_custom_call" | custom-call | tf_op jit(solution)/shard_map/pallas_call | solution.py:167
  30.7 2.1 %collective-permute-start.11 = (f32[4,40,128]{2,1,0:T(8,128)S(1)}, f32[4,40,128]{2,1,0:T(8,128)S(1)}, u32[]{:S(2)}, u32[]{:S(2)}) collective-permute-start(f32[4,40,128]{2,1,0:T(8,128)S(1)} %get-tuple-element.49.refs_5_), channel_id=1, source_target_pairs={{0,1},{1,0},{2,3},{3,2},{4,5},{5,4},{6,7},{7,6},{8,9},{9,8},{10,11... | collective-permute-start | bytes 245768 | tf_op jit(solution)/shard_map/ppermute | solution.py:187
  32.7 2.1 %collective-permute-start.12 = (f32[4,40,128]{2,1,0:T(8,128)S(1)}, f32[4,40,128]{2,1,0:T(8,128)S(1)}, u32[]{:S(2)}, u32[]{:S(2)}) collective-permute-start(f32[4,40,128]{2,1,0:T(8,128)S(1)} %collective-permute-done.10.refs_7_), channel_id=1, source_target_pairs={{0,1},{1,0},{2,3},{3,2},{4,5},{5,4},{6,7},{7,6},{8,9},{9,8},{10,11... | collective-permute-start | bytes 245768 | tf_op jit(solution)/shard_map/ppermute | solution.py:187
  34.9 0.9 %collective-permute-done.12.refs_8_ = f32[4,40,128]{2,1,0:T(8,128)S(1)} collective-permute-done((f32[4,40,128]{2,1,0:T(8,128)S(1)}, f32[4,40,128]{2,1,0:T(8,128)S(1)}, u32[]{:S(2)}, u32[]{:S(2)}) %collective-permute-start.12) | collective-permute-done | bytes 81952 | tf_op jit(solution)/shard_map/ppermute | solution.py:187
  35.8 2.4 %shard_map.144 = (f32[8,128,128]{2,1,0:T(8,128)}, f32[4,64,64]{2,1,0:T(8,128)}, f32[2,32,32]{2,1,0:T(8,128)}, f32[1,16,16]{2,1,0:T(8,128)}) custom-call(f32[4,64,128]{2,1,0:T(8,128)S(1)} %get-tuple-element.42.refs_0_, f32[2,64,128]{2,1,0:T(8,128)S(1)} %get-tuple-element.47.refs_1_, ...), custom_call_target="tpu_custom_call", output_to_operand_aliasing={{0}: (4, {})} | custom-call | tf_op jit(solution)/shard_map/pallas_call | solution.py:167
  (15 shorter events, 0.0 us)
Async XLA Ops:
  2.4 12.4 %copy-start.1 = (f32[4,128,136]{2,1,0:T(8,128)S(1)}, f32[4,128,136]{2,1,0:T(8,128)}, u32[]{:S(2)}) copy-start(f32[4,128,136]{2,1,0:T(8,128)} %constant.22.clone.refs_6_) | copy-start | bytes 835588
  2.4 3.8 %collective-permute-start = (f32[16,1024]{1,0:T(8,128)S(1)}, f32[16,1024]{1,0:T(8,128)S(1)}, u32[]{:S(2)}, u32[]{:S(2)}) collective-permute-start(f32[16,1024]{1,0:T(8,128)S(1)} %get-tuple-element.29), channel_id=1, source_target_pairs={{0,4},{4,0},{1,5},{5,1},{2,6},{6,2},{3,7},{7,3},{8,12},{12,8},{9,1... | collective-permute-start | bytes 196616 | tf_op jit(solution)/shard_map/ppermute | solution.py:180
  7.7 4.7 %collective-permute-start.1 = (f32[24,128]{1,0:T(8,128)S(1)}, f32[24,128]{1,0:T(8,128)S(1)}, u32[]{:S(2)}, u32[]{:S(2)}) collective-permute-start(f32[24,128]{1,0:T(8,128)S(1)} %get-tuple-element.35), channel_id=1, source_target_pairs={{0,24},{8,16},{16,8},{24,0},{1,25},{9,17},{17,9},{25,1},{2,26},{10... | collective-permute-start | bytes 36872 | tf_op jit(solution)/shard_map/ppermute | solution.py:180
  11.3 3.4 %collective-permute-start.2 = (f32[24,128]{1,0:T(8,128)S(1)}, f32[24,128]{1,0:T(8,128)S(1)}, u32[]{:S(2)}, u32[]{:S(2)}) collective-permute-start(f32[24,128]{1,0:T(8,128)S(1)} %get-tuple-element.36), channel_id=1, source_target_pairs={{0,16},{8,24},{16,0},{24,8},{1,17},{9,25},{17,1},{25,9},{2,18},{10... | collective-permute-start | bytes 36872 | tf_op jit(solution)/shard_map/ppermute | solution.py:180
  11.3 3.4 %collective-permute-start.3 = (f32[24,128]{1,0:T(8,128)S(1)}, f32[24,128]{1,0:T(8,128)S(1)}, u32[]{:S(2)}, u32[]{:S(2)}) collective-permute-start(f32[24,128]{1,0:T(8,128)S(1)} %get-tuple-element.37), channel_id=1, source_target_pairs={{0,8},{8,0},{16,24},{24,16},{1,9},{9,1},{17,25},{25,17},{2,10},{10... | collective-permute-start | bytes 36872 | tf_op jit(solution)/shard_map/ppermute | solution.py:180
  14.8 8.0 %copy-start.6 = (f32[4,24,64]{2,1,0:T(8,128)S(1)}, f32[4,24,64]{2,1,0:T(8,128)}, u32[]{:S(2)}) copy-start(f32[4,24,64]{2,1,0:T(8,128)} %constant.28.clone.refs_4_) | copy-start | bytes 73732
  14.8 13.3 %copy-start.2 = (f32[2,512,128]{2,1,0:T(8,128)S(1)}, f32[2,512,128]{2,1,0:T(8,128)}, u32[]{:S(2)}) copy-start(f32[2,512,128]{2,1,0:T(8,128)} %constant.24.clone.refs_6_) | copy-start | bytes 1572868
  14.8 13.3 %copy-start.3 = (f32[4,184,88]{2,1,0:T(8,128)S(1)}, f32[4,184,88]{2,1,0:T(8,128)}, u32[]{:S(2)}) copy-start(f32[4,184,88]{2,1,0:T(8,128)} %constant.23.clone.refs_5_) | copy-start | bytes 777220
  15.5 6.6 %collective-permute-start.4 = (f32[64,128]{1,0:T(8,128)S(1)}, f32[64,128]{1,0:T(8,128)S(1)}, u32[]{:S(2)}, u32[]{:S(2)}) collective-permute-start(f32[64,128]{1,0:T(8,128)S(1)} %get-tuple-element.39), channel_id=1, source_target_pairs={{0,3},{1,2},{2,1},{3,0},{4,7},{5,6},{6,5},{7,4},{8,11},{9,10},{10,... | collective-permute-start | bytes 98312 | tf_op jit(solution)/shard_map/ppermute | solution.py:180
  20.0 2.8 %collective-permute-start.5 = (f32[64,128]{1,0:T(8,128)S(1)}, f32[64,128]{1,0:T(8,128)S(1)}, u32[]{:S(2)}, u32[]{:S(2)}) collective-permute-start(f32[64,128]{1,0:T(8,128)S(1)} %get-tuple-element.40), channel_id=1, source_target_pairs={{0,2},{1,3},{2,0},{3,1},{4,6},{5,7},{6,4},{7,5},{8,10},{9,11},{10,... | collective-permute-start | bytes 98312 | tf_op jit(solution)/shard_map/ppermute | solution.py:180
  20.2 2.5 %collective-permute-start.6 = (f32[64,128]{1,0:T(8,128)S(1)}, f32[64,128]{1,0:T(8,128)S(1)}, u32[]{:S(2)}, u32[]{:S(2)}) collective-permute-start(f32[64,128]{1,0:T(8,128)S(1)} %get-tuple-element.41), channel_id=1, source_target_pairs={{0,1},{1,0},{2,3},{3,2},{4,5},{5,4},{6,7},{7,6},{8,9},{9,8},{10,11... | collective-permute-start | bytes 98312 | tf_op jit(solution)/shard_map/ppermute | solution.py:180
  23.0 4.4 %collective-permute-start.7 = (f32[8,512]{1,0:T(8,128)S(1)}, f32[8,512]{1,0:T(8,128)S(1)}, u32[]{:S(2)}, u32[]{:S(2)}) collective-permute-start(f32[8,512]{1,0:T(8,128)S(1)} %get-tuple-element.44), channel_id=1, source_target_pairs={{0,24},{8,16},{16,8},{24,0},{1,25},{9,17},{17,9},{25,1},{2,26},{10... | collective-permute-start | bytes 49160 | tf_op jit(solution)/shard_map/ppermute | solution.py:180
  24.1 3.8 %collective-permute-start.8 = (f32[8,512]{1,0:T(8,128)S(1)}, f32[8,512]{1,0:T(8,128)S(1)}, u32[]{:S(2)}, u32[]{:S(2)}) collective-permute-start(f32[8,512]{1,0:T(8,128)S(1)} %get-tuple-element.45), channel_id=1, source_target_pairs={{0,16},{8,24},{16,0},{24,8},{1,17},{9,25},{17,1},{25,9},{2,18},{10... | collective-permute-start | bytes 49160 | tf_op jit(solution)/shard_map/ppermute | solution.py:180
  24.7 3.4 %collective-permute-start.9 = (f32[8,512]{1,0:T(8,128)S(1)}, f32[8,512]{1,0:T(8,128)S(1)}, u32[]{:S(2)}, u32[]{:S(2)}) collective-permute-start(f32[8,512]{1,0:T(8,128)S(1)} %get-tuple-element.46), channel_id=1, source_target_pairs={{0,8},{8,0},{16,24},{24,16},{1,9},{9,1},{17,25},{25,17},{2,10},{10... | collective-permute-start | bytes 49160 | tf_op jit(solution)/shard_map/ppermute | solution.py:180
  29.0 6.8 %copy-start = (f32[2,768,128]{2,1,0:T(8,128)S(1)}, f32[2,768,128]{2,1,0:T(8,128)}, u32[]{:S(2)}) copy-start(f32[2,768,128]{2,1,0:T(8,128)} %constant.26.clone.refs_11_) | copy-start | bytes 2359300
  29.0 3.7 %collective-permute-start.10 = (f32[4,40,128]{2,1,0:T(8,128)S(1)}, f32[4,40,128]{2,1,0:T(8,128)S(1)}, u32[]{:S(2)}, u32[]{:S(2)}) collective-permute-start(f32[4,40,128]{2,1,0:T(8,128)S(1)} %get-tuple-element.49.refs_5_), channel_id=1, source_target_pairs={{0,2},{1,3},{2,0},{3,1},{4,6},{5,7},{6,4},{7,5},{8,10},{9,11},{10,... | collective-permute-start | bytes 245768 | tf_op jit(solution)/shard_map/ppermute | solution.py:187
  29.8 5.9 %copy-start.4 = (f32[4,144,40]{2,1,0:T(8,128)S(1)}, f32[4,144,40]{2,1,0:T(8,128)}, u32[]{:S(2)}) copy-start(f32[4,144,40]{2,1,0:T(8,128)} %constant.25.clone.refs_10_) | copy-start | bytes 276484
  29.8 5.9 %copy-start.5 = (f32[128,80]{1,0:T(8,128)S(1)}, f32[128,80]{1,0:T(8,128)}, u32[]{:S(2)}) copy-start(f32[128,80]{1,0:T(8,128)} %constant.29.clone.refs_9_) | copy-start | bytes 122884
  30.7 4.2 %collective-permute-start.11 = (f32[4,40,128]{2,1,0:T(8,128)S(1)}, f32[4,40,128]{2,1,0:T(8,128)S(1)}, u32[]{:S(2)}, u32[]{:S(2)}) collective-permute-start(f32[4,40,128]{2,1,0:T(8,128)S(1)} %get-tuple-element.49.refs_5_), channel_id=1, source_target_pairs={{0,1},{1,0},{2,3},{3,2},{4,5},{5,4},{6,7},{7,6},{8,9},{9,8},{10,11... | collective-permute-start | bytes 245768 | tf_op jit(solution)/shard_map/ppermute | solution.py:187
  32.7 3.0 %collective-permute-start.12 = (f32[4,40,128]{2,1,0:T(8,128)S(1)}, f32[4,40,128]{2,1,0:T(8,128)S(1)}, u32[]{:S(2)}, u32[]{:S(2)}) collective-permute-start(f32[4,40,128]{2,1,0:T(8,128)S(1)} %collective-permute-done.10.refs_7_), channel_id=1, source_target_pairs={{0,1},{1,0},{2,3},{3,2},{4,5},{5,4},{6,7},{7,6},{8,9},{9,8},{10,11... | collective-permute-start | bytes 245768 | tf_op jit(solution)/shard_map/ppermute | solution.py:187

commit v6 on v5

--- a/solution.py
+++ b/solution.py
@@ -226,7 +226,7 @@
     wide = packed = round_up(max(wide1 + 1, 3 * wide2, wide2 + wide1), 128)
     kx = round_up(xtwo.most_sent(), 8)
     rowsx = xtwo.fine + kx * (dx - 1)
-    tall = round_up(max(xtwo.n + xthree.most_needed(), xone.n // 2 + 1), 8)
+    tall = round_up(max(xtwo.n + xthree.most_needed() + 1, xone.n // 2 + 1), 8)
 
     others_y = max(dy - 1, 1)
     fya = np.zeros((dy, others_y * sa8, ly))
@@ -358,6 +358,7 @@
     tables_x3, at_x3 = stacked(tx3, qx3, px3)
     tables_y3, at_y3 = stacked(ty3, qy3, py3, py1)
     hz, hx1 = lz // 2, lx // 2
+    ly2 = round_up(ytwo.fine, 128)
 
     def y_messages(u_hbm, table_hbm, ty_hbm, fx_hbm, u_ref, ty_ref, fx_ref, *refs):
         outs, (table, sems) = refs[:-2], refs[-2:]
@@ -434,8 +435,8 @@
     def x_apply(*refs):
         ta_ref, tsm_ref, iy_ref = refs[:3]
         came = refs[3 : 2 + dx][::-1]
-        tx_ref, ixy_out, zc_out, u1_out = refs[2 + dx : 6 + dx]
-        planes_out, rest = refs[6 + dx : -1], refs[-1]
+        tx_ref, f2x_ref, ixy_out, zc_out, u1_out = refs[2 + dx : 7 + dx]
+        planes_out, xt_outs, rest = refs[7 + dx : 6 + dx + dz], refs[6 + dx + dz : -1], refs[-1]
         jx, jz = lax.axis_index("gx"), lax.axis_index("gz")
         xa, xm, diff = [], [], []
 
@@ -474,11 +475,13 @@
             after = jnp.where(row == lx - 1, jnp.broadcast_to(halo, (lx, ly)), after)
             ixy_out[half] = jnp.where(row % 2 == 1, 0.5 * (before + after), iy)
         scalar = lambda place: chosen_by(zs[:, place], jz)
+        totals = []
         for zc in range(zn):
             total = diff[zc] - scalar(at_first + zc) * xm[0] - scalar(at_last + zc) * xm[hz - 1]
             for z in range(lz):
                 total += scalar(at_local + zc * lz + z) * xa[z]
             u1_out[zc] = total
+            totals.append(total)
         v = -scalar(2 * lz) * xm[hz - 1]
         w = -scalar(2 * lz + 1) * xm[0]
         for z in range(lz):
@@ -486,19 +489,7 @@
             w += scalar(lz + z) * xa[z]
         for k, out in enumerate(planes_out):
             out[...] = jnp.where((jz ^ (k + 1)) > jz, w, v)
-
-    def z_apply(*refs):
-        part_ref, came = refs[0], refs[1:dz][::-1]
-        f2x_ref, u1_out, xt_outs = refs[dz], refs[dz + 1], refs[dz + 2 :]
-        jx, jz = lax.axis_index("gx"), lax.axis_index("gz")
-        totals = []
-        for zc in range(zn):
-            total = part_ref[zc]
-            for k, r in enumerate(came):
-                total += chosen_by(zs[:, at_reach + k * zn + zc], jz) * r[...]
-            u1_out[zc] = total
-            totals.append(total)
-        sent = dot(f2x_ref[jx], jnp.concatenate(totals, axis=1))
+        sent = dot(f2x_ref[jx], jnp.concatenate(totals + [v, w], axis=1))
         for k, out in enumerate(xt_outs):
             out[...] = sent[k * kx : (k + 1) * kx]
 
@@ -510,86 +501,120 @@
                 out_ref[2 * half + 1] = u_ref[2 * half + 1] - 0.5 * (here + ixy_ref[half + 1])
 
     def second_apply(*refs):
-        u1_ref, zc_ref, came = refs[0], refs[1], refs[2 : dx + 1][::-1]
-        tx2_ref, ty2_ref, zt_out, i2_out = refs[dx + 1 :]
-        jx, jy = lax.axis_index("gx"), lax.axis_index("gy")
-        own = jnp.concatenate([u1_ref[z] for z in range(lz2)], axis=1)
-        state = jnp.concatenate([own] + [r[...] for r in came], axis=0)
-        across = dot(tx2_ref[jx], state)
-        spread = across[3 * tall :]
-        for z in range(lz2):
-            cut = across[:, z * wide : (z + 1) * wide]
-            if z % 2 == 1:
-                moved = dot(cut[:tall], ty2_ref[jy, :wide])
-                if z < 4:
-                    begin = xtwo.n * (z // 2)
-                    moved += pltpu.roll(zc_ref[begin : begin + tall], wide2, 1)
-                zt_out[z] = moved
-            else:
-                joined = jnp.concatenate([cut[c * tall : (c + 1) * tall] for c in range(3)], axis=1)
-                zt_out[z] = dot(joined, ty2_ref[jy, : 3 * wide])
-                i2_out[z // 2] = dot(spread[:, z * wide : (z + 1) * wide], ty2_ref[jy, 3 * wide :, : round_up(ytwo.fine, 128)])
+        part_ref, zc_ref = refs[:2]
+        xcame, zcame = refs[2 : dx + 1][::-1], refs[dx + 1 : dz + dx][::-1]
+        tx2_ref, ty2_ref, u1_out, zt_out, i2_out = refs[dz + dx :]
+        jx, jy, jz = lax.axis_index("gx"), lax.axis_index("gy"), lax.axis_index("gz")
+        own = []
+        for zc in range(zn):
+            total = part_ref[zc]
+            for k, r in enumerate(zcame):
+                total += chosen_by(zs[:, at_reach + k * zn + zc], jz) * r[...]
+            u1_out[zc] = total
+            own.append(total)
+        own = jnp.concatenate(own + [jnp.zeros_like(own[0])] * 2, axis=1)
+        across = dot(tx2_ref[jx], jnp.concatenate([own] + [r[...] for r in xcame], axis=0))
+        cut = [across[:, z * wide : (z + 1) * wide] for z in range(zn + 2)]
+        whole = [z for z in range(zn + 2) if z % 2 == 0 or z >= zn]
+        joined = [jnp.concatenate([cut[z][c * tall : (c + 1) * tall] for c in range(3)], axis=1) for z in whole]
+        made = dot(jnp.concatenate(joined, axis=0), ty2_ref[jy, : 3 * wide])
+        for place, z in enumerate(whole):
+            zt_out[z] = made[place * tall : (place + 1) * tall]
+        made = dot(jnp.concatenate([cut[z][:tall] for z in range(1, zn, 2)], axis=0), ty2_ref[jy, :wide])
+        for z in range(1, zn, 2):
+            moved = made[(z // 2) * tall : (z // 2 + 1) * tall]
+            if z < 4:
+                begin = xtwo.n * (z // 2)
+                moved += pltpu.roll(zc_ref[begin : begin + tall], wide2, 1)
+            zt_out[z] = moved
+        for z in (zn, zn + 1):
+            zt_out[z, tall - 1 :] = cut[z][-1:]
+        made = dot(jnp.concatenate([cut[z][3 * tall :] for z in range(0, zn, 2)], axis=0), ty2_ref[jy, 3 * wide :, :ly2])
+        for half in range(zn // 2):
+            i2_out[half] = made[half * xtwo.fine : (half + 1) * xtwo.fine]
 
     def third_apply(*refs):
         u1_ref, i2_ref, u_ref, ixy_ref, _, own_ref = refs[:6]
         came = refs[6 : 5 + dz]
-        px1_ref, tx_ref, ty_ref, fine_out, middle_out, coarse_out, coarsest_out = refs[5 + dz : 12 + dz]
-        zbuf, ubuf, last, middle, sems = refs[12 + dz :]
+        px1_ref, tx_ref, ty_ref, qy2_ref, fine_out, middle_out, coarse_out, coarsest_out = refs[5 + dz : 13 + dz]
+        zbuf, qbuf, ubuf, last, middle, sems = refs[13 + dz :]
         part = lambda ref, j, starts, which: ref[j, starts[which] : starts[which + 1]]
         jx, jy, jz = lax.axis_index("gx"), lax.axis_index("gy"), lax.axis_index("gz")
-        zbuf[pl.ds(jz * lz2, lz2)] = own_ref[...]
+        for k, r in enumerate((own_ref, *came)):
+            zbuf[pl.ds((jz ^ k) * lz2, lz2)] = r[:lz2]
+            qbuf[pl.ds((jz ^ k) * 2, 2)] = r[lz2:]
+        at = jnp.minimum(jz + 1, dz - 1) * lz2
+        plane_halo = dot(px1_ref[...], jnp.concatenate([zbuf[at + 1], zbuf[at + 3]], axis=0))
+        everything = []
+        for j in range(dz):
+            for zc in range(lz2):
+                total = zbuf[j * lz2 + zc]
+                for i in range(dz):
+                    if i != j:
+                        total += float(zone.reach(j, i)[zc]) * qbuf[2 * i + (i < j)]
+                everything.append(total)
+        for z in range(0, z2, lz2):
+            zbuf[z] = everything[z]
+        if lz2 > 2:
+            zbuf[z2 - 2] = everything[z2 - 2]
+        at = jnp.minimum((jz + 1) * lz2, z2 - 2)
+        halo = dot(part(tx_ref, jx, at_x3, 2), zbuf[at])
+        edges = [jnp.zeros((1, wide), jnp.float32)] * (lz2 // 2)
         for k, r in enumerate(came):
-            zbuf[pl.ds((jz ^ (k + 1)) * lz2, lz2)] = r[...]
-        at = jnp.minimum(jz + 1, dz - 1) * lz2
-        first = jnp.concatenate([zbuf[at + 1], zbuf[at + 3]], axis=0)
-        halo = dot(dot(px1_ref[...], first), part(ty_ref, jy, at_y3, 3))
+            line = jnp.where((jz ^ (k + 1)) > jz, r[lz2, tall - 1 :], r[lz2 + 1, tall - 1 :])
+            for half in range(lz2 // 2):
+                edges[half] += chosen_by(zs[:, at_reach + k * zn + 2 * half], jz) * line
+        fy = ytwo.fine
+        edges = dot(jnp.concatenate(edges + [jnp.zeros((8 - lz2 // 2 % 8, wide), jnp.float32)], axis=0), qy2_ref[jy, :, :ly2])
+        plane_halo = dot(plane_halo, part(ty_ref, jy, at_y3, 3))
+        halo = dot(halo, part(ty_ref, jy, at_y3, 2))[:, :fy]
         here = ixy_ref[hz - 1]
-        last[...] = u_ref[lz - 1] - 0.5 * (here + jnp.where(jz == dz - 1, here, halo))
+        last[...] = u_ref[lz - 1] - 0.5 * (here + jnp.where(jz == dz - 1, here, plane_halo))
         copies = [pltpu.make_async_copy(last, fine_out.at[lz - 1], sems.at[0])]
         copies[0].start()
-        fy = ytwo.fine
-        at = jnp.minimum((jz + 1) * lz2, z2 - 2)
-        halo = dot(dot(part(tx_ref, jx, at_x3, 2), zbuf[at]), part(ty_ref, jy, at_y3, 2))[:, :fy]
+        at_end = iota((xtwo.fine, fy), 0) == xtwo.fine - 1
+        spread = [
+            i2_ref[half][:, :fy] + jnp.where(at_end, jnp.broadcast_to(edges[half : half + 1, :fy], (xtwo.fine, fy)), 0.0)
+            for half in range(lz2 // 2)
+        ]
+        spread.append(halo)
         for half in range(lz2 // 2):
-            here = i2_ref[half][:, :fy]
-            after = i2_ref[half + 1][:, :fy] if half + 1 < lz2 // 2 else halo
-            middle[2 * half] = u1_ref[2 * half][:, :fy] - here
-            middle[2 * half + 1] = u1_ref[2 * half + 1][:, :fy] - 0.5 * (here + after)
+            middle[2 * half] = u1_ref[2 * half][:, :fy] - spread[half]
+            middle[2 * half + 1] = u1_ref[2 * half + 1][:, :fy] - 0.5 * (spread[half] + spread[half + 1])
         copies.append(pltpu.make_async_copy(middle, middle_out, sems.at[1]))
         copies[1].start()
-        everything = [zbuf[z] for z in range(z2)]
         evens = [pltpu.roll(everything[z], packed - wide2, 1) for z in range(0, z2, 2)]
         arounds = [pltpu.roll(everything[z], packed - 2 * wide2, 1) for z in range(0, z2, 2)]
+        second = []
         for zc in range(z3):
             total = evens[zc] - arounds[zc] - first2[zc] * arounds[0] - last2[zc] * arounds[-1]
             for z in range(z2):
                 total += az2[zc][z] * everything[z]
             ubuf[zc] = total
-        fy3 = ythree.fine
-        spread = []
-        for half in range(lz3 // 2 + 1):
-            at = jnp.minimum(jz * lz3 + 2 * half, z3 - 2)
-            spread.append(dot(dot(part(tx_ref, jx, at_x3, 1), ubuf[at]), part(ty_ref, jy, at_y3, 1))[:, :fy3])
+            second.append(total)
+        fy3, n3 = ythree.fine, xthree.n
+        at = [jnp.minimum(jz * lz3 + 2 * half, z3 - 2) for half in range(lz3 // 2 + 1)]
+        spread = dot(part(tx_ref, jx, at_x3, 1), jnp.concatenate([ubuf[a] for a in at], axis=1))
+        joined = []
+        for zc in range(lz4):
+            base = zc * (z3 + 2)
+            along = chosen_by(zt[:, base], jz) * second[0]
+            for z in range(1, z3):
+                along += chosen_by(zt[:, base + z], jz) * second[z]
+            even = ubuf[2 * (jz * lz4 + zc)]
+            around = even + chosen_by(zt[:, base + z3], jz) * second[0] + chosen_by(zt[:, base + z3 + 1], jz) * second[z3 - 2]
+            parts = [dot(tx_ref[jx, c * n3 : (c + 1) * n3, :], plane) for c, plane in enumerate((along, even, around))]
+            joined.append(jnp.concatenate(parts, axis=1))
+        spread = jnp.concatenate([spread[:, h * packed : (h + 1) * packed] for h in range(len(at))], axis=0)
+        spread = dot(spread, part(ty_ref, jy, at_y3, 1))[:, :fy3]
+        coarsest = dot(jnp.concatenate(joined, axis=0), part(ty_ref, jy, at_y3, 0))[:, : ythree.n]
+        for zc in range(lz4):
+            coarsest_out[zc] = coarsest[zc * n3 : (zc + 1) * n3]
+        spread = [spread[h * xthree.fine : (h + 1) * xthree.fine] for h in range(len(at))]
         for half in range(lz3 // 2):
             at = jz * lz3 + 2 * half
             coarse_out[2 * half] = ubuf[at][: xthree.fine, :fy3] - spread[half]
             coarse_out[2 * half + 1] = ubuf[at + 1][: xthree.fine, :fy3] - 0.5 * (spread[half] + spread[half + 1])
-        n3 = xthree.n
-        for zc in range(lz4):
-            base = zc * (z3 + 2)
-            along = chosen_by(zt[:, base], jz) * ubuf[0]
-            for z in range(1, z3):
-                along += chosen_by(zt[:, base + z], jz) * ubuf[z]
-            even = ubuf[2 * (jz * lz4 + zc)]
-            around = even + chosen_by(zt[:, base + z3], jz) * ubuf[0] + chosen_by(zt[:, base + z3 + 1], jz) * ubuf[z3 - 2]
-            joined = jnp.concatenate(
-                [
-                    dot(tx_ref[jx, c * n3 : (c + 1) * n3, :], plane)
-                    for c, plane in enumerate((along, even, around))
-                ],
-                axis=1,
-            )
-            coarsest_out[zc] = dot(joined, part(ty_ref, jy, at_y3, 0))[:, : ythree.n]
         for copy in copies:
             copy.wait()
 
@@ -609,32 +634,30 @@
         scratch=[pltpu.VMEM((ss8, hz * hx1), jnp.float32)],
     )
     xcame = swapped(xm, "gx")
-    ixy, zc, u1_part, *planes = kernel_call(
+    ixy, zc, u1_part, *sent = kernel_call(
         x_apply,
-        [(hz, lx, ly), (xtwo.n + tall, wide), (zn, xone.n, wide)] + [(xone.n, wide)] * (dz - 1),
-        [ta_v, tsm_v, iy, *xcame[::-1], tables_x],
+        [(hz, lx, ly), (xtwo.n + tall, wide), (zn, xone.n, wide)]
+        + [(xone.n, wide)] * (dz - 1)
+        + [(kx, (zn + 2) * wide)] * (dx - 1),
+        [ta_v, tsm_v, iy, *xcame[::-1], tables_x, to32(f2x)],
         scratch=[pltpu.VMEM((lz, ext, 2 * wide), jnp.float32)],
     )
-    zcame = swapped(planes, "gz")
-    u1, *xt = kernel_call(
-        z_apply,
-        [(zn, xone.n, wide)] + [(kx, zn * wide)] * (dx - 1),
-        [u1_part, *zcame[::-1], to32(f2x)],
-    )
-    xtcame = swapped(xt, "gx")
-    zmsg, i2 = kernel_call(
+    zcame = swapped(sent[: dz - 1], "gz")
+    xtcame = swapped(sent[dz - 1 :], "gx")
+    u1, zmsg, i2 = kernel_call(
         second_apply,
-        [(lz2, tall, packed), (lz2 // 2, xtwo.fine, round_up(ytwo.fine, 128))],
-        [u1, zc, *xtcame[::-1], tables_x2, tables_y2],
+        [(zn, xone.n, wide), (lz2 + 2, tall, packed), (lz2 // 2, xtwo.fine, ly2)],
+        [u1_part, zc, *xtcame[::-1], *zcame[::-1], tables_x2, tables_y2],
     )
     (fine,) = kernel_call(fine_coefficients, [(lz, lx, ly)], [u, ixy])
     ztcame, fine = gathered(zmsg, "gz", fine)
     return kernel_call(
         third_apply,
         [(lz, lx, ly), (lz2, xtwo.fine, ytwo.fine), (lz3, xthree.fine, ythree.fine), (lz4, xthree.n, ythree.n)],
-        [u1, i2, u, ixy, fine, zmsg, *ztcame, to32(px1), tables_x3, tables_y3],
+        [u1, i2, u, ixy, fine, zmsg, *ztcame, to32(px1), tables_x3, tables_y3, to32(qy2)],
         scratch=[
             pltpu.VMEM((z2, tall, packed), jnp.float32),
+            pltpu.VMEM((2 * dz, tall, packed), jnp.float32),
             pltpu.VMEM((z3, tall, packed), jnp.float32),
             pltpu.VMEM((lx, ly), jnp.float32),
             pltpu.VMEM((lz2, xtwo.fine, ytwo.fine), jnp.float32),

time: 38.7 us -> 38.5 us (level)
  waiting for transfers between devices: 9.53 us -> 7.18 us
  starting transfers between devices: 19.5 us -> 21.5 us
    ppermute x10, waiting for transfers between devices: 8.61 us -> 6.2 us  [swapped(): lax.ppermute(v, axis, [(i, i ^ k) for i in range(count)])]
    ppermute x3, starting transfers between devices: 4.98 us -> 6.75 us  [gathered(): lax.ppermute(what, axis, [(i, i ^ k) for i in range(count)])]
    pallas_call x7 -> x6, Pallas kernels: 8.42 us -> 8.52 us  [kernel_call(): pl.pallas_call(body, out_shape=[jax.ShapeDtypeStruct(shape, jnp.float32)...]
  transfers between devices with their start and end apart: 13 -> 13, of which waited for: 9 -> 6; matrix products, arithmetic and copies ran while one was open for 0% -> 0% of each run, Pallas kernels for 2% -> 2%
where the time goes in v6:
time: 38.5 us; the launch traced here: 38 us
  starting transfers between devices  21.5 us (56%)
  Pallas kernels  8.52 us (22%)
  waiting for transfers between devices  7.18 us (19%)
  between operations  0.73 us (2%)
    ppermute x10, starting transfers between devices, swapped(): lax.ppermute(v, axis, [(i, i ^ k) for i in range(count)])  14.8 us
    pallas_call x6, Pallas kernels, kernel_call(): pl.pallas_call(body, out_shape=[jax.ShapeDtypeStruct(shape, jnp.float32)...  8.52 us
    ppermute x3, starting transfers between devices, gathered(): lax.ppermute(what, axis, [(i, i ^ k) for i in range(count)])  6.75 us
    ppermute x10, waiting for transfers between devices, swapped(): lax.ppermute(v, axis, [(i, i ^ k) for i in range(count)])  6.2 us
    ppermute x3, waiting for transfers between devices, gathered(): lax.ppermute(what, axis, [(i, i ^ k) for i in range(count)])  0.98 us
  transfers between devices with their start and end apart: 13, of which 6 were waited for; matrix products, arithmetic and copies ran while one was open for 0% of the time, Pallas kernels for 2%

profile of v6, /device:TPU:1, one launch (start us, length us, event | category | flops | bytes accessed | tf_op | source)
XLA Modules:
  0.0 38.0 jit_solution(14159292135909128160)
XLA Ops:
  0.6 1.8 %shard_map.147 = (f32[8,128,128]{2,1,0:T(8,128)S(1)}, f32[160,384]{1,0:T(8,128)S(1)}, f32[128,8]{1,0:T(8,128)S(1)}, f32[16,1024]{1,0:T(8,128)S(1)}) custom-call(f32[8,128,128]{2,1,0:T(8,128)} %u_hbm.1, f32[2,32,128]{2,1,0:T(8,128)} %constant.22.clone.table_hbm, f32[2,160,384]{2,1,0:T(8,128)} %constant.23.clone.ty_hbm, f32[4,128,8]{2,1,0:T(8,128)} %constant.29.clone.fx_hbm), custom_call_target="tpu_custom_call" | custom-call | tf_op jit(solution)/shard_map/pallas_call | solution.py:167
  2.4 0.0 copy-start.1
  2.4 2.1 %collective-permute-start = (f32[16,1024]{1,0:T(8,128)S(1)}, f32[16,1024]{1,0:T(8,128)S(1)}, u32[]{:S(2)}, u32[]{:S(2)}) collective-permute-start(f32[16,1024]{1,0:T(8,128)S(1)} %get-tuple-element.29), channel_id=1, source_target_pairs={{0,4},{4,0},{1,5},{5,1},{2,6},{6,2},{3,7},{7,3},{8,12},{12,8},{9,1... | collective-permute-start | bytes 196616 | tf_op jit(solution)/shard_map/ppermute | solution.py:180
  4.5 1.7 %collective-permute-done.refs_1_ = f32[16,1024]{1,0:T(8,128)S(1)} collective-permute-done((f32[16,1024]{1,0:T(8,128)S(1)}, f32[16,1024]{1,0:T(8,128)S(1)}, u32[]{:S(2)}, u32[]{:S(2)}) %collective-permute-start) | collective-permute-done | bytes 65568 | tf_op jit(solution)/shard_map/ppermute | solution.py:180
  6.2 1.5 %shard_map.148 = (f32[1024,128]{1,0:T(8,128)S(1)}, f32[256,256]{1,0:T(8,128)S(1)}, f32[4,128,128]{2,1,0:T(8,128)S(1)}, f32[24,128]{1,0:T(8,128)S(1)}, f32[24,128]{1,0:T(8,128)S(1)}, /*index=5*/f32[24,128]{1,0:T(8,128)S(1)}) custom-call(f32[8,128,128]{2,1,0:T(8,128)S(1)} %get-tuple-element.28.refs_0_.u_ref.refs_2_, ...), custom_call_target="tpu_custom_call" | custom-call | tf_op jit(solution)/shard_map/pallas_call | solution.py:167
  7.7 3.6 %collective-permute-start.1 = (f32[24,128]{1,0:T(8,128)S(1)}, f32[24,128]{1,0:T(8,128)S(1)}, u32[]{:S(2)}, u32[]{:S(2)}) collective-permute-start(f32[24,128]{1,0:T(8,128)S(1)} %get-tuple-element.35), channel_id=1, source_target_pairs={{0,24},{8,16},{16,8},{24,0},{1,25},{9,17},{17,9},{25,1},{2,26},{10... | collective-permute-start | bytes 36872 | tf_op jit(solution)/shard_map/ppermute | solution.py:180
  11.3 0.4 collective-permute-start.3
  11.7 0.7 %collective-permute-done.1.refs_3_ = f32[24,128]{1,0:T(8,128)S(1)} collective-permute-done((f32[24,128]{1,0:T(8,128)S(1)}, f32[24,128]{1,0:T(8,128)S(1)}, u32[]{:S(2)}, u32[]{:S(2)}) %collective-permute-start.1) | collective-permute-done | bytes 12320 | tf_op jit(solution)/shard_map/ppermute | solution.py:180
  12.4 2.4 %collective-permute-done.2.refs_4_ = f32[24,128]{1,0:T(8,128)S(1)} collective-permute-done((f32[24,128]{1,0:T(8,128)S(1)}, f32[24,128]{1,0:T(8,128)S(1)}, u32[]{:S(2)}, u32[]{:S(2)}) %collective-permute-start.2) | collective-permute-done | bytes 12320 | tf_op jit(solution)/shard_map/ppermute | solution.py:180
  14.8 0.0 copy-start.2
  14.8 0.0 copy-start.3
  14.8 0.9 %shard_map.149 = (f32[4,128,128]{2,1,0:T(8,128)S(1)}, f32[72,128]{1,0:T(8,128)S(1)}, f32[4,64,128]{2,1,0:T(8,128)S(1)}, f32[64,128]{1,0:T(8,128)S(1)}, f32[64,12...) custom-call(f32[1024,128]{1,0:T(8,128)S(1)} %get-tuple-element.32.re, ...), custom_call_target="tpu_custom_call" | custom-call | tf_op jit(solution)/shard_map/pallas_call | solution.py:167
  15.7 1.2 %collective-permute-start.4 = (f32[8,768]{1,0:T(8,128)S(1)}, f32[8,768]{1,0:T(8,128)S(1)}, u32[]{:S(2)}, u32[]{:S(2)}) collective-permute-start(f32[8,768]{1,0:T(8,128)S(1)} %get-tuple-element.40), channel_id=1, source_target_pairs={{0,24},{8,16},{16,8},{24,0},{1,25},{9,17},{17,9},{25,1},{2,26},{10... | collective-permute-start | bytes 73736 | tf_op jit(solution)/shard_map/ppermute | solution.py:180
  16.9 4.6 %collective-permute-start.7 = (f32[64,128]{1,0:T(8,128)S(1)}, f32[64,128]{1,0:T(8,128)S(1)}, u32[]{:S(2)}, u32[]{:S(2)}) collective-permute-start(f32[64,128]{1,0:T(8,128)S(1)} %get-tuple-element.43), channel_id=1, source_target_pairs={{0,3},{1,2},{2,1},{3,0},{4,7},{5,6},{6,5},{7,4},{8,11},{9,10},{10,... | collective-permute-start | bytes 98312 | tf_op jit(solution)/shard_map/ppermute | solution.py:180
  21.5 0.3 collective-permute-start.8
  21.8 0.2 collective-permute-start.9
  22.0 0.4 %collective-permute-start.5 = (f32[8,768]{1,0:T(8,128)S(1)}, f32[8,768]{1,0:T(8,128)S(1)}, u32[]{:S(2)}, u32[]{:S(2)}) collective-permute-start(f32[8,768]{1,0:T(8,128)S(1)} %get-tuple-element.41), channel_id=1, source_target_pairs={{0,16},{8,24},{16,0},{24,8},{1,17},{9,25},{17,1},{25,9},{2,18},{10... | collective-permute-start | bytes 73736 | tf_op jit(solution)/shard_map/ppermute | solution.py:180
  22.4 2.0 %collective-permute-start.6 = (f32[8,768]{1,0:T(8,128)S(1)}, f32[8,768]{1,0:T(8,128)S(1)}, u32[]{:S(2)}, u32[]{:S(2)}) collective-permute-start(f32[8,768]{1,0:T(8,128)S(1)} %get-tuple-element.42), channel_id=1, source_target_pairs={{0,8},{8,0},{16,24},{24,16},{1,9},{9,1},{17,25},{25,17},{2,10},{10... | collective-permute-start | bytes 73736 | tf_op jit(solution)/shard_map/ppermute | solution.py:180
  24.3 1.2 %collective-permute-done.5.refs_3_ = f32[8,768]{1,0:T(8,128)S(1)} collective-permute-done((f32[8,768]{1,0:T(8,128)S(1)}, f32[8,768]{1,0:T(8,128)S(1)}, u32[]{:S(2)}, u32[]{:S(2)}) %collective-permute-start.5) | collective-permute-done | bytes 24608 | tf_op jit(solution)/shard_map/ppermute | solution.py:180
  25.6 0.2 collective-permute-done.6.refs_4_
  25.8 0.0 collective-permute-done.7.refs_5_
  25.8 0.0 collective-permute-done.8.refs_6_
  25.8 0.0 collective-permute-done.9.refs_7_
  25.8 1.3 %shard_map.150 = (f32[4,64,128]{2,1,0:T(8,128)S(1)}, f32[6,40,128]{2,1,0:T(8,128)S(1)}, f32[2,64,128]{2,1,0:T(8,128)S(1)}) custom-call(f32[4,64,128]{2,1,0:T(8,128)S(1)} %get-tuple-element.38.refs_0_, f32[72,128]{1,0:T(8,128)S(1)} %get-tuple-element.39.refs_1_, f32[8,768]{1,0:T(8,128)S(1)} %collective-permute-done.4.refs_2_, ...), custom_call_target="tpu_custom_call" | custom-call | tf_op jit(solution)/shard_map/pallas_call | solution.py:167
  27.1 0.0 copy-start
  27.1 1.1 %collective-permute-start.10 = (f32[6,40,128]{2,1,0:T(8,128)S(1)}, f32[6,40,128]{2,1,0:T(8,128)S(1)}, u32[]{:S(2)}, u32[]{:S(2)}) collective-permute-start(f32[6,40,128]{2,1,0:T(8,128)S(1)} %get-tuple-element.49.refs_5_), channel_id=1, source_target_pairs={{0,2},{1,3},{2,0},{3,1},{4,6},{5,7},{6,4},{7,5},{8,10},{9,11},{10,... | collective-permute-start | bytes 368648 | tf_op jit(solution)/shard_map/ppermute | solution.py:187
  28.2 0.8 %shard_map.151.refs_4_ = f32[8,128,128]{2,1,0:T(8,128)} custom-call(f32[8,128,128]{2,1,0:T(8,128)S(1)} %get-tuple-element.28.refs_0_.u_ref.refs_2_, f32[4,128,128]{2,1,0:T(8,128)S(1)} %get-tuple-element.48.ixy_ref.refs_3_), custom_call_target="tpu_custom_call" | custom-call | tf_op jit(solution)/shard_map/pallas_call | solution.py:167
  29.1 3.1 %collective-permute-start.11 = (f32[6,40,128]{2,1,0:T(8,128)S(1)}, f32[6,40,128]{2,1,0:T(8,128)S(1)}, u32[]{:S(2)}, u32[]{:S(2)}) collective-permute-start(f32[6,40,128]{2,1,0:T(8,128)S(1)} %get-tuple-element.49.refs_5_), channel_id=1, source_target_pairs={{0,1},{1,0},{2,3},{3,2},{4,5},{5,4},{6,7},{7,6},{8,9},{9,8},{10,11... | collective-permute-start | bytes 368648 | tf_op jit(solution)/shard_map/ppermute | solution.py:187
  32.2 2.5 %collective-permute-start.12 = (f32[6,40,128]{2,1,0:T(8,128)S(1)}, f32[6,40,128]{2,1,0:T(8,128)S(1)}, u32[]{:S(2)}, u32[]{:S(2)}) collective-permute-start(f32[6,40,128]{2,1,0:T(8,128)S(1)} %collective-permute-done.10.refs_7_), channel_id=1, source_target_pairs={{0,1},{1,0},{2,3},{3,2},{4,5},{5,4},{6,7},{7,6},{8,9},{9,8},{10,11... | collective-permute-start | bytes 368648 | tf_op jit(solution)/shard_map/ppermute | solution.py:187
  34.7 0.0 collective-permute-done.11.refs_6_
  34.7 1.0 %collective-permute-done.12.refs_8_ = f32[6,40,128]{2,1,0:T(8,128)S(1)} collective-permute-done((f32[6,40,128]{2,1,0:T(8,128)S(1)}, f32[6,40,128]{2,1,0:T(8,128)S(1)}, u32[]{:S(2)}, u32[]{:S(2)}) %collective-permute-start.12) | collective-permute-done | bytes 122912 | tf_op jit(solution)/shard_map/ppermute | solution.py:187
  35.7 2.3 %shard_map.152 = (f32[8,128,128]{2,1,0:T(8,128)}, f32[4,64,64]{2,1,0:T(8,128)}, f32[2,32,32]{2,1,0:T(8,128)}, f32[1,16,16]{2,1,0:T(8,128)}) custom-call(f32[4,64,128]{2,1,0:T(8,128)S(1)} %get-tuple-element.46.refs_0_, f32[2,64,128]{2,1,0:T(8,128)S(1)} %get-tuple-element.47.refs_1_, ...), custom_call_target="tpu_custom_call", output_to_operand_aliasing={{0}: (4, {})} | custom-call | tf_op jit(solution)/shard_map/pallas_call | solution.py:167
  (16 shorter events, 0.0 us)
Async XLA Ops:
  2.4 12.4 %copy-start.1 = (f32[4,128,136]{2,1,0:T(8,128)S(1)}, f32[4,128,136]{2,1,0:T(8,128)}, u32[]{:S(2)}) copy-start(f32[4,128,136]{2,1,0:T(8,128)} %constant.24.clone.refs_6_) | copy-start | bytes 835588
  2.4 3.8 %collective-permute-start = (f32[16,1024]{1,0:T(8,128)S(1)}, f32[16,1024]{1,0:T(8,128)S(1)}, u32[]{:S(2)}, u32[]{:S(2)}) collective-permute-start(f32[16,1024]{1,0:T(8,128)S(1)} %get-tuple-element.29), channel_id=1, source_target_pairs={{0,4},{4,0},{1,5},{5,1},{2,6},{6,2},{3,7},{7,3},{8,12},{12,8},{9,1... | collective-permute-start | bytes 196616 | tf_op jit(solution)/shard_map/ppermute | solution.py:180
  6.2 8.6 %copy-start.7 = (f32[4,24,64]{2,1,0:T(8,128)S(1)}, f32[4,24,64]{2,1,0:T(8,128)}, u32[]{:S(2)}) copy-start(f32[4,24,64]{2,1,0:T(8,128)} %constant.30.clone.refs_7_) | copy-start | bytes 73732
  7.7 4.7 %collective-permute-start.1 = (f32[24,128]{1,0:T(8,128)S(1)}, f32[24,128]{1,0:T(8,128)S(1)}, u32[]{:S(2)}, u32[]{:S(2)}) collective-permute-start(f32[24,128]{1,0:T(8,128)S(1)} %get-tuple-element.35), channel_id=1, source_target_pairs={{0,24},{8,16},{16,8},{24,0},{1,25},{9,17},{17,9},{25,1},{2,26},{10... | collective-permute-start | bytes 36872 | tf_op jit(solution)/shard_map/ppermute | solution.py:180
  11.3 3.4 %collective-permute-start.2 = (f32[24,128]{1,0:T(8,128)S(1)}, f32[24,128]{1,0:T(8,128)S(1)}, u32[]{:S(2)}, u32[]{:S(2)}) collective-permute-start(f32[24,128]{1,0:T(8,128)S(1)} %get-tuple-element.36), channel_id=1, source_target_pairs={{0,16},{8,24},{16,0},{24,8},{1,17},{9,25},{17,1},{25,9},{2,18},{10... | collective-permute-start | bytes 36872 | tf_op jit(solution)/shard_map/ppermute | solution.py:180
  11.3 3.4 %collective-permute-start.3 = (f32[24,128]{1,0:T(8,128)S(1)}, f32[24,128]{1,0:T(8,128)S(1)}, u32[]{:S(2)}, u32[]{:S(2)}) collective-permute-start(f32[24,128]{1,0:T(8,128)S(1)} %get-tuple-element.37), channel_id=1, source_target_pairs={{0,8},{8,0},{16,24},{24,16},{1,9},{9,1},{17,25},{25,17},{2,10},{10... | collective-permute-start | bytes 36872 | tf_op jit(solution)/shard_map/ppermute | solution.py:180
  14.8 11.1 %copy-start.2 = (f32[2,512,128]{2,1,0:T(8,128)S(1)}, f32[2,512,128]{2,1,0:T(8,128)}, u32[]{:S(2)}) copy-start(f32[2,512,128]{2,1,0:T(8,128)} %constant.26.clone.refs_9_) | copy-start | bytes 1572868
  14.8 11.1 %copy-start.3 = (f32[4,184,88]{2,1,0:T(8,128)S(1)}, f32[4,184,88]{2,1,0:T(8,128)}, u32[]{:S(2)}) copy-start(f32[4,184,88]{2,1,0:T(8,128)} %constant.25.clone.refs_8_) | copy-start | bytes 777220
  15.7 6.7 %collective-permute-start.4 = (f32[8,768]{1,0:T(8,128)S(1)}, f32[8,768]{1,0:T(8,128)S(1)}, u32[]{:S(2)}, u32[]{:S(2)}) collective-permute-start(f32[8,768]{1,0:T(8,128)S(1)} %get-tuple-element.40), channel_id=1, source_target_pairs={{0,24},{8,16},{16,8},{24,0},{1,25},{9,17},{17,9},{25,1},{2,26},{10... | collective-permute-start | bytes 73736 | tf_op jit(solution)/shard_map/ppermute | solution.py:180
  16.9 8.9 %collective-permute-start.7 = (f32[64,128]{1,0:T(8,128)S(1)}, f32[64,128]{1,0:T(8,128)S(1)}, u32[]{:S(2)}, u32[]{:S(2)}) collective-permute-start(f32[64,128]{1,0:T(8,128)S(1)} %get-tuple-element.43), channel_id=1, source_target_pairs={{0,3},{1,2},{2,1},{3,0},{4,7},{5,6},{6,5},{7,4},{8,11},{9,10},{10,... | collective-permute-start | bytes 98312 | tf_op jit(solution)/shard_map/ppermute | solution.py:180
  21.5 4.3 %collective-permute-start.8 = (f32[64,128]{1,0:T(8,128)S(1)}, f32[64,128]{1,0:T(8,128)S(1)}, u32[]{:S(2)}, u32[]{:S(2)}) collective-permute-start(f32[64,128]{1,0:T(8,128)S(1)} %get-tuple-element.44), channel_id=1, source_target_pairs={{0,2},{1,3},{2,0},{3,1},{4,6},{5,7},{6,4},{7,5},{8,10},{9,11},{10,... | collective-permute-start | bytes 98312 | tf_op jit(solution)/shard_map/ppermute | solution.py:180
  21.8 4.0 %collective-permute-start.9 = (f32[64,128]{1,0:T(8,128)S(1)}, f32[64,128]{1,0:T(8,128)S(1)}, u32[]{:S(2)}, u32[]{:S(2)}) collective-permute-start(f32[64,128]{1,0:T(8,128)S(1)} %get-tuple-element.45), channel_id=1, source_target_pairs={{0,1},{1,0},{2,3},{3,2},{4,5},{5,4},{6,7},{7,6},{8,9},{9,8},{10,11... | collective-permute-start | bytes 98312 | tf_op jit(solution)/shard_map/ppermute | solution.py:180
  22.0 3.6 %collective-permute-start.5 = (f32[8,768]{1,0:T(8,128)S(1)}, f32[8,768]{1,0:T(8,128)S(1)}, u32[]{:S(2)}, u32[]{:S(2)}) collective-permute-start(f32[8,768]{1,0:T(8,128)S(1)} %get-tuple-element.41), channel_id=1, source_target_pairs={{0,16},{8,24},{16,0},{24,8},{1,17},{9,25},{17,1},{25,9},{2,18},{10... | collective-permute-start | bytes 73736 | tf_op jit(solution)/shard_map/ppermute | solution.py:180
  22.4 3.4 %collective-permute-start.6 = (f32[8,768]{1,0:T(8,128)S(1)}, f32[8,768]{1,0:T(8,128)S(1)}, u32[]{:S(2)}, u32[]{:S(2)}) collective-permute-start(f32[8,768]{1,0:T(8,128)S(1)} %get-tuple-element.42), channel_id=1, source_target_pairs={{0,8},{8,0},{16,24},{24,16},{1,9},{9,1},{17,25},{25,17},{2,10},{10... | collective-permute-start | bytes 73736 | tf_op jit(solution)/shard_map/ppermute | solution.py:180
  27.1 8.6 %copy-start = (f32[2,768,128]{2,1,0:T(8,128)S(1)}, f32[2,768,128]{2,1,0:T(8,128)}, u32[]{:S(2)}) copy-start(f32[2,768,128]{2,1,0:T(8,128)} %constant.28.clone.refs_11_) | copy-start | bytes 2359300
  27.1 5.0 %collective-permute-start.10 = (f32[6,40,128]{2,1,0:T(8,128)S(1)}, f32[6,40,128]{2,1,0:T(8,128)S(1)}, u32[]{:S(2)}, u32[]{:S(2)}) collective-permute-start(f32[6,40,128]{2,1,0:T(8,128)S(1)} %get-tuple-element.49.refs_5_), channel_id=1, source_target_pairs={{0,2},{1,3},{2,0},{3,1},{4,6},{5,7},{6,4},{7,5},{8,10},{9,11},{10,... | collective-permute-start | bytes 368648 | tf_op jit(solution)/shard_map/ppermute | solution.py:187
  28.2 7.5 %copy-start.4 = (f32[4,144,40]{2,1,0:T(8,128)S(1)}, f32[4,144,40]{2,1,0:T(8,128)}, u32[]{:S(2)}) copy-start(f32[4,144,40]{2,1,0:T(8,128)} %constant.27.clone.refs_10_) | copy-start | bytes 276484
  28.2 7.5 %copy-start.5 = (f32[2,128,128]{2,1,0:T(8,128)S(1)}, f32[2,128,128]{2,1,0:T(8,128)}, u32[]{:S(2)}) copy-start(f32[2,128,128]{2,1,0:T(8,128)} %constant.32.clone.refs_12_) | copy-start | bytes 393220
  28.2 7.5 %copy-start.6 = (f32[128,80]{1,0:T(8,128)S(1)}, f32[128,80]{1,0:T(8,128)}, u32[]{:S(2)}) copy-start(f32[128,80]{1,0:T(8,128)} %constant.31.clone.refs_9_) | copy-start | bytes 122884
  29.1 5.6 %collective-permute-start.11 = (f32[6,40,128]{2,1,0:T(8,128)S(1)}, f32[6,40,128]{2,1,0:T(8,128)S(1)}, u32[]{:S(2)}, u32[]{:S(2)}) collective-permute-start(f32[6,40,128]{2,1,0:T(8,128)S(1)} %get-tuple-element.49.refs_5_), channel_id=1, source_target_pairs={{0,1},{1,0},{2,3},{3,2},{4,5},{5,4},{6,7},{7,6},{8,9},{9,8},{10,11... | collective-permute-start | bytes 368648 | tf_op jit(solution)/shard_map/ppermute | solution.py:187
  32.2 3.5 %collective-permute-start.12 = (f32[6,40,128]{2,1,0:T(8,128)S(1)}, f32[6,40,128]{2,1,0:T(8,128)S(1)}, u32[]{:S(2)}, u32[]{:S(2)}) collective-permute-start(f32[6,40,128]{2,1,0:T(8,128)S(1)} %collective-permute-done.10.refs_7_), channel_id=1, source_target_pairs={{0,1},{1,0},{2,3},{3,2},{4,5},{5,4},{6,7},{7,6},{8,9},{9,8},{10,11... | collective-permute-start | bytes 368648 | tf_op jit(solution)/shard_map/ppermute | solution.py:187

commit v7 on v6

--- a/solution.py
+++ b/solution.py
@@ -642,8 +642,11 @@
         [ta_v, tsm_v, iy, *xcame[::-1], tables_x, to32(f2x)],
         scratch=[pltpu.VMEM((lz, ext, 2 * wide), jnp.float32)],
     )
+    tails = sent[dz - 1 :]
     zcame = swapped(sent[: dz - 1], "gz")
-    xtcame = swapped(sent[dz - 1 :], "gx")
+    if dz > 1 and dx > 1:
+        zcame[0], tails[0] = lax.optimization_barrier((zcame[0], tails[0]))
+    xtcame = swapped(tails, "gx")
     u1, zmsg, i2 = kernel_call(
         second_apply,
         [(zn, xone.n, wide), (lz2 + 2, tall, packed), (lz2 // 2, xtwo.fine, ly2)],

time: 38.5 us -> 37.6 us (0.977)
  starting transfers between devices: 21.5 us -> 20.3 us
    ppermute x3, starting transfers between devices: 6.75 us -> 5.96 us  [gathered(): lax.ppermute(what, axis, [(i, i ^ k) for i in range(count)])]
  transfers between devices with their start and end apart: 13 -> 13, of which waited for: 6 -> 7; matrix products, arithmetic and copies ran while one was open for 0% -> 0% of each run, Pallas kernels for 2% -> 2%
where the time goes in v7:
time: 37.6 us; the launch traced here: 37.1 us
  starting transfers between devices  20.3 us (54%)
  Pallas kernels  8.52 us (23%)
  waiting for transfers between devices  7.46 us (20%)
  between operations  0.71 us (2%)
    ppermute x10, starting transfers between devices, swapped(): lax.ppermute(v, axis, [(i, i ^ k) for i in range(count)])  14.4 us
    pallas_call x6, Pallas kernels, kernel_call(): pl.pallas_call(body, out_shape=[jax.ShapeDtypeStruct(shape, jnp.float32)...  8.52 us
    ppermute x10, waiting for transfers between devices, swapped(): lax.ppermute(v, axis, [(i, i ^ k) for i in range(count)])  6.49 us
    ppermute x3, starting transfers between devices, gathered(): lax.ppermute(what, axis, [(i, i ^ k) for i in range(count)])  5.96 us
    ppermute x3, waiting for transfers between devices, gathered(): lax.ppermute(what, axis, [(i, i ^ k) for i in range(count)])  0.98 us
  transfers between devices with their start and end apart: 13, of which 7 were waited for; matrix products, arithmetic and copies ran while one was open for 0% of the time, Pallas kernels for 2%

profile of v7, /device:TPU:1, one launch (start us, length us, event | category | flops | bytes accessed | tf_op | source)
XLA Modules:
  0.0 37.1 jit_solution(18073602291514803539)
XLA Ops:
  0.6 1.8 %shard_map.147 = (f32[8,128,128]{2,1,0:T(8,128)S(1)}, f32[160,384]{1,0:T(8,128)S(1)}, f32[128,8]{1,0:T(8,128)S(1)}, f32[16,1024]{1,0:T(8,128)S(1)}) custom-call(f32[8,128,128]{2,1,0:T(8,128)} %u_hbm.1, f32[2,32,128]{2,1,0:T(8,128)} %constant.22.clone.table_hbm, f32[2,160,384]{2,1,0:T(8,128)} %constant.23.clone.ty_hbm, f32[4,128,8]{2,1,0:T(8,128)} %constant.29.clone.fx_hbm), custom_call_target="tpu_custom_call" | custom-call | tf_op jit(solution)/shard_map/pallas_call | solution.py:167
  2.4 0.0 copy-start.1
  2.4 2.1 %collective-permute-start = (f32[16,1024]{1,0:T(8,128)S(1)}, f32[16,1024]{1,0:T(8,128)S(1)}, u32[]{:S(2)}, u32[]{:S(2)}) collective-permute-start(f32[16,1024]{1,0:T(8,128)S(1)} %get-tuple-element.31), channel_id=1, source_target_pairs={{0,4},{4,0},{1,5},{5,1},{2,6},{6,2},{3,7},{7,3},{8,12},{12,8},{9,1... | collective-permute-start | bytes 196616 | tf_op jit(solution)/shard_map/ppermute | solution.py:180
  4.5 1.7 %collective-permute-done.refs_1_ = f32[16,1024]{1,0:T(8,128)S(1)} collective-permute-done((f32[16,1024]{1,0:T(8,128)S(1)}, f32[16,1024]{1,0:T(8,128)S(1)}, u32[]{:S(2)}, u32[]{:S(2)}) %collective-permute-start) | collective-permute-done | bytes 65568 | tf_op jit(solution)/shard_map/ppermute | solution.py:180
  6.2 1.5 %shard_map.148 = (f32[1024,128]{1,0:T(8,128)S(1)}, f32[256,256]{1,0:T(8,128)S(1)}, f32[4,128,128]{2,1,0:T(8,128)S(1)}, f32[24,128]{1,0:T(8,128)S(1)}, f32[24,128]{1,0:T(8,128)S(1)}, /*index=5*/f32[24,128]{1,0:T(8,128)S(1)}) custom-call(f32[8,128,128]{2,1,0:T(8,128)S(1)} %get-tuple-element.30.refs_0_.u_ref.refs_2_, ...), custom_call_target="tpu_custom_call" | custom-call | tf_op jit(solution)/shard_map/pallas_call | solution.py:167
  7.7 3.6 %collective-permute-start.1 = (f32[24,128]{1,0:T(8,128)S(1)}, f32[24,128]{1,0:T(8,128)S(1)}, u32[]{:S(2)}, u32[]{:S(2)}) collective-permute-start(f32[24,128]{1,0:T(8,128)S(1)} %get-tuple-element.37), channel_id=1, source_target_pairs={{0,24},{8,16},{16,8},{24,0},{1,25},{9,17},{17,9},{25,1},{2,26},{10... | collective-permute-start | bytes 36872 | tf_op jit(solution)/shard_map/ppermute | solution.py:180
  11.3 0.0 collective-permute-start.2
  11.3 0.4 collective-permute-start.3
  11.7 0.7 %collective-permute-done.1.refs_3_ = f32[24,128]{1,0:T(8,128)S(1)} collective-permute-done((f32[24,128]{1,0:T(8,128)S(1)}, f32[24,128]{1,0:T(8,128)S(1)}, u32[]{:S(2)}, u32[]{:S(2)}) %collective-permute-start.1) | collective-permute-done | bytes 12320 | tf_op jit(solution)/shard_map/ppermute | solution.py:180
  12.4 2.4 %collective-permute-done.2.refs_4_ = f32[24,128]{1,0:T(8,128)S(1)} collective-permute-done((f32[24,128]{1,0:T(8,128)S(1)}, f32[24,128]{1,0:T(8,128)S(1)}, u32[]{:S(2)}, u32[]{:S(2)}) %collective-permute-start.2) | collective-permute-done | bytes 12320 | tf_op jit(solution)/shard_map/ppermute | solution.py:180
  14.8 0.0 copy-start.2
  14.8 0.0 copy-start.3
  14.8 0.9 %shard_map.149 = (f32[4,128,128]{2,1,0:T(8,128)S(1)}, f32[72,128]{1,0:T(8,128)S(1)}, f32[4,64,128]{2,1,0:T(8,128)S(1)}, f32[64,128]{1,0:T(8,128)S(1)}, f32[64,12...) custom-call(f32[1024,128]{1,0:T(8,128)S(1)} %get-tuple-element.34.re, ...), custom_call_target="tpu_custom_call" | custom-call | tf_op jit(solution)/shard_map/pallas_call | solution.py:167
  15.7 3.3 %collective-permute-start.6 = (f32[64,128]{1,0:T(8,128)S(1)}, f32[64,128]{1,0:T(8,128)S(1)}, u32[]{:S(2)}, u32[]{:S(2)}) collective-permute-start(f32[64,128]{1,0:T(8,128)S(1)} %get-tuple-element.44), channel_id=1, source_target_pairs={{0,1},{1,0},{2,3},{3,2},{4,5},{5,4},{6,7},{7,6},{8,9},{9,8},{10,11... | collective-permute-start | bytes 98312 | tf_op jit(solution)/shard_map/ppermute | solution.py:180
  19.0 1.2 %collective-permute-start.8 = (f32[64,128]{1,0:T(8,128)S(1)}, f32[64,128]{1,0:T(8,128)S(1)}, u32[]{:S(2)}, u32[]{:S(2)}) collective-permute-start(f32[64,128]{1,0:T(8,128)S(1)} %get-tuple-element.47), channel_id=1, source_target_pairs={{0,3},{1,2},{2,1},{3,0},{4,7},{5,6},{6,5},{7,4},{8,11},{9,10},{10,... | collective-permute-start | bytes 98312 | tf_op jit(solution)/shard_map/ppermute | solution.py:180
  20.2 0.3 collective-permute-start.9
  20.4 1.2 %collective-permute-start.4 = (f32[8,768]{1,0:T(8,128)S(1)}, f32[8,768]{1,0:T(8,128)S(1)}, u32[]{:S(2)}, u32[]{:S(2)}) collective-permute-start(f32[8,768]{1,0:T(8,128)S(1)} %get-tuple-element.42), channel_id=1, source_target_pairs={{0,24},{8,16},{16,8},{24,0},{1,25},{9,17},{17,9},{25,1},{2,26},{10... | collective-permute-start | bytes 73736 | tf_op jit(solution)/shard_map/ppermute | solution.py:180
  21.6 0.6 %collective-permute-start.5 = (f32[8,768]{1,0:T(8,128)S(1)}, f32[8,768]{1,0:T(8,128)S(1)}, u32[]{:S(2)}, u32[]{:S(2)}) collective-permute-start(f32[8,768]{1,0:T(8,128)S(1)} %get-tuple-element.43), channel_id=1, source_target_pairs={{0,16},{8,24},{16,0},{24,8},{1,17},{9,25},{17,1},{25,9},{2,18},{10... | collective-permute-start | bytes 73736 | tf_op jit(solution)/shard_map/ppermute | solution.py:180
  22.2 0.0 collective-permute-done.6.refs_7_
  22.2 1.8 %collective-permute-start.7 = (f32[8,768]{1,0:T(8,128)S(1)}, f32[8,768]{1,0:T(8,128)S(1)}, u32[]{:S(2)}, u32[]{:S(2)}) collective-permute-start(f32[8,768]{1,0:T(8,128)S(1)} %get-tuple-element.46), channel_id=1, source_target_pairs={{0,8},{8,0},{16,24},{24,16},{1,9},{9,1},{17,25},{25,17},{2,10},{10... | collective-permute-start | bytes 73736 | tf_op jit(solution)/shard_map/ppermute | solution.py:180
  24.0 0.9 %collective-permute-done.4.refs_2_ = f32[8,768]{1,0:T(8,128)S(1)} collective-permute-done((f32[8,768]{1,0:T(8,128)S(1)}, f32[8,768]{1,0:T(8,128)S(1)}, u32[]{:S(2)}, u32[]{:S(2)}) %collective-permute-start.4) | collective-permute-done | bytes 24608 | tf_op jit(solution)/shard_map/ppermute | solution.py:180
  24.9 0.3 collective-permute-done.5.refs_3_
  25.2 0.0 collective-permute-done.8.refs_5_
  25.2 0.5 %collective-permute-done.7.refs_4_ = f32[8,768]{1,0:T(8,128)S(1)} collective-permute-done((f32[8,768]{1,0:T(8,128)S(1)}, f32[8,768]{1,0:T(8,128)S(1)}, u32[]{:S(2)}, u32[]{:S(2)}) %collective-permute-start.7) | collective-permute-done | bytes 24608 | tf_op jit(solution)/shard_map/ppermute | solution.py:180
  25.7 1.3 %shard_map.150 = (f32[4,64,128]{2,1,0:T(8,128)S(1)}, f32[6,40,128]{2,1,0:T(8,128)S(1)}, f32[2,64,128]{2,1,0:T(8,128)S(1)}) custom-call(f32[4,64,128]{2,1,0:T(8,128)S(1)} %get-tuple-element.40.refs_0_, f32[72,128]{1,0:T(8,128)S(1)} %get-tuple-element.41.refs_1_, f32[8,768]{1,0:T(8,128)S(1)} %collective-permute-done.4.refs_2_, ...), custom_call_target="tpu_custom_call" | custom-call | tf_op jit(solution)/shard_map/pallas_call | solution.py:167
  27.0 0.0 copy-start
  27.0 1.3 %collective-permute-start.10 = (f32[6,40,128]{2,1,0:T(8,128)S(1)}, f32[6,40,128]{2,1,0:T(8,128)S(1)}, u32[]{:S(2)}, u32[]{:S(2)}) collective-permute-start(f32[6,40,128]{2,1,0:T(8,128)S(1)} %get-tuple-element.53.refs_5_), channel_id=1, source_target_pairs={{0,2},{1,3},{2,0},{3,1},{4,6},{5,7},{6,4},{7,5},{8,10},{9,11},{10,... | collective-permute-start | bytes 368648 | tf_op jit(solution)/shard_map/ppermute | solution.py:187
  28.3 0.8 %shard_map.151.refs_4_ = f32[8,128,128]{2,1,0:T(8,128)} custom-call(f32[8,128,128]{2,1,0:T(8,128)S(1)} %get-tuple-element.30.refs_0_.u_ref.refs_2_, f32[4,128,128]{2,1,0:T(8,128)S(1)} %get-tuple-element.52.ixy_ref.refs_3_), custom_call_target="tpu_custom_call" | custom-call | tf_op jit(solution)/shard_map/pallas_call | solution.py:167
  29.1 2.1 %collective-permute-start.11 = (f32[6,40,128]{2,1,0:T(8,128)S(1)}, f32[6,40,128]{2,1,0:T(8,128)S(1)}, u32[]{:S(2)}, u32[]{:S(2)}) collective-permute-start(f32[6,40,128]{2,1,0:T(8,128)S(1)} %get-tuple-element.53.refs_5_), channel_id=1, source_target_pairs={{0,1},{1,0},{2,3},{3,2},{4,5},{5,4},{6,7},{7,6},{8,9},{9,8},{10,11... | collective-permute-start | bytes 368648 | tf_op jit(solution)/shard_map/ppermute | solution.py:187
  31.3 2.5 %collective-permute-start.12 = (f32[6,40,128]{2,1,0:T(8,128)S(1)}, f32[6,40,128]{2,1,0:T(8,128)S(1)}, u32[]{:S(2)}, u32[]{:S(2)}) collective-permute-start(f32[6,40,128]{2,1,0:T(8,128)S(1)} %collective-permute-done.10.refs_7_), channel_id=1, source_target_pairs={{0,1},{1,0},{2,3},{3,2},{4,5},{5,4},{6,7},{7,6},{8,9},{9,8},{10,11... | collective-permute-start | bytes 368648 | tf_op jit(solution)/shard_map/ppermute | solution.py:187
  33.8 1.0 %collective-permute-done.12.refs_8_ = f32[6,40,128]{2,1,0:T(8,128)S(1)} collective-permute-done((f32[6,40,128]{2,1,0:T(8,128)S(1)}, f32[6,40,128]{2,1,0:T(8,128)S(1)}, u32[]{:S(2)}, u32[]{:S(2)}) %collective-permute-start.12) | collective-permute-done | bytes 122912 | tf_op jit(solution)/shard_map/ppermute | solution.py:187
  34.8 2.3 %shard_map.152 = (f32[8,128,128]{2,1,0:T(8,128)}, f32[4,64,64]{2,1,0:T(8,128)}, f32[2,32,32]{2,1,0:T(8,128)}, f32[1,16,16]{2,1,0:T(8,128)}) custom-call(f32[4,64,128]{2,1,0:T(8,128)S(1)} %get-tuple-element.50.refs_0_, f32[2,64,128]{2,1,0:T(8,128)S(1)} %get-tuple-element.51.refs_1_, ...), custom_call_target="tpu_custom_call", output_to_operand_aliasing={{0}: (4, {})} | custom-call | tf_op jit(solution)/shard_map/pallas_call | solution.py:167
  (16 shorter events, 0.0 us)
Async XLA Ops:
  2.4 12.4 %copy-start.1 = (f32[4,128,136]{2,1,0:T(8,128)S(1)}, f32[4,128,136]{2,1,0:T(8,128)}, u32[]{:S(2)}) copy-start(f32[4,128,136]{2,1,0:T(8,128)} %constant.24.clone.refs_6_) | copy-start | bytes 835588
  2.4 3.8 %collective-permute-start = (f32[16,1024]{1,0:T(8,128)S(1)}, f32[16,1024]{1,0:T(8,128)S(1)}, u32[]{:S(2)}, u32[]{:S(2)}) collective-permute-start(f32[16,1024]{1,0:T(8,128)S(1)} %get-tuple-element.31), channel_id=1, source_target_pairs={{0,4},{4,0},{1,5},{5,1},{2,6},{6,2},{3,7},{7,3},{8,12},{12,8},{9,1... | collective-permute-start | bytes 196616 | tf_op jit(solution)/shard_map/ppermute | solution.py:180
  6.2 8.6 %copy-start.7 = (f32[4,24,64]{2,1,0:T(8,128)S(1)}, f32[4,24,64]{2,1,0:T(8,128)}, u32[]{:S(2)}) copy-start(f32[4,24,64]{2,1,0:T(8,128)} %constant.30.clone.refs_7_) | copy-start | bytes 73732
  7.7 4.7 %collective-permute-start.1 = (f32[24,128]{1,0:T(8,128)S(1)}, f32[24,128]{1,0:T(8,128)S(1)}, u32[]{:S(2)}, u32[]{:S(2)}) collective-permute-start(f32[24,128]{1,0:T(8,128)S(1)} %get-tuple-element.37), channel_id=1, source_target_pairs={{0,24},{8,16},{16,8},{24,0},{1,25},{9,17},{17,9},{25,1},{2,26},{10... | collective-permute-start | bytes 36872 | tf_op jit(solution)/shard_map/ppermute | solution.py:180
  11.3 3.4 %collective-permute-start.2 = (f32[24,128]{1,0:T(8,128)S(1)}, f32[24,128]{1,0:T(8,128)S(1)}, u32[]{:S(2)}, u32[]{:S(2)}) collective-permute-start(f32[24,128]{1,0:T(8,128)S(1)} %get-tuple-element.38), channel_id=1, source_target_pairs={{0,16},{8,24},{16,0},{24,8},{1,17},{9,25},{17,1},{25,9},{2,18},{10... | collective-permute-start | bytes 36872 | tf_op jit(solution)/shard_map/ppermute | solution.py:180
  11.3 3.4 %collective-permute-start.3 = (f32[24,128]{1,0:T(8,128)S(1)}, f32[24,128]{1,0:T(8,128)S(1)}, u32[]{:S(2)}, u32[]{:S(2)}) collective-permute-start(f32[24,128]{1,0:T(8,128)S(1)} %get-tuple-element.39), channel_id=1, source_target_pairs={{0,8},{8,0},{16,24},{24,16},{1,9},{9,1},{17,25},{25,17},{2,10},{10... | collective-permute-start | bytes 36872 | tf_op jit(solution)/shard_map/ppermute | solution.py:180
  14.8 11.0 %copy-start.2 = (f32[2,512,128]{2,1,0:T(8,128)S(1)}, f32[2,512,128]{2,1,0:T(8,128)}, u32[]{:S(2)}) copy-start(f32[2,512,128]{2,1,0:T(8,128)} %constant.26.clone.refs_9_) | copy-start | bytes 1572868
  14.8 11.0 %copy-start.3 = (f32[4,184,88]{2,1,0:T(8,128)S(1)}, f32[4,184,88]{2,1,0:T(8,128)}, u32[]{:S(2)}) copy-start(f32[4,184,88]{2,1,0:T(8,128)} %constant.25.clone.refs_8_) | copy-start | bytes 777220
  15.7 6.5 %collective-permute-start.6 = (f32[64,128]{1,0:T(8,128)S(1)}, f32[64,128]{1,0:T(8,128)S(1)}, u32[]{:S(2)}, u32[]{:S(2)}) collective-permute-start(f32[64,128]{1,0:T(8,128)S(1)} %get-tuple-element.44), channel_id=1, source_target_pairs={{0,1},{1,0},{2,3},{3,2},{4,5},{5,4},{6,7},{7,6},{8,9},{9,8},{10,11... | collective-permute-start | bytes 98312 | tf_op jit(solution)/shard_map/ppermute | solution.py:180
  19.0 6.2 %collective-permute-start.8 = (f32[64,128]{1,0:T(8,128)S(1)}, f32[64,128]{1,0:T(8,128)S(1)}, u32[]{:S(2)}, u32[]{:S(2)}) collective-permute-start(f32[64,128]{1,0:T(8,128)S(1)} %get-tuple-element.47), channel_id=1, source_target_pairs={{0,3},{1,2},{2,1},{3,0},{4,7},{5,6},{6,5},{7,4},{8,11},{9,10},{10,... | collective-permute-start | bytes 98312 | tf_op jit(solution)/shard_map/ppermute | solution.py:180
  20.2 5.0 %collective-permute-start.9 = (f32[64,128]{1,0:T(8,128)S(1)}, f32[64,128]{1,0:T(8,128)S(1)}, u32[]{:S(2)}, u32[]{:S(2)}) collective-permute-start(f32[64,128]{1,0:T(8,128)S(1)} %get-tuple-element.48), channel_id=1, source_target_pairs={{0,2},{1,3},{2,0},{3,1},{4,6},{5,7},{6,4},{7,5},{8,10},{9,11},{10,... | collective-permute-start | bytes 98312 | tf_op jit(solution)/shard_map/ppermute | solution.py:180
  20.4 4.5 %collective-permute-start.4 = (f32[8,768]{1,0:T(8,128)S(1)}, f32[8,768]{1,0:T(8,128)S(1)}, u32[]{:S(2)}, u32[]{:S(2)}) collective-permute-start(f32[8,768]{1,0:T(8,128)S(1)} %get-tuple-element.42), channel_id=1, source_target_pairs={{0,24},{8,16},{16,8},{24,0},{1,25},{9,17},{17,9},{25,1},{2,26},{10... | collective-permute-start | bytes 73736 | tf_op jit(solution)/shard_map/ppermute | solution.py:180
  21.6 3.6 %collective-permute-start.5 = (f32[8,768]{1,0:T(8,128)S(1)}, f32[8,768]{1,0:T(8,128)S(1)}, u32[]{:S(2)}, u32[]{:S(2)}) collective-permute-start(f32[8,768]{1,0:T(8,128)S(1)} %get-tuple-element.43), channel_id=1, source_target_pairs={{0,16},{8,24},{16,0},{24,8},{1,17},{9,25},{17,1},{25,9},{2,18},{10... | collective-permute-start | bytes 73736 | tf_op jit(solution)/shard_map/ppermute | solution.py:180
  22.2 3.6 %collective-permute-start.7 = (f32[8,768]{1,0:T(8,128)S(1)}, f32[8,768]{1,0:T(8,128)S(1)}, u32[]{:S(2)}, u32[]{:S(2)}) collective-permute-start(f32[8,768]{1,0:T(8,128)S(1)} %get-tuple-element.46), channel_id=1, source_target_pairs={{0,8},{8,0},{16,24},{24,16},{1,9},{9,1},{17,25},{25,17},{2,10},{10... | collective-permute-start | bytes 73736 | tf_op jit(solution)/shard_map/ppermute | solution.py:180
  27.0 7.8 %copy-start = (f32[2,768,128]{2,1,0:T(8,128)S(1)}, f32[2,768,128]{2,1,0:T(8,128)}, u32[]{:S(2)}) copy-start(f32[2,768,128]{2,1,0:T(8,128)} %constant.28.clone.refs_11_) | copy-start | bytes 2359300
  27.0 4.3 %collective-permute-start.10 = (f32[6,40,128]{2,1,0:T(8,128)S(1)}, f32[6,40,128]{2,1,0:T(8,128)S(1)}, u32[]{:S(2)}, u32[]{:S(2)}) collective-permute-start(f32[6,40,128]{2,1,0:T(8,128)S(1)} %get-tuple-element.53.refs_5_), channel_id=1, source_target_pairs={{0,2},{1,3},{2,0},{3,1},{4,6},{5,7},{6,4},{7,5},{8,10},{9,11},{10,... | collective-permute-start | bytes 368648 | tf_op jit(solution)/shard_map/ppermute | solution.py:187
  28.3 6.5 %copy-start.4 = (f32[4,144,40]{2,1,0:T(8,128)S(1)}, f32[4,144,40]{2,1,0:T(8,128)}, u32[]{:S(2)}) copy-start(f32[4,144,40]{2,1,0:T(8,128)} %constant.27.clone.refs_10_) | copy-start | bytes 276484
  28.3 6.5 %copy-start.5 = (f32[2,128,128]{2,1,0:T(8,128)S(1)}, f32[2,128,128]{2,1,0:T(8,128)}, u32[]{:S(2)}) copy-start(f32[2,128,128]{2,1,0:T(8,128)} %constant.32.clone.refs_12_) | copy-start | bytes 393220
  28.3 6.5 %copy-start.6 = (f32[128,80]{1,0:T(8,128)S(1)}, f32[128,80]{1,0:T(8,128)}, u32[]{:S(2)}) copy-start(f32[128,80]{1,0:T(8,128)} %constant.31.clone.refs_9_) | copy-start | bytes 122884
  29.1 4.7 %collective-permute-start.11 = (f32[6,40,128]{2,1,0:T(8,128)S(1)}, f32[6,40,128]{2,1,0:T(8,128)S(1)}, u32[]{:S(2)}, u32[]{:S(2)}) collective-permute-start(f32[6,40,128]{2,1,0:T(8,128)S(1)} %get-tuple-element.53.refs_5_), channel_id=1, source_target_pairs={{0,1},{1,0},{2,3},{3,2},{4,5},{5,4},{6,7},{7,6},{8,9},{9,8},{10,11... | collective-permute-start | bytes 368648 | tf_op jit(solution)/shard_map/ppermute | solution.py:187
  31.3 3.5 %collective-permute-start.12 = (f32[6,40,128]{2,1,0:T(8,128)S(1)}, f32[6,40,128]{2,1,0:T(8,128)S(1)}, u32[]{:S(2)}, u32[]{:S(2)}) collective-permute-start(f32[6,40,128]{2,1,0:T(8,128)S(1)} %collective-permute-done.10.refs_7_), channel_id=1, source_target_pairs={{0,1},{1,0},{2,3},{3,2},{4,5},{5,4},{6,7},{7,6},{8,9},{9,8},{10,11... | collective-permute-start | bytes 368648 | tf_op jit(solution)/shard_map/ppermute | solution.py:187

commit v8 on v7

--- a/solution.py
+++ b/solution.py
@@ -303,6 +303,7 @@
         for c, table in enumerate(xtwo.tables[j]):
             tx2[j, c * tall : c * tall + table.shape[0], columns] = table.T
         qx2[j][:, columns] = interpolation(xtwo, j, len(columns))
+        tx2[j, tall - 1, xtwo.fine :] = qx2[j, -1, xtwo.fine :]
         for k in range(1, dx):
             mine = xtwo.sent(j, k)
             f2x[j, (k - 1) * kx :][: len(mine)] = xtwo.functionals[j][mine]
@@ -353,8 +354,6 @@
     tables_y, _ = stacked(np.concatenate([ta, tsm], axis=2), np.concatenate([wa, np.zeros((dy, wa.shape[1], 2 * wide))], axis=2),
                           np.concatenate([np.zeros((dy, wsm.shape[1], wide)), wsm], axis=2))
     tables_x, _ = stacked(txa, txm)
-    tables_x2, _ = stacked(tx2, qx2)
-    tables_y2, _ = stacked(ty2, qy2)
     tables_x3, at_x3 = stacked(tx3, qx3, px3)
     tables_y3, at_y3 = stacked(ty3, qy3, py3, py1)
     hz, hx1 = lz // 2, lx // 2
@@ -388,10 +387,21 @@
         for copy in copies[2:]:
             copy.wait()
 
+    def along_y(u, half_halo):
+        lane = iota(u.shape, 1)
+        before, after = pltpu.roll(u, 1, 1), pltpu.roll(u, ly - 1, 1)
+        edge = 0.5 * before + jnp.broadcast_to(half_halo, u.shape)
+        return jnp.where(lane == ly - 1, edge, jnp.where(lane % 2 == 1, 0.5 * (before + after), u))
+
+    def from_next(jx, own, rows):
+        for k, other in enumerate(rows):
+            own = jnp.where((jx ^ (k + 1)) == jx + 1, other, own)
+        return own
+
     def y_apply(*refs):
         u_ref, came = refs[0], refs[1:dy]
-        ty_ref, fx_ref, ta_out, tsm_out, iy_out = refs[dy : dy + 5]
-        xm_outs, points = refs[dy + 5 : -1], refs[-1]
+        ty_ref, fx_ref, ta_out, tsm_out = refs[dy : dy + 4]
+        xm_outs, points = refs[dy + 4 : -1], refs[-1]
         jx = lax.axis_index("gx")
         tn = ((0,), (0,))
         ta_all = dot(u_ref[...].reshape(lz * lx, ly), ty_ref[:ly, :wide])
@@ -409,7 +419,6 @@
             tsm_all += dot(points[...], ty_ref[begin : begin + ss8, wide:], tn)
         ta_out[...] = ta_all
         tsm_out[...] = tsm_all
-        lane = iota((lx, ly), 1)
         weights = [jnp.broadcast_to(fx_ref[:, c : c + 1], (lx, wide)) for c in range(2)]
         for out in xm_outs:
             out[lz + 2 * hz :] = jnp.zeros_like(out[lz + 2 * hz :])
@@ -422,28 +431,18 @@
             if z % 2 == 0:
                 half = z // 2
                 tm = tsm_all[half * hx1 : (half + 1) * hx1, wide:]
-                u = u_ref[z]
-                before, after = pltpu.roll(u, 1, 1), pltpu.roll(u, ly - 1, 1)
-                middle = 0.5 * (before + after)
-                edge = 0.5 * before + jnp.broadcast_to(part[:, wide - 1 : wide], (lx, ly))
-                iy = jnp.where(lane == ly - 1, edge, jnp.where(lane % 2 == 1, middle, u))
-                iy_out[half] = iy
+                iy = along_y(u_ref[z, :8], part[:8, wide - 1 :])
                 for out in xm_outs:
                     out[lz + half : lz + half + 1, :wide] = jnp.where(jx == 0, tm[0:1], tm[hx1 - 1 : hx1])
                     out[lz + hz + half : lz + hz + half + 1, :ly] = iy[0:1]
 
     def x_apply(*refs):
-        ta_ref, tsm_ref, iy_ref = refs[:3]
-        came = refs[3 : 2 + dx][::-1]
-        tx_ref, f2x_ref, ixy_out, zc_out, u1_out = refs[2 + dx : 7 + dx]
-        planes_out, xt_outs, rest = refs[7 + dx : 6 + dx + dz], refs[6 + dx + dz : -1], refs[-1]
+        ta_ref, tsm_ref = refs[:2]
+        came = refs[2 : 1 + dx][::-1]
+        tx_ref, f2x_ref, zc_out, u1_out = refs[1 + dx : 5 + dx]
+        planes_out, xt_outs, rest = refs[5 + dx : 4 + dx + dz], refs[4 + dx + dz : -1], refs[-1]
         jx, jz = lax.axis_index("gx"), lax.axis_index("gz")
         xa, xm, diff = [], [], []
-
-        def from_next(own, rows):
-            for k, other in enumerate(rows):
-                own = jnp.where((jx ^ (k + 1)) == jx + 1, other, own)
-            return own
 
         rest[...] = jnp.zeros_like(rest)
         for k, r in enumerate(came):
@@ -459,8 +458,7 @@
         zc_out[...] = jnp.zeros_like(zc_out)
         zc_out[:hx1] = tsm_ref[:hx1, :wide]
         begin = lz + 2 * hz
-        zc_out[hx1 : hx1 + 1] = from_next(tsm_ref[hx1 - 1 : hx1, :wide], [r[begin : begin + 1, :wide] for r in came])
-        row = iota((lx, ly), 0)
+        zc_out[hx1 : hx1 + 1] = from_next(jx, tsm_ref[hx1 - 1 : hx1, :wide], [r[begin : begin + 1, :wide] for r in came])
         for half in range(0, hz, 2):
             pair = jnp.concatenate([tsm_ref[h * hx1 : (h + 1) * hx1, wide:] for h in (half, half + 1)], axis=1)
             more = jnp.concatenate([rest[half, :, wide:], rest[half + 1, :, wide:]], axis=1)
@@ -468,12 +466,6 @@
             xm += [both[:, :wide], both[:, wide:]]
         for half in range(hz):
             diff.append(tsm_ref[half * hx1 : (half + 1) * hx1, :wide] - xm[half])
-            iy = iy_ref[half]
-            begin = lz + hz + half
-            halo = from_next(iy[lx - 2 : lx - 1], [r[begin : begin + 1, :ly] for r in came])
-            before, after = pltpu.roll(iy, 1, 0), pltpu.roll(iy, lx - 1, 0)
-            after = jnp.where(row == lx - 1, jnp.broadcast_to(halo, (lx, ly)), after)
-            ixy_out[half] = jnp.where(row % 2 == 1, 0.5 * (before + after), iy)
         scalar = lambda place: chosen_by(zs[:, place], jz)
         totals = []
         for zc in range(zn):
@@ -493,17 +485,38 @@
         for k, out in enumerate(xt_outs):
             out[...] = sent[k * kx : (k + 1) * kx]
 
-    def fine_coefficients(u_ref, ixy_ref, out_ref):
+    def interpolate(*refs):
+        u_ref, ta_ref, u1_ref = refs[:3]
+        came, xcame = refs[3 : 2 + dx][::-1], refs[2 + dx : 1 + 2 * dx][::-1]
+        qx2_ref, qy2_ref, fine_out, ixy_out, i2_out = refs[1 + 2 * dx :]
+        jx, jy = lax.axis_index("gx"), lax.axis_index("gy")
+        row = iota((lx, ly), 0)
+        planes = []
         for half in range(hz):
-            here = ixy_ref[half]
-            out_ref[2 * half] = u_ref[2 * half] - here
+            iy = along_y(u_ref[2 * half], ta_ref[2 * half * lx : (2 * half + 1) * lx, wide - 1 :])
+            begin = lz + hz + half
+            halo = from_next(jx, iy[lx - 2 : lx - 1], [r[begin : begin + 1, :ly] for r in came])
+            before, after = pltpu.roll(iy, 1, 0), pltpu.roll(iy, lx - 1, 0)
+            after = jnp.where(row == lx - 1, jnp.broadcast_to(halo, (lx, ly)), after)
+            planes.append(jnp.where(row % 2 == 1, 0.5 * (before + after), iy))
+        for half in range(hz):
+            fine_out[2 * half] = u_ref[2 * half] - planes[half]
             if half + 1 < hz:
-                out_ref[2 * half + 1] = u_ref[2 * half + 1] - 0.5 * (here + ixy_ref[half + 1])
+                fine_out[2 * half + 1] = u_ref[2 * half + 1] - 0.5 * (planes[half] + planes[half + 1])
+        ixy_out[...] = planes[-1]
+        evens = range(0, zn, 2)
+        state = [jnp.concatenate([u1_ref[z] for z in evens], axis=1)]
+        state += [jnp.concatenate([r[:, z * wide : (z + 1) * wide] for z in evens], axis=1) for r in xcame]
+        spread = dot(qx2_ref[jx], jnp.concatenate(state, axis=0))
+        spread = jnp.concatenate([spread[:, half * wide : (half + 1) * wide] for half in range(zn // 2)], axis=0)
+        spread = dot(spread, qy2_ref[jy])
+        for half in range(zn // 2):
+            i2_out[half] = spread[half * xtwo.fine : (half + 1) * xtwo.fine]
 
     def second_apply(*refs):
         part_ref, zc_ref = refs[:2]
         xcame, zcame = refs[2 : dx + 1][::-1], refs[dx + 1 : dz + dx][::-1]
-        tx2_ref, ty2_ref, u1_out, zt_out, i2_out = refs[dz + dx :]
+        tx2_ref, ty2_ref, u1_out, zt_out = refs[dz + dx :]
         jx, jy, jz = lax.axis_index("gx"), lax.axis_index("gy"), lax.axis_index("gz")
         own = []
         for zc in range(zn):
@@ -517,7 +530,7 @@
         cut = [across[:, z * wide : (z + 1) * wide] for z in range(zn + 2)]
         whole = [z for z in range(zn + 2) if z % 2 == 0 or z >= zn]
         joined = [jnp.concatenate([cut[z][c * tall : (c + 1) * tall] for c in range(3)], axis=1) for z in whole]
-        made = dot(jnp.concatenate(joined, axis=0), ty2_ref[jy, : 3 * wide])
+        made = dot(jnp.concatenate(joined, axis=0), ty2_ref[jy])
         for place, z in enumerate(whole):
             zt_out[z] = made[place * tall : (place + 1) * tall]
         made = dot(jnp.concatenate([cut[z][:tall] for z in range(1, zn, 2)], axis=0), ty2_ref[jy, :wide])
@@ -528,10 +541,7 @@
                 moved += pltpu.roll(zc_ref[begin : begin + tall], wide2, 1)
             zt_out[z] = moved
         for z in (zn, zn + 1):
-            zt_out[z, tall - 1 :] = cut[z][-1:]
-        made = dot(jnp.concatenate([cut[z][3 * tall :] for z in range(0, zn, 2)], axis=0), ty2_ref[jy, 3 * wide :, :ly2])
-        for half in range(zn // 2):
-            i2_out[half] = made[half * xtwo.fine : (half + 1) * xtwo.fine]
+            zt_out[z, tall - 1 :] = cut[z][tall - 1 : tall]
 
     def third_apply(*refs):
         u1_ref, i2_ref, u_ref, ixy_ref, _, own_ref = refs[:6]
@@ -565,10 +575,10 @@
             for half in range(lz2 // 2):
                 edges[half] += chosen_by(zs[:, at_reach + k * zn + 2 * half], jz) * line
         fy = ytwo.fine
-        edges = dot(jnp.concatenate(edges + [jnp.zeros((8 - lz2 // 2 % 8, wide), jnp.float32)], axis=0), qy2_ref[jy, :, :ly2])
+        edges = dot(jnp.concatenate(edges + [jnp.zeros((8 - lz2 // 2 % 8, wide), jnp.float32)], axis=0), qy2_ref[jy])
         plane_halo = dot(plane_halo, part(ty_ref, jy, at_y3, 3))
         halo = dot(halo, part(ty_ref, jy, at_y3, 2))[:, :fy]
-        here = ixy_ref[hz - 1]
+        here = ixy_ref[...]
         last[...] = u_ref[lz - 1] - 0.5 * (here + jnp.where(jz == dz - 1, here, plane_halo))
         copies = [pltpu.make_async_copy(last, fine_out.at[lz - 1], sems.at[0])]
         copies[0].start()
@@ -626,20 +636,19 @@
         left=(0, 1, 2, 3),
     )
     ycame = swapped(ym, "gy")
-    ta_v, tsm_v, iy, *xm = kernel_call(
+    ta_v, tsm_v, *xm = kernel_call(
         y_apply,
-        [(lz * lx, wide), (hz * hx1, 2 * wide), (hz, lx, ly)]
-        + [(round_up(lz + 2 * hz + 1, 8), max(wide, ly))] * (dx - 1),
+        [(lz * lx, wide), (hz * hx1, 2 * wide)] + [(round_up(lz + 2 * hz + 1, 8), max(wide, ly))] * (dx - 1),
         [u, *ycame, own_ty, own_fx],
         scratch=[pltpu.VMEM((ss8, hz * hx1), jnp.float32)],
     )
     xcame = swapped(xm, "gx")
-    ixy, zc, u1_part, *sent = kernel_call(
+    zc, u1_part, *sent = kernel_call(
         x_apply,
-        [(hz, lx, ly), (xtwo.n + tall, wide), (zn, xone.n, wide)]
+        [(xtwo.n + tall, wide), (zn, xone.n, wide)]
         + [(xone.n, wide)] * (dz - 1)
         + [(kx, (zn + 2) * wide)] * (dx - 1),
-        [ta_v, tsm_v, iy, *xcame[::-1], tables_x, to32(f2x)],
+        [ta_v, tsm_v, *xcame[::-1], tables_x, to32(f2x)],
         scratch=[pltpu.VMEM((lz, ext, 2 * wide), jnp.float32)],
     )
     tails = sent[dz - 1 :]
@@ -647,13 +656,17 @@
     if dz > 1 and dx > 1:
         zcame[0], tails[0] = lax.optimization_barrier((zcame[0], tails[0]))
     xtcame = swapped(tails, "gx")
-    u1, zmsg, i2 = kernel_call(
+    u1, zmsg = kernel_call(
         second_apply,
-        [(zn, xone.n, wide), (lz2 + 2, tall, packed), (lz2 // 2, xtwo.fine, ly2)],
-        [u1_part, zc, *xtcame[::-1], *zcame[::-1], tables_x2, tables_y2],
+        [(zn, xone.n, wide), (lz2 + 2, tall, packed)],
+        [u1_part, zc, *xtcame[::-1], *zcame[::-1], to32(tx2), to32(ty2)],
     )
-    (fine,) = kernel_call(fine_coefficients, [(lz, lx, ly)], [u, ixy])
-    ztcame, fine = gathered(zmsg, "gz", fine)
+    beside = kernel_call(
+        interpolate,
+        [(lz, lx, ly), (lx, ly), (lz2 // 2, xtwo.fine, ly2)],
+        [u, ta_v, u1, *xcame[::-1], *xtcame[::-1], to32(qx2), to32(qy2)],
+    )
+    ztcame, (fine, ixy, i2) = gathered(zmsg, "gz", beside)
     return kernel_call(
         third_apply,
         [(lz, lx, ly), (lz2, xtwo.fine, ytwo.fine), (lz3, xthree.fine, ythree.fine), (lz4, xthree.n, ythree.n)],

time: 37.6 us -> 37.2 us (0.989)
  transfers between devices with their start and end apart: 13 -> 13, of which waited for: 7 -> 7; matrix products, arithmetic and copies ran while one was open for 0% -> 0% of each run, Pallas kernels for 2% -> 3%
where the time goes in v8:
time: 37.2 us; the launch traced here: 36.7 us
  starting transfers between devices  20 us (54%)
  Pallas kernels  8.4 us (23%)
  waiting for transfers between devices  7.47 us (20%)
  between operations  0.71 us (2%)
    ppermute x10, starting transfers between devices, swapped(): lax.ppermute(v, axis, [(i, i ^ k) for i in range(count)])  14.4 us
    pallas_call x6, Pallas kernels, kernel_call(): pl.pallas_call(body, out_shape=[jax.ShapeDtypeStruct(shape, jnp.float32)...  8.4 us
    ppermute x10, waiting for transfers between devices, swapped(): lax.ppermute(v, axis, [(i, i ^ k) for i in range(count)])  6.49 us
    ppermute x3, starting transfers between devices, gathered(): lax.ppermute(what, axis, [(i, i ^ k) for i in range(count)])  5.68 us
    ppermute x3, waiting for transfers between devices, gathered(): lax.ppermute(what, axis, [(i, i ^ k) for i in range(count)])  0.98 us
  transfers between devices with their start and end apart: 13, of which 7 were waited for; matrix products, arithmetic and copies ran while one was open for 0% of the time, Pallas kernels for 3%

profile of v8, /device:TPU:1, one launch (start us, length us, event | category | flops | bytes accessed | tf_op | source)
XLA Modules:
  0.0 36.7 jit_solution(13536037359364161995)
XLA Ops:
  0.6 1.8 %shard_map.165 = (f32[8,128,128]{2,1,0:T(8,128)S(1)}, f32[160,384]{1,0:T(8,128)S(1)}, f32[128,8]{1,0:T(8,128)S(1)}, f32[16,1024]{1,0:T(8,128)S(1)}) custom-call(f32[8,128,128]{2,1,0:T(8,128)} %u_hbm.1, f32[2,32,128]{2,1,0:T(8,128)} %constant.24.clone.table_hbm, f32[2,160,384]{2,1,0:T(8,128)} %constant.25.clone.ty_hbm, f32[4,128,8]{2,1,0:T(8,128)} %constant.29.clone.fx_hbm), custom_call_target="tpu_custom_call" | custom-call | tf_op jit(solution)/shard_map/pallas_call | solution.py:167
  2.4 0.0 copy-start.2
  2.4 2.1 %collective-permute-start = (f32[16,1024]{1,0:T(8,128)S(1)}, f32[16,1024]{1,0:T(8,128)S(1)}, u32[]{:S(2)}, u32[]{:S(2)}) collective-permute-start(f32[16,1024]{1,0:T(8,128)S(1)} %get-tuple-element.33), channel_id=1, source_target_pairs={{0,4},{4,0},{1,5},{5,1},{2,6},{6,2},{3,7},{7,3},{8,12},{12,8},{9,1... | collective-permute-start | bytes 196616 | tf_op jit(solution)/shard_map/ppermute | solution.py:180
  4.5 1.7 %collective-permute-done.refs_1_ = f32[16,1024]{1,0:T(8,128)S(1)} collective-permute-done((f32[16,1024]{1,0:T(8,128)S(1)}, f32[16,1024]{1,0:T(8,128)S(1)}, u32[]{:S(2)}, u32[]{:S(2)}) %collective-permute-start) | collective-permute-done | bytes 65568 | tf_op jit(solution)/shard_map/ppermute | solution.py:180
  6.2 1.5 %shard_map.166 = (f32[1024,128]{1,0:T(8,128)S(1)}, f32[256,256]{1,0:T(8,128)S(1)}, f32[24,128]{1,0:T(8,128)S(1)}, f32[24,128]{1,0:T(8,128)S(1)}, f32[24,128]{1,0:T(8,128)S(1)}) custom-call(f32[8,128,128]{2,1,0:T(8,128)S(1)} %get-tuple-element.32.refs_0_.refs_2_, f32[16,1024]{1,0:T(8,128)S(1)} %collective-permute-done.refs_1_, ...), custom_call_target="tpu_custom_call" | custom-call | tf_op jit(solution)/shard_map/pallas_call | solution.py:167
  7.7 3.6 %collective-permute-start.1 = (f32[24,128]{1,0:T(8,128)S(1)}, f32[24,128]{1,0:T(8,128)S(1)}, u32[]{:S(2)}, u32[]{:S(2)}) collective-permute-start(f32[24,128]{1,0:T(8,128)S(1)} %get-tuple-element.38), channel_id=1, source_target_pairs={{0,24},{8,16},{16,8},{24,0},{1,25},{9,17},{17,9},{25,1},{2,26},{10... | collective-permute-start | bytes 36872 | tf_op jit(solution)/shard_map/ppermute | solution.py:180
  11.3 0.0 collective-permute-start.2
  11.3 0.4 collective-permute-start.3
  11.6 0.7 %collective-permute-done.1.refs_2_.refs_3_ = f32[24,128]{1,0:T(8,128)S(1)} collective-permute-done((f32[24,128]{1,0:T(8,128)S(1)}, f32[24,128]{1,0:T(8,128)S(1)}, u32[]{:S(2)}, u32[]{:S(2)}) %collective-permute-start.1) | collective-permute-done | bytes 12320 | tf_op jit(solution)/shard_map/ppermute | solution.py:180
  12.3 2.4 %collective-permute-done.2.refs_3_.refs_4_ = f32[24,128]{1,0:T(8,128)S(1)} collective-permute-done((f32[24,128]{1,0:T(8,128)S(1)}, f32[24,128]{1,0:T(8,128)S(1)}, u32[]{:S(2)}, u32[]{:S(2)}) %collective-permute-start.2) | collective-permute-done | bytes 12320 | tf_op jit(solution)/shard_map/ppermute | solution.py:180
  14.7 0.0 collective-permute-done.3.refs_4_.refs_5_
  14.7 0.0 copy-start.3
  14.7 0.0 copy-start.5
  14.7 0.8 %shard_map.167 = (f32[72,128]{1,0:T(8,128)S(1)}, f32[4,64,128]{2,1,0:T(8,128)S(1)}, f32[64,128]{1,0:T(8,128)S(1)}, f32[64,128]{1,0:T(8,128)S(1)}, f32[64,128]{1,...) custom-call(f32[1024,128]{1,0:T(8,128)S(1)} %get-tuple-element.36.refs_0_.refs_1_, ...), custom_call_target="tpu_custom_call" | custom-call | tf_op jit(solution)/shard_map/pallas_call | solution.py:167
  15.5 3.3 %collective-permute-start.6 = (f32[64,128]{1,0:T(8,128)S(1)}, f32[64,128]{1,0:T(8,128)S(1)}, u32[]{:S(2)}, u32[]{:S(2)}) collective-permute-start(f32[64,128]{1,0:T(8,128)S(1)} %get-tuple-element.45), channel_id=1, source_target_pairs={{0,1},{1,0},{2,3},{3,2},{4,5},{5,4},{6,7},{7,6},{8,9},{9,8},{10,11... | collective-permute-start | bytes 98312 | tf_op jit(solution)/shard_map/ppermute | solution.py:180
  18.8 1.2 %collective-permute-start.8 = (f32[64,128]{1,0:T(8,128)S(1)}, f32[64,128]{1,0:T(8,128)S(1)}, u32[]{:S(2)}, u32[]{:S(2)}) collective-permute-start(f32[64,128]{1,0:T(8,128)S(1)} %get-tuple-element.48), channel_id=1, source_target_pairs={{0,3},{1,2},{2,1},{3,0},{4,7},{5,6},{6,5},{7,4},{8,11},{9,10},{10,... | collective-permute-start | bytes 98312 | tf_op jit(solution)/shard_map/ppermute | solution.py:180
  20.0 0.3 collective-permute-start.9
  20.3 1.2 %collective-permute-start.4 = (f32[8,768]{1,0:T(8,128)S(1)}, f32[8,768]{1,0:T(8,128)S(1)}, u32[]{:S(2)}, u32[]{:S(2)}) collective-permute-start(f32[8,768]{1,0:T(8,128)S(1)} %get-tuple-element.43), channel_id=1, source_target_pairs={{0,24},{8,16},{16,8},{24,0},{1,25},{9,17},{17,9},{25,1},{2,26},{10... | collective-permute-start | bytes 73736 | tf_op jit(solution)/shard_map/ppermute | solution.py:180
  21.4 0.6 %collective-permute-start.5 = (f32[8,768]{1,0:T(8,128)S(1)}, f32[8,768]{1,0:T(8,128)S(1)}, u32[]{:S(2)}, u32[]{:S(2)}) collective-permute-start(f32[8,768]{1,0:T(8,128)S(1)} %get-tuple-element.44), channel_id=1, source_target_pairs={{0,16},{8,24},{16,0},{24,8},{1,17},{9,25},{17,1},{25,9},{2,18},{10... | collective-permute-start | bytes 73736 | tf_op jit(solution)/shard_map/ppermute | solution.py:180
  22.0 1.8 %collective-permute-start.7 = (f32[8,768]{1,0:T(8,128)S(1)}, f32[8,768]{1,0:T(8,128)S(1)}, u32[]{:S(2)}, u32[]{:S(2)}) collective-permute-start(f32[8,768]{1,0:T(8,128)S(1)} %get-tuple-element.47), channel_id=1, source_target_pairs={{0,8},{8,0},{16,24},{24,16},{1,9},{9,1},{17,25},{25,17},{2,10},{10... | collective-permute-start | bytes 73736 | tf_op jit(solution)/shard_map/ppermute | solution.py:180
  23.8 0.9 %collective-permute-done.4.refs_2_.refs_6_ = f32[8,768]{1,0:T(8,128)S(1)} collective-permute-done((f32[8,768]{1,0:T(8,128)S(1)}, f32[8,768]{1,0:T(8,128)S(1)}, u32[]{:S(2)}, u32[]{:S(2)}) %collective-permute-start.4) | collective-permute-done | bytes 24608 | tf_op jit(solution)/shard_map/ppermute | solution.py:180
  24.7 0.3 collective-permute-done.5.refs_3_.refs_7_
  25.0 0.0 collective-permute-done.8.refs_5_
  25.0 0.5 %collective-permute-done.7.refs_4_.refs_8_ = f32[8,768]{1,0:T(8,128)S(1)} collective-permute-done((f32[8,768]{1,0:T(8,128)S(1)}, f32[8,768]{1,0:T(8,128)S(1)}, u32[]{:S(2)}, u32[]{:S(2)}) %collective-permute-start.7) | collective-permute-done | bytes 24608 | tf_op jit(solution)/shard_map/ppermute | solution.py:180
  25.6 1.0 %shard_map.168 = (f32[4,64,128]{2,1,0:T(8,128)S(1)}, f32[6,40,128]{2,1,0:T(8,128)S(1)}) custom-call(f32[4,64,128]{2,1,0:T(8,128)S(1)} %get-tuple-element.41.refs_0_, f32[72,128]{1,0:T(8,128)S(1)} %get-tuple-element.42.refs_1_, f32[8,768]{1,0:T(8,128)S(1)} %collective-permute-done.4.refs_2_.refs_6_, f32[8,768]{1,0:T(8,128)S(1)} %collective-permute-done.5.refs_3_.refs_7_, ...), custom_call_target="tpu_custom_call" | custom-call | tf_op jit(solution)/shard_map/pallas_call | solution.py:167
  26.6 0.0 copy-start
  26.6 1.3 %collective-permute-start.10 = (f32[6,40,128]{2,1,0:T(8,128)S(1)}, f32[6,40,128]{2,1,0:T(8,128)S(1)}, u32[]{:S(2)}, u32[]{:S(2)}) collective-permute-start(f32[6,40,128]{2,1,0:T(8,128)S(1)} %get-tuple-element.52.refs_5_), channel_id=1, source_target_pairs={{0,2},{1,3},{2,0},{3,1},{4,6},{5,7},{6,4},{7,5},{8,10},{9,11},{10,... | collective-permute-start | bytes 368648 | tf_op jit(solution)/shard_map/ppermute | solution.py:187
  27.9 2.1 %collective-permute-start.11 = (f32[6,40,128]{2,1,0:T(8,128)S(1)}, f32[6,40,128]{2,1,0:T(8,128)S(1)}, u32[]{:S(2)}, u32[]{:S(2)}) collective-permute-start(f32[6,40,128]{2,1,0:T(8,128)S(1)} %get-tuple-element.52.refs_5_), channel_id=1, source_target_pairs={{0,1},{1,0},{2,3},{3,2},{4,5},{5,4},{6,7},{7,6},{8,9},{9,8},{10,11... | collective-permute-start | bytes 368648 | tf_op jit(solution)/shard_map/ppermute | solution.py:187
  30.0 1.1 %shard_map.169 = (f32[8,128,128]{2,1,0:T(8,128)}, f32[128,128]{1,0:T(8,128)S(1)}, f32[2,64,128]{2,1,0:T(8,128)S(1)}) custom-call(f32[8,128,128]{2,1,0:T(8,128)S(1)} %get-tuple-element.32.refs_0_.refs_2_, f32[1024,128]{1,0:T(8,128)S(1)} %get-tuple-element.36.refs_0_.refs_1_, f32[4,64,128]{2,1,0:T(8,128)S(1)} %get-tuple-element.51.refs_2_.refs_0_, ...), custom_call_target="tpu_custom_call" | custom-call | tf_op jit(solution)/shard_map/pallas_call | solution.py:167
  31.2 2.3 %collective-permute-start.12 = (f32[6,40,128]{2,1,0:T(8,128)S(1)}, f32[6,40,128]{2,1,0:T(8,128)S(1)}, u32[]{:S(2)}, u32[]{:S(2)}) collective-permute-start(f32[6,40,128]{2,1,0:T(8,128)S(1)} %collective-permute-done.10.refs_7_), channel_id=1, source_target_pairs={{0,1},{1,0},{2,3},{3,2},{4,5},{5,4},{6,7},{7,6},{8,9},{9,8},{10,11... | collective-permute-start | bytes 368648 | tf_op jit(solution)/shard_map/ppermute | solution.py:187
  33.4 1.0 %collective-permute-done.12.refs_8_ = f32[6,40,128]{2,1,0:T(8,128)S(1)} collective-permute-done((f32[6,40,128]{2,1,0:T(8,128)S(1)}, f32[6,40,128]{2,1,0:T(8,128)S(1)}, u32[]{:S(2)}, u32[]{:S(2)}) %collective-permute-start.12) | collective-permute-done | bytes 122912 | tf_op jit(solution)/shard_map/ppermute | solution.py:187
  34.4 2.2 %shard_map.170 = (f32[8,128,128]{2,1,0:T(8,128)}, f32[4,64,64]{2,1,0:T(8,128)}, f32[2,32,32]{2,1,0:T(8,128)}, f32[1,16,16]{2,1,0:T(8,128)}) custom-call(f32[4,64,128]{2,1,0:T(8,128)S(1)} %get-tuple-element.51.refs_2_.refs_0_, f32[2,64,128]{2,1,0:T(8,128)S(1)} %get-tuple-element.56.refs_1_, ...), custom_call_target="tpu_custom_call", output_to_operand_aliasing={{0}: (4, {})} | custom-call | tf_op jit(solution)/shard_map/pallas_call | solution.py:167
  (18 shorter events, 0.0 us)
Async XLA Ops:
  2.4 12.3 %copy-start.2 = (f32[4,128,136]{2,1,0:T(8,128)S(1)}, f32[4,128,136]{2,1,0:T(8,128)}, u32[]{:S(2)}) copy-start(f32[4,128,136]{2,1,0:T(8,128)} %constant.26.clone.refs_5_) | copy-start | bytes 835588
  2.4 3.8 %collective-permute-start = (f32[16,1024]{1,0:T(8,128)S(1)}, f32[16,1024]{1,0:T(8,128)S(1)}, u32[]{:S(2)}, u32[]{:S(2)}) collective-permute-start(f32[16,1024]{1,0:T(8,128)S(1)} %get-tuple-element.33), channel_id=1, source_target_pairs={{0,4},{4,0},{1,5},{5,1},{2,6},{6,2},{3,7},{7,3},{8,12},{12,8},{9,1... | collective-permute-start | bytes 196616 | tf_op jit(solution)/shard_map/ppermute | solution.py:180
  6.2 8.5 %copy-start.8 = (f32[4,24,64]{2,1,0:T(8,128)S(1)}, f32[4,24,64]{2,1,0:T(8,128)}, u32[]{:S(2)}) copy-start(f32[4,24,64]{2,1,0:T(8,128)} %constant.30.clone.refs_6_) | copy-start | bytes 73732
  7.7 4.7 %collective-permute-start.1 = (f32[24,128]{1,0:T(8,128)S(1)}, f32[24,128]{1,0:T(8,128)S(1)}, u32[]{:S(2)}, u32[]{:S(2)}) collective-permute-start(f32[24,128]{1,0:T(8,128)S(1)} %get-tuple-element.38), channel_id=1, source_target_pairs={{0,24},{8,16},{16,8},{24,0},{1,25},{9,17},{17,9},{25,1},{2,26},{10... | collective-permute-start | bytes 36872 | tf_op jit(solution)/shard_map/ppermute | solution.py:180
  11.3 3.4 %collective-permute-start.2 = (f32[24,128]{1,0:T(8,128)S(1)}, f32[24,128]{1,0:T(8,128)S(1)}, u32[]{:S(2)}, u32[]{:S(2)}) collective-permute-start(f32[24,128]{1,0:T(8,128)S(1)} %get-tuple-element.39), channel_id=1, source_target_pairs={{0,16},{8,24},{16,0},{24,8},{1,17},{9,25},{17,1},{25,9},{2,18},{10... | collective-permute-start | bytes 36872 | tf_op jit(solution)/shard_map/ppermute | solution.py:180
  11.3 3.4 %collective-permute-start.3 = (f32[24,128]{1,0:T(8,128)S(1)}, f32[24,128]{1,0:T(8,128)S(1)}, u32[]{:S(2)}, u32[]{:S(2)}) collective-permute-start(f32[24,128]{1,0:T(8,128)S(1)} %get-tuple-element.40), channel_id=1, source_target_pairs={{0,8},{8,0},{16,24},{24,16},{1,9},{9,1},{17,25},{25,17},{2,10},{10... | collective-permute-start | bytes 36872 | tf_op jit(solution)/shard_map/ppermute | solution.py:180
  14.7 10.9 %copy-start.3 = (f32[2,384,128]{2,1,0:T(8,128)S(1)}, f32[2,384,128]{2,1,0:T(8,128)}, u32[]{:S(2)}) copy-start(f32[2,384,128]{2,1,0:T(8,128)} %constant.32.clone.refs_9_) | copy-start | bytes 1179652
  14.7 10.8 %copy-start.5 = (f32[4,120,88]{2,1,0:T(8,128)S(1)}, f32[4,120,88]{2,1,0:T(8,128)}, u32[]{:S(2)}) copy-start(f32[4,120,88]{2,1,0:T(8,128)} %constant.31.clone.refs_8_) | copy-start | bytes 506884
  15.5 6.5 %collective-permute-start.6 = (f32[64,128]{1,0:T(8,128)S(1)}, f32[64,128]{1,0:T(8,128)S(1)}, u32[]{:S(2)}, u32[]{:S(2)}) collective-permute-start(f32[64,128]{1,0:T(8,128)S(1)} %get-tuple-element.45), channel_id=1, source_target_pairs={{0,1},{1,0},{2,3},{3,2},{4,5},{5,4},{6,7},{7,6},{8,9},{9,8},{10,11... | collective-permute-start | bytes 98312 | tf_op jit(solution)/shard_map/ppermute | solution.py:180
  18.8 6.2 %collective-permute-start.8 = (f32[64,128]{1,0:T(8,128)S(1)}, f32[64,128]{1,0:T(8,128)S(1)}, u32[]{:S(2)}, u32[]{:S(2)}) collective-permute-start(f32[64,128]{1,0:T(8,128)S(1)} %get-tuple-element.48), channel_id=1, source_target_pairs={{0,3},{1,2},{2,1},{3,0},{4,7},{5,6},{6,5},{7,4},{8,11},{9,10},{10,... | collective-permute-start | bytes 98312 | tf_op jit(solution)/shard_map/ppermute | solution.py:180
  20.0 5.0 %collective-permute-start.9 = (f32[64,128]{1,0:T(8,128)S(1)}, f32[64,128]{1,0:T(8,128)S(1)}, u32[]{:S(2)}, u32[]{:S(2)}) collective-permute-start(f32[64,128]{1,0:T(8,128)S(1)} %get-tuple-element.49), channel_id=1, source_target_pairs={{0,2},{1,3},{2,0},{3,1},{4,6},{5,7},{6,4},{7,5},{8,10},{9,11},{10,... | collective-permute-start | bytes 98312 | tf_op jit(solution)/shard_map/ppermute | solution.py:180
  20.3 4.5 %collective-permute-start.4 = (f32[8,768]{1,0:T(8,128)S(1)}, f32[8,768]{1,0:T(8,128)S(1)}, u32[]{:S(2)}, u32[]{:S(2)}) collective-permute-start(f32[8,768]{1,0:T(8,128)S(1)} %get-tuple-element.43), channel_id=1, source_target_pairs={{0,24},{8,16},{16,8},{24,0},{1,25},{9,17},{17,9},{25,1},{2,26},{10... | collective-permute-start | bytes 73736 | tf_op jit(solution)/shard_map/ppermute | solution.py:180
  21.4 3.6 %collective-permute-start.5 = (f32[8,768]{1,0:T(8,128)S(1)}, f32[8,768]{1,0:T(8,128)S(1)}, u32[]{:S(2)}, u32[]{:S(2)}) collective-permute-start(f32[8,768]{1,0:T(8,128)S(1)} %get-tuple-element.44), channel_id=1, source_target_pairs={{0,16},{8,24},{16,0},{24,8},{1,17},{9,25},{17,1},{25,9},{2,18},{10... | collective-permute-start | bytes 73736 | tf_op jit(solution)/shard_map/ppermute | solution.py:180
  22.0 3.6 %collective-permute-start.7 = (f32[8,768]{1,0:T(8,128)S(1)}, f32[8,768]{1,0:T(8,128)S(1)}, u32[]{:S(2)}, u32[]{:S(2)}) collective-permute-start(f32[8,768]{1,0:T(8,128)S(1)} %get-tuple-element.47), channel_id=1, source_target_pairs={{0,8},{8,0},{16,24},{24,16},{1,9},{9,1},{17,25},{25,17},{2,10},{10... | collective-permute-start | bytes 73736 | tf_op jit(solution)/shard_map/ppermute | solution.py:180
  25.6 4.5 %copy-start.1 = (f32[2,128,128]{2,1,0:T(8,128)S(1)}, f32[2,128,128]{2,1,0:T(8,128)}, u32[]{:S(2)}) copy-start(f32[2,128,128]{2,1,0:T(8,128)} %constant.34.clone.refs_10_.refs_12_) | copy-start | bytes 393220
  25.6 4.5 %copy-start.6 = (f32[4,64,88]{2,1,0:T(8,128)S(1)}, f32[4,64,88]{2,1,0:T(8,128)}, u32[]{:S(2)}) copy-start(f32[4,64,88]{2,1,0:T(8,128)} %constant.33.clone.refs_9_) | copy-start | bytes 270340
  26.6 7.8 %copy-start = (f32[2,768,128]{2,1,0:T(8,128)S(1)}, f32[2,768,128]{2,1,0:T(8,128)}, u32[]{:S(2)}) copy-start(f32[2,768,128]{2,1,0:T(8,128)} %constant.28.clone.refs_11_) | copy-start | bytes 2359300
  26.6 4.5 %collective-permute-start.10 = (f32[6,40,128]{2,1,0:T(8,128)S(1)}, f32[6,40,128]{2,1,0:T(8,128)S(1)}, u32[]{:S(2)}, u32[]{:S(2)}) collective-permute-start(f32[6,40,128]{2,1,0:T(8,128)S(1)} %get-tuple-element.52.refs_5_), channel_id=1, source_target_pairs={{0,2},{1,3},{2,0},{3,1},{4,6},{5,7},{6,4},{7,5},{8,10},{9,11},{10,... | collective-permute-start | bytes 368648 | tf_op jit(solution)/shard_map/ppermute | solution.py:187
  27.9 5.5 %collective-permute-start.11 = (f32[6,40,128]{2,1,0:T(8,128)S(1)}, f32[6,40,128]{2,1,0:T(8,128)S(1)}, u32[]{:S(2)}, u32[]{:S(2)}) collective-permute-start(f32[6,40,128]{2,1,0:T(8,128)S(1)} %get-tuple-element.52.refs_5_), channel_id=1, source_target_pairs={{0,1},{1,0},{2,3},{3,2},{4,5},{5,4},{6,7},{7,6},{8,9},{9,8},{10,11... | collective-permute-start | bytes 368648 | tf_op jit(solution)/shard_map/ppermute | solution.py:187
  30.0 4.4 %copy-start.4 = (f32[4,144,40]{2,1,0:T(8,128)S(1)}, f32[4,144,40]{2,1,0:T(8,128)}, u32[]{:S(2)}) copy-start(f32[4,144,40]{2,1,0:T(8,128)} %constant.27.clone.refs_10_) | copy-start | bytes 276484
  30.0 4.4 %copy-start.7 = (f32[128,80]{1,0:T(8,128)S(1)}, f32[128,80]{1,0:T(8,128)}, u32[]{:S(2)}) copy-start(f32[128,80]{1,0:T(8,128)} %constant.35.clone.refs_9_) | copy-start | bytes 122884
  31.2 3.2 %collective-permute-start.12 = (f32[6,40,128]{2,1,0:T(8,128)S(1)}, f32[6,40,128]{2,1,0:T(8,128)S(1)}, u32[]{:S(2)}, u32[]{:S(2)}) collective-permute-start(f32[6,40,128]{2,1,0:T(8,128)S(1)} %collective-permute-done.10.refs_7_), channel_id=1, source_target_pairs={{0,1},{1,0},{2,3},{3,2},{4,5},{5,4},{6,7},{7,6},{8,9},{9,8},{10,11... | collective-permute-start | bytes 368648 | tf_op jit(solution)/shard_map/ppermute | solution.py:187

commit v9 on v8

--- a/solution.py
+++ b/solution.py
@@ -262,10 +262,16 @@
 
     ext = round_up(max(dx - 1, 1), 8)
     fx = np.zeros((dx, lx, 8))
+    heads = round_up(2 * lz + lz // 2, 8)
+    sums = np.zeros((dx, heads, lz * lx))
     txa = np.zeros((dx, xone.n, lx + ext))
     txm = np.zeros((dx, xone.n, xone.n + ext))
     for j in range(dx):
         fx[j, :, :2] = xone.functionals[j][2:4].T
+        for z in range(lz):
+            sums[j, 2 * z : 2 * z + 2, z * lx : (z + 1) * lx] = xone.functionals[j][2:4]
+        for half in range(lz // 2):
+            sums[j, 2 * lz + half, 2 * half * lx] = 1.0
         product, even, around = xone.tables[j]
         txa[j, :, :lx] = product[:, :lx]
         txm[j, :, : xone.n] = around[:, :lx:2]
@@ -359,7 +365,7 @@
     hz, hx1 = lz // 2, lx // 2
     ly2 = round_up(ytwo.fine, 128)
 
-    def y_messages(u_hbm, table_hbm, ty_hbm, fx_hbm, u_ref, ty_ref, fx_ref, *refs):
+    def y_messages(u_hbm, table_hbm, ty_hbm, fx_hbm, sums_hbm, u_ref, ty_ref, fx_ref, sums_ref, *refs):
         outs, (table, sems) = refs[:-2], refs[-2:]
         j = lax.axis_index("gy")
         nt = ((1,), (1,))
@@ -368,6 +374,7 @@
             pltpu.make_async_copy(u_hbm, u_ref, sems.at[1]),
             pltpu.make_async_copy(ty_hbm.at[j], ty_ref, sems.at[2]),
             pltpu.make_async_copy(fx_hbm.at[lax.axis_index("gx")], fx_ref, sems.at[3]),
+            pltpu.make_async_copy(sums_hbm.at[lax.axis_index("gx")], sums_ref, sems.at[4]),
         ]
         for copy in copies:
             copy.start()
@@ -398,43 +405,75 @@
             own = jnp.where((jx ^ (k + 1)) == jx + 1, other, own)
         return own
 
-    def y_apply(*refs):
-        u_ref, came = refs[0], refs[1:dy]
-        ty_ref, fx_ref, ta_out, tsm_out = refs[dy : dy + 4]
-        xm_outs, points = refs[dy + 4 : -1], refs[-1]
+    def y_own(u_ref, ty_ref, fx_ref, ta_out, tsm_out, heads_out, points_out):
         jx = lax.axis_index("gx")
-        tn = ((0,), (0,))
         ta_all = dot(u_ref[...].reshape(lz * lx, ly), ty_ref[:ly, :wide])
         even = jnp.concatenate([u_ref[2 * z, pl.ds(0, hx1, stride=2), :] for z in range(hz)], axis=0)
         tsm_all = dot(even, ty_ref[:ly, wide:])
+        ta_out[...] = ta_all
+        tsm_out[...] = tsm_all
+        weights = [jnp.broadcast_to(fx_ref[:, c : c + 1], (lx, wide)) for c in range(2)]
+        heads_out[...] = jnp.zeros_like(heads_out)
+        points_out[...] = jnp.zeros_like(points_out)
+        for z in range(lz):
+            part = ta_all[z * lx : (z + 1) * lx]
+            for c in range(2):
+                heads_out[2 * z + c : 2 * z + c + 1] = jnp.sum(part * weights[c], axis=0, keepdims=True)
+        for half in range(hz):
+            heads_out[2 * lz + half : 2 * lz + half + 1] = ta_all[2 * half * lx : 2 * half * lx + 1]
+            tm = tsm_all[half * hx1 : (half + 1) * hx1]
+            points_out[half : half + 1] = jnp.where(jx == 0, tm[0:1], tm[hx1 - 1 : hx1])
+        points_out[hz : hz + 1] = tsm_all[0:1]
+
+    def came_points(ref, points):
+        points[...] = jnp.zeros_like(points)
+        for f in range(ss):
+            begin = hz * hx1 * (f % per_row)
+            row = sa + f // per_row
+            points[f : f + 1] = ref[row : row + 1, begin : begin + hz * hx1]
+        return points[...]
+
+    def x_messages(*refs):
+        u_ref, came = refs[0], refs[1:dy]
+        ty_ref, sums_ref, heads_ref, points_ref = refs[dy : dy + 4]
+        xm_outs, points = refs[dy + 4 : -1], refs[-1]
+        jx = lax.axis_index("gx")
+        nt = ((1,), (1,))
+        head, point = heads_ref[...], points_ref[...]
+        shape = (point.shape[0], hz * hx1)
+        row, lane = iota(shape, 0), iota(shape, 1)
+        line = jnp.where(row == hz, 0, row * hx1 + jnp.where(jx == 0, 0, hx1 - 1))
+        one = jnp.where((lane == line) & (row <= hz), 1.0, 0.0)
+        for k, ref in enumerate(came):
+            begin = ly + rowsy * k
+            head += dot(dot(sums_ref[...], ref[...], nt), ty_ref[begin : begin + rowsy, :wide])
+            begin = ly + rowsy * (dy - 1) + ss8 * k
+            point += dot(dot(one, came_points(ref, points), nt), ty_ref[begin : begin + ss8, wide:])
+        for out in xm_outs:
+            out[lz + 2 * hz :] = jnp.zeros_like(out[lz + 2 * hz :])
+            out[lz + 2 * hz : lz + 2 * hz + 1, :wide] = point[hz : hz + 1, :wide]
+        for z in range(lz):
+            for k, out in enumerate(xm_outs):
+                out[z : z + 1, :wide] = jnp.where((jx ^ (k + 1)) < jx, head[2 * z : 2 * z + 1], head[2 * z + 1 : 2 * z + 2])
+        for half in range(hz):
+            first = head[2 * lz + half : 2 * lz + half + 1, wide - 1 :]
+            iy = along_y(u_ref[2 * half, :8], jnp.broadcast_to(first, (8, 1)))
+            for out in xm_outs:
+                out[lz + half : lz + half + 1, :wide] = point[half : half + 1, wide:]
+                out[lz + hz + half : lz + hz + half + 1, :ly] = iy[0:1]
+
+    def y_apply(*refs):
+        came = refs[: dy - 1]
+        ty_ref, ta_ref, tsm_ref, ta_out, tsm_out, points = refs[dy - 1 :]
+        tn = ((0,), (0,))
+        ta_all, tsm_all = ta_ref[...], tsm_ref[...]
         for k, ref in enumerate(came):
             begin = ly + rowsy * k
             ta_all += dot(ref[...], ty_ref[begin : begin + rowsy, :wide], tn)
-            points[...] = jnp.zeros_like(points)
-            for f in range(ss):
-                begin = hz * hx1 * (f % per_row)
-                row = sa + f // per_row
-                points[f : f + 1] = ref[row : row + 1, begin : begin + hz * hx1]
             begin = ly + rowsy * (dy - 1) + ss8 * k
-            tsm_all += dot(points[...], ty_ref[begin : begin + ss8, wide:], tn)
+            tsm_all += dot(came_points(ref, points), ty_ref[begin : begin + ss8, wide:], tn)
         ta_out[...] = ta_all
         tsm_out[...] = tsm_all
-        weights = [jnp.broadcast_to(fx_ref[:, c : c + 1], (lx, wide)) for c in range(2)]
-        for out in xm_outs:
-            out[lz + 2 * hz :] = jnp.zeros_like(out[lz + 2 * hz :])
-            out[lz + 2 * hz : lz + 2 * hz + 1, :wide] = tsm_all[0:1, :wide]
-        for z in range(lz):
-            part = ta_all[z * lx : (z + 1) * lx]
-            v, w = (jnp.sum(part * weight, axis=0, keepdims=True) for weight in weights)
-            for k, out in enumerate(xm_outs):
-                out[z : z + 1, :wide] = jnp.where((jx ^ (k + 1)) < jx, v, w)
-            if z % 2 == 0:
-                half = z // 2
-                tm = tsm_all[half * hx1 : (half + 1) * hx1, wide:]
-                iy = along_y(u_ref[z, :8], part[:8, wide - 1 :])
-                for out in xm_outs:
-                    out[lz + half : lz + half + 1, :wide] = jnp.where(jx == 0, tm[0:1], tm[hx1 - 1 : hx1])
-                    out[lz + hz + half : lz + hz + half + 1, :ly] = iy[0:1]
 
     def x_apply(*refs):
         ta_ref, tsm_ref = refs[:2]
@@ -628,21 +667,32 @@
         for copy in copies:
             copy.wait()
 
-    u, own_ty, own_fx, *ym = kernel_call(
+    u, own_ty, own_fx, own_sums, *ym = kernel_call(
         y_messages,
-        [(lz, lx, ly), tables_y.shape[1:], fx.shape[1:]] + [(rowsy, lz * lx)] * (dy - 1),
-        [field, messages_y, tables_y, to32(fx)],
-        scratch=[pltpu.VMEM(messages_y.shape[1:], jnp.float32), pltpu.SemaphoreType.DMA((4,))],
-        left=(0, 1, 2, 3),
+        [(lz, lx, ly), tables_y.shape[1:], fx.shape[1:], sums.shape[1:]] + [(rowsy, lz * lx)] * (dy - 1),
+        [field, messages_y, tables_y, to32(fx), to32(sums)],
+        scratch=[pltpu.VMEM(messages_y.shape[1:], jnp.float32), pltpu.SemaphoreType.DMA((5,))],
+        left=(0, 1, 2, 3, 4),
     )
     ycame = swapped(ym, "gy")
-    ta_v, tsm_v, *xm = kernel_call(
+    ta_own, tsm_own, head, point = kernel_call(
+        y_own,
+        [(lz * lx, wide), (hz * hx1, 2 * wide), (heads, wide), (round_up(hz + 1, 8), 2 * wide)],
+        [u, own_ty, own_fx],
+    )
+    xm = kernel_call(
+        x_messages,
+        [(round_up(lz + 2 * hz + 1, 8), max(wide, ly))] * (dx - 1),
+        [u, *ycame, own_ty, own_sums, head, point],
+        scratch=[pltpu.VMEM((ss8, hz * hx1), jnp.float32)],
+    )
+    xcame = swapped(xm, "gx")
+    ta_v, tsm_v = kernel_call(
         y_apply,
-        [(lz * lx, wide), (hz * hx1, 2 * wide)] + [(round_up(lz + 2 * hz + 1, 8), max(wide, ly))] * (dx - 1),
-        [u, *ycame, own_ty, own_fx],
+        [(lz * lx, wide), (hz * hx1, 2 * wide)],
+        [*ycame, own_ty, ta_own, tsm_own],
         scratch=[pltpu.VMEM((ss8, hz * hx1), jnp.float32)],
     )
-    xcame = swapped(xm, "gx")
     zc, u1_part, *sent = kernel_call(
         x_apply,
         [(xtwo.n + tall, wide), (zn, xone.n, wide)]

time: 37.2 us -> 36.3 us (0.976)
  waiting for transfers between devices: 7.47 us -> 5.84 us
  Pallas kernels: 8.4 us -> 9.13 us
    ppermute x10, waiting for transfers between devices: 6.49 us -> 4.86 us  [swapped(): lax.ppermute(v, axis, [(i, i ^ k) for i in range(count)])]
    pallas_call x6 -> x8, Pallas kernels: 8.4 us -> 9.13 us  [kernel_call(): pl.pallas_call(body, out_shape=[jax.ShapeDtypeStruct(shape, jnp.float32)...]
  transfers between devices with their start and end apart: 13 -> 13, of which waited for: 7 -> 6; matrix products, arithmetic and copies ran while one was open for 0% -> 0% of each run, Pallas kernels for 3% -> 8%
where the time goes in v9:
time: 36.3 us; the launch traced here: 35.7 us
  starting transfers between devices  20 us (55%)
  Pallas kernels  9.13 us (25%)
  waiting for transfers between devices  5.84 us (16%)
  between operations  0.73 us (2%)
    ppermute x10, starting transfers between devices, swapped(): lax.ppermute(v, axis, [(i, i ^ k) for i in range(count)])  14.3 us
    pallas_call x8, Pallas kernels, kernel_call(): pl.pallas_call(body, out_shape=[jax.ShapeDtypeStruct(shape, jnp.float32)...  9.13 us
    ppermute x3, starting transfers between devices, gathered(): lax.ppermute(what, axis, [(i, i ^ k) for i in range(count)])  5.68 us
    ppermute x10, waiting for transfers between devices, swapped(): lax.ppermute(v, axis, [(i, i ^ k) for i in range(count)])  4.86 us
    ppermute x3, waiting for transfers between devices, gathered(): lax.ppermute(what, axis, [(i, i ^ k) for i in range(count)])  0.98 us
  transfers between devices with their start and end apart: 13, of which 6 were waited for; matrix products, arithmetic and copies ran while one was open for 0% of the time, Pallas kernels for 8%

profile of v9, /device:TPU:1, one launch (start us, length us, event | category | flops | bytes accessed | tf_op | source)
XLA Modules:
  0.0 35.7 jit_solution(11475727122787854852)
XLA Ops:
  0.6 1.8 %shard_map.174 = (f32[8,128,128]{2,1,0:T(8,128)S(1)}, f32[160,384]{1,0:T(8,128)S(1)}, f32[128,8]{1,0:T(8,128)S(1)}, f32[24,1024]{1,0:T(8,128)S(1)}, f32[16,1024]{1,0:T(8,128)S(1)}) custom-call(f32[8,128,128]{2,1,0:T(8,128)} %u_hbm.1, f32[2,32,128]{2,1,0:T(8,128)} %constant.26.clone.table_hbm, f32[2,160,384]{2,1,0:T(8,128)} %constant.27.clone.ty_hbm, ...), custom_call_target="tpu_custom_call" | custom-call | tf_op jit(solution)/shard_map/pallas_call | solution.py:167
  2.4 2.1 %collective-permute-start = (f32[16,1024]{1,0:T(8,128)S(1)}, f32[16,1024]{1,0:T(8,128)S(1)}, u32[]{:S(2)}, u32[]{:S(2)}) collective-permute-start(f32[16,1024]{1,0:T(8,128)S(1)} %get-tuple-element.37), channel_id=1, source_target_pairs={{0,4},{4,0},{1,5},{5,1},{2,6},{6,2},{3,7},{7,3},{8,12},{12,8},{9,1... | collective-permute-start | bytes 196616 | tf_op jit(solution)/shard_map/ppermute | solution.py:180
  4.5 0.8 %shard_map.175 = (f32[1024,128]{1,0:T(8,128)S(1)}, f32[256,256]{1,0:T(8,128)S(1)}, f32[24,128]{1,0:T(8,128)S(1)}, f32[8,256]{1,0:T(8,128)S(1)}) custom-call(f32[8,128,128]{2,1,0:T(8,128)S(1)} %get-tuple-element.39.u_ref.refs_0_.refs_2_, f32[160,384]{1,0:T(8,128)S(1)} %get-tuple-element.38.ty_ref.refs_1_.refs_2_, f32[128,8]{1,0:T(8,128)S(1)} %get-tuple-element.40.fx_ref), custom_call_target="tpu_custom_call" | custom-call | tf_op jit(solution)/shard_map/pallas_call | solution.py:167
  5.3 0.9 %collective-permute-done.refs_0_.refs_1_ = f32[16,1024]{1,0:T(8,128)S(1)} collective-permute-done((f32[16,1024]{1,0:T(8,128)S(1)}, f32[16,1024]{1,0:T(8,128)S(1)}, u32[]{:S(2)}, u32[]{:S(2)}) %collective-permute-start) | collective-permute-done | bytes 65568 | tf_op jit(solution)/shard_map/ppermute | solution.py:180
  6.2 0.6 %shard_map.177 = (f32[24,128]{1,0:T(8,128)S(1)}, f32[24,128]{1,0:T(8,128)S(1)}, f32[24,128]{1,0:T(8,128)S(1)}) custom-call(f32[8,128,128]{2,1,0:T(8,128)S(1)} %get-tuple-element.39.u_ref.refs_0_.refs_2_, f32[16,1024]{1,0:T(8,128)S(1)} %collective-permute-done.refs_0_.refs_1_, f32[160,384]{1,0:T(8,128)S(1)} %get-tuple-element.38.ty_ref.refs_1_.refs_2_, ...), custom_call_target="tpu_custom_call" | custom-call | tf_op jit(solution)/shard_map/pallas_call | solution.py:167
  6.8 3.6 %collective-permute-start.1 = (f32[24,128]{1,0:T(8,128)S(1)}, f32[24,128]{1,0:T(8,128)S(1)}, u32[]{:S(2)}, u32[]{:S(2)}) collective-permute-start(f32[24,128]{1,0:T(8,128)S(1)} %get-tuple-element.48), channel_id=1, source_target_pairs={{0,24},{8,16},{16,8},{24,0},{1,25},{9,17},{17,9},{25,1},{2,26},{10... | collective-permute-start | bytes 36872 | tf_op jit(solution)/shard_map/ppermute | solution.py:180
  10.3 0.4 %collective-permute-start.3 = (f32[24,128]{1,0:T(8,128)S(1)}, f32[24,128]{1,0:T(8,128)S(1)}, u32[]{:S(2)}, u32[]{:S(2)}) collective-permute-start(f32[24,128]{1,0:T(8,128)S(1)} %get-tuple-element.50), channel_id=1, source_target_pairs={{0,8},{8,0},{16,24},{24,16},{1,9},{9,1},{17,25},{25,17},{2,10},{10... | collective-permute-start | bytes 36872 | tf_op jit(solution)/shard_map/ppermute | solution.py:180
  10.7 0.8 %shard_map.176 = (f32[1024,128]{1,0:T(8,128)S(1)}, f32[256,256]{1,0:T(8,128)S(1)}) custom-call(f32[16,1024]{1,0:T(8,128)S(1)} %collective-permute-done.refs_0_.refs_1_, f32[160,384]{1,0:T(8,128)S(1)} %get-tuple-element.38.ty_ref.refs_1_.refs_2_, f32[1024,128]{1,0:T(8,128)S(1)} %get-tuple-element.41.refs_2_, f32[256,256]{1,0:T(8,128)S(1)} %get-tuple-element.42.refs_3_), custom_call_target="tpu_custom_call" | custom-call | tf_op jit(solution)/shard_map/pallas_call | solution.py:167
  11.5 2.2 %collective-permute-done.2.refs_3_.refs_4_ = f32[24,128]{1,0:T(8,128)S(1)} collective-permute-done((f32[24,128]{1,0:T(8,128)S(1)}, f32[24,128]{1,0:T(8,128)S(1)}, u32[]{:S(2)}, u32[]{:S(2)}) %collective-permute-start.2) | collective-permute-done | bytes 12320 | tf_op jit(solution)/shard_map/ppermute | solution.py:180
  13.8 0.0 copy-start.3
  13.8 0.0 copy-start.5
  13.8 0.8 %shard_map.178 = (f32[72,128]{1,0:T(8,128)S(1)}, f32[4,64,128]{2,1,0:T(8,128)S(1)}, f32[64,128]{1,0:T(8,128)S(1)}, f32[64,128]{1,0:T(8,128)S(1)}, f32[64,128]{1,...) custom-call(f32[1024,128]{1,0:T(8,128)S(1)} %get-tuple-element.43.refs_0_.refs_1_, ...), custom_call_target="tpu_custom_call" | custom-call | tf_op jit(solution)/shard_map/pallas_call | solution.py:167
  14.6 3.3 %collective-permute-start.6 = (f32[64,128]{1,0:T(8,128)S(1)}, f32[64,128]{1,0:T(8,128)S(1)}, u32[]{:S(2)}, u32[]{:S(2)}) collective-permute-start(f32[64,128]{1,0:T(8,128)S(1)} %get-tuple-element.55), channel_id=1, source_target_pairs={{0,1},{1,0},{2,3},{3,2},{4,5},{5,4},{6,7},{7,6},{8,9},{9,8},{10,11... | collective-permute-start | bytes 98312 | tf_op jit(solution)/shard_map/ppermute | solution.py:180
  17.9 1.2 %collective-permute-start.8 = (f32[64,128]{1,0:T(8,128)S(1)}, f32[64,128]{1,0:T(8,128)S(1)}, u32[]{:S(2)}, u32[]{:S(2)}) collective-permute-start(f32[64,128]{1,0:T(8,128)S(1)} %get-tuple-element.58), channel_id=1, source_target_pairs={{0,3},{1,2},{2,1},{3,0},{4,7},{5,6},{6,5},{7,4},{8,11},{9,10},{10,... | collective-permute-start | bytes 98312 | tf_op jit(solution)/shard_map/ppermute | solution.py:180
  19.1 0.3 collective-permute-start.9
  19.4 1.2 %collective-permute-start.4 = (f32[8,768]{1,0:T(8,128)S(1)}, f32[8,768]{1,0:T(8,128)S(1)}, u32[]{:S(2)}, u32[]{:S(2)}) collective-permute-start(f32[8,768]{1,0:T(8,128)S(1)} %get-tuple-element.53), channel_id=1, source_target_pairs={{0,24},{8,16},{16,8},{24,0},{1,25},{9,17},{17,9},{25,1},{2,26},{10... | collective-permute-start | bytes 73736 | tf_op jit(solution)/shard_map/ppermute | solution.py:180
  20.5 0.6 %collective-permute-start.5 = (f32[8,768]{1,0:T(8,128)S(1)}, f32[8,768]{1,0:T(8,128)S(1)}, u32[]{:S(2)}, u32[]{:S(2)}) collective-permute-start(f32[8,768]{1,0:T(8,128)S(1)} %get-tuple-element.54), channel_id=1, source_target_pairs={{0,16},{8,24},{16,0},{24,8},{1,17},{9,25},{17,1},{25,9},{2,18},{10... | collective-permute-start | bytes 73736 | tf_op jit(solution)/shard_map/ppermute | solution.py:180
  21.1 0.0 collective-permute-done.6.refs_7_
  21.1 1.8 %collective-permute-start.7 = (f32[8,768]{1,0:T(8,128)S(1)}, f32[8,768]{1,0:T(8,128)S(1)}, u32[]{:S(2)}, u32[]{:S(2)}) collective-permute-start(f32[8,768]{1,0:T(8,128)S(1)} %get-tuple-element.57), channel_id=1, source_target_pairs={{0,8},{8,0},{16,24},{24,16},{1,9},{9,1},{17,25},{25,17},{2,10},{10... | collective-permute-start | bytes 73736 | tf_op jit(solution)/shard_map/ppermute | solution.py:180
  22.9 0.9 %collective-permute-done.4.refs_2_.refs_6_ = f32[8,768]{1,0:T(8,128)S(1)} collective-permute-done((f32[8,768]{1,0:T(8,128)S(1)}, f32[8,768]{1,0:T(8,128)S(1)}, u32[]{:S(2)}, u32[]{:S(2)}) %collective-permute-start.4) | collective-permute-done | bytes 24608 | tf_op jit(solution)/shard_map/ppermute | solution.py:180
  23.8 0.3 collective-permute-done.5.refs_3_.refs_7_
  24.1 0.0 collective-permute-done.8.refs_5_
  24.1 0.0 collective-permute-done.9.refs_6_
  24.1 0.5 %collective-permute-done.7.refs_4_.refs_8_ = f32[8,768]{1,0:T(8,128)S(1)} collective-permute-done((f32[8,768]{1,0:T(8,128)S(1)}, f32[8,768]{1,0:T(8,128)S(1)}, u32[]{:S(2)}, u32[]{:S(2)}) %collective-permute-start.7) | collective-permute-done | bytes 24608 | tf_op jit(solution)/shard_map/ppermute | solution.py:180
  24.7 1.0 %shard_map.179 = (f32[4,64,128]{2,1,0:T(8,128)S(1)}, f32[6,40,128]{2,1,0:T(8,128)S(1)}) custom-call(f32[4,64,128]{2,1,0:T(8,128)S(1)} %get-tuple-element.51.refs_0_, f32[72,128]{1,0:T(8,128)S(1)} %get-tuple-element.52.refs_1_, f32[8,768]{1,0:T(8,128)S(1)} %collective-permute-done.4.refs_2_.refs_6_, f32[8,768]{1,0:T(8,128)S(1)} %collective-permute-done.5.refs_3_.refs_7_, ...), custom_call_target="tpu_custom_call" | custom-call | tf_op jit(solution)/shard_map/pallas_call | solution.py:167
  25.7 0.0 copy-start
  25.7 1.3 %collective-permute-start.10 = (f32[6,40,128]{2,1,0:T(8,128)S(1)}, f32[6,40,128]{2,1,0:T(8,128)S(1)}, u32[]{:S(2)}, u32[]{:S(2)}) collective-permute-start(f32[6,40,128]{2,1,0:T(8,128)S(1)} %get-tuple-element.62.refs_5_), channel_id=1, source_target_pairs={{0,2},{1,3},{2,0},{3,1},{4,6},{5,7},{6,4},{7,5},{8,10},{9,11},{10,... | collective-permute-start | bytes 368648 | tf_op jit(solution)/shard_map/ppermute | solution.py:187
  27.0 2.1 %collective-permute-start.11 = (f32[6,40,128]{2,1,0:T(8,128)S(1)}, f32[6,40,128]{2,1,0:T(8,128)S(1)}, u32[]{:S(2)}, u32[]{:S(2)}) collective-permute-start(f32[6,40,128]{2,1,0:T(8,128)S(1)} %get-tuple-element.62.refs_5_), channel_id=1, source_target_pairs={{0,1},{1,0},{2,3},{3,2},{4,5},{5,4},{6,7},{7,6},{8,9},{9,8},{10,11... | collective-permute-start | bytes 368648 | tf_op jit(solution)/shard_map/ppermute | solution.py:187
  29.1 1.1 %shard_map.180 = (f32[8,128,128]{2,1,0:T(8,128)}, f32[128,128]{1,0:T(8,128)S(1)}, f32[2,64,128]{2,1,0:T(8,128)S(1)}) custom-call(f32[8,128,128]{2,1,0:T(8,128)S(1)} %get-tuple-element.39.u_ref.refs_0_.refs_2_, f32[1024,128]{1,0:T(8,128)S(1)} %get-tuple-element.43.refs_0_.refs_1_, f32[4,64,128]{2,1,0:T(8,128)S(1)} %get-tuple-element.61.refs_2_.refs_0_, ...), custom_call_target="tpu_custom_call" | custom-call | tf_op jit(solution)/shard_map/pallas_call | solution.py:167
  30.2 2.3 %collective-permute-start.12 = (f32[6,40,128]{2,1,0:T(8,128)S(1)}, f32[6,40,128]{2,1,0:T(8,128)S(1)}, u32[]{:S(2)}, u32[]{:S(2)}) collective-permute-start(f32[6,40,128]{2,1,0:T(8,128)S(1)} %collective-permute-done.10.refs_7_), channel_id=1, source_target_pairs={{0,1},{1,0},{2,3},{3,2},{4,5},{5,4},{6,7},{7,6},{8,9},{9,8},{10,11... | collective-permute-start | bytes 368648 | tf_op jit(solution)/shard_map/ppermute | solution.py:187
  32.5 1.0 %collective-permute-done.12.refs_8_ = f32[6,40,128]{2,1,0:T(8,128)S(1)} collective-permute-done((f32[6,40,128]{2,1,0:T(8,128)S(1)}, f32[6,40,128]{2,1,0:T(8,128)S(1)}, u32[]{:S(2)}, u32[]{:S(2)}) %collective-permute-start.12) | collective-permute-done | bytes 122912 | tf_op jit(solution)/shard_map/ppermute | solution.py:187
  33.5 2.3 %shard_map.181 = (f32[8,128,128]{2,1,0:T(8,128)}, f32[4,64,64]{2,1,0:T(8,128)}, f32[2,32,32]{2,1,0:T(8,128)}, f32[1,16,16]{2,1,0:T(8,128)}) custom-call(f32[4,64,128]{2,1,0:T(8,128)S(1)} %get-tuple-element.61.refs_2_.refs_0_, f32[2,64,128]{2,1,0:T(8,128)S(1)} %get-tuple-element.66.refs_1_, ...), custom_call_target="tpu_custom_call", output_to_operand_aliasing={{0}: (4, {})} | custom-call | tf_op jit(solution)/shard_map/pallas_call | solution.py:167
  (20 shorter events, 0.0 us)
Async XLA Ops:
  2.4 3.8 %collective-permute-start = (f32[16,1024]{1,0:T(8,128)S(1)}, f32[16,1024]{1,0:T(8,128)S(1)}, u32[]{:S(2)}, u32[]{:S(2)}) collective-permute-start(f32[16,1024]{1,0:T(8,128)S(1)} %get-tuple-element.37), channel_id=1, source_target_pairs={{0,4},{4,0},{1,5},{5,1},{2,6},{6,2},{3,7},{7,3},{8,12},{12,8},{9,1... | collective-permute-start | bytes 196616 | tf_op jit(solution)/shard_map/ppermute | solution.py:180
  6.8 4.8 %collective-permute-start.1 = (f32[24,128]{1,0:T(8,128)S(1)}, f32[24,128]{1,0:T(8,128)S(1)}, u32[]{:S(2)}, u32[]{:S(2)}) collective-permute-start(f32[24,128]{1,0:T(8,128)S(1)} %get-tuple-element.48), channel_id=1, source_target_pairs={{0,24},{8,16},{16,8},{24,0},{1,25},{9,17},{17,9},{25,1},{2,26},{10... | collective-permute-start | bytes 36872 | tf_op jit(solution)/shard_map/ppermute | solution.py:180
  10.3 3.4 %collective-permute-start.2 = (f32[24,128]{1,0:T(8,128)S(1)}, f32[24,128]{1,0:T(8,128)S(1)}, u32[]{:S(2)}, u32[]{:S(2)}) collective-permute-start(f32[24,128]{1,0:T(8,128)S(1)} %get-tuple-element.49), channel_id=1, source_target_pairs={{0,16},{8,24},{16,0},{24,8},{1,17},{9,25},{17,1},{25,9},{2,18},{10... | collective-permute-start | bytes 36872 | tf_op jit(solution)/shard_map/ppermute | solution.py:180
  10.3 3.4 %collective-permute-start.3 = (f32[24,128]{1,0:T(8,128)S(1)}, f32[24,128]{1,0:T(8,128)S(1)}, u32[]{:S(2)}, u32[]{:S(2)}) collective-permute-start(f32[24,128]{1,0:T(8,128)S(1)} %get-tuple-element.50), channel_id=1, source_target_pairs={{0,8},{8,0},{16,24},{24,16},{1,9},{9,1},{17,25},{25,17},{2,10},{10... | collective-permute-start | bytes 36872 | tf_op jit(solution)/shard_map/ppermute | solution.py:180
  10.7 3.1 %copy-start.2 = (f32[4,128,136]{2,1,0:T(8,128)S(1)}, f32[4,128,136]{2,1,0:T(8,128)}, u32[]{:S(2)}) copy-start(f32[4,128,136]{2,1,0:T(8,128)} %constant.28.clone.refs_5_) | copy-start | bytes 835588
  10.7 3.1 %copy-start.8 = (f32[4,24,64]{2,1,0:T(8,128)S(1)}, f32[4,24,64]{2,1,0:T(8,128)}, u32[]{:S(2)}) copy-start(f32[4,24,64]{2,1,0:T(8,128)} %constant.33.clone.refs_6_) | copy-start | bytes 73732
  13.8 10.9 %copy-start.3 = (f32[2,384,128]{2,1,0:T(8,128)S(1)}, f32[2,384,128]{2,1,0:T(8,128)}, u32[]{:S(2)}) copy-start(f32[2,384,128]{2,1,0:T(8,128)} %constant.35.clone.refs_9_) | copy-start | bytes 1179652
  13.8 10.8 %copy-start.5 = (f32[4,120,88]{2,1,0:T(8,128)S(1)}, f32[4,120,88]{2,1,0:T(8,128)}, u32[]{:S(2)}) copy-start(f32[4,120,88]{2,1,0:T(8,128)} %constant.34.clone.refs_8_) | copy-start | bytes 506884
  14.6 6.5 %collective-permute-start.6 = (f32[64,128]{1,0:T(8,128)S(1)}, f32[64,128]{1,0:T(8,128)S(1)}, u32[]{:S(2)}, u32[]{:S(2)}) collective-permute-start(f32[64,128]{1,0:T(8,128)S(1)} %get-tuple-element.55), channel_id=1, source_target_pairs={{0,1},{1,0},{2,3},{3,2},{4,5},{5,4},{6,7},{7,6},{8,9},{9,8},{10,11... | collective-permute-start | bytes 98312 | tf_op jit(solution)/shard_map/ppermute | solution.py:180
  17.9 6.2 %collective-permute-start.8 = (f32[64,128]{1,0:T(8,128)S(1)}, f32[64,128]{1,0:T(8,128)S(1)}, u32[]{:S(2)}, u32[]{:S(2)}) collective-permute-start(f32[64,128]{1,0:T(8,128)S(1)} %get-tuple-element.58), channel_id=1, source_target_pairs={{0,3},{1,2},{2,1},{3,0},{4,7},{5,6},{6,5},{7,4},{8,11},{9,10},{10,... | collective-permute-start | bytes 98312 | tf_op jit(solution)/shard_map/ppermute | solution.py:180
  19.1 5.0 %collective-permute-start.9 = (f32[64,128]{1,0:T(8,128)S(1)}, f32[64,128]{1,0:T(8,128)S(1)}, u32[]{:S(2)}, u32[]{:S(2)}) collective-permute-start(f32[64,128]{1,0:T(8,128)S(1)} %get-tuple-element.59), channel_id=1, source_target_pairs={{0,2},{1,3},{2,0},{3,1},{4,6},{5,7},{6,4},{7,5},{8,10},{9,11},{10,... | collective-permute-start | bytes 98312 | tf_op jit(solution)/shard_map/ppermute | solution.py:180
  19.4 4.5 %collective-permute-start.4 = (f32[8,768]{1,0:T(8,128)S(1)}, f32[8,768]{1,0:T(8,128)S(1)}, u32[]{:S(2)}, u32[]{:S(2)}) collective-permute-start(f32[8,768]{1,0:T(8,128)S(1)} %get-tuple-element.53), channel_id=1, source_target_pairs={{0,24},{8,16},{16,8},{24,0},{1,25},{9,17},{17,9},{25,1},{2,26},{10... | collective-permute-start | bytes 73736 | tf_op jit(solution)/shard_map/ppermute | solution.py:180
  20.5 3.6 %collective-permute-start.5 = (f32[8,768]{1,0:T(8,128)S(1)}, f32[8,768]{1,0:T(8,128)S(1)}, u32[]{:S(2)}, u32[]{:S(2)}) collective-permute-start(f32[8,768]{1,0:T(8,128)S(1)} %get-tuple-element.54), channel_id=1, source_target_pairs={{0,16},{8,24},{16,0},{24,8},{1,17},{9,25},{17,1},{25,9},{2,18},{10... | collective-permute-start | bytes 73736 | tf_op jit(solution)/shard_map/ppermute | solution.py:180
  21.1 3.6 %collective-permute-start.7 = (f32[8,768]{1,0:T(8,128)S(1)}, f32[8,768]{1,0:T(8,128)S(1)}, u32[]{:S(2)}, u32[]{:S(2)}) collective-permute-start(f32[8,768]{1,0:T(8,128)S(1)} %get-tuple-element.57), channel_id=1, source_target_pairs={{0,8},{8,0},{16,24},{24,16},{1,9},{9,1},{17,25},{25,17},{2,10},{10... | collective-permute-start | bytes 73736 | tf_op jit(solution)/shard_map/ppermute | solution.py:180
  24.7 4.5 %copy-start.1 = (f32[2,128,128]{2,1,0:T(8,128)S(1)}, f32[2,128,128]{2,1,0:T(8,128)}, u32[]{:S(2)}) copy-start(f32[2,128,128]{2,1,0:T(8,128)} %constant.37.clone.refs_10_.refs_12_) | copy-start | bytes 393220
  24.7 4.5 %copy-start.6 = (f32[4,64,88]{2,1,0:T(8,128)S(1)}, f32[4,64,88]{2,1,0:T(8,128)}, u32[]{:S(2)}) copy-start(f32[4,64,88]{2,1,0:T(8,128)} %constant.36.clone.refs_9_) | copy-start | bytes 270340
  25.7 7.8 %copy-start = (f32[2,768,128]{2,1,0:T(8,128)S(1)}, f32[2,768,128]{2,1,0:T(8,128)}, u32[]{:S(2)}) copy-start(f32[2,768,128]{2,1,0:T(8,128)} %constant.30.clone.refs_11_) | copy-start | bytes 2359300
  25.7 4.5 %collective-permute-start.10 = (f32[6,40,128]{2,1,0:T(8,128)S(1)}, f32[6,40,128]{2,1,0:T(8,128)S(1)}, u32[]{:S(2)}, u32[]{:S(2)}) collective-permute-start(f32[6,40,128]{2,1,0:T(8,128)S(1)} %get-tuple-element.62.refs_5_), channel_id=1, source_target_pairs={{0,2},{1,3},{2,0},{3,1},{4,6},{5,7},{6,4},{7,5},{8,10},{9,11},{10,... | collective-permute-start | bytes 368648 | tf_op jit(solution)/shard_map/ppermute | solution.py:187
  27.0 5.5 %collective-permute-start.11 = (f32[6,40,128]{2,1,0:T(8,128)S(1)}, f32[6,40,128]{2,1,0:T(8,128)S(1)}, u32[]{:S(2)}, u32[]{:S(2)}) collective-permute-start(f32[6,40,128]{2,1,0:T(8,128)S(1)} %get-tuple-element.62.refs_5_), channel_id=1, source_target_pairs={{0,1},{1,0},{2,3},{3,2},{4,5},{5,4},{6,7},{7,6},{8,9},{9,8},{10,11... | collective-permute-start | bytes 368648 | tf_op jit(solution)/shard_map/ppermute | solution.py:187
  29.1 4.4 %copy-start.4 = (f32[4,144,40]{2,1,0:T(8,128)S(1)}, f32[4,144,40]{2,1,0:T(8,128)}, u32[]{:S(2)}) copy-start(f32[4,144,40]{2,1,0:T(8,128)} %constant.29.clone.refs_10_) | copy-start | bytes 276484
  29.1 4.4 %copy-start.7 = (f32[128,80]{1,0:T(8,128)S(1)}, f32[128,80]{1,0:T(8,128)}, u32[]{:S(2)}) copy-start(f32[128,80]{1,0:T(8,128)} %constant.38.clone.refs_9_) | copy-start | bytes 122884
  30.2 3.2 %collective-permute-start.12 = (f32[6,40,128]{2,1,0:T(8,128)S(1)}, f32[6,40,128]{2,1,0:T(8,128)S(1)}, u32[]{:S(2)}, u32[]{:S(2)}) collective-permute-start(f32[6,40,128]{2,1,0:T(8,128)S(1)} %collective-permute-done.10.refs_7_), channel_id=1, source_target_pairs={{0,1},{1,0},{2,3},{3,2},{4,5},{5,4},{6,7},{7,6},{8,9},{9,8},{10,11... | collective-permute-start | bytes 368648 | tf_op jit(solution)/shard_map/ppermute | solution.py:187

commit v10 on v9

--- a/solution.py
+++ b/solution.py
@@ -359,7 +359,9 @@
     messages_y, _ = stacked(fya, fys)
     tables_y, _ = stacked(np.concatenate([ta, tsm], axis=2), np.concatenate([wa, np.zeros((dy, wa.shape[1], 2 * wide))], axis=2),
                           np.concatenate([np.zeros((dy, wsm.shape[1], wide)), wsm], axis=2))
-    tables_x, _ = stacked(txa, txm)
+    tables_x, _ = stacked(txa[:, :, :lx], txm[:, :, : xone.n])
+    rows_x = np.concatenate([txa[:, :, lx:], txm[:, :, xone.n :]], axis=2)
+    rows_x = np.concatenate([rows_x, f2x @ rows_x], axis=1)
     tables_x3, at_x3 = stacked(tx3, qx3, px3)
     tables_y3, at_y3 = stacked(ty3, qy3, py3, py1)
     hz, hx1 = lz // 2, lx // 2
@@ -464,7 +466,8 @@
 
     def y_apply(*refs):
         came = refs[: dy - 1]
-        ty_ref, ta_ref, tsm_ref, ta_out, tsm_out, points = refs[dy - 1 :]
+        ty_ref, ta_ref, tsm_ref, tx_ref, f2x_ref, ta_out, zc_out, six_out, sent_out, points = refs[dy - 1 :]
+        jx, jz = lax.axis_index("gx"), lax.axis_index("gz")
         tn = ((0,), (0,))
         ta_all, tsm_all = ta_ref[...], tsm_ref[...]
         for k, ref in enumerate(came):
@@ -473,54 +476,64 @@
             begin = ly + rowsy * (dy - 1) + ss8 * k
             tsm_all += dot(came_points(ref, points), ty_ref[begin : begin + ss8, wide:], tn)
         ta_out[...] = ta_all
-        tsm_out[...] = tsm_all
-
-    def x_apply(*refs):
-        ta_ref, tsm_ref = refs[:2]
-        came = refs[2 : 1 + dx][::-1]
-        tx_ref, f2x_ref, zc_out, u1_out = refs[1 + dx : 5 + dx]
-        planes_out, xt_outs, rest = refs[5 + dx : 4 + dx + dz], refs[4 + dx + dz : -1], refs[-1]
-        jx, jz = lax.axis_index("gx"), lax.axis_index("gz")
-        xa, xm, diff = [], [], []
-
-        rest[...] = jnp.zeros_like(rest)
-        for k, r in enumerate(came):
-            for z in range(lz):
-                rest[z, k : k + 1, :wide] = r[z : z + 1, :wide]
-            for half in range(hz):
-                rest[half, k : k + 1, wide:] = r[lz + half : lz + half + 1, :wide]
+        zc_out[...] = jnp.zeros_like(zc_out)
+        zc_out[:hx1] = tsm_all[:hx1, :wide]
+        xa, xm = [], []
         for z in range(0, lz, 2):
-            pair = jnp.concatenate([ta_ref[z * lx : (z + 1) * lx, :], ta_ref[(z + 1) * lx : (z + 2) * lx, :]], axis=1)
-            more = jnp.concatenate([rest[z, :, :wide], rest[z + 1, :, :wide]], axis=1)
-            both = dot(tx_ref[jx, : xone.n], jnp.concatenate([pair, more], axis=0))
+            pair = jnp.concatenate([ta_all[z * lx : (z + 1) * lx], ta_all[(z + 1) * lx : (z + 2) * lx]], axis=1)
+            both = dot(tx_ref[jx, : xone.n], pair)
             xa += [both[:, :wide], both[:, wide:]]
-        zc_out[...] = jnp.zeros_like(zc_out)
-        zc_out[:hx1] = tsm_ref[:hx1, :wide]
-        begin = lz + 2 * hz
-        zc_out[hx1 : hx1 + 1] = from_next(jx, tsm_ref[hx1 - 1 : hx1, :wide], [r[begin : begin + 1, :wide] for r in came])
         for half in range(0, hz, 2):
-            pair = jnp.concatenate([tsm_ref[h * hx1 : (h + 1) * hx1, wide:] for h in (half, half + 1)], axis=1)
-            more = jnp.concatenate([rest[half, :, wide:], rest[half + 1, :, wide:]], axis=1)
-            both = dot(tx_ref[jx, xone.n :, : xone.n + ext], jnp.concatenate([pair, more], axis=0))
+            pair = jnp.concatenate([tsm_all[h * hx1 : (h + 1) * hx1, wide:] for h in (half, half + 1)], axis=1)
+            both = dot(tx_ref[jx, xone.n :, : xone.n], pair)
             xm += [both[:, :wide], both[:, wide:]]
+        six = along_planes(jz, xa, xm)
         for half in range(hz):
-            diff.append(tsm_ref[half * hx1 : (half + 1) * hx1, :wide] - xm[half])
+            six[half] += tsm_all[half * hx1 : (half + 1) * hx1, :wide]
+        six = jnp.concatenate(six, axis=1)
+        six_out[...] = six
+        sent_out[...] = dot(f2x_ref[jx], six)
+
+    def along_planes(jz, xa, xm):
         scalar = lambda place: chosen_by(zs[:, place], jz)
-        totals = []
+        made = []
         for zc in range(zn):
-            total = diff[zc] - scalar(at_first + zc) * xm[0] - scalar(at_last + zc) * xm[hz - 1]
+            total = -xm[zc] - scalar(at_first + zc) * xm[0] - scalar(at_last + zc) * xm[hz - 1]
             for z in range(lz):
                 total += scalar(at_local + zc * lz + z) * xa[z]
-            u1_out[zc] = total
-            totals.append(total)
+            made.append(total)
         v = -scalar(2 * lz) * xm[hz - 1]
         w = -scalar(2 * lz + 1) * xm[0]
         for z in range(lz):
             v += scalar(z) * xa[z]
             w += scalar(lz + z) * xa[z]
+        return made + [v, w]
+
+    def x_apply(*refs):
+        own_zc_ref, six_ref, own_sent_ref = refs[:3]
+        came = refs[3 : 2 + dx][::-1]
+        rows_ref, zc_out, u1_out = refs[2 + dx : 5 + dx]
+        planes_out, xt_outs, rest = refs[5 + dx : 4 + dx + dz], refs[4 + dx + dz : -1], refs[-1]
+        jx, jz = lax.axis_index("gx"), lax.axis_index("gz")
+        rest[...] = jnp.zeros_like(rest)
+        for k, r in enumerate(came):
+            for z in range(lz + hz):
+                rest[z, k : k + 1] = r[z : z + 1, :wide]
+        zero = [jnp.zeros_like(rest[0])]
+        lines_a = along_planes(jz, [rest[z] for z in range(lz)], zero * hz)
+        lines_m = along_planes(jz, zero * lz, [rest[lz + half] for half in range(hz)])
+        lines = jnp.concatenate([jnp.concatenate(lines_a, axis=1), jnp.concatenate(lines_m, axis=1)], axis=0)
+        added = dot(rows_ref[jx], lines)
+        six = six_ref[...] + added[: xone.n]
+        sent = own_sent_ref[...] + added[xone.n :]
+        zc_out[...] = own_zc_ref[...]
+        begin = lz + 2 * hz
+        zc_out[hx1 : hx1 + 1] = from_next(jx, own_zc_ref[hx1 - 1 : hx1], [r[begin : begin + 1, :wide] for r in came])
+        for zc in range(zn):
+            u1_out[zc] = six[:, zc * wide : (zc + 1) * wide]
+        v, w = six[:, zn * wide : (zn + 1) * wide], six[:, (zn + 1) * wide :]
         for k, out in enumerate(planes_out):
             out[...] = jnp.where((jz ^ (k + 1)) > jz, w, v)
-        sent = dot(f2x_ref[jx], jnp.concatenate(totals + [v, w], axis=1))
         for k, out in enumerate(xt_outs):
             out[...] = sent[k * kx : (k + 1) * kx]
 
@@ -687,19 +700,18 @@
         scratch=[pltpu.VMEM((ss8, hz * hx1), jnp.float32)],
     )
     xcame = swapped(xm, "gx")
-    ta_v, tsm_v = kernel_call(
+    six_cols = (zn + 2) * wide
+    ta_v, own_zc, six, own_sent = kernel_call(
         y_apply,
-        [(lz * lx, wide), (hz * hx1, 2 * wide)],
-        [*ycame, own_ty, ta_own, tsm_own],
+        [(lz * lx, wide), (xtwo.n + tall, wide), (xone.n, six_cols), (f2x.shape[1], six_cols)],
+        [*ycame, own_ty, ta_own, tsm_own, tables_x, to32(f2x)],
         scratch=[pltpu.VMEM((ss8, hz * hx1), jnp.float32)],
     )
     zc, u1_part, *sent = kernel_call(
         x_apply,
-        [(xtwo.n + tall, wide), (zn, xone.n, wide)]
-        + [(xone.n, wide)] * (dz - 1)
-        + [(kx, (zn + 2) * wide)] * (dx - 1),
-        [ta_v, tsm_v, *xcame[::-1], tables_x, to32(f2x)],
-        scratch=[pltpu.VMEM((lz, ext, 2 * wide), jnp.float32)],
+        [(xtwo.n + tall, wide), (zn, xone.n, wide)] + [(xone.n, wide)] * (dz - 1) + [(kx, six_cols)] * (dx - 1),
+        [own_zc, six, own_sent, *xcame[::-1], to32(rows_x)],
+        scratch=[pltpu.VMEM((lz + hz, ext, wide), jnp.float32)],
     )
     tails = sent[dz - 1 :]
     zcame = swapped(sent[: dz - 1], "gz")

time: 36.3 us -> 36 us (level)
  waiting for transfers between devices: 5.84 us -> 4.58 us
  Pallas kernels: 9.13 us -> 9.75 us
    ppermute x10, waiting for transfers between devices: 4.86 us -> 3.6 us  [swapped(): lax.ppermute(v, axis, [(i, i ^ k) for i in range(count)])]
    pallas_call x8, Pallas kernels: 9.13 us -> 9.75 us  [kernel_call(): pl.pallas_call(body, out_shape=[jax.ShapeDtypeStruct(shape, jnp.float32)...]
  transfers between devices with their start and end apart: 13 -> 13, of which waited for: 6 -> 5; matrix products, arithmetic and copies ran while one was open for 0% -> 0% of each run, Pallas kernels for 8% -> 11%
where the time goes in v10:
time: 36 us; the launch traced here: 35.4 us
  starting transfers between devices  20.3 us (56%)
  Pallas kernels  9.75 us (27%)
  waiting for transfers between devices  4.58 us (13%)
  between operations  0.72 us (2%)
    ppermute x10, starting transfers between devices, swapped(): lax.ppermute(v, axis, [(i, i ^ k) for i in range(count)])  14.4 us
    pallas_call x8, Pallas kernels, kernel_call(): pl.pallas_call(body, out_shape=[jax.ShapeDtypeStruct(shape, jnp.float32)...  9.75 us
    ppermute x3, starting transfers between devices, gathered(): lax.ppermute(what, axis, [(i, i ^ k) for i in range(count)])  5.97 us
    ppermute x10, waiting for transfers between devices, swapped(): lax.ppermute(v, axis, [(i, i ^ k) for i in range(count)])  3.6 us
    ppermute x3, waiting for transfers between devices, gathered(): lax.ppermute(what, axis, [(i, i ^ k) for i in range(count)])  0.98 us
  transfers between devices with their start and end apart: 13, of which 5 were waited for; matrix products, arithmetic and copies ran while one was open for 0% of the time, Pallas kernels for 11%

profile of v10, /device:TPU:1, one launch (start us, length us, event | category | flops | bytes accessed | tf_op | source)
XLA Modules:
  0.0 35.4 jit_solution(4146283589686083090)
XLA Ops:
  0.6 1.8 %shard_map.183 = (f32[8,128,128]{2,1,0:T(8,128)S(1)}, f32[160,384]{1,0:T(8,128)S(1)}, f32[128,8]{1,0:T(8,128)S(1)}, f32[24,1024]{1,0:T(8,128)S(1)}, f32[16,1024]{1,0:T(8,128)S(1)}) custom-call(f32[8,128,128]{2,1,0:T(8,128)} %u_hbm.1, f32[2,32,128]{2,1,0:T(8,128)} %constant.28.clone.table_hbm, f32[2,160,384]{2,1,0:T(8,128)} %constant.29.clone.ty_hbm, ...), custom_call_target="tpu_custom_call" | custom-call | tf_op jit(solution)/shard_map/pallas_call | solution.py:167
  2.4 2.1 %collective-permute-start = (f32[16,1024]{1,0:T(8,128)S(1)}, f32[16,1024]{1,0:T(8,128)S(1)}, u32[]{:S(2)}, u32[]{:S(2)}) collective-permute-start(f32[16,1024]{1,0:T(8,128)S(1)} %get-tuple-element.39), channel_id=1, source_target_pairs={{0,4},{4,0},{1,5},{5,1},{2,6},{6,2},{3,7},{7,3},{8,12},{12,8},{9,1... | collective-permute-start | bytes 196616 | tf_op jit(solution)/shard_map/ppermute | solution.py:180
  4.5 0.8 %shard_map.184 = (f32[1024,128]{1,0:T(8,128)S(1)}, f32[256,256]{1,0:T(8,128)S(1)}, f32[24,128]{1,0:T(8,128)S(1)}, f32[8,256]{1,0:T(8,128)S(1)}) custom-call(f32[8,128,128]{2,1,0:T(8,128)S(1)} %get-tuple-element.41.u_ref.refs_0_.refs_2_, f32[160,384]{1,0:T(8,128)S(1)} %get-tuple-element.40.ty_ref.refs_1_.refs_2_, f32[128,8]{1,0:T(8,128)S(1)} %get-tuple-element.42.fx_ref), custom_call_target="tpu_custom_call" | custom-call | tf_op jit(solution)/shard_map/pallas_call | solution.py:167
  5.3 0.9 %collective-permute-done.refs_0_.refs_1_ = f32[16,1024]{1,0:T(8,128)S(1)} collective-permute-done((f32[16,1024]{1,0:T(8,128)S(1)}, f32[16,1024]{1,0:T(8,128)S(1)}, u32[]{:S(2)}, u32[]{:S(2)}) %collective-permute-start) | collective-permute-done | bytes 65568 | tf_op jit(solution)/shard_map/ppermute | solution.py:180
  6.2 0.6 %shard_map.186 = (f32[24,128]{1,0:T(8,128)S(1)}, f32[24,128]{1,0:T(8,128)S(1)}, f32[24,128]{1,0:T(8,128)S(1)}) custom-call(f32[8,128,128]{2,1,0:T(8,128)S(1)} %get-tuple-element.41.u_ref.refs_0_.refs_2_, f32[16,1024]{1,0:T(8,128)S(1)} %collective-permute-done.refs_0_.refs_1_, f32[160,384]{1,0:T(8,128)S(1)} %get-tuple-element.40.ty_ref.refs_1_.refs_2_, ...), custom_call_target="tpu_custom_call" | custom-call | tf_op jit(solution)/shard_map/pallas_call | solution.py:167
  6.8 3.6 %collective-permute-start.1 = (f32[24,128]{1,0:T(8,128)S(1)}, f32[24,128]{1,0:T(8,128)S(1)}, u32[]{:S(2)}, u32[]{:S(2)}) collective-permute-start(f32[24,128]{1,0:T(8,128)S(1)} %get-tuple-element.51), channel_id=1, source_target_pairs={{0,24},{8,16},{16,8},{24,0},{1,25},{9,17},{17,9},{25,1},{2,26},{10... | collective-permute-start | bytes 36872 | tf_op jit(solution)/shard_map/ppermute | solution.py:180
  10.3 0.0 collective-permute-start.2
  10.3 0.4 %collective-permute-start.3 = (f32[24,128]{1,0:T(8,128)S(1)}, f32[24,128]{1,0:T(8,128)S(1)}, u32[]{:S(2)}, u32[]{:S(2)}) collective-permute-start(f32[24,128]{1,0:T(8,128)S(1)} %get-tuple-element.53), channel_id=1, source_target_pairs={{0,8},{8,0},{16,24},{24,16},{1,9},{9,1},{17,25},{25,17},{2,10},{10... | collective-permute-start | bytes 36872 | tf_op jit(solution)/shard_map/ppermute | solution.py:180
  10.7 1.8 %shard_map.185 = (f32[1024,128]{1,0:T(8,128)S(1)}, f32[72,128]{1,0:T(8,128)S(1)}, f32[64,768]{1,0:T(8,128)S(1)}, f32[24,768]{1,0:T(8,128)S(1)}) custom-call(f32[16,1024]{1,0:T(8,128)S(1)} %collective-permute-done.refs_0_.refs_1_, f32[160,384]{1,0:T(8,128)S(1)} %get-tuple-element.40.ty_ref.refs_1_.refs_2_, f32[1024,128]{1,0:T(8,128)S(1)} %get-tuple-element.43.refs_2_, ...), custom_call_target="tpu_custom_call" | custom-call | tf_op jit(solution)/shard_map/pallas_call | solution.py:167
  12.6 0.0 collective-permute-done.1.refs_3_
  12.6 1.2 %collective-permute-done.2.refs_4_ = f32[24,128]{1,0:T(8,128)S(1)} collective-permute-done((f32[24,128]{1,0:T(8,128)S(1)}, f32[24,128]{1,0:T(8,128)S(1)}, u32[]{:S(2)}, u32[]{:S(2)}) %collective-permute-start.2) | collective-permute-done | bytes 12320 | tf_op jit(solution)/shard_map/ppermute | solution.py:180
  13.8 0.0 collective-permute-done.3.refs_5_
  13.8 0.4 %shard_map.187 = (f32[72,128]{1,0:T(8,128)S(1)}, f32[4,64,128]{2,1,0:T(8,128)S(1)}, f32[64,128]{1,0:T(8,128)S(1)}, f32[64,128]{1,0:T(8,128)S(1)}, f32[64,128]{1,...) custom-call(f32[72,128]{1,0:T(8,128)S(1)} %get-tuple-element.45.refs_0_, ...), custom_call_target="tpu_custom_call" | custom-call | tf_op jit(solution)/shard_map/pallas_call | solution.py:167
  14.2 3.3 %collective-permute-start.6 = (f32[64,128]{1,0:T(8,128)S(1)}, f32[64,128]{1,0:T(8,128)S(1)}, u32[]{:S(2)}, u32[]{:S(2)}) collective-permute-start(f32[64,128]{1,0:T(8,128)S(1)} %get-tuple-element.58), channel_id=1, source_target_pairs={{0,1},{1,0},{2,3},{3,2},{4,5},{5,4},{6,7},{7,6},{8,9},{9,8},{10,11... | collective-permute-start | bytes 98312 | tf_op jit(solution)/shard_map/ppermute | solution.py:180
  17.5 1.2 %collective-permute-start.8 = (f32[64,128]{1,0:T(8,128)S(1)}, f32[64,128]{1,0:T(8,128)S(1)}, u32[]{:S(2)}, u32[]{:S(2)}) collective-permute-start(f32[64,128]{1,0:T(8,128)S(1)} %get-tuple-element.61), channel_id=1, source_target_pairs={{0,3},{1,2},{2,1},{3,0},{4,7},{5,6},{6,5},{7,4},{8,11},{9,10},{10,... | collective-permute-start | bytes 98312 | tf_op jit(solution)/shard_map/ppermute | solution.py:180
  18.7 0.3 collective-permute-start.9
  19.0 1.4 %collective-permute-start.4 = (f32[8,768]{1,0:T(8,128)S(1)}, f32[8,768]{1,0:T(8,128)S(1)}, u32[]{:S(2)}, u32[]{:S(2)}) collective-permute-start(f32[8,768]{1,0:T(8,128)S(1)} %get-tuple-element.56), channel_id=1, source_target_pairs={{0,24},{8,16},{16,8},{24,0},{1,25},{9,17},{17,9},{25,1},{2,26},{10... | collective-permute-start | bytes 73736 | tf_op jit(solution)/shard_map/ppermute | solution.py:180
  20.4 0.3 collective-permute-start.5
  20.7 0.0 collective-permute-done.6.refs_7_
  20.7 1.8 %collective-permute-start.7 = (f32[8,768]{1,0:T(8,128)S(1)}, f32[8,768]{1,0:T(8,128)S(1)}, u32[]{:S(2)}, u32[]{:S(2)}) collective-permute-start(f32[8,768]{1,0:T(8,128)S(1)} %get-tuple-element.60), channel_id=1, source_target_pairs={{0,8},{8,0},{16,24},{24,16},{1,9},{9,1},{17,25},{25,17},{2,10},{10... | collective-permute-start | bytes 73736 | tf_op jit(solution)/shard_map/ppermute | solution.py:180
  22.5 0.9 %collective-permute-done.4.refs_2_.refs_6_ = f32[8,768]{1,0:T(8,128)S(1)} collective-permute-done((f32[8,768]{1,0:T(8,128)S(1)}, f32[8,768]{1,0:T(8,128)S(1)}, u32[]{:S(2)}, u32[]{:S(2)}) %collective-permute-start.4) | collective-permute-done | bytes 24608 | tf_op jit(solution)/shard_map/ppermute | solution.py:180
  23.4 0.6 %collective-permute-done.5.refs_3_.refs_7_ = f32[8,768]{1,0:T(8,128)S(1)} collective-permute-done((f32[8,768]{1,0:T(8,128)S(1)}, f32[8,768]{1,0:T(8,128)S(1)}, u32[]{:S(2)}, u32[]{:S(2)}) %collective-permute-start.5) | collective-permute-done | bytes 24608 | tf_op jit(solution)/shard_map/ppermute | solution.py:180
  24.0 0.0 collective-permute-done.7.refs_4_.refs_8_
  24.0 1.0 %shard_map.188 = (f32[4,64,128]{2,1,0:T(8,128)S(1)}, f32[6,40,128]{2,1,0:T(8,128)S(1)}) custom-call(f32[4,64,128]{2,1,0:T(8,128)S(1)} %get-tuple-element.54.refs_0_, f32[72,128]{1,0:T(8,128)S(1)} %get-tuple-element.55.refs_1_, f32[8,768]{1,0:T(8,128)S(1)} %collective-permute-done.4.refs_2_.refs_6_, f32[8,768]{1,0:T(8,128)S(1)} %collective-permute-done.5.refs_3_.refs_7_, ...), custom_call_target="tpu_custom_call" | custom-call | tf_op jit(solution)/shard_map/pallas_call | solution.py:167
  25.1 0.0 copy-start
  25.1 1.3 %collective-permute-start.10 = (f32[6,40,128]{2,1,0:T(8,128)S(1)}, f32[6,40,128]{2,1,0:T(8,128)S(1)}, u32[]{:S(2)}, u32[]{:S(2)}) collective-permute-start(f32[6,40,128]{2,1,0:T(8,128)S(1)} %get-tuple-element.65.refs_5_), channel_id=1, source_target_pairs={{0,2},{1,3},{2,0},{3,1},{4,6},{5,7},{6,4},{7,5},{8,10},{9,11},{10,... | collective-permute-start | bytes 368648 | tf_op jit(solution)/shard_map/ppermute | solution.py:187
  26.4 2.4 %collective-permute-start.11 = (f32[6,40,128]{2,1,0:T(8,128)S(1)}, f32[6,40,128]{2,1,0:T(8,128)S(1)}, u32[]{:S(2)}, u32[]{:S(2)}) collective-permute-start(f32[6,40,128]{2,1,0:T(8,128)S(1)} %get-tuple-element.65.refs_5_), channel_id=1, source_target_pairs={{0,1},{1,0},{2,3},{3,2},{4,5},{5,4},{6,7},{7,6},{8,9},{9,8},{10,11... | collective-permute-start | bytes 368648 | tf_op jit(solution)/shard_map/ppermute | solution.py:187
  28.8 1.1 %shard_map.189 = (f32[8,128,128]{2,1,0:T(8,128)}, f32[128,128]{1,0:T(8,128)S(1)}, f32[2,64,128]{2,1,0:T(8,128)S(1)}) custom-call(f32[8,128,128]{2,1,0:T(8,128)S(1)} %get-tuple-element.41.u_ref.refs_0_.refs_2_, f32[1024,128]{1,0:T(8,128)S(1)} %get-tuple-element.66.refs_1_, f32[4,64,128]{2,1,0:T(8,128)S(1)} %get-tuple-element.64.refs_2_.refs_0_, ...), custom_call_target="tpu_custom_call" | custom-call | tf_op jit(solution)/shard_map/pallas_call | solution.py:167
  29.9 2.3 %collective-permute-start.12 = (f32[6,40,128]{2,1,0:T(8,128)S(1)}, f32[6,40,128]{2,1,0:T(8,128)S(1)}, u32[]{:S(2)}, u32[]{:S(2)}) collective-permute-start(f32[6,40,128]{2,1,0:T(8,128)S(1)} %collective-permute-done.10.refs_7_), channel_id=1, source_target_pairs={{0,1},{1,0},{2,3},{3,2},{4,5},{5,4},{6,7},{7,6},{8,9},{9,8},{10,11... | collective-permute-start | bytes 368648 | tf_op jit(solution)/shard_map/ppermute | solution.py:187
  32.2 0.0 collective-permute-done.11.refs_6_
  32.2 1.0 %collective-permute-done.12.refs_8_ = f32[6,40,128]{2,1,0:T(8,128)S(1)} collective-permute-done((f32[6,40,128]{2,1,0:T(8,128)S(1)}, f32[6,40,128]{2,1,0:T(8,128)S(1)}, u32[]{:S(2)}, u32[]{:S(2)}) %collective-permute-start.12) | collective-permute-done | bytes 122912 | tf_op jit(solution)/shard_map/ppermute | solution.py:187
  33.2 2.2 %shard_map.190 = (f32[8,128,128]{2,1,0:T(8,128)}, f32[4,64,64]{2,1,0:T(8,128)}, f32[2,32,32]{2,1,0:T(8,128)}, f32[1,16,16]{2,1,0:T(8,128)}) custom-call(f32[4,64,128]{2,1,0:T(8,128)S(1)} %get-tuple-element.64.refs_2_.refs_0_, f32[2,64,128]{2,1,0:T(8,128)S(1)} %get-tuple-element.70.refs_1_, ...), custom_call_target="tpu_custom_call", output_to_operand_aliasing={{0}: (4, {})} | custom-call | tf_op jit(solution)/shard_map/pallas_call | solution.py:167
  (22 shorter events, 0.0 us)
Async XLA Ops:
  2.4 3.8 %collective-permute-start = (f32[16,1024]{1,0:T(8,128)S(1)}, f32[16,1024]{1,0:T(8,128)S(1)}, u32[]{:S(2)}, u32[]{:S(2)}) collective-permute-start(f32[16,1024]{1,0:T(8,128)S(1)} %get-tuple-element.39), channel_id=1, source_target_pairs={{0,4},{4,0},{1,5},{5,1},{2,6},{6,2},{3,7},{7,3},{8,12},{12,8},{9,1... | collective-permute-start | bytes 196616 | tf_op jit(solution)/shard_map/ppermute | solution.py:180
  6.2 4.5 %copy-start.4 = (f32[4,128,128]{2,1,0:T(8,128)S(1)}, f32[4,128,128]{2,1,0:T(8,128)}, u32[]{:S(2)}) copy-start(f32[4,128,128]{2,1,0:T(8,128)} %constant.30.clone.refs_4_) | copy-start | bytes 786436
  6.2 4.5 %copy-start.9 = (f32[4,24,64]{2,1,0:T(8,128)S(1)}, f32[4,24,64]{2,1,0:T(8,128)}, u32[]{:S(2)}) copy-start(f32[4,24,64]{2,1,0:T(8,128)} %constant.35.clone.refs_5_) | copy-start | bytes 73732
  6.8 5.8 %collective-permute-start.1 = (f32[24,128]{1,0:T(8,128)S(1)}, f32[24,128]{1,0:T(8,128)S(1)}, u32[]{:S(2)}, u32[]{:S(2)}) collective-permute-start(f32[24,128]{1,0:T(8,128)S(1)} %get-tuple-element.51), channel_id=1, source_target_pairs={{0,24},{8,16},{16,8},{24,0},{1,25},{9,17},{17,9},{25,1},{2,26},{10... | collective-permute-start | bytes 36872 | tf_op jit(solution)/shard_map/ppermute | solution.py:180
  10.3 3.4 %collective-permute-start.2 = (f32[24,128]{1,0:T(8,128)S(1)}, f32[24,128]{1,0:T(8,128)S(1)}, u32[]{:S(2)}, u32[]{:S(2)}) collective-permute-start(f32[24,128]{1,0:T(8,128)S(1)} %get-tuple-element.52), channel_id=1, source_target_pairs={{0,16},{8,24},{16,0},{24,8},{1,17},{9,25},{17,1},{25,9},{2,18},{10... | collective-permute-start | bytes 36872 | tf_op jit(solution)/shard_map/ppermute | solution.py:180
  10.3 3.4 %collective-permute-start.3 = (f32[24,128]{1,0:T(8,128)S(1)}, f32[24,128]{1,0:T(8,128)S(1)}, u32[]{:S(2)}, u32[]{:S(2)}) collective-permute-start(f32[24,128]{1,0:T(8,128)S(1)} %get-tuple-element.53), channel_id=1, source_target_pairs={{0,8},{8,0},{16,24},{24,16},{1,9},{9,1},{17,25},{25,17},{2,10},{10... | collective-permute-start | bytes 36872 | tf_op jit(solution)/shard_map/ppermute | solution.py:180
  10.7 3.1 %copy-start.6 = (f32[4,88,16]{2,1,0:T(8,128)S(1)}, f32[4,88,16]{2,1,0:T(8,128)}, u32[]{:S(2)}) copy-start(f32[4,88,16]{2,1,0:T(8,128)} %constant.36.clone.refs_6_) | copy-start | bytes 67588
  10.7 13.3 %copy-start.5 = (f32[4,120,88]{2,1,0:T(8,128)S(1)}, f32[4,120,88]{2,1,0:T(8,128)}, u32[]{:S(2)}) copy-start(f32[4,120,88]{2,1,0:T(8,128)} %constant.37.clone.refs_8_) | copy-start | bytes 506884
  12.6 11.5 %copy-start.2 = (f32[2,384,128]{2,1,0:T(8,128)S(1)}, f32[2,384,128]{2,1,0:T(8,128)}, u32[]{:S(2)}) copy-start(f32[2,384,128]{2,1,0:T(8,128)} %constant.38.clone.refs_9_) | copy-start | bytes 1179652
  14.2 6.5 %collective-permute-start.6 = (f32[64,128]{1,0:T(8,128)S(1)}, f32[64,128]{1,0:T(8,128)S(1)}, u32[]{:S(2)}, u32[]{:S(2)}) collective-permute-start(f32[64,128]{1,0:T(8,128)S(1)} %get-tuple-element.58), channel_id=1, source_target_pairs={{0,1},{1,0},{2,3},{3,2},{4,5},{5,4},{6,7},{7,6},{8,9},{9,8},{10,11... | collective-permute-start | bytes 98312 | tf_op jit(solution)/shard_map/ppermute | solution.py:180
  17.5 6.5 %collective-permute-start.8 = (f32[64,128]{1,0:T(8,128)S(1)}, f32[64,128]{1,0:T(8,128)S(1)}, u32[]{:S(2)}, u32[]{:S(2)}) collective-permute-start(f32[64,128]{1,0:T(8,128)S(1)} %get-tuple-element.61), channel_id=1, source_target_pairs={{0,3},{1,2},{2,1},{3,0},{4,7},{5,6},{6,5},{7,4},{8,11},{9,10},{10,... | collective-permute-start | bytes 98312 | tf_op jit(solution)/shard_map/ppermute | solution.py:180
  18.7 5.3 %collective-permute-start.9 = (f32[64,128]{1,0:T(8,128)S(1)}, f32[64,128]{1,0:T(8,128)S(1)}, u32[]{:S(2)}, u32[]{:S(2)}) collective-permute-start(f32[64,128]{1,0:T(8,128)S(1)} %get-tuple-element.62), channel_id=1, source_target_pairs={{0,2},{1,3},{2,0},{3,1},{4,6},{5,7},{6,4},{7,5},{8,10},{9,11},{10,... | collective-permute-start | bytes 98312 | tf_op jit(solution)/shard_map/ppermute | solution.py:180
  19.0 4.5 %collective-permute-start.4 = (f32[8,768]{1,0:T(8,128)S(1)}, f32[8,768]{1,0:T(8,128)S(1)}, u32[]{:S(2)}, u32[]{:S(2)}) collective-permute-start(f32[8,768]{1,0:T(8,128)S(1)} %get-tuple-element.56), channel_id=1, source_target_pairs={{0,24},{8,16},{16,8},{24,0},{1,25},{9,17},{17,9},{25,1},{2,26},{10... | collective-permute-start | bytes 73736 | tf_op jit(solution)/shard_map/ppermute | solution.py:180
  20.4 3.6 %collective-permute-start.5 = (f32[8,768]{1,0:T(8,128)S(1)}, f32[8,768]{1,0:T(8,128)S(1)}, u32[]{:S(2)}, u32[]{:S(2)}) collective-permute-start(f32[8,768]{1,0:T(8,128)S(1)} %get-tuple-element.57), channel_id=1, source_target_pairs={{0,16},{8,24},{16,0},{24,8},{1,17},{9,25},{17,1},{25,9},{2,18},{10... | collective-permute-start | bytes 73736 | tf_op jit(solution)/shard_map/ppermute | solution.py:180
  20.7 3.3 %collective-permute-start.7 = (f32[8,768]{1,0:T(8,128)S(1)}, f32[8,768]{1,0:T(8,128)S(1)}, u32[]{:S(2)}, u32[]{:S(2)}) collective-permute-start(f32[8,768]{1,0:T(8,128)S(1)} %get-tuple-element.60), channel_id=1, source_target_pairs={{0,8},{8,0},{16,24},{24,16},{1,9},{9,1},{17,25},{25,17},{2,10},{10... | collective-permute-start | bytes 73736 | tf_op jit(solution)/shard_map/ppermute | solution.py:180
  24.0 4.8 %copy-start.1 = (f32[2,128,128]{2,1,0:T(8,128)S(1)}, f32[2,128,128]{2,1,0:T(8,128)}, u32[]{:S(2)}) copy-start(f32[2,128,128]{2,1,0:T(8,128)} %constant.40.clone.refs_10_.refs_12_) | copy-start | bytes 393220
  24.0 4.8 %copy-start.7 = (f32[4,64,88]{2,1,0:T(8,128)S(1)}, f32[4,64,88]{2,1,0:T(8,128)}, u32[]{:S(2)}) copy-start(f32[4,64,88]{2,1,0:T(8,128)} %constant.39.clone.refs_9_) | copy-start | bytes 270340
  25.1 8.1 %copy-start = (f32[2,768,128]{2,1,0:T(8,128)S(1)}, f32[2,768,128]{2,1,0:T(8,128)}, u32[]{:S(2)}) copy-start(f32[2,768,128]{2,1,0:T(8,128)} %constant.32.clone.refs_11_) | copy-start | bytes 2359300
  25.1 4.8 %collective-permute-start.10 = (f32[6,40,128]{2,1,0:T(8,128)S(1)}, f32[6,40,128]{2,1,0:T(8,128)S(1)}, u32[]{:S(2)}, u32[]{:S(2)}) collective-permute-start(f32[6,40,128]{2,1,0:T(8,128)S(1)} %get-tuple-element.65.refs_5_), channel_id=1, source_target_pairs={{0,2},{1,3},{2,0},{3,1},{4,6},{5,7},{6,4},{7,5},{8,10},{9,11},{10,... | collective-permute-start | bytes 368648 | tf_op jit(solution)/shard_map/ppermute | solution.py:187
  26.4 5.8 %collective-permute-start.11 = (f32[6,40,128]{2,1,0:T(8,128)S(1)}, f32[6,40,128]{2,1,0:T(8,128)S(1)}, u32[]{:S(2)}, u32[]{:S(2)}) collective-permute-start(f32[6,40,128]{2,1,0:T(8,128)S(1)} %get-tuple-element.65.refs_5_), channel_id=1, source_target_pairs={{0,1},{1,0},{2,3},{3,2},{4,5},{5,4},{6,7},{7,6},{8,9},{9,8},{10,11... | collective-permute-start | bytes 368648 | tf_op jit(solution)/shard_map/ppermute | solution.py:187
  28.8 4.4 %copy-start.3 = (f32[4,144,40]{2,1,0:T(8,128)S(1)}, f32[4,144,40]{2,1,0:T(8,128)}, u32[]{:S(2)}) copy-start(f32[4,144,40]{2,1,0:T(8,128)} %constant.31.clone.refs_10_) | copy-start | bytes 276484
  28.8 4.4 %copy-start.8 = (f32[128,80]{1,0:T(8,128)S(1)}, f32[128,80]{1,0:T(8,128)}, u32[]{:S(2)}) copy-start(f32[128,80]{1,0:T(8,128)} %constant.41.clone.refs_9_) | copy-start | bytes 122884
  29.9 3.2 %collective-permute-start.12 = (f32[6,40,128]{2,1,0:T(8,128)S(1)}, f32[6,40,128]{2,1,0:T(8,128)S(1)}, u32[]{:S(2)}, u32[]{:S(2)}) collective-permute-start(f32[6,40,128]{2,1,0:T(8,128)S(1)} %collective-permute-done.10.refs_7_), channel_id=1, source_target_pairs={{0,1},{1,0},{2,3},{3,2},{4,5},{5,4},{6,7},{7,6},{8,9},{9,8},{10,11... | collective-permute-start | bytes 368648 | tf_op jit(solution)/shard_map/ppermute | solution.py:187

commit v11 on v10

--- a/solution.py
+++ b/solution.py
@@ -565,11 +565,10 @@
         for half in range(zn // 2):
             i2_out[half] = spread[half * xtwo.fine : (half + 1) * xtwo.fine]
 
-    def second_apply(*refs):
-        part_ref, zc_ref = refs[:2]
-        xcame, zcame = refs[2 : dx + 1][::-1], refs[dx + 1 : dz + dx][::-1]
-        tx2_ref, ty2_ref, u1_out, zt_out = refs[dz + dx :]
-        jx, jy, jz = lax.axis_index("gx"), lax.axis_index("gy"), lax.axis_index("gz")
+    def second_own(*refs):
+        part_ref, zcame = refs[0], refs[1:dz][::-1]
+        tx2_ref, u1_out, across_out = refs[dz:]
+        jx, jz = lax.axis_index("gx"), lax.axis_index("gz")
         own = []
         for zc in range(zn):
             total = part_ref[zc]
@@ -577,8 +576,13 @@
                 total += chosen_by(zs[:, at_reach + k * zn + zc], jz) * r[...]
             u1_out[zc] = total
             own.append(total)
-        own = jnp.concatenate(own + [jnp.zeros_like(own[0])] * 2, axis=1)
-        across = dot(tx2_ref[jx], jnp.concatenate([own] + [r[...] for r in xcame], axis=0))
+        across_out[...] = dot(tx2_ref[jx, :, : xtwo.fine], jnp.concatenate(own, axis=1))
+
+    def second_apply(across_ref, zc_ref, *refs):
+        xcame, (tx2_ref, ty2_ref, zt_out) = refs[:-3][::-1], refs[-3:]
+        jx, jy = lax.axis_index("gx"), lax.axis_index("gy")
+        across = dot(tx2_ref[jx, :, xtwo.fine :], jnp.concatenate([r[...] for r in xcame], axis=0))
+        across = jnp.concatenate([across_ref[...] + across[:, : zn * wide], across[:, zn * wide :]], axis=1)
         cut = [across[:, z * wide : (z + 1) * wide] for z in range(zn + 2)]
         whole = [z for z in range(zn + 2) if z % 2 == 0 or z >= zn]
         joined = [jnp.concatenate([cut[z][c * tall : (c + 1) * tall] for c in range(3)], axis=1) for z in whole]
@@ -718,10 +722,12 @@
     if dz > 1 and dx > 1:
         zcame[0], tails[0] = lax.optimization_barrier((zcame[0], tails[0]))
     xtcame = swapped(tails, "gx")
-    u1, zmsg = kernel_call(
-        second_apply,
-        [(zn, xone.n, wide), (lz2 + 2, tall, packed)],
-        [u1_part, zc, *xtcame[::-1], *zcame[::-1], to32(tx2), to32(ty2)],
+    tables_x2 = to32(tx2)
+    u1, across = kernel_call(
+        second_own, [(zn, xone.n, wide), (3 * tall, zn * wide)], [u1_part, *zcame[::-1], tables_x2]
+    )
+    (zmsg,) = kernel_call(
+        second_apply, [(lz2 + 2, tall, packed)], [across, zc, *xtcame[::-1], tables_x2, to32(ty2)]
     )
     beside = kernel_call(
         interpolate,

time: 36 us -> 36.1 us (level)
  Pallas kernels: 9.75 us -> 10.2 us
    pallas_call x8 -> x9, Pallas kernels: 9.75 us -> 10.2 us  [kernel_call(): pl.pallas_call(body, out_shape=[jax.ShapeDtypeStruct(shape, jnp.float32)...]
    ppermute x10, waiting for transfers between devices: 3.6 us -> 3.24 us  [swapped(): lax.ppermute(v, axis, [(i, i ^ k) for i in range(count)])]
  transfers between devices with their start and end apart: 13 -> 13, of which waited for: 5 -> 5; matrix products, arithmetic and copies ran while one was open for 0% -> 0% of each run, Pallas kernels for 11% -> 12%
where the time goes in v11:
time: 36.1 us; the launch traced here: 35.5 us
  starting transfers between devices  20.3 us (56%)
  Pallas kernels  10.2 us (28%)
  waiting for transfers between devices  4.22 us (12%)
  between operations  0.72 us (2%)
    ppermute x10, starting transfers between devices, swapped(): lax.ppermute(v, axis, [(i, i ^ k) for i in range(count)])  14.4 us
    pallas_call x9, Pallas kernels, kernel_call(): pl.pallas_call(body, out_shape=[jax.ShapeDtypeStruct(shape, jnp.float32)...  10.2 us
    ppermute x3, starting transfers between devices, gathered(): lax.ppermute(what, axis, [(i, i ^ k) for i in range(count)])  5.94 us
    ppermute x10, waiting for transfers between devices, swapped(): lax.ppermute(v, axis, [(i, i ^ k) for i in range(count)])  3.24 us
    ppermute x3, waiting for transfers between devices, gathered(): lax.ppermute(what, axis, [(i, i ^ k) for i in range(count)])  0.98 us
  transfers between devices with their start and end apart: 13, of which 5 were waited for; matrix products, arithmetic and copies ran while one was open for 0% of the time, Pallas kernels for 12%

profile of v11, /device:TPU:1, one launch (start us, length us, event | category | flops | bytes accessed | tf_op | source)
XLA Modules:
  0.0 35.5 jit_solution(26623960028426470)
XLA Ops:
  0.6 1.8 %shard_map.183 = (f32[8,128,128]{2,1,0:T(8,128)S(1)}, f32[160,384]{1,0:T(8,128)S(1)}, f32[128,8]{1,0:T(8,128)S(1)}, f32[24,1024]{1,0:T(8,128)S(1)}, f32[16,1024]{1,0:T(8,128)S(1)}) custom-call(f32[8,128,128]{2,1,0:T(8,128)} %u_hbm.1, f32[2,32,128]{2,1,0:T(8,128)} %constant.28.clone.table_hbm, f32[2,160,384]{2,1,0:T(8,128)} %constant.29.clone.ty_hbm, ...), custom_call_target="tpu_custom_call" | custom-call | tf_op jit(solution)/shard_map/pallas_call | solution.py:167
  2.4 2.1 %collective-permute-start = (f32[16,1024]{1,0:T(8,128)S(1)}, f32[16,1024]{1,0:T(8,128)S(1)}, u32[]{:S(2)}, u32[]{:S(2)}) collective-permute-start(f32[16,1024]{1,0:T(8,128)S(1)} %get-tuple-element.39), channel_id=1, source_target_pairs={{0,4},{4,0},{1,5},{5,1},{2,6},{6,2},{3,7},{7,3},{8,12},{12,8},{9,1... | collective-permute-start | bytes 196616 | tf_op jit(solution)/shard_map/ppermute | solution.py:180
  4.5 0.8 %shard_map.184 = (f32[1024,128]{1,0:T(8,128)S(1)}, f32[256,256]{1,0:T(8,128)S(1)}, f32[24,128]{1,0:T(8,128)S(1)}, f32[8,256]{1,0:T(8,128)S(1)}) custom-call(f32[8,128,128]{2,1,0:T(8,128)S(1)} %get-tuple-element.41.u_ref.refs_0_.refs_2_, f32[160,384]{1,0:T(8,128)S(1)} %get-tuple-element.40.ty_ref.refs_1_.refs_2_, f32[128,8]{1,0:T(8,128)S(1)} %get-tuple-element.42.fx_ref), custom_call_target="tpu_custom_call" | custom-call | tf_op jit(solution)/shard_map/pallas_call | solution.py:167
  5.3 0.9 %collective-permute-done.refs_0_.refs_1_ = f32[16,1024]{1,0:T(8,128)S(1)} collective-permute-done((f32[16,1024]{1,0:T(8,128)S(1)}, f32[16,1024]{1,0:T(8,128)S(1)}, u32[]{:S(2)}, u32[]{:S(2)}) %collective-permute-start) | collective-permute-done | bytes 65568 | tf_op jit(solution)/shard_map/ppermute | solution.py:180
  6.2 0.6 %shard_map.186 = (f32[24,128]{1,0:T(8,128)S(1)}, f32[24,128]{1,0:T(8,128)S(1)}, f32[24,128]{1,0:T(8,128)S(1)}) custom-call(f32[8,128,128]{2,1,0:T(8,128)S(1)} %get-tuple-element.41.u_ref.refs_0_.refs_2_, f32[16,1024]{1,0:T(8,128)S(1)} %collective-permute-done.refs_0_.refs_1_, f32[160,384]{1,0:T(8,128)S(1)} %get-tuple-element.40.ty_ref.refs_1_.refs_2_, ...), custom_call_target="tpu_custom_call" | custom-call | tf_op jit(solution)/shard_map/pallas_call | solution.py:167
  6.8 3.6 %collective-permute-start.1 = (f32[24,128]{1,0:T(8,128)S(1)}, f32[24,128]{1,0:T(8,128)S(1)}, u32[]{:S(2)}, u32[]{:S(2)}) collective-permute-start(f32[24,128]{1,0:T(8,128)S(1)} %get-tuple-element.51), channel_id=1, source_target_pairs={{0,24},{8,16},{16,8},{24,0},{1,25},{9,17},{17,9},{25,1},{2,26},{10... | collective-permute-start | bytes 36872 | tf_op jit(solution)/shard_map/ppermute | solution.py:180
  10.3 0.0 collective-permute-start.2
  10.3 0.4 %collective-permute-start.3 = (f32[24,128]{1,0:T(8,128)S(1)}, f32[24,128]{1,0:T(8,128)S(1)}, u32[]{:S(2)}, u32[]{:S(2)}) collective-permute-start(f32[24,128]{1,0:T(8,128)S(1)} %get-tuple-element.53), channel_id=1, source_target_pairs={{0,8},{8,0},{16,24},{24,16},{1,9},{9,1},{17,25},{25,17},{2,10},{10... | collective-permute-start | bytes 36872 | tf_op jit(solution)/shard_map/ppermute | solution.py:180
  10.7 1.8 %shard_map.185 = (f32[1024,128]{1,0:T(8,128)S(1)}, f32[72,128]{1,0:T(8,128)S(1)}, f32[64,768]{1,0:T(8,128)S(1)}, f32[24,768]{1,0:T(8,128)S(1)}) custom-call(f32[16,1024]{1,0:T(8,128)S(1)} %collective-permute-done.refs_0_.refs_1_, f32[160,384]{1,0:T(8,128)S(1)} %get-tuple-element.40.ty_ref.refs_1_.refs_2_, f32[1024,128]{1,0:T(8,128)S(1)} %get-tuple-element.43.refs_2_, ...), custom_call_target="tpu_custom_call" | custom-call | tf_op jit(solution)/shard_map/pallas_call | solution.py:167
  12.5 0.0 collective-permute-done.1.refs_3_
  12.5 1.2 %collective-permute-done.2.refs_4_ = f32[24,128]{1,0:T(8,128)S(1)} collective-permute-done((f32[24,128]{1,0:T(8,128)S(1)}, f32[24,128]{1,0:T(8,128)S(1)}, u32[]{:S(2)}, u32[]{:S(2)}) %collective-permute-start.2) | collective-permute-done | bytes 12320 | tf_op jit(solution)/shard_map/ppermute | solution.py:180
  13.8 0.0 copy-start.3
  13.8 0.4 %shard_map.187 = (f32[72,128]{1,0:T(8,128)S(1)}, f32[4,64,128]{2,1,0:T(8,128)S(1)}, f32[64,128]{1,0:T(8,128)S(1)}, f32[64,128]{1,0:T(8,128)S(1)}, f32[64,128]{1,...) custom-call(f32[72,128]{1,0:T(8,128)S(1)} %get-tuple-element.45.refs_0_, ...), custom_call_target="tpu_custom_call" | custom-call | tf_op jit(solution)/shard_map/pallas_call | solution.py:167
  14.2 3.3 %collective-permute-start.6 = (f32[64,128]{1,0:T(8,128)S(1)}, f32[64,128]{1,0:T(8,128)S(1)}, u32[]{:S(2)}, u32[]{:S(2)}) collective-permute-start(f32[64,128]{1,0:T(8,128)S(1)} %get-tuple-element.57), channel_id=1, source_target_pairs={{0,1},{1,0},{2,3},{3,2},{4,5},{5,4},{6,7},{7,6},{8,9},{9,8},{10,11... | collective-permute-start | bytes 98312 | tf_op jit(solution)/shard_map/ppermute | solution.py:180
  17.5 1.2 %collective-permute-start.4 = (f32[64,128]{1,0:T(8,128)S(1)}, f32[64,128]{1,0:T(8,128)S(1)}, u32[]{:S(2)}, u32[]{:S(2)}) collective-permute-start(f32[64,128]{1,0:T(8,128)S(1)} %get-tuple-element.55), channel_id=1, source_target_pairs={{0,3},{1,2},{2,1},{3,0},{4,7},{5,6},{6,5},{7,4},{8,11},{9,10},{10,... | collective-permute-start | bytes 98312 | tf_op jit(solution)/shard_map/ppermute | solution.py:180
  18.7 0.3 collective-permute-start.5
  19.0 1.4 %collective-permute-start.7 = (f32[8,768]{1,0:T(8,128)S(1)}, f32[8,768]{1,0:T(8,128)S(1)}, u32[]{:S(2)}, u32[]{:S(2)}) collective-permute-start(f32[8,768]{1,0:T(8,128)S(1)} %get-tuple-element.63), channel_id=1, source_target_pairs={{0,24},{8,16},{16,8},{24,0},{1,25},{9,17},{17,9},{25,1},{2,26},{10... | collective-permute-start | bytes 73736 | tf_op jit(solution)/shard_map/ppermute | solution.py:180
  20.4 0.3 collective-permute-start.8
  20.7 1.8 %collective-permute-start.9 = (f32[8,768]{1,0:T(8,128)S(1)}, f32[8,768]{1,0:T(8,128)S(1)}, u32[]{:S(2)}, u32[]{:S(2)}) collective-permute-start(f32[8,768]{1,0:T(8,128)S(1)} %get-tuple-element.65), channel_id=1, source_target_pairs={{0,8},{8,0},{16,24},{24,16},{1,9},{9,1},{17,25},{25,17},{2,10},{10... | collective-permute-start | bytes 73736 | tf_op jit(solution)/shard_map/ppermute | solution.py:180
  22.5 0.0 collective-permute-done.4.refs_1_
  22.5 0.4 %shard_map.188 = (f32[4,64,128]{2,1,0:T(8,128)S(1)}, f32[120,512]{1,0:T(8,128)S(1)}) custom-call(f32[4,64,128]{2,1,0:T(8,128)S(1)} %get-tuple-element.54.refs_0_, f32[64,128]{1,0:T(8,128)S(1)} %collective-permute-done.4.refs_1_, f32[64,128]{1,0:T(8,128)S(1)} %collective-permute-done.5.refs_2_, f32[64,128]{1,0:T(8,128)S(1)} %collective-permute-done.6.refs_3_, ...), custom_call_target="tpu_custom_call" | custom-call | tf_op jit(solution)/shard_map/pallas_call | solution.py:167
  22.9 0.5 %collective-permute-done.7.refs_0_.refs_6_ = f32[8,768]{1,0:T(8,128)S(1)} collective-permute-done((f32[8,768]{1,0:T(8,128)S(1)}, f32[8,768]{1,0:T(8,128)S(1)}, u32[]{:S(2)}, u32[]{:S(2)}) %collective-permute-start.7) | collective-permute-done | bytes 24608 | tf_op jit(solution)/shard_map/ppermute | solution.py:180
  23.5 0.6 %collective-permute-done.8.refs_1_.refs_7_ = f32[8,768]{1,0:T(8,128)S(1)} collective-permute-done((f32[8,768]{1,0:T(8,128)S(1)}, f32[8,768]{1,0:T(8,128)S(1)}, u32[]{:S(2)}, u32[]{:S(2)}) %collective-permute-start.8) | collective-permute-done | bytes 24608 | tf_op jit(solution)/shard_map/ppermute | solution.py:180
  24.0 0.0 collective-permute-done.9.refs_2_.refs_8_
  24.1 1.1 %shard_map.189.refs_5_ = f32[6,40,128]{2,1,0:T(8,128)S(1)} custom-call(f32[120,512]{1,0:T(8,128)S(1)} %get-tuple-element.61.across_ref, f32[72,128]{1,0:T(8,128)S(1)} %get-tuple-element.62.zc_ref, f32[8,768]{1,0:T(8,128)S(1)} %collective-permute-done.7.refs_0_.refs_6_, f32[8,768]{1,0:T(8,128)S(1)} %collective-permute-done.8.refs_1_.refs_7_, ...), custom_call_target="tpu_custom_call" | custom-call | tf_op jit(solution)/shard_map/pallas_call | solution.py:167
  25.2 0.0 copy-start.1
  25.2 1.3 %collective-permute-start.10 = (f32[6,40,128]{2,1,0:T(8,128)S(1)}, f32[6,40,128]{2,1,0:T(8,128)S(1)}, u32[]{:S(2)}, u32[]{:S(2)}) collective-permute-start(f32[6,40,128]{2,1,0:T(8,128)S(1)} %shard_map.189.refs_5_), channel_id=1, source_target_pairs={{0,2},{1,3},{2,0},{3,1},{4,6},{5,7},{6,4},{7,5},{8,10},{9,11},{10,... | collective-permute-start | bytes 368648 | tf_op jit(solution)/shard_map/ppermute | solution.py:187
  26.5 2.4 %collective-permute-start.11 = (f32[6,40,128]{2,1,0:T(8,128)S(1)}, f32[6,40,128]{2,1,0:T(8,128)S(1)}, u32[]{:S(2)}, u32[]{:S(2)}) collective-permute-start(f32[6,40,128]{2,1,0:T(8,128)S(1)} %shard_map.189.refs_5_), channel_id=1, source_target_pairs={{0,1},{1,0},{2,3},{3,2},{4,5},{5,4},{6,7},{7,6},{8,9},{9,8},{10,11... | collective-permute-start | bytes 368648 | tf_op jit(solution)/shard_map/ppermute | solution.py:187
  28.9 1.1 %shard_map.190 = (f32[8,128,128]{2,1,0:T(8,128)}, f32[128,128]{1,0:T(8,128)S(1)}, f32[2,64,128]{2,1,0:T(8,128)S(1)}) custom-call(f32[8,128,128]{2,1,0:T(8,128)S(1)} %get-tuple-element.41.u_ref.refs_0_.refs_2_, f32[1024,128]{1,0:T(8,128)S(1)} %get-tuple-element.66.refs_1_, f32[4,64,128]{2,1,0:T(8,128)S(1)} %get-tuple-element.60.refs_2_.refs_0_, ...), custom_call_target="tpu_custom_call" | custom-call | tf_op jit(solution)/shard_map/pallas_call | solution.py:167
  30.0 2.3 %collective-permute-start.12 = (f32[6,40,128]{2,1,0:T(8,128)S(1)}, f32[6,40,128]{2,1,0:T(8,128)S(1)}, u32[]{:S(2)}, u32[]{:S(2)}) collective-permute-start(f32[6,40,128]{2,1,0:T(8,128)S(1)} %collective-permute-done.10.refs_7_), channel_id=1, source_target_pairs={{0,1},{1,0},{2,3},{3,2},{4,5},{5,4},{6,7},{7,6},{8,9},{9,8},{10,11... | collective-permute-start | bytes 368648 | tf_op jit(solution)/shard_map/ppermute | solution.py:187
  32.3 1.0 %collective-permute-done.12.refs_8_ = f32[6,40,128]{2,1,0:T(8,128)S(1)} collective-permute-done((f32[6,40,128]{2,1,0:T(8,128)S(1)}, f32[6,40,128]{2,1,0:T(8,128)S(1)}, u32[]{:S(2)}, u32[]{:S(2)}) %collective-permute-start.12) | collective-permute-done | bytes 122912 | tf_op jit(solution)/shard_map/ppermute | solution.py:187
  33.2 2.3 %shard_map.191 = (f32[8,128,128]{2,1,0:T(8,128)}, f32[4,64,64]{2,1,0:T(8,128)}, f32[2,32,32]{2,1,0:T(8,128)}, f32[1,16,16]{2,1,0:T(8,128)}) custom-call(f32[4,64,128]{2,1,0:T(8,128)S(1)} %get-tuple-element.60.refs_2_.refs_0_, f32[2,64,128]{2,1,0:T(8,128)S(1)} %get-tuple-element.70.refs_1_, ...), custom_call_target="tpu_custom_call", output_to_operand_aliasing={{0}: (4, {})} | custom-call | tf_op jit(solution)/shard_map/pallas_call | solution.py:167
  (23 shorter events, 0.0 us)
Async XLA Ops:
  2.4 3.8 %collective-permute-start = (f32[16,1024]{1,0:T(8,128)S(1)}, f32[16,1024]{1,0:T(8,128)S(1)}, u32[]{:S(2)}, u32[]{:S(2)}) collective-permute-start(f32[16,1024]{1,0:T(8,128)S(1)} %get-tuple-element.39), channel_id=1, source_target_pairs={{0,4},{4,0},{1,5},{5,1},{2,6},{6,2},{3,7},{7,3},{8,12},{12,8},{9,1... | collective-permute-start | bytes 196616 | tf_op jit(solution)/shard_map/ppermute | solution.py:180
  6.2 4.5 %copy-start.5 = (f32[4,128,128]{2,1,0:T(8,128)S(1)}, f32[4,128,128]{2,1,0:T(8,128)}, u32[]{:S(2)}) copy-start(f32[4,128,128]{2,1,0:T(8,128)} %constant.30.clone.refs_4_) | copy-start | bytes 786436
  6.2 4.5 %copy-start.9 = (f32[4,24,64]{2,1,0:T(8,128)S(1)}, f32[4,24,64]{2,1,0:T(8,128)}, u32[]{:S(2)}) copy-start(f32[4,24,64]{2,1,0:T(8,128)} %constant.35.clone.refs_5_) | copy-start | bytes 73732
  6.8 5.8 %collective-permute-start.1 = (f32[24,128]{1,0:T(8,128)S(1)}, f32[24,128]{1,0:T(8,128)S(1)}, u32[]{:S(2)}, u32[]{:S(2)}) collective-permute-start(f32[24,128]{1,0:T(8,128)S(1)} %get-tuple-element.51), channel_id=1, source_target_pairs={{0,24},{8,16},{16,8},{24,0},{1,25},{9,17},{17,9},{25,1},{2,26},{10... | collective-permute-start | bytes 36872 | tf_op jit(solution)/shard_map/ppermute | solution.py:180
  10.3 3.4 %collective-permute-start.2 = (f32[24,128]{1,0:T(8,128)S(1)}, f32[24,128]{1,0:T(8,128)S(1)}, u32[]{:S(2)}, u32[]{:S(2)}) collective-permute-start(f32[24,128]{1,0:T(8,128)S(1)} %get-tuple-element.52), channel_id=1, source_target_pairs={{0,16},{8,24},{16,0},{24,8},{1,17},{9,25},{17,1},{25,9},{2,18},{10... | collective-permute-start | bytes 36872 | tf_op jit(solution)/shard_map/ppermute | solution.py:180
  10.3 3.4 %collective-permute-start.3 = (f32[24,128]{1,0:T(8,128)S(1)}, f32[24,128]{1,0:T(8,128)S(1)}, u32[]{:S(2)}, u32[]{:S(2)}) collective-permute-start(f32[24,128]{1,0:T(8,128)S(1)} %get-tuple-element.53), channel_id=1, source_target_pairs={{0,8},{8,0},{16,24},{24,16},{1,9},{9,1},{17,25},{25,17},{2,10},{10... | collective-permute-start | bytes 36872 | tf_op jit(solution)/shard_map/ppermute | solution.py:180
  10.7 3.1 %copy-start.6 = (f32[4,88,16]{2,1,0:T(8,128)S(1)}, f32[4,88,16]{2,1,0:T(8,128)}, u32[]{:S(2)}) copy-start(f32[4,88,16]{2,1,0:T(8,128)} %constant.36.clone.refs_6_) | copy-start | bytes 67588
  13.8 8.7 %copy-start = (f32[4,120,88]{2,1,0:T(8,128)S(1)}, f32[4,120,88]{2,1,0:T(8,128)}, u32[]{:S(2)}) copy-start(f32[4,120,88]{2,1,0:T(8,128)} %constant.37.clone.refs_4_.refs_3_) | copy-start | bytes 506884
  13.8 10.3 %copy-start.3 = (f32[2,384,128]{2,1,0:T(8,128)S(1)}, f32[2,384,128]{2,1,0:T(8,128)}, u32[]{:S(2)}) copy-start(f32[2,384,128]{2,1,0:T(8,128)} %constant.38.clone.refs_4_) | copy-start | bytes 1179652
  14.2 6.5 %collective-permute-start.6 = (f32[64,128]{1,0:T(8,128)S(1)}, f32[64,128]{1,0:T(8,128)S(1)}, u32[]{:S(2)}, u32[]{:S(2)}) collective-permute-start(f32[64,128]{1,0:T(8,128)S(1)} %get-tuple-element.57), channel_id=1, source_target_pairs={{0,1},{1,0},{2,3},{3,2},{4,5},{5,4},{6,7},{7,6},{8,9},{9,8},{10,11... | collective-permute-start | bytes 98312 | tf_op jit(solution)/shard_map/ppermute | solution.py:180
  17.5 5.0 %collective-permute-start.4 = (f32[64,128]{1,0:T(8,128)S(1)}, f32[64,128]{1,0:T(8,128)S(1)}, u32[]{:S(2)}, u32[]{:S(2)}) collective-permute-start(f32[64,128]{1,0:T(8,128)S(1)} %get-tuple-element.55), channel_id=1, source_target_pairs={{0,3},{1,2},{2,1},{3,0},{4,7},{5,6},{6,5},{7,4},{8,11},{9,10},{10,... | collective-permute-start | bytes 98312 | tf_op jit(solution)/shard_map/ppermute | solution.py:180
  18.7 3.8 %collective-permute-start.5 = (f32[64,128]{1,0:T(8,128)S(1)}, f32[64,128]{1,0:T(8,128)S(1)}, u32[]{:S(2)}, u32[]{:S(2)}) collective-permute-start(f32[64,128]{1,0:T(8,128)S(1)} %get-tuple-element.56), channel_id=1, source_target_pairs={{0,2},{1,3},{2,0},{3,1},{4,6},{5,7},{6,4},{7,5},{8,10},{9,11},{10,... | collective-permute-start | bytes 98312 | tf_op jit(solution)/shard_map/ppermute | solution.py:180
  19.0 4.5 %collective-permute-start.7 = (f32[8,768]{1,0:T(8,128)S(1)}, f32[8,768]{1,0:T(8,128)S(1)}, u32[]{:S(2)}, u32[]{:S(2)}) collective-permute-start(f32[8,768]{1,0:T(8,128)S(1)} %get-tuple-element.63), channel_id=1, source_target_pairs={{0,24},{8,16},{16,8},{24,0},{1,25},{9,17},{17,9},{25,1},{2,26},{10... | collective-permute-start | bytes 73736 | tf_op jit(solution)/shard_map/ppermute | solution.py:180
  20.4 3.6 %collective-permute-start.8 = (f32[8,768]{1,0:T(8,128)S(1)}, f32[8,768]{1,0:T(8,128)S(1)}, u32[]{:S(2)}, u32[]{:S(2)}) collective-permute-start(f32[8,768]{1,0:T(8,128)S(1)} %get-tuple-element.64), channel_id=1, source_target_pairs={{0,16},{8,24},{16,0},{24,8},{1,17},{9,25},{17,1},{25,9},{2,18},{10... | collective-permute-start | bytes 73736 | tf_op jit(solution)/shard_map/ppermute | solution.py:180
  20.7 3.3 %collective-permute-start.9 = (f32[8,768]{1,0:T(8,128)S(1)}, f32[8,768]{1,0:T(8,128)S(1)}, u32[]{:S(2)}, u32[]{:S(2)}) collective-permute-start(f32[8,768]{1,0:T(8,128)S(1)} %get-tuple-element.65), channel_id=1, source_target_pairs={{0,8},{8,0},{16,24},{24,16},{1,9},{9,1},{17,25},{25,17},{2,10},{10... | collective-permute-start | bytes 73736 | tf_op jit(solution)/shard_map/ppermute | solution.py:180
  24.1 4.8 %copy-start.2 = (f32[2,128,128]{2,1,0:T(8,128)S(1)}, f32[2,128,128]{2,1,0:T(8,128)}, u32[]{:S(2)}) copy-start(f32[2,128,128]{2,1,0:T(8,128)} %constant.40.clone.refs_10_.refs_12_) | copy-start | bytes 393220
  24.1 4.8 %copy-start.7 = (f32[4,64,88]{2,1,0:T(8,128)S(1)}, f32[4,64,88]{2,1,0:T(8,128)}, u32[]{:S(2)}) copy-start(f32[4,64,88]{2,1,0:T(8,128)} %constant.39.clone.refs_9_) | copy-start | bytes 270340
  25.2 8.1 %copy-start.1 = (f32[2,768,128]{2,1,0:T(8,128)S(1)}, f32[2,768,128]{2,1,0:T(8,128)}, u32[]{:S(2)}) copy-start(f32[2,768,128]{2,1,0:T(8,128)} %constant.32.clone.refs_11_) | copy-start | bytes 2359300
  25.2 4.8 %collective-permute-start.10 = (f32[6,40,128]{2,1,0:T(8,128)S(1)}, f32[6,40,128]{2,1,0:T(8,128)S(1)}, u32[]{:S(2)}, u32[]{:S(2)}) collective-permute-start(f32[6,40,128]{2,1,0:T(8,128)S(1)} %shard_map.189.refs_5_), channel_id=1, source_target_pairs={{0,2},{1,3},{2,0},{3,1},{4,6},{5,7},{6,4},{7,5},{8,10},{9,11},{10,... | collective-permute-start | bytes 368648 | tf_op jit(solution)/shard_map/ppermute | solution.py:187
  26.5 5.8 %collective-permute-start.11 = (f32[6,40,128]{2,1,0:T(8,128)S(1)}, f32[6,40,128]{2,1,0:T(8,128)S(1)}, u32[]{:S(2)}, u32[]{:S(2)}) collective-permute-start(f32[6,40,128]{2,1,0:T(8,128)S(1)} %shard_map.189.refs_5_), channel_id=1, source_target_pairs={{0,1},{1,0},{2,3},{3,2},{4,5},{5,4},{6,7},{7,6},{8,9},{9,8},{10,11... | collective-permute-start | bytes 368648 | tf_op jit(solution)/shard_map/ppermute | solution.py:187
  28.9 4.4 %copy-start.4 = (f32[4,144,40]{2,1,0:T(8,128)S(1)}, f32[4,144,40]{2,1,0:T(8,128)}, u32[]{:S(2)}) copy-start(f32[4,144,40]{2,1,0:T(8,128)} %constant.31.clone.refs_10_) | copy-start | bytes 276484
  28.9 4.4 %copy-start.8 = (f32[128,80]{1,0:T(8,128)S(1)}, f32[128,80]{1,0:T(8,128)}, u32[]{:S(2)}) copy-start(f32[128,80]{1,0:T(8,128)} %constant.41.clone.refs_9_) | copy-start | bytes 122884
  30.0 3.2 %collective-permute-start.12 = (f32[6,40,128]{2,1,0:T(8,128)S(1)}, f32[6,40,128]{2,1,0:T(8,128)S(1)}, u32[]{:S(2)}, u32[]{:S(2)}) collective-permute-start(f32[6,40,128]{2,1,0:T(8,128)S(1)} %collective-permute-done.10.refs_7_), channel_id=1, source_target_pairs={{0,1},{1,0},{2,3},{3,2},{4,5},{5,4},{6,7},{7,6},{8,9},{9,8},{10,11... | collective-permute-start | bytes 368648 | tf_op jit(solution)/shard_map/ppermute | solution.py:187

commit v12 on v11

--- a/solution.py
+++ b/solution.py
@@ -613,11 +613,16 @@
         plane_halo = dot(px1_ref[...], jnp.concatenate([zbuf[at + 1], zbuf[at + 3]], axis=0))
         everything = []
         for j in range(dz):
+            sides = []
+            for near, blocks in ((j - 1, range(j)), (j + 1, range(j + 1, dz))):
+                if len(blocks):
+                    reach = zone.reach(j, near)
+                    gain = lambda i: float(zone.reach(j, i)[0] / reach[0])
+                    sides.append((reach, sum(gain(i) * qbuf[2 * i + (i < j)] for i in blocks)))
             for zc in range(lz2):
                 total = zbuf[j * lz2 + zc]
-                for i in range(dz):
-                    if i != j:
-                        total += float(zone.reach(j, i)[zc]) * qbuf[2 * i + (i < j)]
+                for reach, lines in sides:
+                    total += float(reach[zc]) * lines
                 everything.append(total)
         for z in range(0, z2, lz2):
             zbuf[z] = everything[z]

time: 36.1 us -> 35.8 us (level)
  no operation moved by 1% of the time
where the time goes in v12:
time: 35.8 us; the launch traced here: 35.2 us
  starting transfers between devices  20.3 us (57%)
  Pallas kernels  9.95 us (28%)
  waiting for transfers between devices  4.22 us (12%)
  between operations  0.72 us (2%)
    ppermute x10, starting transfers between devices, swapped(): lax.ppermute(v, axis, [(i, i ^ k) for i in range(count)])  14.4 us
    pallas_call x9, Pallas kernels, kernel_call(): pl.pallas_call(body, out_shape=[jax.ShapeDtypeStruct(shape, jnp.float32)...  9.95 us
    ppermute x3, starting transfers between devices, gathered(): lax.ppermute(what, axis, [(i, i ^ k) for i in range(count)])  5.94 us
    ppermute x10, waiting for transfers between devices, swapped(): lax.ppermute(v, axis, [(i, i ^ k) for i in range(count)])  3.24 us
    ppermute x3, waiting for transfers between devices, gathered(): lax.ppermute(what, axis, [(i, i ^ k) for i in range(count)])  0.98 us
  transfers between devices with their start and end apart: 13, of which 5 were waited for; matrix products, arithmetic and copies ran while one was open for 0% of the time, Pallas kernels for 12%

profile of v12, /device:TPU:1, one launch (start us, length us, event | category | flops | bytes accessed | tf_op | source)
XLA Modules:
  0.0 35.2 jit_solution(8383846945760820849)
XLA Ops:
  0.6 1.8 %shard_map.183 = (f32[8,128,128]{2,1,0:T(8,128)S(1)}, f32[160,384]{1,0:T(8,128)S(1)}, f32[128,8]{1,0:T(8,128)S(1)}, f32[24,1024]{1,0:T(8,128)S(1)}, f32[16,1024]{1,0:T(8,128)S(1)}) custom-call(f32[8,128,128]{2,1,0:T(8,128)} %u_hbm.1, f32[2,32,128]{2,1,0:T(8,128)} %constant.28.clone.table_hbm, f32[2,160,384]{2,1,0:T(8,128)} %constant.29.clone.ty_hbm, ...), custom_call_target="tpu_custom_call" | custom-call | tf_op jit(solution)/shard_map/pallas_call | solution.py:167
  2.4 2.1 %collective-permute-start = (f32[16,1024]{1,0:T(8,128)S(1)}, f32[16,1024]{1,0:T(8,128)S(1)}, u32[]{:S(2)}, u32[]{:S(2)}) collective-permute-start(f32[16,1024]{1,0:T(8,128)S(1)} %get-tuple-element.39), channel_id=1, source_target_pairs={{0,4},{4,0},{1,5},{5,1},{2,6},{6,2},{3,7},{7,3},{8,12},{12,8},{9,1... | collective-permute-start | bytes 196616 | tf_op jit(solution)/shard_map/ppermute | solution.py:180
  4.5 0.8 %shard_map.184 = (f32[1024,128]{1,0:T(8,128)S(1)}, f32[256,256]{1,0:T(8,128)S(1)}, f32[24,128]{1,0:T(8,128)S(1)}, f32[8,256]{1,0:T(8,128)S(1)}) custom-call(f32[8,128,128]{2,1,0:T(8,128)S(1)} %get-tuple-element.41.u_ref.refs_0_.refs_2_, f32[160,384]{1,0:T(8,128)S(1)} %get-tuple-element.40.ty_ref.refs_1_.refs_2_, f32[128,8]{1,0:T(8,128)S(1)} %get-tuple-element.42.fx_ref), custom_call_target="tpu_custom_call" | custom-call | tf_op jit(solution)/shard_map/pallas_call | solution.py:167
  5.3 0.9 %collective-permute-done.refs_0_.refs_1_ = f32[16,1024]{1,0:T(8,128)S(1)} collective-permute-done((f32[16,1024]{1,0:T(8,128)S(1)}, f32[16,1024]{1,0:T(8,128)S(1)}, u32[]{:S(2)}, u32[]{:S(2)}) %collective-permute-start) | collective-permute-done | bytes 65568 | tf_op jit(solution)/shard_map/ppermute | solution.py:180
  6.2 0.6 %shard_map.186 = (f32[24,128]{1,0:T(8,128)S(1)}, f32[24,128]{1,0:T(8,128)S(1)}, f32[24,128]{1,0:T(8,128)S(1)}) custom-call(f32[8,128,128]{2,1,0:T(8,128)S(1)} %get-tuple-element.41.u_ref.refs_0_.refs_2_, f32[16,1024]{1,0:T(8,128)S(1)} %collective-permute-done.refs_0_.refs_1_, f32[160,384]{1,0:T(8,128)S(1)} %get-tuple-element.40.ty_ref.refs_1_.refs_2_, ...), custom_call_target="tpu_custom_call" | custom-call | tf_op jit(solution)/shard_map/pallas_call | solution.py:167
  6.8 3.6 %collective-permute-start.1 = (f32[24,128]{1,0:T(8,128)S(1)}, f32[24,128]{1,0:T(8,128)S(1)}, u32[]{:S(2)}, u32[]{:S(2)}) collective-permute-start(f32[24,128]{1,0:T(8,128)S(1)} %get-tuple-element.51), channel_id=1, source_target_pairs={{0,24},{8,16},{16,8},{24,0},{1,25},{9,17},{17,9},{25,1},{2,26},{10... | collective-permute-start | bytes 36872 | tf_op jit(solution)/shard_map/ppermute | solution.py:180
  10.3 0.0 collective-permute-start.2
  10.3 0.4 %collective-permute-start.3 = (f32[24,128]{1,0:T(8,128)S(1)}, f32[24,128]{1,0:T(8,128)S(1)}, u32[]{:S(2)}, u32[]{:S(2)}) collective-permute-start(f32[24,128]{1,0:T(8,128)S(1)} %get-tuple-element.53), channel_id=1, source_target_pairs={{0,8},{8,0},{16,24},{24,16},{1,9},{9,1},{17,25},{25,17},{2,10},{10... | collective-permute-start | bytes 36872 | tf_op jit(solution)/shard_map/ppermute | solution.py:180
  10.7 1.8 %shard_map.185 = (f32[1024,128]{1,0:T(8,128)S(1)}, f32[72,128]{1,0:T(8,128)S(1)}, f32[64,768]{1,0:T(8,128)S(1)}, f32[24,768]{1,0:T(8,128)S(1)}) custom-call(f32[16,1024]{1,0:T(8,128)S(1)} %collective-permute-done.refs_0_.refs_1_, f32[160,384]{1,0:T(8,128)S(1)} %get-tuple-element.40.ty_ref.refs_1_.refs_2_, f32[1024,128]{1,0:T(8,128)S(1)} %get-tuple-element.43.refs_2_, ...), custom_call_target="tpu_custom_call" | custom-call | tf_op jit(solution)/shard_map/pallas_call | solution.py:167
  12.5 0.0 collective-permute-done.1.refs_3_
  12.5 1.2 %collective-permute-done.2.refs_4_ = f32[24,128]{1,0:T(8,128)S(1)} collective-permute-done((f32[24,128]{1,0:T(8,128)S(1)}, f32[24,128]{1,0:T(8,128)S(1)}, u32[]{:S(2)}, u32[]{:S(2)}) %collective-permute-start.2) | collective-permute-done | bytes 12320 | tf_op jit(solution)/shard_map/ppermute | solution.py:180
  13.8 0.0 copy-start.3
  13.8 0.4 %shard_map.187 = (f32[72,128]{1,0:T(8,128)S(1)}, f32[4,64,128]{2,1,0:T(8,128)S(1)}, f32[64,128]{1,0:T(8,128)S(1)}, f32[64,128]{1,0:T(8,128)S(1)}, f32[64,128]{1,...) custom-call(f32[72,128]{1,0:T(8,128)S(1)} %get-tuple-element.45.refs_0_, ...), custom_call_target="tpu_custom_call" | custom-call | tf_op jit(solution)/shard_map/pallas_call | solution.py:167
  14.2 3.3 %collective-permute-start.6 = (f32[64,128]{1,0:T(8,128)S(1)}, f32[64,128]{1,0:T(8,128)S(1)}, u32[]{:S(2)}, u32[]{:S(2)}) collective-permute-start(f32[64,128]{1,0:T(8,128)S(1)} %get-tuple-element.57), channel_id=1, source_target_pairs={{0,1},{1,0},{2,3},{3,2},{4,5},{5,4},{6,7},{7,6},{8,9},{9,8},{10,11... | collective-permute-start | bytes 98312 | tf_op jit(solution)/shard_map/ppermute | solution.py:180
  17.5 1.2 %collective-permute-start.4 = (f32[64,128]{1,0:T(8,128)S(1)}, f32[64,128]{1,0:T(8,128)S(1)}, u32[]{:S(2)}, u32[]{:S(2)}) collective-permute-start(f32[64,128]{1,0:T(8,128)S(1)} %get-tuple-element.55), channel_id=1, source_target_pairs={{0,3},{1,2},{2,1},{3,0},{4,7},{5,6},{6,5},{7,4},{8,11},{9,10},{10,... | collective-permute-start | bytes 98312 | tf_op jit(solution)/shard_map/ppermute | solution.py:180
  18.7 0.3 collective-permute-start.5
  19.0 1.4 %collective-permute-start.7 = (f32[8,768]{1,0:T(8,128)S(1)}, f32[8,768]{1,0:T(8,128)S(1)}, u32[]{:S(2)}, u32[]{:S(2)}) collective-permute-start(f32[8,768]{1,0:T(8,128)S(1)} %get-tuple-element.63), channel_id=1, source_target_pairs={{0,24},{8,16},{16,8},{24,0},{1,25},{9,17},{17,9},{25,1},{2,26},{10... | collective-permute-start | bytes 73736 | tf_op jit(solution)/shard_map/ppermute | solution.py:180
  20.4 0.3 collective-permute-start.8
  20.7 1.8 %collective-permute-start.9 = (f32[8,768]{1,0:T(8,128)S(1)}, f32[8,768]{1,0:T(8,128)S(1)}, u32[]{:S(2)}, u32[]{:S(2)}) collective-permute-start(f32[8,768]{1,0:T(8,128)S(1)} %get-tuple-element.65), channel_id=1, source_target_pairs={{0,8},{8,0},{16,24},{24,16},{1,9},{9,1},{17,25},{25,17},{2,10},{10... | collective-permute-start | bytes 73736 | tf_op jit(solution)/shard_map/ppermute | solution.py:180
  22.5 0.0 collective-permute-done.4.refs_1_
  22.5 0.4 %shard_map.188 = (f32[4,64,128]{2,1,0:T(8,128)S(1)}, f32[120,512]{1,0:T(8,128)S(1)}) custom-call(f32[4,64,128]{2,1,0:T(8,128)S(1)} %get-tuple-element.54.refs_0_, f32[64,128]{1,0:T(8,128)S(1)} %collective-permute-done.4.refs_1_, f32[64,128]{1,0:T(8,128)S(1)} %collective-permute-done.5.refs_2_, f32[64,128]{1,0:T(8,128)S(1)} %collective-permute-done.6.refs_3_, ...), custom_call_target="tpu_custom_call" | custom-call | tf_op jit(solution)/shard_map/pallas_call | solution.py:167
  22.9 0.5 %collective-permute-done.7.refs_0_.refs_6_ = f32[8,768]{1,0:T(8,128)S(1)} collective-permute-done((f32[8,768]{1,0:T(8,128)S(1)}, f32[8,768]{1,0:T(8,128)S(1)}, u32[]{:S(2)}, u32[]{:S(2)}) %collective-permute-start.7) | collective-permute-done | bytes 24608 | tf_op jit(solution)/shard_map/ppermute | solution.py:180
  23.5 0.6 %collective-permute-done.8.refs_1_.refs_7_ = f32[8,768]{1,0:T(8,128)S(1)} collective-permute-done((f32[8,768]{1,0:T(8,128)S(1)}, f32[8,768]{1,0:T(8,128)S(1)}, u32[]{:S(2)}, u32[]{:S(2)}) %collective-permute-start.8) | collective-permute-done | bytes 24608 | tf_op jit(solution)/shard_map/ppermute | solution.py:180
  24.0 0.0 collective-permute-done.9.refs_2_.refs_8_
  24.1 1.1 %shard_map.189.refs_5_ = f32[6,40,128]{2,1,0:T(8,128)S(1)} custom-call(f32[120,512]{1,0:T(8,128)S(1)} %get-tuple-element.61.across_ref, f32[72,128]{1,0:T(8,128)S(1)} %get-tuple-element.62.zc_ref, f32[8,768]{1,0:T(8,128)S(1)} %collective-permute-done.7.refs_0_.refs_6_, f32[8,768]{1,0:T(8,128)S(1)} %collective-permute-done.8.refs_1_.refs_7_, ...), custom_call_target="tpu_custom_call" | custom-call | tf_op jit(solution)/shard_map/pallas_call | solution.py:167
  25.2 0.0 copy-start.1
  25.2 1.3 %collective-permute-start.10 = (f32[6,40,128]{2,1,0:T(8,128)S(1)}, f32[6,40,128]{2,1,0:T(8,128)S(1)}, u32[]{:S(2)}, u32[]{:S(2)}) collective-permute-start(f32[6,40,128]{2,1,0:T(8,128)S(1)} %shard_map.189.refs_5_), channel_id=1, source_target_pairs={{0,2},{1,3},{2,0},{3,1},{4,6},{5,7},{6,4},{7,5},{8,10},{9,11},{10,... | collective-permute-start | bytes 368648 | tf_op jit(solution)/shard_map/ppermute | solution.py:187
  26.5 2.4 %collective-permute-start.11 = (f32[6,40,128]{2,1,0:T(8,128)S(1)}, f32[6,40,128]{2,1,0:T(8,128)S(1)}, u32[]{:S(2)}, u32[]{:S(2)}) collective-permute-start(f32[6,40,128]{2,1,0:T(8,128)S(1)} %shard_map.189.refs_5_), channel_id=1, source_target_pairs={{0,1},{1,0},{2,3},{3,2},{4,5},{5,4},{6,7},{7,6},{8,9},{9,8},{10,11... | collective-permute-start | bytes 368648 | tf_op jit(solution)/shard_map/ppermute | solution.py:187
  28.9 1.1 %shard_map.190 = (f32[8,128,128]{2,1,0:T(8,128)}, f32[128,128]{1,0:T(8,128)S(1)}, f32[2,64,128]{2,1,0:T(8,128)S(1)}) custom-call(f32[8,128,128]{2,1,0:T(8,128)S(1)} %get-tuple-element.41.u_ref.refs_0_.refs_2_, f32[1024,128]{1,0:T(8,128)S(1)} %get-tuple-element.66.refs_1_, f32[4,64,128]{2,1,0:T(8,128)S(1)} %get-tuple-element.60.refs_2_.refs_0_, ...), custom_call_target="tpu_custom_call" | custom-call | tf_op jit(solution)/shard_map/pallas_call | solution.py:167
  30.0 2.3 %collective-permute-start.12 = (f32[6,40,128]{2,1,0:T(8,128)S(1)}, f32[6,40,128]{2,1,0:T(8,128)S(1)}, u32[]{:S(2)}, u32[]{:S(2)}) collective-permute-start(f32[6,40,128]{2,1,0:T(8,128)S(1)} %collective-permute-done.10.refs_7_), channel_id=1, source_target_pairs={{0,1},{1,0},{2,3},{3,2},{4,5},{5,4},{6,7},{7,6},{8,9},{9,8},{10,11... | collective-permute-start | bytes 368648 | tf_op jit(solution)/shard_map/ppermute | solution.py:187
  32.3 1.0 %collective-permute-done.12.refs_8_ = f32[6,40,128]{2,1,0:T(8,128)S(1)} collective-permute-done((f32[6,40,128]{2,1,0:T(8,128)S(1)}, f32[6,40,128]{2,1,0:T(8,128)S(1)}, u32[]{:S(2)}, u32[]{:S(2)}) %collective-permute-start.12) | collective-permute-done | bytes 122912 | tf_op jit(solution)/shard_map/ppermute | solution.py:187
  33.2 2.0 %shard_map.191 = (f32[8,128,128]{2,1,0:T(8,128)}, f32[4,64,64]{2,1,0:T(8,128)}, f32[2,32,32]{2,1,0:T(8,128)}, f32[1,16,16]{2,1,0:T(8,128)}) custom-call(f32[4,64,128]{2,1,0:T(8,128)S(1)} %get-tuple-element.60.refs_2_.refs_0_, f32[2,64,128]{2,1,0:T(8,128)S(1)} %get-tuple-element.70.refs_1_, ...), custom_call_target="tpu_custom_call", output_to_operand_aliasing={{0}: (4, {})} | custom-call | tf_op jit(solution)/shard_map/pallas_call | solution.py:167
  (23 shorter events, 0.0 us)
Async XLA Ops:
  2.4 3.8 %collective-permute-start = (f32[16,1024]{1,0:T(8,128)S(1)}, f32[16,1024]{1,0:T(8,128)S(1)}, u32[]{:S(2)}, u32[]{:S(2)}) collective-permute-start(f32[16,1024]{1,0:T(8,128)S(1)} %get-tuple-element.39), channel_id=1, source_target_pairs={{0,4},{4,0},{1,5},{5,1},{2,6},{6,2},{3,7},{7,3},{8,12},{12,8},{9,1... | collective-permute-start | bytes 196616 | tf_op jit(solution)/shard_map/ppermute | solution.py:180
  6.2 4.5 %copy-start.5 = (f32[4,128,128]{2,1,0:T(8,128)S(1)}, f32[4,128,128]{2,1,0:T(8,128)}, u32[]{:S(2)}) copy-start(f32[4,128,128]{2,1,0:T(8,128)} %constant.30.clone.refs_4_) | copy-start | bytes 786436
  6.2 4.5 %copy-start.9 = (f32[4,24,64]{2,1,0:T(8,128)S(1)}, f32[4,24,64]{2,1,0:T(8,128)}, u32[]{:S(2)}) copy-start(f32[4,24,64]{2,1,0:T(8,128)} %constant.35.clone.refs_5_) | copy-start | bytes 73732
  6.8 5.8 %collective-permute-start.1 = (f32[24,128]{1,0:T(8,128)S(1)}, f32[24,128]{1,0:T(8,128)S(1)}, u32[]{:S(2)}, u32[]{:S(2)}) collective-permute-start(f32[24,128]{1,0:T(8,128)S(1)} %get-tuple-element.51), channel_id=1, source_target_pairs={{0,24},{8,16},{16,8},{24,0},{1,25},{9,17},{17,9},{25,1},{2,26},{10... | collective-permute-start | bytes 36872 | tf_op jit(solution)/shard_map/ppermute | solution.py:180
  10.3 3.4 %collective-permute-start.2 = (f32[24,128]{1,0:T(8,128)S(1)}, f32[24,128]{1,0:T(8,128)S(1)}, u32[]{:S(2)}, u32[]{:S(2)}) collective-permute-start(f32[24,128]{1,0:T(8,128)S(1)} %get-tuple-element.52), channel_id=1, source_target_pairs={{0,16},{8,24},{16,0},{24,8},{1,17},{9,25},{17,1},{25,9},{2,18},{10... | collective-permute-start | bytes 36872 | tf_op jit(solution)/shard_map/ppermute | solution.py:180
  10.3 3.4 %collective-permute-start.3 = (f32[24,128]{1,0:T(8,128)S(1)}, f32[24,128]{1,0:T(8,128)S(1)}, u32[]{:S(2)}, u32[]{:S(2)}) collective-permute-start(f32[24,128]{1,0:T(8,128)S(1)} %get-tuple-element.53), channel_id=1, source_target_pairs={{0,8},{8,0},{16,24},{24,16},{1,9},{9,1},{17,25},{25,17},{2,10},{10... | collective-permute-start | bytes 36872 | tf_op jit(solution)/shard_map/ppermute | solution.py:180
  10.7 3.1 %copy-start.6 = (f32[4,88,16]{2,1,0:T(8,128)S(1)}, f32[4,88,16]{2,1,0:T(8,128)}, u32[]{:S(2)}) copy-start(f32[4,88,16]{2,1,0:T(8,128)} %constant.36.clone.refs_6_) | copy-start | bytes 67588
  13.8 8.7 %copy-start = (f32[4,120,88]{2,1,0:T(8,128)S(1)}, f32[4,120,88]{2,1,0:T(8,128)}, u32[]{:S(2)}) copy-start(f32[4,120,88]{2,1,0:T(8,128)} %constant.37.clone.refs_4_.refs_3_) | copy-start | bytes 506884
  13.8 10.3 %copy-start.3 = (f32[2,384,128]{2,1,0:T(8,128)S(1)}, f32[2,384,128]{2,1,0:T(8,128)}, u32[]{:S(2)}) copy-start(f32[2,384,128]{2,1,0:T(8,128)} %constant.38.clone.refs_4_) | copy-start | bytes 1179652
  14.2 6.5 %collective-permute-start.6 = (f32[64,128]{1,0:T(8,128)S(1)}, f32[64,128]{1,0:T(8,128)S(1)}, u32[]{:S(2)}, u32[]{:S(2)}) collective-permute-start(f32[64,128]{1,0:T(8,128)S(1)} %get-tuple-element.57), channel_id=1, source_target_pairs={{0,1},{1,0},{2,3},{3,2},{4,5},{5,4},{6,7},{7,6},{8,9},{9,8},{10,11... | collective-permute-start | bytes 98312 | tf_op jit(solution)/shard_map/ppermute | solution.py:180
  17.5 5.0 %collective-permute-start.4 = (f32[64,128]{1,0:T(8,128)S(1)}, f32[64,128]{1,0:T(8,128)S(1)}, u32[]{:S(2)}, u32[]{:S(2)}) collective-permute-start(f32[64,128]{1,0:T(8,128)S(1)} %get-tuple-element.55), channel_id=1, source_target_pairs={{0,3},{1,2},{2,1},{3,0},{4,7},{5,6},{6,5},{7,4},{8,11},{9,10},{10,... | collective-permute-start | bytes 98312 | tf_op jit(solution)/shard_map/ppermute | solution.py:180
  18.7 3.8 %collective-permute-start.5 = (f32[64,128]{1,0:T(8,128)S(1)}, f32[64,128]{1,0:T(8,128)S(1)}, u32[]{:S(2)}, u32[]{:S(2)}) collective-permute-start(f32[64,128]{1,0:T(8,128)S(1)} %get-tuple-element.56), channel_id=1, source_target_pairs={{0,2},{1,3},{2,0},{3,1},{4,6},{5,7},{6,4},{7,5},{8,10},{9,11},{10,... | collective-permute-start | bytes 98312 | tf_op jit(solution)/shard_map/ppermute | solution.py:180
  19.0 4.5 %collective-permute-start.7 = (f32[8,768]{1,0:T(8,128)S(1)}, f32[8,768]{1,0:T(8,128)S(1)}, u32[]{:S(2)}, u32[]{:S(2)}) collective-permute-start(f32[8,768]{1,0:T(8,128)S(1)} %get-tuple-element.63), channel_id=1, source_target_pairs={{0,24},{8,16},{16,8},{24,0},{1,25},{9,17},{17,9},{25,1},{2,26},{10... | collective-permute-start | bytes 73736 | tf_op jit(solution)/shard_map/ppermute | solution.py:180
  20.4 3.6 %collective-permute-start.8 = (f32[8,768]{1,0:T(8,128)S(1)}, f32[8,768]{1,0:T(8,128)S(1)}, u32[]{:S(2)}, u32[]{:S(2)}) collective-permute-start(f32[8,768]{1,0:T(8,128)S(1)} %get-tuple-element.64), channel_id=1, source_target_pairs={{0,16},{8,24},{16,0},{24,8},{1,17},{9,25},{17,1},{25,9},{2,18},{10... | collective-permute-start | bytes 73736 | tf_op jit(solution)/shard_map/ppermute | solution.py:180
  20.7 3.3 %collective-permute-start.9 = (f32[8,768]{1,0:T(8,128)S(1)}, f32[8,768]{1,0:T(8,128)S(1)}, u32[]{:S(2)}, u32[]{:S(2)}) collective-permute-start(f32[8,768]{1,0:T(8,128)S(1)} %get-tuple-element.65), channel_id=1, source_target_pairs={{0,8},{8,0},{16,24},{24,16},{1,9},{9,1},{17,25},{25,17},{2,10},{10... | collective-permute-start | bytes 73736 | tf_op jit(solution)/shard_map/ppermute | solution.py:180
  24.1 4.8 %copy-start.2 = (f32[2,128,128]{2,1,0:T(8,128)S(1)}, f32[2,128,128]{2,1,0:T(8,128)}, u32[]{:S(2)}) copy-start(f32[2,128,128]{2,1,0:T(8,128)} %constant.40.clone.refs_10_.refs_12_) | copy-start | bytes 393220
  24.1 4.8 %copy-start.7 = (f32[4,64,88]{2,1,0:T(8,128)S(1)}, f32[4,64,88]{2,1,0:T(8,128)}, u32[]{:S(2)}) copy-start(f32[4,64,88]{2,1,0:T(8,128)} %constant.39.clone.refs_9_) | copy-start | bytes 270340
  25.2 8.1 %copy-start.1 = (f32[2,768,128]{2,1,0:T(8,128)S(1)}, f32[2,768,128]{2,1,0:T(8,128)}, u32[]{:S(2)}) copy-start(f32[2,768,128]{2,1,0:T(8,128)} %constant.32.clone.refs_11_) | copy-start | bytes 2359300
  25.2 4.8 %collective-permute-start.10 = (f32[6,40,128]{2,1,0:T(8,128)S(1)}, f32[6,40,128]{2,1,0:T(8,128)S(1)}, u32[]{:S(2)}, u32[]{:S(2)}) collective-permute-start(f32[6,40,128]{2,1,0:T(8,128)S(1)} %shard_map.189.refs_5_), channel_id=1, source_target_pairs={{0,2},{1,3},{2,0},{3,1},{4,6},{5,7},{6,4},{7,5},{8,10},{9,11},{10,... | collective-permute-start | bytes 368648 | tf_op jit(solution)/shard_map/ppermute | solution.py:187
  26.5 5.8 %collective-permute-start.11 = (f32[6,40,128]{2,1,0:T(8,128)S(1)}, f32[6,40,128]{2,1,0:T(8,128)S(1)}, u32[]{:S(2)}, u32[]{:S(2)}) collective-permute-start(f32[6,40,128]{2,1,0:T(8,128)S(1)} %shard_map.189.refs_5_), channel_id=1, source_target_pairs={{0,1},{1,0},{2,3},{3,2},{4,5},{5,4},{6,7},{7,6},{8,9},{9,8},{10,11... | collective-permute-start | bytes 368648 | tf_op jit(solution)/shard_map/ppermute | solution.py:187
  28.9 4.4 %copy-start.4 = (f32[4,144,40]{2,1,0:T(8,128)S(1)}, f32[4,144,40]{2,1,0:T(8,128)}, u32[]{:S(2)}) copy-start(f32[4,144,40]{2,1,0:T(8,128)} %constant.31.clone.refs_10_) | copy-start | bytes 276484
  28.9 4.4 %copy-start.8 = (f32[128,80]{1,0:T(8,128)S(1)}, f32[128,80]{1,0:T(8,128)}, u32[]{:S(2)}) copy-start(f32[128,80]{1,0:T(8,128)} %constant.41.clone.refs_9_) | copy-start | bytes 122884
  30.0 3.2 %collective-permute-start.12 = (f32[6,40,128]{2,1,0:T(8,128)S(1)}, f32[6,40,128]{2,1,0:T(8,128)S(1)}, u32[]{:S(2)}, u32[]{:S(2)}) collective-permute-start(f32[6,40,128]{2,1,0:T(8,128)S(1)} %collective-permute-done.10.refs_7_), channel_id=1, source_target_pairs={{0,1},{1,0},{2,3},{3,2},{4,5},{5,4},{6,7},{7,6},{8,9},{9,8},{10,11... | collective-permute-start | bytes 368648 | tf_op jit(solution)/shard_map/ppermute | solution.py:187
